TPU v7x, 32 devices: a whole 2x2x4 slice. The times are simulated.
32 devices in a mesh: tile: 8 (over y, x, core), slab: 4 (over z).
Axes of the slice: x: 2, y: 2, z: 4, core: 2. Of those that a mesh axis runs over, the one named last changes fastest.
Arguments:
- intensities: bfloat16 [448, 256, 256], P(('tile', 'slab')), may hold values from 0 to 0.5
- object_field: float32 [2, 2, 2048, 384], P(None, None, ('tile', 'slab')), may hold values from -3 to 3
- probe_wave: float32 [256, 512], replicated, may hold values from -6 to 6
- owner_tile: int32 [448], replicated, may hold values from 0 to 7, as said below
- row_offset: int32 [448], replicated, may hold values from 0 to 255
- col_offset: int32 [448], replicated, may hold values from 0 to 1
Outputs:
- gradient: float32 [2, 2, 2048, 384], P(None, None, ('tile', 'slab'))
Inputs may be any that keep to these rules, and one draw needn't show every extreme that they name: `owner_tile`: read row r is read by device r // 14 of the tile+slab order. Among the 8 devices of one slab index, the rows of one device name one tile at most 2 times, and each tile is named by at most 16 of their rows; some tile reaches 16 and some device reaches 2 for some tile, for every slab index.
All inputs are finite; a program needn't handle non-finite values.
Results may differ from a plain program's by a relative error of at most 0.006.
The roundings to bfloat16 on the way count: a program that leaves them out, or rounds other values in their place, can miss the bound.
Values may be sent and summed in bfloat16 or wider, within the bound.
No kernel may reach another device: no remote copies, remote signals or barrier semaphores. Data moves between devices by JAX's collectives and lax.ppermute only.
A program may use at most 64 MiB of HBM per device.

v0:
```python
import math

import jax
import jax.numpy as jnp
from jax import lax
from jax.sharding import PartitionSpec as P

COL_STEP = 128
K = 16
CAP = 2


chirp_strength = 40.0


def passed_along(value, axis, steps):
    count = lax.axis_size(axis)
    pairs = [(source, (source + steps) % count) for source in range(count)]
    return lax.ppermute(value, axis, pairs)


def make_tables(extent):
    counter = jnp.arange(extent, dtype=jnp.int32)
    product_index = counter[:, None] * counter[None, :] % extent
    angles = product_index.astype(jnp.float32) * (2.0 * math.pi / extent)
    scaling = 1.0 / math.sqrt(extent)
    cosine = (jnp.cos(angles) * scaling).astype(jnp.bfloat16)
    sine_part = (jnp.sin(angles) * scaling).astype(jnp.bfloat16)
    forward = jnp.concatenate(
        [jnp.concatenate([cosine, -sine_part], 1), jnp.concatenate([sine_part, cosine], 1)], 0
    )
    inverse = jnp.concatenate(
        [jnp.concatenate([cosine, sine_part], 1), jnp.concatenate([-sine_part, cosine], 1)], 0
    )
    frequency = ((counter + extent // 2) % extent - extent // 2).astype(jnp.float32) / extent
    phases = chirp_strength * (frequency[:, None] ** 2 + frequency[None, :] ** 2)
    kernel = jnp.concatenate([jnp.cos(phases), -jnp.sin(phases)], 1)
    return (cosine, sine_part, forward, inverse, kernel)


def transform(field, tables, backward):
    cosine, sine_part, forward, inverse, kernel = tables
    extent = cosine.shape[0]
    halfway = jnp.dot(
        field, inverse if backward else forward, preferred_element_type=jnp.float32
    ).astype(jnp.bfloat16)
    with_cosine = jnp.dot(cosine, halfway, preferred_element_type=jnp.float32)
    with_sine = jnp.dot(sine_part, halfway, preferred_element_type=jnp.float32)
    if backward:
        real_part = with_cosine[:, :extent] - with_sine[:, extent:]
        imag_part = with_cosine[:, extent:] + with_sine[:, :extent]
    else:
        real_part = with_cosine[:, :extent] + with_sine[:, extent:]
        imag_part = with_cosine[:, extent:] - with_sine[:, :extent]
    return jnp.concatenate([real_part, imag_part], 1)


def complex_product(left, right, conjugate):
    extent = left.shape[1] // 2
    left_real = left[:, :extent]
    left_imag = -left[:, extent:] if conjugate else left[:, extent:]
    right_real = right[:, :extent]
    right_imag = right[:, extent:]
    return jnp.concatenate(
        [
            left_real * right_real - left_imag * right_imag,
            left_real * right_imag + left_imag * right_real,
        ],
        1,
    )


def position_gradient(window, probe_wave, measured, tables):
    kernel = tables[4]
    extent = measured.shape[0]
    layers = window.shape[0]
    pieces = [
        jnp.concatenate([window[slice_index, 0], window[slice_index, 1]], 1)
        for slice_index in range(layers)
    ]
    incoming = [probe_wave]
    entering = complex_product(probe_wave, pieces[0], False).astype(jnp.bfloat16)
    slice_index = 1
    spread_wave = complex_product(kernel, transform(entering, tables, False), False).astype(
        jnp.bfloat16
    )
    arrived = transform(spread_wave, tables, True)
    incoming.append(arrived)
    entering = complex_product(arrived, pieces[slice_index], False).astype(jnp.bfloat16)
    farfield = transform(entering, tables, False)
    modelled = farfield[:, :extent] ** 2 + farfield[:, extent:] ** 2
    misfit = modelled - measured.astype(jnp.float32)
    far_grad = (farfield * jnp.concatenate([misfit, misfit], 1)).astype(jnp.bfloat16)
    exit_grad = transform(far_grad, tables, True)
    slice_terms = [None] * layers
    for slice_index in range(layers - 1, -1, -1):
        slice_terms[slice_index] = complex_product(incoming[slice_index], exit_grad, True)
        if slice_index > 0:
            back_wave = complex_product(pieces[slice_index], exit_grad, True).astype(jnp.bfloat16)
            back_spread = complex_product(kernel, transform(back_wave, tables, False), True).astype(
                jnp.bfloat16
            )
            exit_grad = transform(back_spread, tables, True)
    return jnp.stack(
        [jnp.stack([one_term[:, :extent], one_term[:, extent:]]) for one_term in slice_terms]
    )


def send_ranks(column_group):
    reads_dev = column_group.shape[1]
    counter = jnp.arange(reads_dev, dtype=jnp.int32)
    earlier = counter[None, :] < counter[:, None]
    matching = column_group[:, :, None] == column_group[:, None, :]
    return jnp.sum((matching & earlier[None]).astype(jnp.int32), 2, dtype=jnp.int32)


def arrivals(column_group, order_set, tile_here, slab_number, slab_count, capacity):
    tile_count = column_group.shape[0]
    reads_dev = column_group.shape[1]
    sender = jnp.arange(tile_count, dtype=jnp.int32)[:, None]
    position = jnp.arange(reads_dev, dtype=jnp.int32)[None, :]
    ours = (column_group == tile_here).reshape(-1)
    landing = (sender * capacity + order_set).reshape(-1)
    read_row = ((sender * slab_count + slab_number) * reads_dev + position).reshape(-1)
    buffer_index = jnp.arange(tile_count * capacity, dtype=jnp.int32)
    matched = ours[None, :] & (landing[None, :] == buffer_index[:, None])
    active_position = jnp.any(matched, 1)
    slot_row = jnp.sum(jnp.where(matched, read_row[None, :], 0), 1, dtype=jnp.int32)
    return (active_position, slot_row)


def compact_order(active_position, space_count):
    live_flags = active_position.astype(jnp.int32)
    before = jnp.cumsum(live_flags, dtype=jnp.int32) - live_flags
    wanted = jnp.arange(space_count, dtype=jnp.int32)
    return active_position[None, :] & (before[None, :] == wanted[:, None])


def shards(intensities, object_field, probe_wave, owner_tile, row_offset, col_offset):
    tile_count = lax.axis_size("tile")
    slab_count = lax.axis_size("slab")
    tile_here = lax.axis_index("tile")
    slab_here = lax.axis_index("slab")
    reads_dev = intensities.shape[0]
    extent = intensities.shape[1]
    pixels = extent * extent
    capacity = CAP
    space_count = K
    owner_table = owner_tile.reshape(tile_count, slab_count, reads_dev)
    columns = lax.dynamic_index_in_dim(owner_table, slab_here, 1, keepdims=False)
    send_order = send_ranks(columns)
    my_dest = lax.dynamic_index_in_dim(columns, tile_here, 0, keepdims=False)
    my_rank = lax.dynamic_index_in_dim(send_order, tile_here, 0, keepdims=False)
    target = my_dest * capacity + my_rank
    buffer_index = jnp.arange(tile_count * capacity, dtype=jnp.int32)
    packing = (buffer_index[:, None] == target[None, :]).astype(jnp.bfloat16)
    outgoing = jnp.dot(
        packing, intensities.reshape(reads_dev, pixels), preferred_element_type=jnp.float32
    ).astype(jnp.bfloat16)
    received = lax.all_to_all(outgoing, "tile", split_axis=0, concat_axis=0, tiled=True)
    slab_numbers = jnp.arange(slab_count, dtype=jnp.int32)
    all_live, all_rows = jax.vmap(
        lambda column_group, slab_number: arrivals(
            column_group, send_ranks(column_group), tile_here, slab_number, slab_count, capacity
        )
    )(jnp.transpose(owner_table, (1, 0, 2)), slab_numbers)
    all_picks = jax.vmap(lambda live_set: compact_order(live_set, space_count))(all_live)
    item_rows = jnp.sum(jnp.where(all_picks, all_rows[:, None, :], 0), 2, dtype=jnp.int32)
    counts_all = jnp.sum(all_live.astype(jnp.int32), 1, dtype=jnp.int32)
    starts = jnp.cumsum(counts_all, dtype=jnp.int32) - counts_all
    my_pick = lax.dynamic_index_in_dim(all_picks, slab_here, 0, keepdims=False)
    holding = jnp.dot(
        my_pick.astype(jnp.bfloat16), received, preferred_element_type=jnp.float32
    ).astype(jnp.bfloat16)
    my_count = lax.dynamic_index_in_dim(counts_all, slab_here, 0, keepdims=False)
    my_start = lax.dynamic_index_in_dim(starts, slab_here, 0, keepdims=False)
    per_peer = space_count // slab_count
    item_index = jnp.arange(space_count, dtype=jnp.int32)
    group_place = my_start + item_index
    send_slot = group_place % slab_count * per_peer + item_index // slab_count
    regroup = (
        (item_index[None, :] < my_count) & (send_slot[None, :] == item_index[:, None])
    ).astype(jnp.bfloat16)
    leaving = jnp.dot(regroup, holding, preferred_element_type=jnp.float32).astype(jnp.bfloat16)
    shared = lax.all_to_all(leaving, "slab", split_axis=0, concat_axis=0, tiled=True)
    source_first = (slab_here - starts[:, None]) % slab_count
    item_of = source_first + jnp.arange(per_peer, dtype=jnp.int32)[None, :] * slab_count
    live_share = (item_of < counts_all[:, None]).reshape(-1)
    share_rows = jnp.take_along_axis(item_rows, jnp.minimum(item_of, space_count - 1), 1).reshape(
        -1
    )
    share_place = ((starts[:, None] + item_of) // slab_count).reshape(-1)
    chosen_final = live_share[None, :] & (share_place[None, :] == item_index[:, None])
    patterns = jnp.dot(
        chosen_final.astype(jnp.bfloat16), shared, preferred_element_type=jnp.float32
    ).astype(jnp.bfloat16)
    pattern_rows = jnp.sum(jnp.where(chosen_final, share_rows[None, :], 0), 1, dtype=jnp.int32)
    pattern_count = jnp.sum(live_share.astype(jnp.int32), dtype=jnp.int32)
    own_rows = lax.all_gather(object_field, "slab", axis=2, tiled=True)
    next_part = passed_along(own_rows, "tile", -1)
    extended = jnp.concatenate([own_rows, next_part], 2)
    tables = make_tables(extent)
    depth = object_field.shape[0]
    images = patterns.reshape(space_count, extent, extent)

    def accumulate(item_number, totals):
        source_row = lax.dynamic_index_in_dim(pattern_rows, item_number, 0, keepdims=False)
        top_row = lax.dynamic_index_in_dim(row_offset, source_row, 0, keepdims=False)
        left_col = lax.dynamic_index_in_dim(col_offset, source_row, 0, keepdims=False) * COL_STEP
        zero_index = jnp.zeros((), jnp.int32)
        starting = (zero_index, zero_index, top_row, left_col)
        window = lax.dynamic_slice(extended, starting, (depth, 2, extent, extent))
        measured = lax.dynamic_index_in_dim(images, item_number, 0, keepdims=False)
        gradient_part = position_gradient(window, probe_wave, measured, tables)
        current = lax.dynamic_slice(totals, starting, (depth, 2, extent, extent))
        return lax.dynamic_update_slice(totals, current + gradient_part, starting)

    totals = lax.fori_loop(0, pattern_count, accumulate, jnp.zeros(extended.shape, jnp.float32))
    tile_height = own_rows.shape[2]
    lower = totals[:, :, tile_height:]
    padding = jnp.zeros((depth, 2, tile_height - extent, totals.shape[3]), jnp.float32)
    moved = passed_along(lower, "tile", 1)
    combined = totals[:, :, :tile_height] + jnp.concatenate([moved, padding], 2)
    return lax.psum_scatter(combined, "slab", scatter_dimension=2, tiled=True)


def solution(mesh):
    placed = (
        P(("tile", "slab"), None, None),
        P(None, None, ("tile", "slab"), None),
        P(),
        P(),
        P(),
        P(),
    )
    return jax.shard_map(
        shards,
        mesh=mesh,
        in_specs=placed,
        out_specs=P(None, None, ("tile", "slab"), None),
        check_vma=False,
    )
```

profile of v0, /device:TPU:0, one launch (start us, length us, event | category | flops | bytes accessed | tf_op | source)
XLA Modules:
  0.0 879.3 jit_solution(5115952478242218003)
XLA Ops:
  6.5 2.0 copy.68
  9.6 1.7 pad.30
  13.8 2.4 all_to_all.16
  16.2 5.2 all-to-all-start
  26.4 21.6 %all-to-all-done = bf16[8,2,65536]{2,1,0:T(2,128)(2,1)S(1)} async-done(((bf16[8,2,65536]{2,1,0:T(2,128)(2,1)}), bf16[8,2,65536]{2,1,0:T(2,128)(2,1)S(1)}, u32[]{:S(2)}, u32[]{:S(2)}) %all-to-all-start) | async-done | bytes 2097184 | tf_op jit(solution)/shard_map/all_to_all | solution.py:160
  48.0 1.9 all_to_all.18
  49.8 2.8 convolution_convert_fusion.7
  52.7 1.8 all_to_all.19
  54.4 5.0 all-to-all-start.1
  67.3 12.3 %collective-permute-done = f32[2,2,256,384]{3,1,0,2:T(2,128)S(1)} collective-permute-done((f32[2,2,256,384]{3,1,0,2:T(2,128)}, f32[2,2,256,384]{3,1,0,2:T(2,128)S(1)}, u32[]{:S(2)}, u32[]{:S(2)}) %collective-permute-start) | collective-permute-done | bytes 1572896 | tf_op jit(solution)/shard_map/ppermute | solution.py:19
  79.6 3.0 pad_maximum_fusion
  82.6 22.4 %all-to-all-done.1 = bf16[4,4,65536]{2,1,0:T(4,128)(2,1)} async-done(((bf16[4,4,65536]{2,1,0:T(4,128)(2,1)}), bf16[4,4,65536]{2,1,0:T(4,128)(2,1)}, u32[]{:S(2)}, u32[]{:S(2)}) %all-to-all-start.1) | async-done | bytes 2097184 | tf_op jit(solution)/shard_map/all_to_all | solution.py:185
  105.0 1.8 all_to_all.21
  107.5 1.8 copy.88
  109.3 1.9 broadcast_in_dim.30.clone
  111.2 654.4 %while.14 = (s32[]{:T(128)}, f32[2,2,512,384]{3,2,1,0:T(8,128)}, s32[]{:T(128)}, s32[16]{0:T(128)S(1)}, s32[448]{0:T(512)}, /*index=5*/s32[448]{0:T(512)}, f32[2...) while((s32[]{:T(128)}, f32[2,2,512,384]{3,2,1,0:T(8,128)}, ...), condition=%wide.region_11.12_spmd.clone.clone.clone, body=%wide.region_10.11_spmd.clone.clone.clone.sunk | while | flops 1632960512 | bytes 54661612 | solution.py:218
  117.5 1.3 dynamic_slice.96
  120.5 3.0 constant_dynamic-slice_fusion.11
  145.5 1.6 constant_dynamic-slice_fusion.10
  147.9 10.4 %dynamic_update_slice.8 = f32[2,2,512,384]{3,2,1,0:T(8,128)} dynamic-update-slice(f32[2,2,512,384]{3,2,1,0:T(8,128)} %get-tuple-element.643, f32[2,2,256,256]{3,2,1,0:T(8,128)S(1)} %copy.106, s32[]{:T(128)} %constant.175.clone.1..sunk, s32[]{:T(128)} %constant.175.clone.1..sunk, s32[]{:T(128)S(6)} %select_n.327, s32[]{:T(128)S(6)} %select_n.328) | dynamic-update-slice | bytes 2097156 | tf_op jit(solution)/shard_map/while/body/dynamic_update_slice | solution.py:216
  167.7 3.1 constant_dynamic-slice_fusion.11
  192.8 1.6 constant_dynamic-slice_fusion.10
  195.2 9.3 %dynamic_update_slice.8 = f32[2,2,512,384]{3,2,1,0:T(8,128)} dynamic-update-slice(f32[2,2,512,384]{3,2,1,0:T(8,128)} %get-tuple-element.643, f32[2,2,256,256]{3,2,1,0:T(8,128)S(1)} %copy.106, s32[]{:T(128)} %constant.175.clone.1..sunk, s32[]{:T(128)} %constant.175.clone.1..sunk, s32[]{:T(128)S(6)} %select_n.327, s32[]{:T(128)S(6)} %select_n.328) | dynamic-update-slice | bytes 2097156 | tf_op jit(solution)/shard_map/while/body/dynamic_update_slice | solution.py:216
  213.8 3.0 constant_dynamic-slice_fusion.11
  238.9 1.6 constant_dynamic-slice_fusion.10
  241.3 9.7 %dynamic_update_slice.8 = f32[2,2,512,384]{3,2,1,0:T(8,128)} dynamic-update-slice(f32[2,2,512,384]{3,2,1,0:T(8,128)} %get-tuple-element.643, f32[2,2,256,256]{3,2,1,0:T(8,128)S(1)} %copy.106, s32[]{:T(128)} %constant.175.clone.1..sunk, s32[]{:T(128)} %constant.175.clone.1..sunk, s32[]{:T(128)S(6)} %select_n.327, s32[]{:T(128)S(6)} %select_n.328) | dynamic-update-slice | bytes 2097156 | tf_op jit(solution)/shard_map/while/body/dynamic_update_slice | solution.py:216
  260.3 3.0 constant_dynamic-slice_fusion.11
  285.3 1.6 constant_dynamic-slice_fusion.10
  287.8 9.8 %dynamic_update_slice.8 = f32[2,2,512,384]{3,2,1,0:T(8,128)} dynamic-update-slice(f32[2,2,512,384]{3,2,1,0:T(8,128)} %get-tuple-element.643, f32[2,2,256,256]{3,2,1,0:T(8,128)S(1)} %copy.106, s32[]{:T(128)} %constant.175.clone.1..sunk, s32[]{:T(128)} %constant.175.clone.1..sunk, s32[]{:T(128)S(6)} %select_n.327, s32[]{:T(128)S(6)} %select_n.328) | dynamic-update-slice | bytes 2097156 | tf_op jit(solution)/shard_map/while/body/dynamic_update_slice | solution.py:216
  306.9 3.0 constant_dynamic-slice_fusion.11
  331.9 1.6 constant_dynamic-slice_fusion.10
  334.4 9.8 %dynamic_update_slice.8 = f32[2,2,512,384]{3,2,1,0:T(8,128)} dynamic-update-slice(f32[2,2,512,384]{3,2,1,0:T(8,128)} %get-tuple-element.643, f32[2,2,256,256]{3,2,1,0:T(8,128)S(1)} %copy.106, s32[]{:T(128)} %constant.175.clone.1..sunk, s32[]{:T(128)} %constant.175.clone.1..sunk, s32[]{:T(128)S(6)} %select_n.327, s32[]{:T(128)S(6)} %select_n.328) | dynamic-update-slice | bytes 2097156 | tf_op jit(solution)/shard_map/while/body/dynamic_update_slice | solution.py:216
  353.5 3.0 constant_dynamic-slice_fusion.11
  378.5 1.6 constant_dynamic-slice_fusion.10
  380.9 10.3 %dynamic_update_slice.8 = f32[2,2,512,384]{3,2,1,0:T(8,128)} dynamic-update-slice(f32[2,2,512,384]{3,2,1,0:T(8,128)} %get-tuple-element.643, f32[2,2,256,256]{3,2,1,0:T(8,128)S(1)} %copy.106, s32[]{:T(128)} %constant.175.clone.1..sunk, s32[]{:T(128)} %constant.175.clone.1..sunk, s32[]{:T(128)S(6)} %select_n.327, s32[]{:T(128)S(6)} %select_n.328) | dynamic-update-slice | bytes 2097156 | tf_op jit(solution)/shard_map/while/body/dynamic_update_slice | solution.py:216
  400.5 3.0 constant_dynamic-slice_fusion.11
  425.6 1.6 constant_dynamic-slice_fusion.10
  428.0 9.7 %dynamic_update_slice.8 = f32[2,2,512,384]{3,2,1,0:T(8,128)} dynamic-update-slice(f32[2,2,512,384]{3,2,1,0:T(8,128)} %get-tuple-element.643, f32[2,2,256,256]{3,2,1,0:T(8,128)S(1)} %copy.106, s32[]{:T(128)} %constant.175.clone.1..sunk, s32[]{:T(128)} %constant.175.clone.1..sunk, s32[]{:T(128)S(6)} %select_n.327, s32[]{:T(128)S(6)} %select_n.328) | dynamic-update-slice | bytes 2097156 | tf_op jit(solution)/shard_map/while/body/dynamic_update_slice | solution.py:216
  446.9 3.0 constant_dynamic-slice_fusion.11
  471.9 1.6 constant_dynamic-slice_fusion.10
  474.4 10.1 %dynamic_update_slice.8 = f32[2,2,512,384]{3,2,1,0:T(8,128)} dynamic-update-slice(f32[2,2,512,384]{3,2,1,0:T(8,128)} %get-tuple-element.643, f32[2,2,256,256]{3,2,1,0:T(8,128)S(1)} %copy.106, s32[]{:T(128)} %constant.175.clone.1..sunk, s32[]{:T(128)} %constant.175.clone.1..sunk, s32[]{:T(128)S(6)} %select_n.327, s32[]{:T(128)S(6)} %select_n.328) | dynamic-update-slice | bytes 2097156 | tf_op jit(solution)/shard_map/while/body/dynamic_update_slice | solution.py:216
  493.8 2.9 constant_dynamic-slice_fusion.11
  518.8 1.6 constant_dynamic-slice_fusion.10
  521.2 10.6 %dynamic_update_slice.8 = f32[2,2,512,384]{3,2,1,0:T(8,128)} dynamic-update-slice(f32[2,2,512,384]{3,2,1,0:T(8,128)} %get-tuple-element.643, f32[2,2,256,256]{3,2,1,0:T(8,128)S(1)} %copy.106, s32[]{:T(128)} %constant.175.clone.1..sunk, s32[]{:T(128)} %constant.175.clone.1..sunk, s32[]{:T(128)S(6)} %select_n.327, s32[]{:T(128)S(6)} %select_n.328) | dynamic-update-slice | bytes 2097156 | tf_op jit(solution)/shard_map/while/body/dynamic_update_slice | solution.py:216
  541.1 3.0 constant_dynamic-slice_fusion.11
  566.1 1.6 constant_dynamic-slice_fusion.10
  568.6 9.1 %dynamic_update_slice.8 = f32[2,2,512,384]{3,2,1,0:T(8,128)} dynamic-update-slice(f32[2,2,512,384]{3,2,1,0:T(8,128)} %get-tuple-element.643, f32[2,2,256,256]{3,2,1,0:T(8,128)S(1)} %copy.106, s32[]{:T(128)} %constant.175.clone.1..sunk, s32[]{:T(128)} %constant.175.clone.1..sunk, s32[]{:T(128)S(6)} %select_n.327, s32[]{:T(128)S(6)} %select_n.328) | dynamic-update-slice | bytes 2097156 | tf_op jit(solution)/shard_map/while/body/dynamic_update_slice | solution.py:216
  587.0 2.9 constant_dynamic-slice_fusion.11
  612.0 1.6 constant_dynamic-slice_fusion.10
  614.4 10.3 %dynamic_update_slice.8 = f32[2,2,512,384]{3,2,1,0:T(8,128)} dynamic-update-slice(f32[2,2,512,384]{3,2,1,0:T(8,128)} %get-tuple-element.643, f32[2,2,256,256]{3,2,1,0:T(8,128)S(1)} %copy.106, s32[]{:T(128)} %constant.175.clone.1..sunk, s32[]{:T(128)} %constant.175.clone.1..sunk, s32[]{:T(128)S(6)} %select_n.327, s32[]{:T(128)S(6)} %select_n.328) | dynamic-update-slice | bytes 2097156 | tf_op jit(solution)/shard_map/while/body/dynamic_update_slice | solution.py:216
  634.0 3.0 constant_dynamic-slice_fusion.11
  659.0 1.6 constant_dynamic-slice_fusion.10
  661.5 9.5 %dynamic_update_slice.8 = f32[2,2,512,384]{3,2,1,0:T(8,128)} dynamic-update-slice(f32[2,2,512,384]{3,2,1,0:T(8,128)} %get-tuple-element.643, f32[2,2,256,256]{3,2,1,0:T(8,128)S(1)} %copy.106, s32[]{:T(128)} %constant.175.clone.1..sunk, s32[]{:T(128)} %constant.175.clone.1..sunk, s32[]{:T(128)S(6)} %select_n.327, s32[]{:T(128)S(6)} %select_n.328) | dynamic-update-slice | bytes 2097156 | tf_op jit(solution)/shard_map/while/body/dynamic_update_slice | solution.py:216
  680.3 3.0 constant_dynamic-slice_fusion.11
  705.3 1.6 constant_dynamic-slice_fusion.10
  707.8 10.4 %dynamic_update_slice.8 = f32[2,2,512,384]{3,2,1,0:T(8,128)} dynamic-update-slice(f32[2,2,512,384]{3,2,1,0:T(8,128)} %get-tuple-element.643, f32[2,2,256,256]{3,2,1,0:T(8,128)S(1)} %copy.106, s32[]{:T(128)} %constant.175.clone.1..sunk, s32[]{:T(128)} %constant.175.clone.1..sunk, s32[]{:T(128)S(6)} %select_n.327, s32[]{:T(128)S(6)} %select_n.328) | dynamic-update-slice | bytes 2097156 | tf_op jit(solution)/shard_map/while/body/dynamic_update_slice | solution.py:216
  727.4 3.0 constant_dynamic-slice_fusion.11
  752.5 1.6 constant_dynamic-slice_fusion.10
  754.9 10.1 %dynamic_update_slice.8 = f32[2,2,512,384]{3,2,1,0:T(8,128)} dynamic-update-slice(f32[2,2,512,384]{3,2,1,0:T(8,128)} %get-tuple-element.643, f32[2,2,256,256]{3,2,1,0:T(8,128)S(1)} %copy.106, s32[]{:T(128)} %constant.175.clone.1..sunk, s32[]{:T(128)} %constant.175.clone.1..sunk, s32[]{:T(128)S(6)} %select_n.327, s32[]{:T(128)S(6)} %select_n.328) | dynamic-update-slice | bytes 2097156 | tf_op jit(solution)/shard_map/while/body/dynamic_update_slice | solution.py:216
  765.7 1.7 slice.133
  767.3 43.0 %collective-permute-start.1 = (f32[2,2,256,384]{3,2,1,0:T(8,128)S(1)}, f32[2,2,256,384]{3,2,1,0:T(8,128)S(1)}, u32[]{:S(2)}, u32[]{:S(2)}) collective-permute-start(f32[2,2,256,384]{3,2,1,0:T(8,128)S(1)} %slice.133), channel_id=1, source_target_pairs={{0,4},{4,8},{8,12},{12,16},{16,20},{20,24},{24,28},{28,0},{1,5},{5... | collective-permute-start | bytes 4718600 | tf_op jit(solution)/shard_map/ppermute | solution.py:19
  810.3 3.0 collective-permute-done.1
  813.4 1.3 slice_add_fusion.6
  814.7 57.7 %reduce-scatter.2.cloned.1.call-done = f32[2,2,64,384]{3,2,1,0:T(8,128)} async-done(((f32[2,2,256,384]{3,2,1,0:T(8,128)}), f32[2,2,64,384]{3,2,1,0:T(8,128)}) %reduce-scatter.2.cloned.1.call-update) | async-done | bytes 393232 | tf_op jit(solution)/shard_map/reduce_scatter | solution.py:224
  (696 shorter events, 391.2 us)
Async XLA Ops:
  6.5 54.8 %all-gather.2.cloned.1.call-start = ((), (), s32[]{:S(2)}) async-start(), calls=%async_computation.3 | async-start | bytes 1966080 | tf_op jit(solution)/shard_map/all_gather | solution.py:199
  16.2 31.8 %all-to-all-start = ((bf16[8,2,65536]{2,1,0:T(2,128)(2,1)}), bf16[8,2,65536]{2,1,0:T(2,128)(2,1)S(1)}, u32[]{:S(2)}, u32[]{:S(2)}) async-start(bf16[8,2,65536]{2,1,0:T(2,128)(2,1)} %all_to_all.16), calls=%async_computation | async-start | bytes 4194304 | tf_op jit(solution)/shard_map/all_to_all | solution.py:160
  54.4 5.8 copy-start.2
  54.4 50.5 %all-to-all-start.1 = ((bf16[4,4,65536]{2,1,0:T(4,128)(2,1)}), bf16[4,4,65536]{2,1,0:T(4,128)(2,1)}, u32[]{:S(2)}, u32[]{:S(2)}) async-start(bf16[4,4,65536]{2,1,0:T(4,128)(2,1)} %all_to_all.19), calls=%async_computation.1 | async-start | bytes 4194304 | tf_op jit(solution)/shard_map/all_to_all | solution.py:185
  59.5 813.0 %reduce-scatter.2.cloned.1.call-start = ((), (), s32[]{:S(2)}) async-start(), calls=%async_computation.4 | async-start | bytes 1966080 | tf_op jit(solution)/shard_map/reduce_scatter | solution.py:224
  61.4 18.3 %collective-permute-start = (f32[2,2,256,384]{3,1,0,2:T(2,128)}, f32[2,2,256,384]{3,1,0,2:T(2,128)S(1)}, u32[]{:S(2)}, u32[]{:S(2)}) collective-permute-start(f32[2,2,256,384]{3,1,0,2:T(2,128)} %all-gather.2.cloned.1.call-done), channel_id=1, source_target_pairs={{0,28},{4,0},{8,4},{12,8},{16,12},{20,16},{24,20},{28,24},{1,29},{... | collective-permute-start | bytes 4718600 | tf_op jit(solution)/shard_map/ppermute | solution.py:19
  61.7 18.0 %copy-start.1 = (f32[2,2,256,384]{3,1,0,2:T(2,128)S(1)}, f32[2,2,256,384]{3,1,0,2:T(2,128)}, u32[]{:S(2)}) copy-start(f32[2,2,256,384]{3,1,0,2:T(2,128)} %all-gather.2.cloned.1.call-done) | copy-start | bytes 4718596
  109.3 1.9 copy-start.3
  109.3 1.9 copy-start.5
  147.6 10.8 %copy-start.4 = (bf16[512,512]{1,0:T(8,128)(2,1)S(1)}, bf16[512,512]{1,0:T(8,128)(2,1)}, u32[]{:S(2)}) copy-start(bf16[512,512]{1,0:T(8,128)(2,1)} %get-tuple-element.719) | copy-start | bytes 1572868 | tf_op jit(solution)/shard_map/while
  147.9 10.5 %copy-start.6 = (bf16[512,512]{1,0:T(8,128)(2,1)S(1)}, bf16[512,512]{1,0:T(8,128)(2,1)}, u32[]{:S(2)}) copy-start(bf16[512,512]{1,0:T(8,128)(2,1)} %get-tuple-element.742) | copy-start | bytes 1572868 | tf_op jit(solution)/shard_map/while
  194.9 9.7 %copy-start.4 = (bf16[512,512]{1,0:T(8,128)(2,1)S(1)}, bf16[512,512]{1,0:T(8,128)(2,1)}, u32[]{:S(2)}) copy-start(bf16[512,512]{1,0:T(8,128)(2,1)} %get-tuple-element.719) | copy-start | bytes 1572868 | tf_op jit(solution)/shard_map/while
  195.2 9.4 %copy-start.6 = (bf16[512,512]{1,0:T(8,128)(2,1)S(1)}, bf16[512,512]{1,0:T(8,128)(2,1)}, u32[]{:S(2)}) copy-start(bf16[512,512]{1,0:T(8,128)(2,1)} %get-tuple-element.742) | copy-start | bytes 1572868 | tf_op jit(solution)/shard_map/while
  241.0 10.1 %copy-start.4 = (bf16[512,512]{1,0:T(8,128)(2,1)S(1)}, bf16[512,512]{1,0:T(8,128)(2,1)}, u32[]{:S(2)}) copy-start(bf16[512,512]{1,0:T(8,128)(2,1)} %get-tuple-element.719) | copy-start | bytes 1572868 | tf_op jit(solution)/shard_map/while
  241.3 9.7 %copy-start.6 = (bf16[512,512]{1,0:T(8,128)(2,1)S(1)}, bf16[512,512]{1,0:T(8,128)(2,1)}, u32[]{:S(2)}) copy-start(bf16[512,512]{1,0:T(8,128)(2,1)} %get-tuple-element.742) | copy-start | bytes 1572868 | tf_op jit(solution)/shard_map/while
  287.4 10.1 %copy-start.4 = (bf16[512,512]{1,0:T(8,128)(2,1)S(1)}, bf16[512,512]{1,0:T(8,128)(2,1)}, u32[]{:S(2)}) copy-start(bf16[512,512]{1,0:T(8,128)(2,1)} %get-tuple-element.719) | copy-start | bytes 1572868 | tf_op jit(solution)/shard_map/while
  287.8 9.8 %copy-start.6 = (bf16[512,512]{1,0:T(8,128)(2,1)S(1)}, bf16[512,512]{1,0:T(8,128)(2,1)}, u32[]{:S(2)}) copy-start(bf16[512,512]{1,0:T(8,128)(2,1)} %get-tuple-element.742) | copy-start | bytes 1572868 | tf_op jit(solution)/shard_map/while
  334.0 10.2 %copy-start.4 = (bf16[512,512]{1,0:T(8,128)(2,1)S(1)}, bf16[512,512]{1,0:T(8,128)(2,1)}, u32[]{:S(2)}) copy-start(bf16[512,512]{1,0:T(8,128)(2,1)} %get-tuple-element.719) | copy-start | bytes 1572868 | tf_op jit(solution)/shard_map/while
  334.3 9.9 %copy-start.6 = (bf16[512,512]{1,0:T(8,128)(2,1)S(1)}, bf16[512,512]{1,0:T(8,128)(2,1)}, u32[]{:S(2)}) copy-start(bf16[512,512]{1,0:T(8,128)(2,1)} %get-tuple-element.742) | copy-start | bytes 1572868 | tf_op jit(solution)/shard_map/while
  380.6 10.7 %copy-start.4 = (bf16[512,512]{1,0:T(8,128)(2,1)S(1)}, bf16[512,512]{1,0:T(8,128)(2,1)}, u32[]{:S(2)}) copy-start(bf16[512,512]{1,0:T(8,128)(2,1)} %get-tuple-element.719) | copy-start | bytes 1572868 | tf_op jit(solution)/shard_map/while
  380.9 10.3 %copy-start.6 = (bf16[512,512]{1,0:T(8,128)(2,1)S(1)}, bf16[512,512]{1,0:T(8,128)(2,1)}, u32[]{:S(2)}) copy-start(bf16[512,512]{1,0:T(8,128)(2,1)} %get-tuple-element.742) | copy-start | bytes 1572868 | tf_op jit(solution)/shard_map/while
  427.6 10.0 %copy-start.4 = (bf16[512,512]{1,0:T(8,128)(2,1)S(1)}, bf16[512,512]{1,0:T(8,128)(2,1)}, u32[]{:S(2)}) copy-start(bf16[512,512]{1,0:T(8,128)(2,1)} %get-tuple-element.719) | copy-start | bytes 1572868 | tf_op jit(solution)/shard_map/while
  428.0 9.7 %copy-start.6 = (bf16[512,512]{1,0:T(8,128)(2,1)S(1)}, bf16[512,512]{1,0:T(8,128)(2,1)}, u32[]{:S(2)}) copy-start(bf16[512,512]{1,0:T(8,128)(2,1)} %get-tuple-element.742) | copy-start | bytes 1572868 | tf_op jit(solution)/shard_map/while
  474.0 10.5 %copy-start.4 = (bf16[512,512]{1,0:T(8,128)(2,1)S(1)}, bf16[512,512]{1,0:T(8,128)(2,1)}, u32[]{:S(2)}) copy-start(bf16[512,512]{1,0:T(8,128)(2,1)} %get-tuple-element.719) | copy-start | bytes 1572868 | tf_op jit(solution)/shard_map/while
  474.4 10.2 %copy-start.6 = (bf16[512,512]{1,0:T(8,128)(2,1)S(1)}, bf16[512,512]{1,0:T(8,128)(2,1)}, u32[]{:S(2)}) copy-start(bf16[512,512]{1,0:T(8,128)(2,1)} %get-tuple-element.742) | copy-start | bytes 1572868 | tf_op jit(solution)/shard_map/while
  520.9 10.9 %copy-start.4 = (bf16[512,512]{1,0:T(8,128)(2,1)S(1)}, bf16[512,512]{1,0:T(8,128)(2,1)}, u32[]{:S(2)}) copy-start(bf16[512,512]{1,0:T(8,128)(2,1)} %get-tuple-element.719) | copy-start | bytes 1572868 | tf_op jit(solution)/shard_map/while
  521.2 10.6 %copy-start.6 = (bf16[512,512]{1,0:T(8,128)(2,1)S(1)}, bf16[512,512]{1,0:T(8,128)(2,1)}, u32[]{:S(2)}) copy-start(bf16[512,512]{1,0:T(8,128)(2,1)} %get-tuple-element.742) | copy-start | bytes 1572868 | tf_op jit(solution)/shard_map/while
  568.2 9.5 %copy-start.4 = (bf16[512,512]{1,0:T(8,128)(2,1)S(1)}, bf16[512,512]{1,0:T(8,128)(2,1)}, u32[]{:S(2)}) copy-start(bf16[512,512]{1,0:T(8,128)(2,1)} %get-tuple-element.719) | copy-start | bytes 1572868 | tf_op jit(solution)/shard_map/while
  568.6 9.1 %copy-start.6 = (bf16[512,512]{1,0:T(8,128)(2,1)S(1)}, bf16[512,512]{1,0:T(8,128)(2,1)}, u32[]{:S(2)}) copy-start(bf16[512,512]{1,0:T(8,128)(2,1)} %get-tuple-element.742) | copy-start | bytes 1572868 | tf_op jit(solution)/shard_map/while
  614.1 10.7 %copy-start.4 = (bf16[512,512]{1,0:T(8,128)(2,1)S(1)}, bf16[512,512]{1,0:T(8,128)(2,1)}, u32[]{:S(2)}) copy-start(bf16[512,512]{1,0:T(8,128)(2,1)} %get-tuple-element.719) | copy-start | bytes 1572868 | tf_op jit(solution)/shard_map/while
  614.4 10.3 %copy-start.6 = (bf16[512,512]{1,0:T(8,128)(2,1)S(1)}, bf16[512,512]{1,0:T(8,128)(2,1)}, u32[]{:S(2)}) copy-start(bf16[512,512]{1,0:T(8,128)(2,1)} %get-tuple-element.742) | copy-start | bytes 1572868 | tf_op jit(solution)/shard_map/while
  661.1 9.9 %copy-start.4 = (bf16[512,512]{1,0:T(8,128)(2,1)S(1)}, bf16[512,512]{1,0:T(8,128)(2,1)}, u32[]{:S(2)}) copy-start(bf16[512,512]{1,0:T(8,128)(2,1)} %get-tuple-element.719) | copy-start | bytes 1572868 | tf_op jit(solution)/shard_map/while
  661.5 9.6 %copy-start.6 = (bf16[512,512]{1,0:T(8,128)(2,1)S(1)}, bf16[512,512]{1,0:T(8,128)(2,1)}, u32[]{:S(2)}) copy-start(bf16[512,512]{1,0:T(8,128)(2,1)} %get-tuple-element.742) | copy-start | bytes 1572868 | tf_op jit(solution)/shard_map/while
  707.4 10.8 %copy-start.4 = (bf16[512,512]{1,0:T(8,128)(2,1)S(1)}, bf16[512,512]{1,0:T(8,128)(2,1)}, u32[]{:S(2)}) copy-start(bf16[512,512]{1,0:T(8,128)(2,1)} %get-tuple-element.719) | copy-start | bytes 1572868 | tf_op jit(solution)/shard_map/while
  707.8 10.4 %copy-start.6 = (bf16[512,512]{1,0:T(8,128)(2,1)S(1)}, bf16[512,512]{1,0:T(8,128)(2,1)}, u32[]{:S(2)}) copy-start(bf16[512,512]{1,0:T(8,128)(2,1)} %get-tuple-element.742) | copy-start | bytes 1572868 | tf_op jit(solution)/shard_map/while
  754.6 10.4 %copy-start.4 = (bf16[512,512]{1,0:T(8,128)(2,1)S(1)}, bf16[512,512]{1,0:T(8,128)(2,1)}, u32[]{:S(2)}) copy-start(bf16[512,512]{1,0:T(8,128)(2,1)} %get-tuple-element.719) | copy-start | bytes 1572868 | tf_op jit(solution)/shard_map/while
  754.9 10.1 %copy-start.6 = (bf16[512,512]{1,0:T(8,128)(2,1)S(1)}, bf16[512,512]{1,0:T(8,128)(2,1)}, u32[]{:S(2)}) copy-start(bf16[512,512]{1,0:T(8,128)(2,1)} %get-tuple-element.742) | copy-start | bytes 1572868 | tf_op jit(solution)/shard_map/while
  765.7 47.7 %copy-start = (f32[2,2,512,384]{3,2,1,0:T(8,128)S(1)}, f32[2,2,512,384]{3,2,1,0:T(8,128)}, u32[]{:S(2)}) copy-start(f32[2,2,512,384]{3,2,1,0:T(8,128)} %get-tuple-element.721) | copy-start | bytes 9437188
  767.3 46.0 %collective-permute-start.1 = (f32[2,2,256,384]{3,2,1,0:T(8,128)S(1)}, f32[2,2,256,384]{3,2,1,0:T(8,128)S(1)}, u32[]{:S(2)}, u32[]{:S(2)}) collective-permute-start(f32[2,2,256,384]{3,2,1,0:T(8,128)S(1)} %slice.133), channel_id=1, source_target_pairs={{0,4},{4,8},{8,12},{12,16},{16,20},{20,24},{24,28},{28,0},{1,5},{5... | collective-permute-start | bytes 4718600 | tf_op jit(solution)/shard_map/ppermute | solution.py:19
Sparse Core Ops, SparseCore 0:
  8.9 39.7 all-gather.1
  814.8 57.5 reduce-scatter.1
where the time goes:
time: 884 us; the launch traced here: 879 us
  local copies, waits for them, and re-layouts  303 us (34%)
  matrix products  229 us (26%)
  waiting for transfers between devices  117 us (13%)
  other arithmetic  88.2 us (10%)
  loops' own time  75.3 us (9%)
  starting transfers between devices  53.2 us (6%)
  between operations  13.6 us (2%)
    dynamic_update_slice x28, local copies, waits for them, and re-layouts, accumulate(): return lax.dynamic_update_slice(totals, current + gradient_part, starting)  144 us
    dot_general x84, matrix products, transform(): with_sine = jnp.dot(sine_part, halfway, preferred_element_type=jnp.float32)  99.6 us
    dot_general x84, matrix products, transform(): with_cosine = jnp.dot(cosine, halfway, preferred_element_type=jnp.float32)  98.5 us
    another operation x1, loops' own time, shards(): lax.fori_loop(0, pattern_count, accumulate, jnp.zeros(extended.shape, jnp...  75.3 us
    reduce_scatter x1, waiting for transfers between devices, shards(): return lax.psum_scatter(combined, 'slab', scatter_dimension=2, tiled=True)  57.7 us
    another operation x85, other arithmetic  54.6 us
    ppermute x2, starting transfers between devices, passed_along(): return lax.ppermute(value, axis, pairs)  43 us
    slice x14, local copies, waits for them, and re-layouts, position_gradient(): window[slice_index, 0]  41.9 us
  transfers between devices with their start and end apart: 6, of which 5 were waited for; matrix products, arithmetic and copies ran while one was open for 3% of the time, Pallas kernels for 0%

commit v1 on v0

v1 whole, which is shorter than its diff:
```python
import functools
import math

import jax
import jax.numpy as jnp
import ml_dtypes
import numpy as np
from jax import lax
from jax.experimental import pallas as pl
from jax.experimental.pallas import tpu as pltpu
from jax.sharding import PartitionSpec as P

K = 16
CAP = 2
COLS = 128
chirp_strength = 40.0
bf16 = jnp.bfloat16
f32 = jnp.float32


def make_tables(extent):
    counter = np.arange(extent, dtype=np.int64)
    angles = (counter[:, None] * counter[None, :] % extent).astype(np.float32) * np.float32(
        2.0 * math.pi / extent
    )
    scaling = np.float32(1.0 / math.sqrt(extent))
    cosine = (np.cos(angles) * scaling).astype(ml_dtypes.bfloat16)
    sine_part = (np.sin(angles) * scaling).astype(ml_dtypes.bfloat16)
    half = extent // 2
    tables = []
    for parity in (0, 1):
        c, s = cosine[:half, parity::2], sine_part[:half, parity::2]
        table = np.concatenate([np.concatenate([c, -s], 1), np.concatenate([s, c], 1)], 0)
        tables += [table, np.ascontiguousarray(table.T)]
    order = np.concatenate([counter[0::2], counter[1::2]])
    frequency = (((counter + half) % extent - half).astype(np.float32) / extent)[order]
    phases = np.float32(chirp_strength) * (frequency[:, None] ** 2 + frequency[None, :] ** 2)
    kernel = np.stack([np.cos(phases), -np.sin(phases)]).astype(np.float32)
    permute = (counter[:, None] == order[None, :]).astype(ml_dtypes.bfloat16)
    return [jnp.asarray(t) for t in tables], jnp.asarray(kernel), jnp.asarray(permute)


def dot(a, b):
    return jnp.dot(a, b, preferred_element_type=f32)


def quads(a, b, h):
    return jnp.concatenate(
        [
            jnp.concatenate([a[:, :h], b[:, :h]], 1),
            jnp.concatenate([a[:, h:], b[:, h:]], 1),
        ],
        0,
    )


def forward(items, tabs):
    a_even, t_even, a_odd, t_odd = tabs
    h = a_even.shape[0] // 2
    sums = [jnp.concatenate([l[0] + r[0], l[1] + r[1]], 1).astype(bf16) for l, r in items]
    diffs = [jnp.concatenate([l[0] - r[0], l[1] - r[1]], 1).astype(bf16) for l, r in items]
    even = [dot(x, a_even) for x in sums]
    odd = [dot(x, a_odd) for x in diffs]
    plus = [quads(a[:h] + a[h:], b[:h] + b[h:], h).astype(bf16) for a, b in zip(even, odd)]
    minus = [quads(a[:h] - a[h:], b[:h] - b[h:], h).astype(bf16) for a, b in zip(even, odd)]
    return list(zip([dot(t_even, x) for x in plus], [dot(t_odd, x) for x in minus]))


def inverse(items, tabs):
    a_even, t_even, a_odd, t_odd = tabs
    h = a_even.shape[0] // 2

    def side(x, k):
        lanes = slice(k * h, (k + 1) * h)
        return jnp.concatenate(
            [jnp.concatenate([part[:h, lanes], part[h:, lanes]], 1) for part in x], 0
        )

    even = [dot(side(x, 0), t_even) for x in items]
    odd = [dot(side(x, 1), t_odd) for x in items]
    plus = [a + b for a, b in zip(even, odd)]
    minus = [a - b for a, b in zip(even, odd)]
    low = [dot(a_even, quads(a[:h], b[:h], h).astype(bf16)) for a, b in zip(plus, minus)]
    high = [dot(a_odd, quads(a[h:], b[h:], h).astype(bf16)) for a, b in zip(plus, minus)]
    out = []
    for a, b in zip(low, high):
        s, d = a + b, a - b
        out.append(
            (jnp.concatenate([s[:h], d[:h]], 0), jnp.concatenate([s[h:], d[h:]], 0))
        )
    return out


def product(a, b):
    return a[0] * b[0] - a[1] * b[1], a[0] * b[1] + a[1] * b[0]


def product_conj(a, b):
    return a[0] * b[0] + a[1] * b[1], a[0] * b[1] - a[1] * b[0]


def halves(x, h=COLS):
    return (x[0][:, :h], x[1][:, :h]), (x[0][:, h:], x[1][:, h:])


def by_kernel(field, kernel_ref, conjugate):
    out = []
    h = field[0].shape[0] // 2
    op = product_conj if conjugate else product
    for k, part in enumerate(field):
        rows = slice(k * h, (k + 1) * h)
        spread = op((kernel_ref[0, rows, :], kernel_ref[1, rows, :]), (part[:h], part[h:]))
        out.append(jnp.concatenate(spread, 0).astype(bf16))
    return out


def window(rows_ref, top, col, extent):
    return tuple(
        tuple(rows_ref[plane, col + j, pl.ds(top, extent), :] for plane in (0, 1)) for j in (0, 1)
    )


def load_rows(here_ref, next_ref, rows_ref):
    count, _, _, height, _ = here_ref.shape
    for side, ref in enumerate((here_ref, next_ref)):
        for k in range(count):
            start = (side * count + k) * height
            rows_ref[:, :, start : start + height, :] = ref[k].astype(f32)


def add_window(totals_ref, top, col, term):
    extent = term[0][0].shape[0]
    for j in (0, 1):
        for plane in (0, 1):
            place = (plane, col + j, pl.ds(top, extent), slice(None))
            totals_ref[place] += term[j][plane]


def route_kernel(here_ref, owner_ref, row_ref, col_ref, images_ref, permute_ref, out_ref, meta_ref, second_ref):
    reads = images_ref.shape[0]
    tiles = out_ref.shape[1]
    tile_here, slab_here, slabs = here_ref[0], here_ref[1], here_ref[2]
    mine = (tile_here * slabs + slab_here) * reads

    def pack(i, _):
        owner = owner_ref[mine + i]
        rank = jnp.int32(0)
        rank = lax.fori_loop(
            0, i, lambda j, r: r + (owner_ref[mine + j] == owner).astype(jnp.int32), rank
        )
        image = images_ref[i]
        turned = dot(image, permute_ref[0]).astype(bf16)
        out_ref[rank, owner] = dot(permute_ref[1], turned).astype(bf16)
        return 0

    lax.fori_loop(0, reads, pack, 0)

    def clear(i, _):
        for f in range(4):
            meta_ref[f * K + i] = 0
        return 0

    lax.fori_loop(0, K, clear, 0)

    def sender(g, counts):
        base = (g * slabs + slab_here) * reads

        def read(i, state):
            first, later, seen = state
            match = (owner_ref[base + i] == tile_here).astype(jnp.int32)

            @pl.when((match == 1) & (seen == 0))
            def _():
                meta_ref[first] = g
                meta_ref[K + first] = row_ref[base + i]
                meta_ref[2 * K + first] = col_ref[base + i]

            @pl.when((match == 1) & (seen == 1))
            def _():
                second_ref[later] = tiles + g
                second_ref[K + later] = row_ref[base + i]
                second_ref[2 * K + later] = col_ref[base + i]

            fresh = match * (1 - seen)
            return first + fresh, later + match - fresh, seen + match

        first, later, _ = lax.fori_loop(0, reads, read, (counts[0], counts[1], jnp.int32(0)))
        return first, later

    first, later = lax.fori_loop(0, tiles, sender, (jnp.int32(0), jnp.int32(0)))

    def join(i, _):
        for f in range(3):
            meta_ref[f * K + first + i] = second_ref[f * K + i]
        return 0

    lax.fori_loop(0, later, join, 0)
    total = first + later
    meta_ref[4 * K] = total
    meta_ref[4 * K + 1] = first

    def target(i, _):
        meta_ref[3 * K + i] = jnp.where(i < total, meta_ref[K + i], 2 * images_ref.shape[1])
        return 0

    lax.fori_loop(0, K, target, 0)


def wave_kernel(meta_ref, here_ref, next_ref, probe_ref, kernel_ref, a0, t0, a1, t1, wave_ref, rows_ref):
    step = pl.program_id(0)
    extent = probe_ref.shape[0]

    @pl.when(step == 0)
    def _():
        load_rows(here_ref, next_ref, rows_ref)

    @pl.when(2 * step < meta_ref[4 * K])
    def _():
        tabs = a0[...], t0[...], a1[...], t1[...]
        probe = halves((probe_ref[:, :extent], probe_ref[:, extent:]))
        items = []
        for i in (0, 1):
            at = 2 * step + i
            w = window(rows_ref, meta_ref[K + at], meta_ref[2 * K + at], extent)
            items.append(tuple(product(p, q) for p, q in zip(probe, w)))
        spread = [by_kernel(x, kernel_ref, False) for x in forward(items, tabs)]
        for i, wave in enumerate(inverse(spread, tabs)):
            wave_ref[i, 0] = wave[0]
            wave_ref[i, 1] = wave[1]


def misfit_kernel(
    meta_ref, here_ref, next_ref, wave_ref, image0, image1, kernel_ref, a0, t0, a1, t1,
    back_ref, out_ref, rows_ref, totals_ref,
):
    step = pl.program_id(0)
    extent = image0.shape[1]
    h = extent // 2

    @pl.when(step == 0)
    def _():
        load_rows(here_ref, next_ref, rows_ref)
        totals_ref[...] = jnp.zeros_like(totals_ref)

    @pl.when(2 * step < meta_ref[4 * K])
    def _():
        tabs = a0[...], t0[...], a1[...], t1[...]
        items = []
        for i in (0, 1):
            at = 2 * step + i
            w = window(rows_ref, meta_ref[K + at], meta_ref[2 * K + at], extent)
            wave = halves((wave_ref[i, 0], wave_ref[i, 1]))
            items.append(tuple(product(p, q) for p, q in zip(wave, w)))
        far_grads = []
        for i, far in enumerate(forward(items, tabs)):
            image = (image0, image1)[i]
            parts = []
            for k, part in enumerate(far):
                re, im = part[:h], part[h:]
                misfit = re * re + im * im - image[0, k * h : (k + 1) * h, :].astype(f32)
                parts.append(jnp.concatenate([re * misfit, im * misfit], 0).astype(bf16))
            far_grads.append(parts)
        back = []
        for i, grad in enumerate(inverse(far_grads, tabs)):
            at = 2 * step + i
            grad = halves(grad)
            wave = halves((wave_ref[i, 0], wave_ref[i, 1]))
            col = meta_ref[2 * K + at]
            add_window(
                totals_ref, meta_ref[3 * K + at], col,
                [product_conj(p, q) for p, q in zip(wave, grad)],
            )
            w = window(rows_ref, meta_ref[K + at], col, extent)
            back.append(tuple(product_conj(p, q) for p, q in zip(w, grad)))
        for i, field in enumerate(forward(back, tabs)):
            for k, part in enumerate(by_kernel(field, kernel_ref, True)):
                back_ref[i, k] = part

    @pl.when(step == pl.num_programs(0) - 1)
    def _():
        out_ref[...] = totals_ref[:, :, : 2 * extent, :].astype(out_ref.dtype)


def exit_kernel(meta_ref, back_ref, probe_ref, a0, t0, a1, t1, out_ref, totals_ref):
    step = pl.program_id(0)
    extent = probe_ref.shape[0]

    @pl.when(step == 0)
    def _():
        totals_ref[...] = jnp.zeros_like(totals_ref)

    @pl.when(2 * step < meta_ref[4 * K])
    def _():
        tabs = a0[...], t0[...], a1[...], t1[...]
        probe = halves((probe_ref[:, :extent], probe_ref[:, extent:]))
        fields = [(back_ref[i, 0], back_ref[i, 1]) for i in (0, 1)]
        for i, grad in enumerate(inverse(fields, tabs)):
            at = 2 * step + i
            add_window(
                totals_ref, meta_ref[3 * K + at], meta_ref[2 * K + at],
                [product_conj(p, q) for p, q in zip(probe, halves(grad))],
            )

    @pl.when(step == pl.num_programs(0) - 1)
    def _():
        out_ref[...] = totals_ref[:, :, : 2 * extent, :].astype(out_ref.dtype)


def whole(shape):
    return pl.BlockSpec(shape, lambda *_: (0,) * len(shape))


VMEM = 56 * 1024 * 1024


def params():
    return pltpu.CompilerParams(vmem_limit_bytes=VMEM, dimension_semantics=("arbitrary",))


def route(images, here, owner_tile, row_offset, col_offset, permute, tiles):
    reads, extent = images.shape[:2]
    smem = pl.BlockSpec(memory_space=pltpu.SMEM)
    vmem = pl.BlockSpec(memory_space=pltpu.VMEM)
    return pl.pallas_call(
        route_kernel,
        in_specs=[smem, smem, smem, smem, vmem, vmem],
        out_specs=[vmem, smem],
        out_shape=[
            jax.ShapeDtypeStruct((CAP, tiles, extent, extent), bf16),
            jax.ShapeDtypeStruct((4 * K + 8,), jnp.int32),
        ],
        scratch_shapes=[pltpu.SMEM((4 * K,), jnp.int32)],
        compiler_params=pltpu.CompilerParams(vmem_limit_bytes=VMEM),
        name="route",
    )(here, owner_tile, row_offset, col_offset, images, permute)


def waves(meta, rows_here, rows_next, probe, kernel, tabs):
    extent = probe.shape[0]
    ins = [rows_here, rows_next, probe, kernel] + tabs
    total = 2 * extent
    return pl.pallas_call(
        wave_kernel,
        grid_spec=pltpu.PrefetchScalarGridSpec(
            num_scalar_prefetch=1,
            grid=(K // 2,),
            in_specs=[whole(x.shape) for x in ins],
            out_specs=pl.BlockSpec((2, 2, extent, extent), lambda i, m: (i, 0, 0, 0)),
            scratch_shapes=[pltpu.VMEM((2, rows_here.shape[2], total, COLS), f32)],
        ),
        out_shape=jax.ShapeDtypeStruct((K, 2, extent, extent), f32),
        compiler_params=params(),
        name="waves",
    )(meta, *ins)


def misfits(meta, rows_here, rows_next, wave, images, kernel, tabs):
    extent = images.shape[1]
    total = 2 * extent
    blocks = rows_here.shape[2]
    once = [rows_here, rows_next]
    tail = [kernel] + tabs
    pair = pl.BlockSpec((2, 2, extent, extent), lambda i, m: (i, 0, 0, 0))
    one = [
        pl.BlockSpec((1, extent, extent), lambda i, m, k=k: (m[2 * i + k], 0, 0)) for k in (0, 1)
    ]
    return pl.pallas_call(
        misfit_kernel,
        grid_spec=pltpu.PrefetchScalarGridSpec(
            num_scalar_prefetch=1,
            grid=(K // 2,),
            in_specs=[whole(x.shape) for x in once] + [pair] + one + [whole(x.shape) for x in tail],
            out_specs=[pair, whole((2, blocks, total, COLS))],
            scratch_shapes=[
                pltpu.VMEM((2, blocks, total, COLS), f32),
                pltpu.VMEM((2, blocks, total + extent, COLS), f32),
            ],
        ),
        out_shape=[
            jax.ShapeDtypeStruct((K, 2, extent, extent), bf16),
            jax.ShapeDtypeStruct((2, blocks, total, COLS), f32),
        ],
        compiler_params=params(),
        name="misfits",
    )(meta, *once, wave, images, images, *tail)


def exits(meta, back, probe, tabs, blocks):
    extent = probe.shape[0]
    total = 2 * extent
    pair = pl.BlockSpec((2, 2, extent, extent), lambda i, m: (i, 0, 0, 0))
    tail = [probe] + tabs
    return pl.pallas_call(
        exit_kernel,
        grid_spec=pltpu.PrefetchScalarGridSpec(
            num_scalar_prefetch=1,
            grid=(K // 2,),
            in_specs=[pair] + [whole(x.shape) for x in tail],
            out_specs=whole((2, blocks, total, COLS)),
            scratch_shapes=[pltpu.VMEM((2, blocks, total + extent, COLS), f32)],
        ),
        out_shape=jax.ShapeDtypeStruct((2, blocks, total, COLS), f32),
        compiler_params=params(),
        name="exits",
    )(meta, back, *tail)


def passed_along(value, axis, steps):
    count = lax.axis_size(axis)
    pairs = [(source, (source + steps) % count) for source in range(count)]
    return lax.ppermute(value, axis, pairs)


def shards(intensities, object_field, probe_wave, owner_tile, row_offset, col_offset):
    tile_count = lax.axis_size("tile")
    slab_count = lax.axis_size("slab")
    extent = intensities.shape[1]
    depth, _, height, width = object_field.shape
    blocks = width // COLS
    tabs, kernel, permute = make_tables(extent)
    here = jnp.stack(
        [lax.axis_index("tile"), lax.axis_index("slab"), jnp.int32(slab_count)]
    ).astype(jnp.int32)
    packed, meta = route(
        intensities, here, owner_tile, row_offset, col_offset,
        jnp.stack([permute, permute.T]), tile_count,
    )
    images = [
        lax.all_to_all(packed[rank], "tile", split_axis=0, concat_axis=0, tiled=True)
        for rank in range(CAP)
    ]
    images = jnp.concatenate(images, 0)
    own = jnp.transpose(
        object_field.reshape(depth, 2, height, blocks, COLS), (0, 1, 3, 2, 4)
    ).astype(bf16)
    gathered = [lax.all_gather(own[s], "slab", axis=0, tiled=False) for s in range(depth)]
    following = [passed_along(rows, "tile", -1) for rows in gathered]
    wave = waves(meta, gathered[0], following[0], probe_wave, kernel, tabs)
    back, total1 = misfits(meta, gathered[1], following[1], wave, images, kernel, tabs)
    total0 = exits(meta, back, probe_wave, tabs, blocks)
    grads = []
    tile_rows = height * slab_count
    for total in (total0, total1):
        moved = passed_along(total[:, :, tile_rows:].astype(bf16), "tile", 1)
        combined = total[:, :, :tile_rows] + moved.astype(f32)
        grads.append(lax.psum_scatter(combined, "slab", scatter_dimension=2, tiled=True))
    gradient = jnp.stack(grads)
    return jnp.transpose(gradient, (0, 1, 3, 2, 4)).reshape(depth, 2, height, width)


def solution(mesh):
    placed = (
        P(("tile", "slab"), None, None),
        P(None, None, ("tile", "slab"), None),
        P(),
        P(),
        P(),
        P(),
    )
    return jax.shard_map(
        shards,
        mesh=mesh,
        in_specs=placed,
        out_specs=P(None, None, ("tile", "slab"), None),
        check_vma=False,
    )
```

time: 884 us -> 185 us (0.21)
  local copies, waits for them, and re-layouts: 303 us -> 6.82 us
  matrix products: 229 us -> 0 us
  other arithmetic: 88.2 us -> 8.17 us
  loops' own time: 75.3 us -> 0 us
  waiting for transfers between devices: 117 us -> 43.7 us
  Pallas kernels: 0 us -> 54.7 us
  blocking collectives: 0 us -> 50 us
  starting transfers between devices: 53.2 us -> 8.34 us
    dot_general x255 -> x0, matrix products: 229 us -> none  [the longest x84 99.6 us: transform(): with_sine = jnp.dot(sine_part, halfway, preferred_element_type=jnp.float32)]
    dynamic_update_slice x28 -> x0, local copies, waits for them, and re-layouts: 144 us -> none  [accumulate(): return lax.dynamic_update_slice(totals, current + gradient_part, starting)]
    dynamic_slice x101 -> x0, local copies, waits for them, and re-layouts: 87 us -> none  [the longest x28 27.2 us: accumulate(): current = lax.dynamic_slice(totals, starting, (depth, 2, extent, extent))]
    another operation x1 -> x0, loops' own time: 75.3 us -> none  [shards(): lax.fori_loop(0, pattern_count, accumulate, jnp.zeros(extended.shape, jnp...]
    another operation x128 -> x1, other arithmetic: 72.2 us -> 0.58 us  [shards(): jnp.stack([lax.axis_index('tile'), lax.axis_index('slab'), jnp.int32(slab...]
    pallas_call x0 -> x4, Pallas kernels: none -> 54.7 us  [the longest x1 20.7 us: misfits(): pl.pallas_call(misfit_kernel, grid_spec=pltpu.PrefetchScalarGridSpec(num_...]
    all_to_all x2 -> x1, waiting for transfers between devices: 43.9 us -> 0.01 us  [shards(): lax.all_to_all(packed[rank], 'tile', split_axis=0, concat_axis=0, tiled=T...]
    slice x15 -> x5, local copies, waits for them, and re-layouts: 43.6 us -> 2.5 us  [the longest x2 2.37 us: shards(): moved = passed_along(total[:, :, tile_rows:].astype(bf16), 'tile', 1)]
  transfers between devices with their start and end apart: 6 -> 7, of which waited for: 5 -> 4; matrix products, arithmetic and copies ran while one was open for 3% -> 3% of each run, Pallas kernels for 0% -> 12%
where the time goes in v1:
time: 185 us
  Pallas kernels  54.7 us (30%)
  blocking collectives  50 us (27%)
  waiting for transfers between devices  43.7 us (24%)
  between operations  13.5 us (7%)
  starting transfers between devices  8.34 us (5%)
  other arithmetic  8.17 us (4%)
  local copies, waits for them, and re-layouts  6.82 us (4%)
    reduce_scatter x2, waiting for transfers between devices, shards(): lax.psum_scatter(combined, 'slab', scatter_dimension=2, tiled=True)  29.8 us
    all_gather x2, blocking collectives, shards(): lax.all_gather(own[s], 'slab', axis=0, tiled=False)  29.6 us
    pallas_call x1, Pallas kernels, misfits(): pl.pallas_call(misfit_kernel, grid_spec=pltpu.PrefetchScalarGridSpec(num_...  20.7 us
    all_to_all x1, blocking collectives, shards(): lax.all_to_all(packed[rank], 'tile', split_axis=0, concat_axis=0, tiled=T...  20.4 us
    ppermute x4, waiting for transfers between devices, passed_along(): return lax.ppermute(value, axis, pairs)  13.9 us
    pallas_call x1, Pallas kernels, waves(): pl.pallas_call(wave_kernel, grid_spec=pltpu.PrefetchScalarGridSpec(num_sc...  12.6 us
    pallas_call x1, Pallas kernels, route(): pl.pallas_call(route_kernel, in_specs=[smem, smem, smem, smem, vmem, vmem...  11.3 us
    pallas_call x1, Pallas kernels, exits(): pl.pallas_call(exit_kernel, grid_spec=pltpu.PrefetchScalarGridSpec(num_sc...  10 us
  transfers between devices with their start and end apart: 7, of which 4 were waited for; matrix products, arithmetic and copies ran while one was open for 3% of the time, Pallas kernels for 12%

profile of v1, /device:TPU:0, one launch (start us, length us, event | category | flops | bytes accessed | tf_op | source)
XLA Modules:
  0.0 185.3 jit_solution(16930031639887984490)
XLA Ops:
  6.5 0.6 pad_add_fusion.here_ref
  7.1 11.3 %route.1 = (bf16[2,8,256,256]{3,2,1,0:T(8,128)(2,1)}, s32[72]{0:T(128)}) custom-call(s32[3]{0:T(128)} %pad_add_fusion.here_ref, s32[448]{0:T(512)} %owner_ref.1, s32[448]{0:T(512)} %row_ref.1, s32[448]{0:T(512)} %col_ref.1, bf16[14,256,256]{2,1,0:T(8,128)(2,1)} %images_ref.1, bf16[2,256,256]{2,1,0:T(8,128)(2,1)} %constant.33.permute_ref), custom_call_target="tpu_custom_call" | custom-call | tf_op jit(solution)/shard_map/route/pallas_call | solution.py:324
  18.5 2.7 %slice_bitcast_fusion.1 = (bf16[8,256,256]{2,1,0:T(8,128)(2,1)S(1)}, bf16[8,256,256]{2,1,0:T(8,128)(2,1)}) fusion(bf16[2,8,256,256]{3,2,1,0:T(8,128)(2,1)} %get-tuple-element.10), kind=kLoop, calls=%fused_computation.2 | loop fusion | bytes 4194304 | tf_op jit(solution)/shard_map/squeeze | solution.py:429
  21.2 0.0 copy-start.3
  21.2 20.4 %all_to_all.10 = bf16[8,256,256]{2,1,0:T(8,128)(2,1)S(1)} all-to-all(bf16[8,256,256]{2,1,0:T(8,128)(2,1)S(1)} %get-tuple-element.13), channel_id=1, replica_groups=mesh['tile'=8,'slab'=4] {'tile'}, dimensions={0} | all-to-all | bytes 2097152 | tf_op jit(solution)/shard_map/all_to_all | solution.py:429
  41.7 3.6 %all-to-all-start.1 = ((bf16[8,256,256]{2,1,0:T(8,128)(2,1)}), bf16[8,256,256]{2,1,0:T(8,128)(2,1)S(1)}, u32[]{:S(2)}, u32[]{:S(2)}) async-start(bf16[8,256,256]{2,1,0:T(8,128)(2,1)} %get-tuple-element.14), calls=%async_computation.1 | async-start | bytes 2097152 | tf_op jit(solution)/shard_map/all_to_all | solution.py:429
  45.2 0.0 reduce-scatter.5.cloned.1.call-start
  45.3 0.0 copy-done.3
  45.3 0.1 convert_element_type.18
  45.4 0.1 fusion
  45.5 14.9 %all_gather.7.here_ref = bf16[4,2,3,64,128]{4,3,2,1,0:T(8,128)(2,1)S(1)} all-gather(bf16[1,2,3,64,128]{4,3,2,1,0:T(8,128)(2,1)S(1)} %copy.16), channel_id=1, replica_groups=mesh['tile'=8,'slab'=4] {'slab'}, dimensions={0}, use_global_device_ids=true | all-gather | bytes 491520 | tf_op jit(solution)/shard_map/all_gather | solution.py:436
  60.4 0.0 copy-start
  60.4 0.9 collective-permute-start.1
  61.4 14.6 %all_gather.6.here_ref = bf16[4,2,3,64,128]{4,3,2,1,0:T(8,128)(2,1)S(1)} all-gather(bf16[1,2,3,64,128]{4,3,2,1,0:T(8,128)(2,1)S(1)} %copy.15), channel_id=1, replica_groups=mesh['tile'=8,'slab'=4] {'slab'}, dimensions={0}, use_global_device_ids=true | all-gather | bytes 491520 | tf_op jit(solution)/shard_map/all_gather | solution.py:436
  76.0 0.0 copy-start.1
  76.0 1.4 collective-permute-start
  77.4 0.0 collective-permute-done.1.next_ref
  77.4 0.0 copy-start.2
  77.4 0.0 copy-done
  77.4 0.7 copy-done.2
  78.1 12.6 %waves.1.wave_ref = f32[16,2,256,256]{3,2,1,0:T(8,128)} custom-call(s32[72]{0:T(128)} %get-tuple-element.9.meta_ref, bf16[4,2,3,64,128]{4,3,2,1,0:T(8,128)(2,1)} %copy-done, bf16[4,2,3,64,128]{4,3,2,1,0:T(8,128)(2,1)} %copy-done.2, f32[256,512]{1,0:T(8,128)} %probe_ref.3, f32[2,256,256]{2,1,0:T(8,128)} %constant.27.clone.kernel_ref, ...), custom_call_target="tpu_custom_call" | custom-call | tf_op jit(solution)/shard_map/waves/pallas_call | solution.py:342
  90.7 0.0 copy-done.1
  90.7 0.0 all-to-all-done.1
  90.7 1.5 pad_maximum_fusion.image0.image1
  92.3 0.0 collective-permute-done.next_ref
  92.3 0.0 copy-start.4
  92.3 0.8 copy-done.4
  93.0 20.7 %misfits.1 = (bf16[16,2,256,256]{3,2,1,0:T(8,128)(2,1)}, f32[2,3,512,128]{3,2,1,0:T(8,128)}) custom-call(s32[72]{0:T(128)} %get-tuple-element.9.meta_ref, bf16[4,2,3,64,128]{4,3,2,1,0:T(8,128)(2,1)} %copy-done.1, bf16[4,2,3,64,128]{4,3,2,1,0:T(8,128)(2,1)} %copy-done.4, f32[16,2,256,256]{3,2,1,0:T(8,128)} %waves.1.wave_ref, ...), custom_call_target="tpu_custom_call" | custom-call | tf_op jit(solution)/shard_map/misfits/pallas_call | solution.py:367
  113.8 1.2 slice.45
  115.0 2.3 %collective-permute-start.3 = (bf16[2,3,256,128]{3,2,1,0:T(8,128)(2,1)S(1)}, bf16[2,3,256,128]{3,2,1,0:T(8,128)(2,1)S(1)}, u32[]{:S(2)}, u32[]{:S(2)}) collective-permute-start(bf16[2,3,256,128]{3,2,1,0:T(8,128)(2,1)S(1)} %slice.45), channel_id=1, source_target_pairs={{0,4},{4,8},{8,12},{12,16},{16,20},{20,24},{24,28},{28,0},{1,5},{5... | collective-permute-start | bytes 1179656 | tf_op jit(solution)/shard_map/ppermute | solution.py:411
  117.3 5.8 %collective-permute-done.3 = bf16[2,3,256,128]{3,2,1,0:T(8,128)(2,1)S(1)} collective-permute-done((bf16[2,3,256,128]{3,2,1,0:T(8,128)(2,1)S(1)}, bf16[2,3,256,128]{3,2,1,0:T(8,128)(2,1)S(1)}, u32[]{:S(2)}, u32[]{:S(2)}) %collective-permute-start.3) | collective-permute-done | bytes 393248 | tf_op jit(solution)/shard_map/ppermute | solution.py:411
  123.1 2.2 %convert_add_fusion = f32[2,3,256,128]{3,2,1,0:T(8,128)} fusion(bf16[2,3,256,128]{3,2,1,0:T(8,128)(2,1)S(1)} %collective-permute-done.3, f32[2,3,512,128]{3,2,1,0:T(8,128)} %get-tuple-element.12), kind=kLoop, calls=%fused_computation.6 | loop fusion | flops 393216 | bytes 1966080 | tf_op jit(solution)/shard_map/add | solution.py:445
  125.3 0.0 reduce-scatter.5.cloned.1.call-update
  125.3 0.0 reduce-scatter.3.cloned.1.call-start
  125.3 10.0 %exits.1 = f32[2,3,512,128]{3,2,1,0:T(8,128)} custom-call(s32[72]{0:T(128)} %get-tuple-element.9.meta_ref, bf16[16,2,256,256]{3,2,1,0:T(8,128)(2,1)} %get-tuple-element.11.back_ref, f32[256,512]{1,0:T(8,128)} %probe_ref.3, bf16[256,256]{1,0:T(8,128)(2,1)} %constant.23.clone.a0, bf16[256,256]{1,0:T(8,128)(2,1)} %constant.24.clone.t0, ...), custom_call_target="tpu_custom_call" | custom-call | tf_op jit(solution)/shard_map/exits/pallas_call | solution.py:393
  135.4 1.2 slice.46
  136.6 0.1 collective-permute-start.2
  136.6 8.1 %collective-permute-done.2 = bf16[2,3,256,128]{3,2,1,0:T(8,128)(2,1)S(1)} collective-permute-done((bf16[2,3,256,128]{3,2,1,0:T(8,128)(2,1)S(1)}, bf16[2,3,256,128]{3,2,1,0:T(8,128)(2,1)S(1)}, u32[]{:S(2)}, u32[]{:S(2)}) %collective-permute-start.2) | collective-permute-done | bytes 393248 | tf_op jit(solution)/shard_map/ppermute | solution.py:411
  144.7 2.1 %slice_add_fusion = f32[2,3,256,128]{3,2,1,0:T(8,128)} fusion(f32[2,3,512,128]{3,2,1,0:T(8,128)} %exits.1, bf16[2,3,256,128]{3,2,1,0:T(8,128)(2,1)S(1)} %collective-permute-done.2), kind=kLoop, calls=%fused_computation.5 | loop fusion | flops 393216 | bytes 1966080 | tf_op jit(solution)/shard_map/add | solution.py:445
  146.8 0.0 reduce-scatter.3.cloned.1.call-update
  146.8 4.8 %reduce-scatter.5.cloned.1.call-done = f32[2,3,64,128]{3,2,1,0:T(8,128)} async-done(((f32[2,3,256,128]{3,2,1,0:T(8,128)}), f32[2,3,64,128]{3,2,1,0:T(8,128)}) %reduce-scatter.5.cloned.1.call-update) | async-done | bytes 196624 | tf_op jit(solution)/shard_map/reduce_scatter | solution.py:446
  151.7 25.0 %reduce-scatter.3.cloned.1.call-done = f32[2,3,64,128]{3,2,1,0:T(8,128)} async-done(((f32[2,3,256,128]{3,2,1,0:T(8,128)}), f32[2,3,64,128]{3,2,1,0:T(8,128)}) %reduce-scatter.3.cloned.1.call-update) | async-done | bytes 196624 | tf_op jit(solution)/shard_map/reduce_scatter | solution.py:446
  176.6 1.8 copy_bitcast_fusion
  (3 shorter events, 0.1 us)
Async XLA Ops:
  21.2 24.1 %copy-start.3 = (f32[2,2,64,384]{3,2,1,0:T(8,128)S(1)}, f32[2,2,64,384]{3,2,1,0:T(8,128)}, u32[]{:S(2)}) copy-start(f32[2,2,64,384]{3,2,1,0:T(8,128)} %param.13) | copy-start | bytes 1179652
  41.7 49.1 %all-to-all-start.1 = ((bf16[8,256,256]{2,1,0:T(8,128)(2,1)}), bf16[8,256,256]{2,1,0:T(8,128)(2,1)S(1)}, u32[]{:S(2)}, u32[]{:S(2)}) async-start(bf16[8,256,256]{2,1,0:T(8,128)(2,1)} %get-tuple-element.14), calls=%async_computation.1 | async-start | bytes 2097152 | tf_op jit(solution)/shard_map/all_to_all | solution.py:429
  45.2 106.5 %reduce-scatter.5.cloned.1.call-start = ((), (), s32[]{:S(2)}) async-start(), calls=%async_computation.5 | async-start | bytes 983040 | tf_op jit(solution)/shard_map/reduce_scatter | solution.py:446
  60.4 17.0 %copy-start = (bf16[4,2,3,64,128]{4,3,2,1,0:T(8,128)(2,1)}, bf16[4,2,3,64,128]{4,3,2,1,0:T(8,128)(2,1)S(1)}, u32[]{:S(2)}) copy-start(bf16[4,2,3,64,128]{4,3,2,1,0:T(8,128)(2,1)S(1)} %all_gather.7.here_ref) | copy-start | bytes 1179652
  60.4 17.0 %collective-permute-start.1 = (bf16[4,2,3,64,128]{4,3,2,1,0:T(8,128)(2,1)S(1)}, bf16[4,2,3,64,128]{4,3,2,1,0:T(8,128)(2,1)S(1)}, u32[]{:S(2)}, u32[]{:S(2)}) collective-permute-start(bf16[4,2,3,64,128]{4,3,2,1,0:T(8,128)(2,1)S(1)} %all_gather.7.here_ref), channel_id=1, source_target_pairs={{0,28},{4,0},{8,4},{12,8},{16,12},{20,16},{24,20},{28,24},{1,29},{... | collective-permute-start | bytes 1179656 | tf_op jit(solution)/shard_map/ppermute | solution.py:411
  76.0 14.7 %copy-start.1 = (bf16[4,2,3,64,128]{4,3,2,1,0:T(8,128)(2,1)}, bf16[4,2,3,64,128]{4,3,2,1,0:T(8,128)(2,1)S(1)}, u32[]{:S(2)}) copy-start(bf16[4,2,3,64,128]{4,3,2,1,0:T(8,128)(2,1)S(1)} %all_gather.6.here_ref) | copy-start | bytes 1179652
  76.0 16.2 %collective-permute-start = (bf16[4,2,3,64,128]{4,3,2,1,0:T(8,128)(2,1)S(1)}, bf16[4,2,3,64,128]{4,3,2,1,0:T(8,128)(2,1)S(1)}, u32[]{:S(2)}, u32[]{:S(2)}) collective-permute-start(bf16[4,2,3,64,128]{4,3,2,1,0:T(8,128)(2,1)S(1)} %all_gather.6.here_ref), channel_id=1, source_target_pairs={{0,28},{4,0},{8,4},{12,8},{16,12},{20,16},{24,20},{28,24},{1,29},{... | collective-permute-start | bytes 1179656 | tf_op jit(solution)/shard_map/ppermute | solution.py:411
  77.4 0.8 copy-start.2
  92.3 0.8 copy-start.4
  115.0 8.2 %collective-permute-start.3 = (bf16[2,3,256,128]{3,2,1,0:T(8,128)(2,1)S(1)}, bf16[2,3,256,128]{3,2,1,0:T(8,128)(2,1)S(1)}, u32[]{:S(2)}, u32[]{:S(2)}) collective-permute-start(bf16[2,3,256,128]{3,2,1,0:T(8,128)(2,1)S(1)} %slice.45), channel_id=1, source_target_pairs={{0,4},{4,8},{8,12},{12,16},{16,20},{20,24},{24,28},{28,0},{1,5},{5... | collective-permute-start | bytes 1179656 | tf_op jit(solution)/shard_map/ppermute | solution.py:411
  125.3 51.3 %reduce-scatter.3.cloned.1.call-start = ((), (), s32[]{:S(2)}) async-start(), calls=%async_computation.4 | async-start | bytes 983040 | tf_op jit(solution)/shard_map/reduce_scatter | solution.py:446
  136.6 8.2 %collective-permute-start.2 = (bf16[2,3,256,128]{3,2,1,0:T(8,128)(2,1)S(1)}, bf16[2,3,256,128]{3,2,1,0:T(8,128)(2,1)S(1)}, u32[]{:S(2)}, u32[]{:S(2)}) collective-permute-start(bf16[2,3,256,128]{3,2,1,0:T(8,128)(2,1)S(1)} %slice.46), channel_id=1, source_target_pairs={{0,4},{4,8},{8,12},{12,16},{16,20},{20,24},{24,28},{28,0},{1,5},{5... | collective-permute-start | bytes 1179656 | tf_op jit(solution)/shard_map/ppermute | solution.py:411
Sparse Core Ops, SparseCore 0:
  125.4 26.2 reduce-scatter.4
  154.0 22.6 reduce-scatter.2

commit v2 on v1

v2 whole, which is shorter than its diff:
```python
import functools
import math

import jax
import jax.numpy as jnp
import ml_dtypes
import numpy as np
from jax import lax
from jax.experimental import pallas as pl
from jax.experimental.pallas import tpu as pltpu
from jax.sharding import PartitionSpec as P

K = 16
CAP = 2
COLS = 128
chirp_strength = 40.0
bf16 = jnp.bfloat16
f32 = jnp.float32


def make_tables(extent):
    counter = np.arange(extent, dtype=np.int64)
    angles = (counter[:, None] * counter[None, :] % extent).astype(np.float32) * np.float32(
        2.0 * math.pi / extent
    )
    scaling = np.float32(1.0 / math.sqrt(extent))
    cosine = (np.cos(angles) * scaling).astype(ml_dtypes.bfloat16)
    sine_part = (np.sin(angles) * scaling).astype(ml_dtypes.bfloat16)
    half = extent // 2
    tables = []
    for parity in (0, 1):
        c, s = cosine[:half, parity::2], sine_part[:half, parity::2]
        table = np.concatenate([np.concatenate([c, -s], 1), np.concatenate([s, c], 1)], 0)
        tables += [table, np.ascontiguousarray(table.T)]
    order = np.concatenate([counter[0::2], counter[1::2]])
    frequency = (((counter + half) % extent - half).astype(np.float32) / extent)[order]
    phases = np.float32(chirp_strength) * (frequency[:, None] ** 2 + frequency[None, :] ** 2)
    kernel = np.stack([np.cos(phases), -np.sin(phases)]).astype(np.float32)
    permute = (counter[:, None] == order[None, :]).astype(ml_dtypes.bfloat16)
    return [jnp.asarray(t) for t in tables], jnp.asarray(kernel), jnp.asarray(permute)


def dot(a, b):
    return jnp.dot(a, b, preferred_element_type=f32)


def quads(a, b, h):
    return jnp.concatenate(
        [
            jnp.concatenate([a[:, :h], b[:, :h]], 1),
            jnp.concatenate([a[:, h:], b[:, h:]], 1),
        ],
        0,
    )


def forward(items, tabs):
    a_even, t_even, a_odd, t_odd = tabs
    h = a_even.shape[0] // 2
    sums = [jnp.concatenate([l[0] + r[0], l[1] + r[1]], 1).astype(bf16) for l, r in items]
    diffs = [jnp.concatenate([l[0] - r[0], l[1] - r[1]], 1).astype(bf16) for l, r in items]
    even = [dot(x, a_even) for x in sums]
    odd = [dot(x, a_odd) for x in diffs]
    plus = [quads(a[:h] + a[h:], b[:h] + b[h:], h).astype(bf16) for a, b in zip(even, odd)]
    minus = [quads(a[:h] - a[h:], b[:h] - b[h:], h).astype(bf16) for a, b in zip(even, odd)]
    return list(zip([dot(t_even, x) for x in plus], [dot(t_odd, x) for x in minus]))


def inverse(items, tabs):
    a_even, t_even, a_odd, t_odd = tabs
    h = a_even.shape[0] // 2

    def side(x, k):
        lanes = slice(k * h, (k + 1) * h)
        return jnp.concatenate(
            [jnp.concatenate([part[:h, lanes], part[h:, lanes]], 1) for part in x], 0
        )

    even = [dot(side(x, 0), t_even) for x in items]
    odd = [dot(side(x, 1), t_odd) for x in items]
    plus = [a + b for a, b in zip(even, odd)]
    minus = [a - b for a, b in zip(even, odd)]
    low = [dot(a_even, quads(a[:h], b[:h], h).astype(bf16)) for a, b in zip(plus, minus)]
    high = [dot(a_odd, quads(a[h:], b[h:], h).astype(bf16)) for a, b in zip(plus, minus)]
    out = []
    for a, b in zip(low, high):
        s, d = a + b, a - b
        out.append(
            (jnp.concatenate([s[:h], d[:h]], 0), jnp.concatenate([s[h:], d[h:]], 0))
        )
    return out


def product(a, b):
    return a[0] * b[0] - a[1] * b[1], a[0] * b[1] + a[1] * b[0]


def product_conj(a, b):
    return a[0] * b[0] + a[1] * b[1], a[0] * b[1] - a[1] * b[0]


def halves(x, h=COLS):
    return (x[0][:, :h], x[1][:, :h]), (x[0][:, h:], x[1][:, h:])


def by_kernel(field, kernel_ref, conjugate):
    out = []
    h = field[0].shape[0] // 2
    op = product_conj if conjugate else product
    for k, part in enumerate(field):
        rows = slice(k * h, (k + 1) * h)
        spread = op((kernel_ref[0, rows, :], kernel_ref[1, rows, :]), (part[:h], part[h:]))
        out.append(jnp.concatenate(spread, 0).astype(bf16))
    return out


def window(rows_ref, top, col, extent):
    return tuple(
        tuple(rows_ref[plane, col + j, pl.ds(top, extent), :] for plane in (0, 1)) for j in (0, 1)
    )


def load_rows(slab_here, chunks, rows_ref):
    joined = len(chunks[0].shape) == 5
    count = len(chunks) if joined else len(chunks) // 2
    height = chunks[0].shape[-2]
    for side in (0, 1):
        for k in range(count):
            place = lax.rem(slab_here + count - k, count)
            start = pl.multiple_of((side * count + place) * height, height)
            shard = chunks[k][side] if joined else chunks[side * count + k][...]
            rows_ref[:, :, pl.ds(start, height), :] = shard.astype(f32)


def add_window(totals_ref, top, col, term):
    extent = term[0][0].shape[0]
    for j in (0, 1):
        for plane in (0, 1):
            place = (plane, col + j, pl.ds(top, extent), slice(None))
            totals_ref[place] += term[j][plane]


def route_kernel(here_ref, owner_ref, row_ref, col_ref, images_ref, permute_ref, out_ref, meta_ref, second_ref, turned_ref):
    reads, extent, _ = images_ref.shape
    tiles = out_ref.shape[0] // CAP
    tile_here, slab_here, slabs = here_ref[0], here_ref[1], here_ref[2]
    mine = (tile_here * slabs + slab_here) * reads

    owners = [owner_ref[mine + i] for i in range(reads)]
    for i in range(reads):
        turned_ref[i] = dot(images_ref[i], permute_ref[0]).astype(bf16)
    for i in range(reads):
        rank = jnp.int32(0)
        for j in range(i):
            rank += (owners[j] == owners[i]).astype(jnp.int32)
        out_ref[owners[i] * CAP + rank] = dot(permute_ref[1], turned_ref[i]).astype(bf16)

    def sender(g, counts):
        base = (g * slabs + slab_here) * reads
        first, later = counts
        seen = jnp.int32(0)
        for i in range(reads):
            match = (owner_ref[base + i] == tile_here).astype(jnp.int32)
            meta_ref[first] = base + i
            second_ref[later] = base + i
            fresh = match * (1 - seen)
            first, later, seen = first + fresh, later + match - fresh, seen + match
        return first, later

    first, later = lax.fori_loop(0, tiles, sender, (jnp.int32(0), jnp.int32(0)))
    total = first + later
    for i in range(K):
        in_first = i < first
        live = i < total
        row = jnp.where(in_first, meta_ref[i], second_ref[jnp.maximum(i - first, 0)])
        row = jnp.where(live, row, 0)
        group = row // (slabs * reads)
        meta_ref[i] = group * CAP + jnp.where(in_first, 0, 1)
        meta_ref[K + i] = row_ref[row]
        meta_ref[2 * K + i] = col_ref[row]
        meta_ref[3 * K + i] = jnp.where(live, row_ref[row], 2 * extent)
    meta_ref[4 * K] = total
    meta_ref[4 * K + 1] = first
    meta_ref[4 * K + 2] = slab_here


def give_totals(totals_ref, own_ref, lower_ref):
    rows = own_ref.shape[2]
    own_ref[...] = totals_ref[:, :, :rows, :]
    lower_ref[...] = totals_ref[:, :, rows : 2 * rows, :].astype(bf16)


def combine_kernel(here_ref, own_ref, moved_ref, mine_ref, *send_refs):
    height = mine_ref.shape[2]
    count = len(send_refs) + 1
    for k in range(count):
        place = lax.rem(here_ref[1] + k, count)
        rows = pl.ds(pl.multiple_of(place * height, height), height)
        both = own_ref[:, :, rows, :] + moved_ref[:, :, rows, :].astype(f32)
        if k == 0:
            mine_ref[...] = both
        else:
            send_refs[k - 1][...] = both.astype(bf16)


def finish_kernel(count, *refs):
    out_ref = refs[-1]
    for s in range(out_ref.shape[0]):
        parts = refs[s * count : (s + 1) * count]
        for plane in (0, 1):
            for block in range(parts[0].shape[1]):
                total = parts[0][plane, block]
                for part in parts[1:]:
                    total = total + part[plane, block].astype(f32)
                out_ref[s, plane, :, block * COLS : (block + 1) * COLS] = total


def pair_loop(meta_ref, body):
    def step(i, carry):
        body(2 * i, 2 * i + 1)
        return carry

    lax.fori_loop(0, lax.div(meta_ref[4 * K] + 1, 2), step, 0)


def wave_kernel(count, meta_ref, *refs):
    chunks, (probe_ref, kernel_ref, a0, t0, a1, t1, wave_ref, rows_ref) = refs[:count], refs[count:]
    extent = probe_ref.shape[0]
    load_rows(meta_ref[4 * K + 2], chunks, rows_ref)

    def body(*pair):
        tabs = a0[...], t0[...], a1[...], t1[...]
        probe = halves((probe_ref[:, :extent], probe_ref[:, extent:]))
        items = []
        for at in pair:
            w = window(rows_ref, meta_ref[K + at], meta_ref[2 * K + at], extent)
            items.append(tuple(product(p, q) for p, q in zip(probe, w)))
        spread = [by_kernel(x, kernel_ref, False) for x in forward(items, tabs)]
        for at, wave in zip(pair, inverse(spread, tabs)):
            wave_ref[at, 0] = wave[0]
            wave_ref[at, 1] = wave[1]

    pair_loop(meta_ref, body)


def misfit_kernel(count, meta_ref, *refs):
    chunks = refs[:count]
    wave_ref, images_ref, kernel_ref, a0, t0, a1, t1 = refs[count : count + 7]
    back_ref, own_ref, lower_ref, rows_ref, totals_ref = refs[count + 7 :]
    extent = images_ref.shape[1]
    h = extent // 2
    load_rows(meta_ref[4 * K + 2], chunks, rows_ref)
    totals_ref[...] = jnp.zeros_like(totals_ref)

    def body(*pair):
        tabs = a0[...], t0[...], a1[...], t1[...]
        items = []
        for at in pair:
            w = window(rows_ref, meta_ref[K + at], meta_ref[2 * K + at], extent)
            wave = halves((wave_ref[at, 0], wave_ref[at, 1]))
            items.append(tuple(product(p, q) for p, q in zip(wave, w)))
        far_grads = []
        for at, far in zip(pair, forward(items, tabs)):
            slot = meta_ref[at]
            parts = []
            for k, part in enumerate(far):
                re, im = part[:h], part[h:]
                image = images_ref[slot, k * h : (k + 1) * h, :].astype(f32)
                misfit = re * re + im * im - image
                parts.append(jnp.concatenate([re * misfit, im * misfit], 0).astype(bf16))
            far_grads.append(parts)
        back = []
        for at, grad in zip(pair, inverse(far_grads, tabs)):
            grad = halves(grad)
            wave = halves((wave_ref[at, 0], wave_ref[at, 1]))
            col = meta_ref[2 * K + at]
            add_window(
                totals_ref, meta_ref[3 * K + at], col,
                [product_conj(p, q) for p, q in zip(wave, grad)],
            )
            w = window(rows_ref, meta_ref[K + at], col, extent)
            back.append(tuple(product_conj(p, q) for p, q in zip(w, grad)))
        for at, field in zip(pair, forward(back, tabs)):
            for k, part in enumerate(by_kernel(field, kernel_ref, True)):
                back_ref[at, k] = part

    pair_loop(meta_ref, body)
    give_totals(totals_ref, own_ref, lower_ref)


def exit_kernel(meta_ref, back_ref, probe_ref, a0, t0, a1, t1, own_ref, lower_ref, totals_ref):
    extent = probe_ref.shape[0]
    totals_ref[...] = jnp.zeros_like(totals_ref)

    def body(*pair):
        tabs = a0[...], t0[...], a1[...], t1[...]
        probe = halves((probe_ref[:, :extent], probe_ref[:, extent:]))
        fields = [(back_ref[at, 0], back_ref[at, 1]) for at in pair]
        for at, grad in zip(pair, inverse(fields, tabs)):
            add_window(
                totals_ref, meta_ref[3 * K + at], meta_ref[2 * K + at],
                [product_conj(p, q) for p, q in zip(probe, halves(grad))],
            )

    pair_loop(meta_ref, body)
    give_totals(totals_ref, own_ref, lower_ref)


VMEM = 32 * 1024 * 1024


def call(kernel, name, ins, outs, scratch, estimate):
    smem = pl.BlockSpec(memory_space=pltpu.SMEM)
    vmem = pl.BlockSpec(memory_space=pltpu.VMEM)
    single = not isinstance(outs, list)
    return pl.pallas_call(
        kernel,
        in_specs=[smem if x.dtype == jnp.int32 else vmem for x in ins],
        out_specs=vmem if single else [smem if x.dtype == jnp.int32 else vmem for x in outs],
        out_shape=outs,
        scratch_shapes=scratch,
        compiler_params=pltpu.CompilerParams(vmem_limit_bytes=VMEM),
        cost_estimate=estimate,
        name=name,
    )(*ins)


def cost(transforms, extent):
    return pl.CostEstimate(
        flops=int(K * transforms * 8 * 2 * extent**3), bytes_accessed=0, transcendentals=0
    )


def route(images, here, owner_tile, row_offset, col_offset, permute, tiles):
    reads, extent = images.shape[:2]
    outs = [
        jax.ShapeDtypeStruct((CAP * tiles, extent, extent), bf16),
        jax.ShapeDtypeStruct((4 * K + 8,), jnp.int32),
    ]
    scratch = [pltpu.SMEM((K + 8,), jnp.int32), pltpu.VMEM(images.shape, bf16)]
    ins = [here, owner_tile, row_offset, col_offset, images, permute]
    return call(route_kernel, "route", ins, outs, scratch, cost(0.25, extent))


def waves(meta, chunks, probe, kernel, tabs):
    extent = probe.shape[0]
    return call(
        functools.partial(wave_kernel, len(chunks)),
        "waves",
        [meta] + chunks + [probe, kernel] + tabs,
        jax.ShapeDtypeStruct((K, 2, extent, extent), f32),
        [pltpu.VMEM((2, chunks[0].shape[-3], 2 * extent, COLS), f32)],
        cost(2, extent),
    )


def totals_out(extent, blocks):
    shape = (2, blocks, extent, COLS)
    outs = [jax.ShapeDtypeStruct(shape, f32), jax.ShapeDtypeStruct(shape, bf16)]
    return outs, pltpu.VMEM((2, blocks, 3 * extent, COLS), f32)


def misfits(meta, chunks, wave, images, kernel, tabs):
    extent = images.shape[1]
    blocks = chunks[0].shape[-3]
    outs, totals = totals_out(extent, blocks)
    return call(
        functools.partial(misfit_kernel, len(chunks)),
        "misfits",
        [meta] + chunks + [wave, images, kernel] + tabs,
        [jax.ShapeDtypeStruct((K, 2, extent, extent), bf16)] + outs,
        [pltpu.VMEM((2, blocks, 2 * extent, COLS), f32), totals],
        cost(3, extent),
    )


def exits(meta, back, probe, tabs, blocks):
    extent = probe.shape[0]
    outs, totals = totals_out(extent, blocks)
    return call(
        exit_kernel, "exits", [meta, back, probe] + tabs, outs, [totals], cost(1, extent)
    )


def combine(here, own, moved, count):
    shape = own.shape[:2] + (own.shape[2] // count, COLS)
    outs = [jax.ShapeDtypeStruct(shape, f32 if k == 0 else bf16) for k in range(count)]
    return call(combine_kernel, "combine", [here, own, moved], outs, [], None)


def finish(parts, count):
    blocks, height = parts[0].shape[1:3]
    out = jax.ShapeDtypeStruct((len(parts) // count, 2, height, blocks * COLS), f32)
    return call(functools.partial(finish_kernel, count), "finish", parts, out, [], None)


def passed_along(value, axis, steps):
    count = lax.axis_size(axis)
    pairs = [(source, (source + steps) % count) for source in range(count)]
    return lax.ppermute(value, axis, pairs)


def shards(intensities, object_field, probe_wave, owner_tile, row_offset, col_offset):
    tile_count = lax.axis_size("tile")
    slab_count = lax.axis_size("slab")
    extent = intensities.shape[1]
    depth, _, height, width = object_field.shape
    blocks = width // COLS
    tabs, kernel, permute = make_tables(extent)
    here = jnp.stack(
        [lax.axis_index("tile"), lax.axis_index("slab"), jnp.int32(slab_count)]
    ).astype(jnp.int32)
    own = jnp.transpose(
        object_field.reshape(depth, 2, height, blocks, COLS), (0, 1, 3, 2, 4)
    ).astype(bf16)
    following = passed_along(own, "tile", -1)
    packed, meta = route(
        intensities, here, owner_tile, row_offset, col_offset,
        jnp.stack([permute, permute.T]), tile_count,
    )
    packed, following = lax.optimization_barrier((packed, following))
    images = lax.all_to_all(packed, "tile", split_axis=0, concat_axis=0, tiled=True)
    first = [
        side[0] if k == 0 else passed_along(side[0], "slab", k)
        for side in (own, following)
        for k in range(slab_count)
    ]
    second = jnp.stack([own[1], following[1]])
    *first, second = lax.optimization_barrier((*first, second))
    second = [second if k == 0 else passed_along(second, "slab", k) for k in range(slab_count)]
    wave = waves(meta, first, probe_wave, kernel, tabs)
    back, own1, lower1 = misfits(meta, second, wave, images, kernel, tabs)
    own0, lower0 = exits(meta, back, probe_wave, tabs, blocks)
    parts = []
    for total, lower in ((own0, lower0), (own1, lower1)):
        moved = passed_along(lower, "tile", 1)
        mine, *sends = combine(here, total, moved, slab_count)
        parts.append(mine)
        parts += [passed_along(x, "slab", k + 1) for k, x in enumerate(sends)]
    return finish(parts, slab_count)


def solution(mesh):
    placed = (
        P(("tile", "slab"), None, None),
        P(None, None, ("tile", "slab"), None),
        P(),
        P(),
        P(),
        P(),
    )
    return jax.shard_map(
        shards,
        mesh=mesh,
        in_specs=placed,
        out_specs=P(None, None, ("tile", "slab"), None),
        check_vma=False,
    )
```

time: 185 us -> 120 us (0.65)
  blocking collectives: 50 us -> 0 us
  starting transfers between devices: 8.34 us -> 34.8 us
  waiting for transfers between devices: 43.7 us -> 25.7 us
  Pallas kernels: 54.7 us -> 37.5 us
  between operations: 13.5 us -> 0.16 us
  local copies, waits for them, and re-layouts: 6.82 us -> 20 us
  other arithmetic: 8.17 us -> 1.12 us
    reduce_scatter x2 -> x0, waiting for transfers between devices: 29.8 us -> none  [shards(): lax.psum_scatter(combined, 'slab', scatter_dimension=2, tiled=True)]
    all_gather x2 -> x0, blocking collectives: 29.6 us -> none  [shards(): lax.all_gather(own[s], 'slab', axis=0, tiled=False)]
    ppermute x4 -> x18, starting transfers between devices: 4.7 us -> 31 us  [passed_along(): return lax.ppermute(value, axis, pairs)]
    all_to_all x1 -> x0, blocking collectives: 20.4 us -> none  [shards(): lax.all_to_all(packed[rank], 'tile', split_axis=0, concat_axis=0, tiled=T...]
    unnamed x10 -> x36, local copies, waits for them, and re-layouts: 1.52 us -> 20 us
    pallas_call x4 -> x7, Pallas kernels: 54.7 us -> 37.5 us  [call(): pl.pallas_call(kernel, in_specs=[smem if x.dtype == jnp.int32 else vmem f...]
    ppermute x4 -> x18, waiting for transfers between devices: 13.9 us -> 25.7 us  [passed_along(): return lax.ppermute(value, axis, pairs)]
    add x2 -> x0, other arithmetic: 4.25 us -> none  [shards(): combined = total[:, :, :tile_rows] + moved.astype(f32)]
  transfers between devices with their start and end apart: 7 -> 19, of which waited for: 4 -> 5; matrix products, arithmetic and copies ran while one was open for 3% -> 0% of each run, Pallas kernels for 12% -> 11%
where the time goes in v2:
time: 120 us; the launch traced here: 119 us
  Pallas kernels  37.5 us (31%)
  starting transfers between devices  34.8 us (29%)
  waiting for transfers between devices  25.7 us (21%)
  local copies, waits for them, and re-layouts  20 us (17%)
    pallas_call x7, Pallas kernels, call(): pl.pallas_call(kernel, in_specs=[smem if x.dtype == jnp.int32 else vmem f...  37.5 us
    ppermute x18, starting transfers between devices, passed_along(): return lax.ppermute(value, axis, pairs)  31 us
    ppermute x18, waiting for transfers between devices, passed_along(): return lax.ppermute(value, axis, pairs)  25.7 us
    unnamed x36, local copies, waits for them, and re-layouts  20 us
    all_to_all x1, starting transfers between devices, shards(): lax.all_to_all(packed, 'tile', split_axis=0, concat_axis=0, tiled=True)  3.73 us
  transfers between devices with their start and end apart: 19, of which 5 were waited for; matrix products, arithmetic and copies ran while one was open for 0% of the time, Pallas kernels for 11%

profile of v2, /device:TPU:0, one launch (start us, length us, event | category | flops | bytes accessed | tf_op | source)
XLA Modules:
  0.0 119.3 jit_solution(1245182986535286781)
XLA Ops:
  0.0 1.0 bitcast_bitcast_fusion
  1.0 3.4 %collective-permute-start.3 = (bf16[2,2,3,64,128]{4,3,2,1,0:T(8,128)(2,1)S(1)}, bf16[2,2,3,64,128]{4,3,2,1,0:T(8,128)(2,1)S(1)}, u32[]{:S(2)}, u32[]{:S(2)}) collective-permute-start(bf16[2,2,3,64,128]{4,3,2,1,0:T(8,128)(2,1)S(1)} %bitcast_bitcast_fusion), channel_id=1, source_target_pairs={{0,28},{4,0},{8,4},{12,8},{16,12},{20,16},{24,20},{28,24},{1,29},{... | collective-permute-start | bytes 589832 | tf_op jit(solution)/shard_map/ppermute | solution.py:400
  4.4 0.1 pad_add_fusion.here_ref
  4.5 1.5 %copy-done.1 = bf16[14,256,256]{2,1,0:T(8,128)(2,1)S(1)} copy-done((bf16[14,256,256]{2,1,0:T(8,128)(2,1)S(1)}, bf16[14,256,256]{2,1,0:T(8,128)(2,1)}, u32[]{:S(2)}) %copy-start.1) | copy-done | bytes 1835032
  6.0 0.7 copy-done.3
  6.7 0.7 copy-done.4
  7.4 0.7 copy-done.5
  8.0 0.9 copy-done.8
  9.0 3.1 %route.1 = (bf16[16,256,256]{2,1,0:T(8,128)(2,1)S(1)}, s32[72]{0:T(128)S(1)}) custom-call(s32[3]{0:T(128)S(1)} %pad_add_fusion.here_ref, s32[448]{0:T(512)S(1)} %copy-done.3, s32[448]{0:T(512)S(1)} %copy-done.4, s32[448]{0:T(512)S(1)} %copy-done.5, bf16[14,256,256]{2,1,0:T(8,128)(2,1)S(1)} %copy-done.1, bf16[2,256,256]{2,1,0:T(8,128)(2,1)S(1)} %copy-done.8), custom_call_target="tpu_custom_call" | custom-call | flops 1073741824 | tf_op jit(solution)/shard_map/route/pallas_call | solution.py:316
  12.1 1.3 %copy-done = bf16[16,256,256]{2,1,0:T(8,128)(2,1)} copy-done((bf16[16,256,256]{2,1,0:T(8,128)(2,1)}, bf16[16,256,256]{2,1,0:T(8,128)(2,1)S(1)}, u32[]{:S(2)}) %copy-start) | copy-done | bytes 2097176
  13.4 0.0 collective-permute-done.3
  13.4 3.7 %all-to-all-start = ((bf16[16,256,256]{2,1,0:T(8,128)(2,1)}), bf16[16,256,256]{2,1,0:T(8,128)(2,1)S(1)}, u32[]{:S(2)}, u32[]{:S(2)}) async-start(bf16[16,256,256]{2,1,0:T(8,128)(2,1)} %copy-done), calls=%async_computation | async-start | bytes 4194304 | tf_op jit(solution)/shard_map/all_to_all | solution.py:422
  17.2 3.7 %collective-permute-start.2 = (bf16[2,3,64,128]{3,2,1,0:T(8,128)(2,1)S(1)}, bf16[2,3,64,128]{3,2,1,0:T(8,128)(2,1)S(1)}, u32[]{:S(2)}, u32[]{:S(2)}) collective-permute-start(bf16[2,3,64,128]{3,2,1,0:T(8,128)(2,1)S(1)} %get-tuple-element.35.refs_0_), channel_id=1, source_target_pairs={{0,3},{1,0},{2,1},{3,2},{4,7},{5,4},{6,5},{7,6},{8,11},{9,8},{10,9... | collective-permute-start | bytes 294920 | tf_op jit(solution)/shard_map/ppermute | solution.py:400
  20.8 0.0 collective-permute-start.1
  20.8 1.0 collective-permute-start
  21.9 2.9 %collective-permute-start.6 = (bf16[2,3,64,128]{3,2,1,0:T(8,128)(2,1)S(1)}, bf16[2,3,64,128]{3,2,1,0:T(8,128)(2,1)S(1)}, u32[]{:S(2)}, u32[]{:S(2)}) collective-permute-start(bf16[2,3,64,128]{3,2,1,0:T(8,128)(2,1)S(1)} %get-tuple-element.39.refs_4_), channel_id=1, source_target_pairs={{0,3},{1,0},{2,1},{3,2},{4,7},{5,4},{6,5},{7,6},{8,11},{9,8},{10,9... | collective-permute-start | bytes 294920 | tf_op jit(solution)/shard_map/ppermute | solution.py:400
  24.7 1.1 collective-permute-start.5
  25.9 0.0 collective-permute-done.2.refs_3_
  25.9 0.0 collective-permute-start.4
  25.9 5.4 %collective-permute-done.1.refs_2_ = bf16[2,3,64,128]{3,2,1,0:T(8,128)(2,1)S(1)} collective-permute-done((bf16[2,3,64,128]{3,2,1,0:T(8,128)(2,1)S(1)}, bf16[2,3,64,128]{3,2,1,0:T(8,128)(2,1)S(1)}, u32[]{:S(2)}, u32[]{:S(2)}) %collective-permute-start.1) | collective-permute-done | bytes 98336 | tf_op jit(solution)/shard_map/ppermute | solution.py:400
  31.3 0.0 collective-permute-done.refs_1_
  31.3 0.0 collective-permute-done.6.refs_7_
  31.3 7.7 %collective-permute-done.5.refs_6_ = bf16[2,3,64,128]{3,2,1,0:T(8,128)(2,1)S(1)} collective-permute-done((bf16[2,3,64,128]{3,2,1,0:T(8,128)(2,1)S(1)}, bf16[2,3,64,128]{3,2,1,0:T(8,128)(2,1)S(1)}, u32[]{:S(2)}, u32[]{:S(2)}) %collective-permute-start.5) | collective-permute-done | bytes 98336 | tf_op jit(solution)/shard_map/ppermute | solution.py:400
  39.0 0.0 collective-permute-done.4.refs_5_
  39.0 1.5 %collective-permute-start.9 = (bf16[2,2,3,64,128]{4,3,2,1,0:T(8,128)(2,1)S(1)}, bf16[2,2,3,64,128]{4,3,2,1,0:T(8,128)(2,1)S(1)}, u32[]{:S(2)}, u32[]{:S(2)}) collective-permute-start(bf16[2,2,3,64,128]{4,3,2,1,0:T(8,128)(2,1)S(1)} %pad_maximum_fusion.refs_0_), channel_id=1, source_target_pairs={{0,3},{1,0},{2,1},{3,2},{4,7},{5,4},{6,5},{7,6},{8,11},{9,8},{10,9... | collective-permute-start | bytes 589832 | tf_op jit(solution)/shard_map/ppermute | solution.py:400
  40.5 0.4 collective-permute-start.8
  40.9 2.0 %collective-permute-start.7 = (bf16[2,2,3,64,128]{4,3,2,1,0:T(8,128)(2,1)S(1)}, bf16[2,2,3,64,128]{4,3,2,1,0:T(8,128)(2,1)S(1)}, u32[]{:S(2)}, u32[]{:S(2)}) collective-permute-start(bf16[2,2,3,64,128]{4,3,2,1,0:T(8,128)(2,1)S(1)} %pad_maximum_fusion.refs_0_), channel_id=1, source_target_pairs={{0,1},{1,2},{2,3},{3,0},{4,5},{5,6},{6,7},{7,4},{8,9},{9,10},{10,1... | collective-permute-start | bytes 589832 | tf_op jit(solution)/shard_map/ppermute | solution.py:400
  42.9 1.0 copy-done.6
  44.0 0.9 copy-done.10
  44.9 0.9 copy-done.12
  45.8 0.9 copy-done.14
  46.7 9.2 %waves.1.refs_4_ = f32[16,2,256,256]{3,2,1,0:T(8,128)S(1)} custom-call(s32[72]{0:T(128)S(1)} %get-tuple-element.31.meta_ref, bf16[2,3,64,128]{3,2,1,0:T(8,128)(2,1)S(1)} %get-tuple-element.35.refs_0_, bf16[2,3,64,128]{3,2,1,0:T(8,128)(2,1)S(1)} %collective-permute-done.refs_1_, bf16[2,3,64,128]{3,2,1,0:T(8,128)(2,1)S(1)} %collective-permute-done.1.refs_2_, ...), custom_call_target="tpu_custom_call" | custom-call | flops 8589934592 | tf_op jit(solution)/shard_map/waves/pallas_call | solution.py:316
  55.9 3.3 %copy-done.16 = f32[16,2,256,256]{3,2,1,0:T(8,128)} copy-done((f32[16,2,256,256]{3,2,1,0:T(8,128)}, f32[16,2,256,256]{3,2,1,0:T(8,128)S(1)}, u32[]{:S(2)}) %copy-start.16) | copy-done | bytes 8388632
  59.2 0.0 collective-permute-done.9.refs_3_
  59.2 0.0 collective-permute-done.8.refs_2_
  59.2 0.0 collective-permute-done.7.refs_1_
  59.2 0.0 all-to-all-done.refs_5_
  59.2 0.0 copy-start.7
  59.2 1.0 copy-done.7
  60.2 0.9 copy-done.11
  61.1 0.9 copy-done.13
  62.1 0.9 copy-done.15
  63.0 3.4 %copy-done.17 = f32[16,2,256,256]{3,2,1,0:T(8,128)S(1)} copy-done((f32[16,2,256,256]{3,2,1,0:T(8,128)S(1)}, f32[16,2,256,256]{3,2,1,0:T(8,128)}, u32[]{:S(2)}) %copy-start.17) | copy-done | bytes 8388632
  66.3 16.7 %misfits.1 = (bf16[16,2,256,256]{3,2,1,0:T(8,128)(2,1)S(1)}, f32[2,3,256,128]{3,2,1,0:T(8,128)S(1)}, bf16[2,3,256,128]{3,2,1,0:T(8,128)(2,1)S(1)}) custom-call(s32[72]{0:T(128)S(1)} %get-tuple-element.31.meta_ref, bf16[2,2,3,64,128]{4,3,2,1,0:T(8,128)(2,1)S(1)} %pad_maximum_fusion.refs_0_, bf16[2,2,3,64,128]{4,3,2,1,0:T(8,128)(2,1)S(1)} %collective-permute-done.7.refs_1_, ...), custom_call_target="tpu_custom_call" | custom-call | flops 12884901888 | tf_op jit(solution)/shard_map/misfits/pallas_call | solution.py:316
  83.0 6.5 %exits.1 = (f32[2,3,256,128]{3,2,1,0:T(8,128)S(1)}, bf16[2,3,256,128]{3,2,1,0:T(8,128)(2,1)S(1)}) custom-call(s32[72]{0:T(128)S(1)} %get-tuple-element.31.meta_ref, bf16[16,2,256,256]{3,2,1,0:T(8,128)(2,1)S(1)} %get-tuple-element.44.back_ref, f32[256,512]{1,0:T(8,128)S(1)} %copy-done.2, bf16[256,256]{1,0:T(8,128)(2,1)S(1)} %copy-done.15, ...), custom_call_target="tpu_custom_call" | custom-call | flops 4294967296 | tf_op jit(solution)/shard_map/exits/pallas_call | solution.py:316
  89.5 0.1 collective-permute-start.10
  89.6 6.1 %collective-permute-start.14 = (bf16[2,3,256,128]{3,2,1,0:T(8,128)(2,1)S(1)}, bf16[2,3,256,128]{3,2,1,0:T(8,128)(2,1)S(1)}, u32[]{:S(2)}, u32[]{:S(2)}) collective-permute-start(bf16[2,3,256,128]{3,2,1,0:T(8,128)(2,1)S(1)} %get-tuple-element.52), channel_id=1, source_target_pairs={{0,4},{4,8},{8,12},{12,16},{16,20},{20,24},{24,28},{28,0},{1,5},{5... | collective-permute-start | bytes 1179656 | tf_op jit(solution)/shard_map/ppermute | solution.py:400
  95.7 2.0 %collective-permute-done.10.moved_ref = bf16[2,3,256,128]{3,2,1,0:T(8,128)(2,1)S(1)} collective-permute-done((bf16[2,3,256,128]{3,2,1,0:T(8,128)(2,1)S(1)}, bf16[2,3,256,128]{3,2,1,0:T(8,128)(2,1)S(1)}, u32[]{:S(2)}, u32[]{:S(2)}) %collective-permute-start.10) | collective-permute-done | bytes 393248 | tf_op jit(solution)/shard_map/ppermute | solution.py:400
  97.7 0.6 combine.2
  98.3 1.3 %collective-permute-start.11 = (bf16[2,3,64,128]{3,2,1,0:T(8,128)(2,1)S(1)}, bf16[2,3,64,128]{3,2,1,0:T(8,128)(2,1)S(1)}, u32[]{:S(2)}, u32[]{:S(2)}) collective-permute-start(bf16[2,3,64,128]{3,2,1,0:T(8,128)(2,1)S(1)} %get-tuple-element.48), channel_id=1, source_target_pairs={{0,1},{1,2},{2,3},{3,0},{4,5},{5,6},{6,7},{7,4},{8,9},{9,10},{10,1... | collective-permute-start | bytes 294920 | tf_op jit(solution)/shard_map/ppermute | solution.py:400
  99.6 1.4 %collective-permute-start.12 = (bf16[2,3,64,128]{3,2,1,0:T(8,128)(2,1)S(1)}, bf16[2,3,64,128]{3,2,1,0:T(8,128)(2,1)S(1)}, u32[]{:S(2)}, u32[]{:S(2)}) collective-permute-start(bf16[2,3,64,128]{3,2,1,0:T(8,128)(2,1)S(1)} %get-tuple-element.49), channel_id=1, source_target_pairs={{0,2},{1,3},{2,0},{3,1},{4,6},{5,7},{6,4},{7,5},{8,10},{9,11},{10,... | collective-permute-start | bytes 294920 | tf_op jit(solution)/shard_map/ppermute | solution.py:400
  101.0 1.4 %collective-permute-start.13 = (bf16[2,3,64,128]{3,2,1,0:T(8,128)(2,1)S(1)}, bf16[2,3,64,128]{3,2,1,0:T(8,128)(2,1)S(1)}, u32[]{:S(2)}, u32[]{:S(2)}) collective-permute-start(bf16[2,3,64,128]{3,2,1,0:T(8,128)(2,1)S(1)} %get-tuple-element.50), channel_id=1, source_target_pairs={{0,3},{1,0},{2,1},{3,2},{4,7},{5,4},{6,5},{7,6},{8,11},{9,8},{10,9... | collective-permute-start | bytes 294920 | tf_op jit(solution)/shard_map/ppermute | solution.py:400
  102.4 0.0 collective-permute-done.14.moved_ref
  102.4 0.6 combine.3
  103.1 0.8 collective-permute-start.15
  103.8 1.4 %collective-permute-start.16 = (bf16[2,3,64,128]{3,2,1,0:T(8,128)(2,1)S(1)}, bf16[2,3,64,128]{3,2,1,0:T(8,128)(2,1)S(1)}, u32[]{:S(2)}, u32[]{:S(2)}) collective-permute-start(bf16[2,3,64,128]{3,2,1,0:T(8,128)(2,1)S(1)} %get-tuple-element.55), channel_id=1, source_target_pairs={{0,2},{1,3},{2,0},{3,1},{4,6},{5,7},{6,4},{7,5},{8,10},{9,11},{10,... | collective-permute-start | bytes 294920 | tf_op jit(solution)/shard_map/ppermute | solution.py:400
  105.2 0.0 collective-permute-done.11.refs_1_
  105.2 2.6 %collective-permute-start.17 = (bf16[2,3,64,128]{3,2,1,0:T(8,128)(2,1)S(1)}, bf16[2,3,64,128]{3,2,1,0:T(8,128)(2,1)S(1)}, u32[]{:S(2)}, u32[]{:S(2)}) collective-permute-start(bf16[2,3,64,128]{3,2,1,0:T(8,128)(2,1)S(1)} %get-tuple-element.56), channel_id=1, source_target_pairs={{0,3},{1,0},{2,1},{3,2},{4,7},{5,4},{6,5},{7,6},{8,11},{9,8},{10,9... | collective-permute-start | bytes 294920 | tf_op jit(solution)/shard_map/ppermute | solution.py:400
  107.8 3.7 %collective-permute-done.12.refs_2_ = bf16[2,3,64,128]{3,2,1,0:T(8,128)(2,1)S(1)} collective-permute-done((bf16[2,3,64,128]{3,2,1,0:T(8,128)(2,1)S(1)}, bf16[2,3,64,128]{3,2,1,0:T(8,128)(2,1)S(1)}, u32[]{:S(2)}, u32[]{:S(2)}) %collective-permute-start.12) | collective-permute-done | bytes 98336 | tf_op jit(solution)/shard_map/ppermute | solution.py:400
  111.5 0.0 collective-permute-done.13.refs_3_
  111.5 0.0 collective-permute-done.15.refs_5_
  111.5 6.9 %collective-permute-done.16.refs_6_ = bf16[2,3,64,128]{3,2,1,0:T(8,128)(2,1)S(1)} collective-permute-done((bf16[2,3,64,128]{3,2,1,0:T(8,128)(2,1)S(1)}, bf16[2,3,64,128]{3,2,1,0:T(8,128)(2,1)S(1)}, u32[]{:S(2)}, u32[]{:S(2)}) %collective-permute-start.16) | collective-permute-done | bytes 98336 | tf_op jit(solution)/shard_map/ppermute | solution.py:400
  118.5 0.0 collective-permute-done.17.refs_7_
  118.5 0.8 finish.1
  (22 shorter events, 0.1 us)
Async XLA Ops:
  1.0 12.4 %collective-permute-start.3 = (bf16[2,2,3,64,128]{4,3,2,1,0:T(8,128)(2,1)S(1)}, bf16[2,2,3,64,128]{4,3,2,1,0:T(8,128)(2,1)S(1)}, u32[]{:S(2)}, u32[]{:S(2)}) collective-permute-start(bf16[2,2,3,64,128]{4,3,2,1,0:T(8,128)(2,1)S(1)} %bitcast_bitcast_fusion), channel_id=1, source_target_pairs={{0,28},{4,0},{8,4},{12,8},{16,12},{20,16},{24,20},{28,24},{1,29},{... | collective-permute-start | bytes 589832 | tf_op jit(solution)/shard_map/ppermute | solution.py:400
  4.5 1.5 %copy-start.1 = (bf16[14,256,256]{2,1,0:T(8,128)(2,1)S(1)}, bf16[14,256,256]{2,1,0:T(8,128)(2,1)}, u32[]{:S(2)}) copy-start(bf16[14,256,256]{2,1,0:T(8,128)(2,1)} %images_ref.1) | copy-start | bytes 5505028
  6.0 0.7 copy-start.3
  6.7 0.7 copy-start.4
  7.4 0.7 copy-start.5
  8.0 0.9 copy-start.8
  12.1 1.3 %copy-start = (bf16[16,256,256]{2,1,0:T(8,128)(2,1)}, bf16[16,256,256]{2,1,0:T(8,128)(2,1)S(1)}, u32[]{:S(2)}) copy-start(bf16[16,256,256]{2,1,0:T(8,128)(2,1)S(1)} %get-tuple-element.43) | copy-start | bytes 6291460
  13.4 29.5 %copy-start.2 = (f32[256,512]{1,0:T(8,128)S(1)}, f32[256,512]{1,0:T(8,128)}, u32[]{:S(2)}) copy-start(f32[256,512]{1,0:T(8,128)} %probe_ref.1) | copy-start | bytes 1572868
  13.4 29.5 %copy-start.9 = (bf16[256,256]{1,0:T(8,128)(2,1)S(1)}, bf16[256,256]{1,0:T(8,128)(2,1)}, u32[]{:S(2)}) copy-start(bf16[256,256]{1,0:T(8,128)(2,1)} %constant.26.clone.refs_13_.refs_10_.t1) | copy-start | bytes 393220
  13.4 45.8 %all-to-all-start = ((bf16[16,256,256]{2,1,0:T(8,128)(2,1)}), bf16[16,256,256]{2,1,0:T(8,128)(2,1)S(1)}, u32[]{:S(2)}, u32[]{:S(2)}) async-start(bf16[16,256,256]{2,1,0:T(8,128)(2,1)} %copy-done), calls=%async_computation | async-start | bytes 4194304 | tf_op jit(solution)/shard_map/all_to_all | solution.py:422
  17.2 8.7 %collective-permute-start.2 = (bf16[2,3,64,128]{3,2,1,0:T(8,128)(2,1)S(1)}, bf16[2,3,64,128]{3,2,1,0:T(8,128)(2,1)S(1)}, u32[]{:S(2)}, u32[]{:S(2)}) collective-permute-start(bf16[2,3,64,128]{3,2,1,0:T(8,128)(2,1)S(1)} %get-tuple-element.35.refs_0_), channel_id=1, source_target_pairs={{0,3},{1,0},{2,1},{3,2},{4,7},{5,4},{6,5},{7,6},{8,11},{9,8},{10,9... | collective-permute-start | bytes 294920 | tf_op jit(solution)/shard_map/ppermute | solution.py:400
  20.8 10.5 %collective-permute-start.1 = (bf16[2,3,64,128]{3,2,1,0:T(8,128)(2,1)S(1)}, bf16[2,3,64,128]{3,2,1,0:T(8,128)(2,1)S(1)}, u32[]{:S(2)}, u32[]{:S(2)}) collective-permute-start(bf16[2,3,64,128]{3,2,1,0:T(8,128)(2,1)S(1)} %get-tuple-element.35.refs_0_), channel_id=1, source_target_pairs={{0,2},{1,3},{2,0},{3,1},{4,6},{5,7},{6,4},{7,5},{8,10},{9,11},{10,... | collective-permute-start | bytes 294920 | tf_op jit(solution)/shard_map/ppermute | solution.py:400
  20.8 10.5 %collective-permute-start = (bf16[2,3,64,128]{3,2,1,0:T(8,128)(2,1)S(1)}, bf16[2,3,64,128]{3,2,1,0:T(8,128)(2,1)S(1)}, u32[]{:S(2)}, u32[]{:S(2)}) collective-permute-start(bf16[2,3,64,128]{3,2,1,0:T(8,128)(2,1)S(1)} %get-tuple-element.35.refs_0_), channel_id=1, source_target_pairs={{0,1},{1,2},{2,3},{3,0},{4,5},{5,6},{6,7},{7,4},{8,9},{9,10},{10,1... | collective-permute-start | bytes 294920 | tf_op jit(solution)/shard_map/ppermute | solution.py:400
  21.9 9.5 %collective-permute-start.6 = (bf16[2,3,64,128]{3,2,1,0:T(8,128)(2,1)S(1)}, bf16[2,3,64,128]{3,2,1,0:T(8,128)(2,1)S(1)}, u32[]{:S(2)}, u32[]{:S(2)}) collective-permute-start(bf16[2,3,64,128]{3,2,1,0:T(8,128)(2,1)S(1)} %get-tuple-element.39.refs_4_), channel_id=1, source_target_pairs={{0,3},{1,0},{2,1},{3,2},{4,7},{5,4},{6,5},{7,6},{8,11},{9,8},{10,9... | collective-permute-start | bytes 294920 | tf_op jit(solution)/shard_map/ppermute | solution.py:400
  24.7 14.3 %collective-permute-start.5 = (bf16[2,3,64,128]{3,2,1,0:T(8,128)(2,1)S(1)}, bf16[2,3,64,128]{3,2,1,0:T(8,128)(2,1)S(1)}, u32[]{:S(2)}, u32[]{:S(2)}) collective-permute-start(bf16[2,3,64,128]{3,2,1,0:T(8,128)(2,1)S(1)} %get-tuple-element.39.refs_4_), channel_id=1, source_target_pairs={{0,2},{1,3},{2,0},{3,1},{4,6},{5,7},{6,4},{7,5},{8,10},{9,11},{10,... | collective-permute-start | bytes 294920 | tf_op jit(solution)/shard_map/ppermute | solution.py:400
  25.9 13.1 %collective-permute-start.4 = (bf16[2,3,64,128]{3,2,1,0:T(8,128)(2,1)S(1)}, bf16[2,3,64,128]{3,2,1,0:T(8,128)(2,1)S(1)}, u32[]{:S(2)}, u32[]{:S(2)}) collective-permute-start(bf16[2,3,64,128]{3,2,1,0:T(8,128)(2,1)S(1)} %get-tuple-element.39.refs_4_), channel_id=1, source_target_pairs={{0,1},{1,2},{2,3},{3,0},{4,5},{5,6},{6,7},{7,4},{8,9},{9,10},{10,1... | collective-permute-start | bytes 294920 | tf_op jit(solution)/shard_map/ppermute | solution.py:400
  39.0 20.2 %collective-permute-start.9 = (bf16[2,2,3,64,128]{4,3,2,1,0:T(8,128)(2,1)S(1)}, bf16[2,2,3,64,128]{4,3,2,1,0:T(8,128)(2,1)S(1)}, u32[]{:S(2)}, u32[]{:S(2)}) collective-permute-start(bf16[2,2,3,64,128]{4,3,2,1,0:T(8,128)(2,1)S(1)} %pad_maximum_fusion.refs_0_), channel_id=1, source_target_pairs={{0,3},{1,0},{2,1},{3,2},{4,7},{5,4},{6,5},{7,6},{8,11},{9,8},{10,9... | collective-permute-start | bytes 589832 | tf_op jit(solution)/shard_map/ppermute | solution.py:400
  40.5 18.7 %collective-permute-start.8 = (bf16[2,2,3,64,128]{4,3,2,1,0:T(8,128)(2,1)S(1)}, bf16[2,2,3,64,128]{4,3,2,1,0:T(8,128)(2,1)S(1)}, u32[]{:S(2)}, u32[]{:S(2)}) collective-permute-start(bf16[2,2,3,64,128]{4,3,2,1,0:T(8,128)(2,1)S(1)} %pad_maximum_fusion.refs_0_), channel_id=1, source_target_pairs={{0,2},{1,3},{2,0},{3,1},{4,6},{5,7},{6,4},{7,5},{8,10},{9,11},{10,... | collective-permute-start | bytes 589832 | tf_op jit(solution)/shard_map/ppermute | solution.py:400
  40.9 18.3 %collective-permute-start.7 = (bf16[2,2,3,64,128]{4,3,2,1,0:T(8,128)(2,1)S(1)}, bf16[2,2,3,64,128]{4,3,2,1,0:T(8,128)(2,1)S(1)}, u32[]{:S(2)}, u32[]{:S(2)}) collective-permute-start(bf16[2,2,3,64,128]{4,3,2,1,0:T(8,128)(2,1)S(1)} %pad_maximum_fusion.refs_0_), channel_id=1, source_target_pairs={{0,1},{1,2},{2,3},{3,0},{4,5},{5,6},{6,7},{7,4},{8,9},{9,10},{10,1... | collective-permute-start | bytes 589832 | tf_op jit(solution)/shard_map/ppermute | solution.py:400
  42.9 1.0 copy-start.6
  44.0 0.9 copy-start.10
  44.9 0.9 copy-start.12
  45.8 0.9 copy-start.14
  55.9 3.3 %copy-start.16 = (f32[16,2,256,256]{3,2,1,0:T(8,128)}, f32[16,2,256,256]{3,2,1,0:T(8,128)S(1)}, u32[]{:S(2)}) copy-start(f32[16,2,256,256]{3,2,1,0:T(8,128)S(1)} %waves.1.refs_4_) | copy-start | bytes 25165828
  59.2 1.0 copy-start.7
  60.2 0.9 copy-start.11
  61.1 0.9 copy-start.13
  62.0 0.9 copy-start.15
  63.0 3.4 %copy-start.17 = (f32[16,2,256,256]{3,2,1,0:T(8,128)S(1)}, f32[16,2,256,256]{3,2,1,0:T(8,128)}, u32[]{:S(2)}) copy-start(f32[16,2,256,256]{3,2,1,0:T(8,128)} %copy-done.16) | copy-start | bytes 25165828
  89.5 8.2 %collective-permute-start.10 = (bf16[2,3,256,128]{3,2,1,0:T(8,128)(2,1)S(1)}, bf16[2,3,256,128]{3,2,1,0:T(8,128)(2,1)S(1)}, u32[]{:S(2)}, u32[]{:S(2)}) collective-permute-start(bf16[2,3,256,128]{3,2,1,0:T(8,128)(2,1)S(1)} %get-tuple-element.46), channel_id=1, source_target_pairs={{0,4},{4,8},{8,12},{12,16},{16,20},{20,24},{24,28},{28,0},{1,5},{5... | collective-permute-start | bytes 1179656 | tf_op jit(solution)/shard_map/ppermute | solution.py:400
  89.6 12.8 %collective-permute-start.14 = (bf16[2,3,256,128]{3,2,1,0:T(8,128)(2,1)S(1)}, bf16[2,3,256,128]{3,2,1,0:T(8,128)(2,1)S(1)}, u32[]{:S(2)}, u32[]{:S(2)}) collective-permute-start(bf16[2,3,256,128]{3,2,1,0:T(8,128)(2,1)S(1)} %get-tuple-element.52), channel_id=1, source_target_pairs={{0,4},{4,8},{8,12},{12,16},{16,20},{20,24},{24,28},{28,0},{1,5},{5... | collective-permute-start | bytes 1179656 | tf_op jit(solution)/shard_map/ppermute | solution.py:400
  98.3 6.9 %collective-permute-start.11 = (bf16[2,3,64,128]{3,2,1,0:T(8,128)(2,1)S(1)}, bf16[2,3,64,128]{3,2,1,0:T(8,128)(2,1)S(1)}, u32[]{:S(2)}, u32[]{:S(2)}) collective-permute-start(bf16[2,3,64,128]{3,2,1,0:T(8,128)(2,1)S(1)} %get-tuple-element.48), channel_id=1, source_target_pairs={{0,1},{1,2},{2,3},{3,0},{4,5},{5,6},{6,7},{7,4},{8,9},{9,10},{10,1... | collective-permute-start | bytes 294920 | tf_op jit(solution)/shard_map/ppermute | solution.py:400
  99.6 11.9 %collective-permute-start.12 = (bf16[2,3,64,128]{3,2,1,0:T(8,128)(2,1)S(1)}, bf16[2,3,64,128]{3,2,1,0:T(8,128)(2,1)S(1)}, u32[]{:S(2)}, u32[]{:S(2)}) collective-permute-start(bf16[2,3,64,128]{3,2,1,0:T(8,128)(2,1)S(1)} %get-tuple-element.49), channel_id=1, source_target_pairs={{0,2},{1,3},{2,0},{3,1},{4,6},{5,7},{6,4},{7,5},{8,10},{9,11},{10,... | collective-permute-start | bytes 294920 | tf_op jit(solution)/shard_map/ppermute | solution.py:400
  101.0 10.5 %collective-permute-start.13 = (bf16[2,3,64,128]{3,2,1,0:T(8,128)(2,1)S(1)}, bf16[2,3,64,128]{3,2,1,0:T(8,128)(2,1)S(1)}, u32[]{:S(2)}, u32[]{:S(2)}) collective-permute-start(bf16[2,3,64,128]{3,2,1,0:T(8,128)(2,1)S(1)} %get-tuple-element.50), channel_id=1, source_target_pairs={{0,3},{1,0},{2,1},{3,2},{4,7},{5,4},{6,5},{7,6},{8,11},{9,8},{10,9... | collective-permute-start | bytes 294920 | tf_op jit(solution)/shard_map/ppermute | solution.py:400
  103.1 8.5 %collective-permute-start.15 = (bf16[2,3,64,128]{3,2,1,0:T(8,128)(2,1)S(1)}, bf16[2,3,64,128]{3,2,1,0:T(8,128)(2,1)S(1)}, u32[]{:S(2)}, u32[]{:S(2)}) collective-permute-start(bf16[2,3,64,128]{3,2,1,0:T(8,128)(2,1)S(1)} %get-tuple-element.54), channel_id=1, source_target_pairs={{0,1},{1,2},{2,3},{3,0},{4,5},{5,6},{6,7},{7,4},{8,9},{9,10},{10,1... | collective-permute-start | bytes 294920 | tf_op jit(solution)/shard_map/ppermute | solution.py:400
  103.8 14.6 %collective-permute-start.16 = (bf16[2,3,64,128]{3,2,1,0:T(8,128)(2,1)S(1)}, bf16[2,3,64,128]{3,2,1,0:T(8,128)(2,1)S(1)}, u32[]{:S(2)}, u32[]{:S(2)}) collective-permute-start(bf16[2,3,64,128]{3,2,1,0:T(8,128)(2,1)S(1)} %get-tuple-element.55), channel_id=1, source_target_pairs={{0,2},{1,3},{2,0},{3,1},{4,6},{5,7},{6,4},{7,5},{8,10},{9,11},{10,... | collective-permute-start | bytes 294920 | tf_op jit(solution)/shard_map/ppermute | solution.py:400
  105.2 13.2 %collective-permute-start.17 = (bf16[2,3,64,128]{3,2,1,0:T(8,128)(2,1)S(1)}, bf16[2,3,64,128]{3,2,1,0:T(8,128)(2,1)S(1)}, u32[]{:S(2)}, u32[]{:S(2)}) collective-permute-start(bf16[2,3,64,128]{3,2,1,0:T(8,128)(2,1)S(1)} %get-tuple-element.56), channel_id=1, source_target_pairs={{0,3},{1,0},{2,1},{3,2},{4,7},{5,4},{6,5},{7,6},{8,11},{9,8},{10,9... | collective-permute-start | bytes 294920 | tf_op jit(solution)/shard_map/ppermute | solution.py:400

commit v3 on v2

v3 whole, which is shorter than its diff:
```python
import functools
import math

import jax
import jax.numpy as jnp
import ml_dtypes
import numpy as np
from jax import lax
from jax.experimental import pallas as pl
from jax.experimental.pallas import tpu as pltpu
from jax.sharding import PartitionSpec as P

K = 16
CAP = 2
GROUP = 4
COLS = 128
chirp_strength = 40.0
bf16 = jnp.bfloat16
f32 = jnp.float32


def make_tables(extent):
    counter = np.arange(extent, dtype=np.int64)
    angles = (counter[:, None] * counter[None, :] % extent).astype(np.float32) * np.float32(
        2.0 * math.pi / extent
    )
    scaling = np.float32(1.0 / math.sqrt(extent))
    cosine = (np.cos(angles) * scaling).astype(ml_dtypes.bfloat16)
    sine_part = (np.sin(angles) * scaling).astype(ml_dtypes.bfloat16)
    half = extent // 2
    tables = []
    for parity in (0, 1):
        c, s = cosine[:half, parity::2], sine_part[:half, parity::2]
        table = np.concatenate([np.concatenate([c, -s], 1), np.concatenate([s, c], 1)], 0)
        tables += [table, np.ascontiguousarray(table.T)]
    order = np.concatenate([counter[0::2], counter[1::2]])
    frequency = (((counter + half) % extent - half).astype(np.float32) / extent)[order]
    phases = np.float32(chirp_strength) * (frequency[:, None] ** 2 + frequency[None, :] ** 2)
    kernel = np.stack([np.cos(phases), -np.sin(phases)]).astype(np.float32)
    permute = (counter[:, None] == order[None, :]).astype(ml_dtypes.bfloat16)
    return [jnp.asarray(t) for t in tables], jnp.asarray(kernel), jnp.asarray(permute)


def dot(a, b):
    return jnp.dot(a, b, preferred_element_type=f32)


def row_dot(fields, table):
    n = fields[0].shape[0]
    out = dot(jnp.concatenate(fields, 0), table)
    return [out[i * n : (i + 1) * n] for i in range(len(fields))]


def quads(a, b, h):
    return jnp.concatenate(
        [
            jnp.concatenate([a[:, :h], b[:, :h]], 1),
            jnp.concatenate([a[:, h:], b[:, h:]], 1),
        ],
        0,
    )


def forward(items, tabs):
    a_even, t_even, a_odd, t_odd = tabs
    h = a_even.shape[0] // 2
    sums = [jnp.concatenate([l[0] + r[0], l[1] + r[1]], 1).astype(bf16) for l, r in items]
    diffs = [jnp.concatenate([l[0] - r[0], l[1] - r[1]], 1).astype(bf16) for l, r in items]
    even = row_dot(sums, a_even)
    odd = row_dot(diffs, a_odd)
    plus = [quads(a[:h] + a[h:], b[:h] + b[h:], h).astype(bf16) for a, b in zip(even, odd)]
    minus = [quads(a[:h] - a[h:], b[:h] - b[h:], h).astype(bf16) for a, b in zip(even, odd)]
    return list(zip([dot(t_even, x) for x in plus], [dot(t_odd, x) for x in minus]))


def inverse(items, tabs):
    a_even, t_even, a_odd, t_odd = tabs
    h = a_even.shape[0] // 2

    def side(x, k):
        lanes = slice(k * h, (k + 1) * h)
        return jnp.concatenate(
            [jnp.concatenate([part[:h, lanes], part[h:, lanes]], 1) for part in x], 0
        )

    even = row_dot([side(x, 0) for x in items], t_even)
    odd = row_dot([side(x, 1) for x in items], t_odd)
    plus = [a + b for a, b in zip(even, odd)]
    minus = [a - b for a, b in zip(even, odd)]
    low = [dot(a_even, quads(a[:h], b[:h], h).astype(bf16)) for a, b in zip(plus, minus)]
    high = [dot(a_odd, quads(a[h:], b[h:], h).astype(bf16)) for a, b in zip(plus, minus)]
    out = []
    for a, b in zip(low, high):
        s, d = a + b, a - b
        out.append(
            (jnp.concatenate([s[:h], d[:h]], 0), jnp.concatenate([s[h:], d[h:]], 0))
        )
    return out


def product(a, b):
    return a[0] * b[0] - a[1] * b[1], a[0] * b[1] + a[1] * b[0]


def product_conj(a, b):
    return a[0] * b[0] + a[1] * b[1], a[0] * b[1] - a[1] * b[0]


def halves(x, h=COLS):
    return (x[0][:, :h], x[1][:, :h]), (x[0][:, h:], x[1][:, h:])


def by_kernel(field, kernel_ref, conjugate):
    out = []
    h = field[0].shape[0] // 2
    op = product_conj if conjugate else product
    for k, part in enumerate(field):
        rows = slice(k * h, (k + 1) * h)
        spread = op((kernel_ref[0, rows, :], kernel_ref[1, rows, :]), (part[:h], part[h:]))
        out.append(jnp.concatenate(spread, 0).astype(bf16))
    return out


def window(rows_ref, top, col, extent):
    return tuple(
        tuple(rows_ref[plane, col + j, pl.ds(top, extent), :] for plane in (0, 1)) for j in (0, 1)
    )


def start_all(copies):
    for copy in copies:
        copy.start()
    return copies


def wait_all(copies):
    for copy in copies:
        copy.wait()


def copies_of(pairs, sems):
    return [pltpu.make_async_copy(a, b, sems.at[i]) for i, (a, b) in enumerate(pairs)]


def shard_copies(refs, shards):
    count = shards.shape[1]
    if len(refs) == count:
        return [(ref.at[side], shards.at[side, k]) for k, ref in enumerate(refs) for side in (0, 1)]
    return [(ref, shards.at[i // count, i % count]) for i, ref in enumerate(refs)]


def load_rows(slab_here, shards, rows_ref):
    count = shards.shape[1]
    height = shards.shape[-2]
    for side in (0, 1):
        for k in range(count):
            place = lax.rem(slab_here + count - k, count)
            start = pl.multiple_of((side * count + place) * height, height)
            rows_ref[:, :, pl.ds(start, height), :] = shards[side, k].astype(f32)


def group_count(meta_ref):
    return lax.div(meta_ref[4 * K] + GROUP - 1, GROUP)


def group_loop(meta_ref, ready, body, incoming=None, outgoing=None):
    last = group_count(meta_ref)

    def each(make, group, do):
        if make is not None:
            for copy in make(group, lax.rem(group, 2)):
                do(copy)

    @pl.when(last > 0)
    def _():
        each(incoming, 0, lambda c: c.start())

    ready()

    def step(group, carry):
        @pl.when(group + 1 < last)
        def _():
            each(incoming, group + 1, lambda c: c.start())

        each(incoming, group, lambda c: c.wait())

        @pl.when(group >= 2)
        def _():
            each(outgoing, group - 2, lambda c: c.wait())

        body([GROUP * group + j for j in range(GROUP)], group, lax.rem(group, 2))
        each(outgoing, group, lambda c: c.start())
        return carry

    lax.fori_loop(0, last, step, 0)
    for back in (2, 1):

        @pl.when(last >= back)
        def _():
            each(outgoing, last - back, lambda c: c.wait())


def add_window(totals_ref, top, col, term):
    extent = term[0][0].shape[0]
    for j in (0, 1):
        for plane in (0, 1):
            place = (plane, col + j, pl.ds(top, extent), slice(None))
            totals_ref[place] += term[j][plane]


def route_kernel(
    here_ref, owner_hbm, row_hbm, col_hbm, images_hbm, permute_hbm, out_hbm, meta_ref,
    owner_ref, row_ref, col_ref, second_ref, images_ref, permute_ref, turned_ref, packed_ref,
    sems, in_sems, out_sems,
):
    reads, extent, _ = images_ref.shape
    tiles = out_hbm.shape[0] // CAP
    tile_here, slab_here, slabs = here_ref[0], here_ref[1], here_ref[2]
    mine = (tile_here * slabs + slab_here) * reads
    small = copies_of(
        [(owner_hbm, owner_ref), (row_hbm, row_ref), (col_hbm, col_ref), (permute_hbm, permute_ref)], sems
    )
    start_all(small)
    arriving = copies_of([(images_hbm.at[i], images_ref.at[i]) for i in range(reads)], in_sems)
    start_all(arriving)
    wait_all(small)
    owners = [owner_ref[mine + i] for i in range(reads)]
    leaving = []
    for group in (range(reads // 2), range(reads // 2, reads)):
        for i in group:
            arriving[i].wait()
        for i in group:
            turned_ref[i] = dot(images_ref[i], permute_ref[0]).astype(bf16)
        for i in group:
            packed_ref[i] = dot(permute_ref[1], turned_ref[i]).astype(bf16)
        for i in group:
            rank = jnp.int32(0)
            for j in range(i):
                rank += (owners[j] == owners[i]).astype(jnp.int32)
            copy = pltpu.make_async_copy(
                packed_ref.at[i], out_hbm.at[owners[i] * CAP + rank], out_sems.at[i]
            )
            copy.start()
            leaving.append(copy)

    def sender(g, counts):
        base = (g * slabs + slab_here) * reads
        first, later = counts
        seen = jnp.int32(0)
        for i in range(reads):
            match = (owner_ref[base + i] == tile_here).astype(jnp.int32)
            meta_ref[first] = base + i
            second_ref[later] = base + i
            fresh = match * (1 - seen)
            first, later, seen = first + fresh, later + match - fresh, seen + match
        return first, later

    first, later = lax.fori_loop(0, tiles, sender, (jnp.int32(0), jnp.int32(0)))
    total = first + later
    for i in range(K):
        in_first = i < first
        live = i < total
        row = jnp.where(in_first, meta_ref[i], second_ref[jnp.maximum(i - first, 0)])
        row = jnp.where(live, row, 0)
        group = row // (slabs * reads)
        meta_ref[i] = group * CAP + jnp.where(in_first, 0, 1)
        meta_ref[K + i] = row_ref[row]
        meta_ref[2 * K + i] = col_ref[row]
        meta_ref[3 * K + i] = jnp.where(live, row_ref[row], 2 * extent)
    meta_ref[4 * K] = total
    meta_ref[4 * K + 1] = first
    meta_ref[4 * K + 2] = slab_here
    wait_all(leaving)


def give_lower(totals_ref, lower_ref):
    rows = lower_ref.shape[2]
    lower_ref[...] = totals_ref[:, :, rows : 2 * rows, :].astype(bf16)


def combine_kernel(here_ref, own_ref, moved_ref, mine_ref, *send_refs):
    height = mine_ref.shape[2]
    count = len(send_refs) + 1
    for k in range(count):
        place = lax.rem(here_ref[1] + k, count)
        rows = pl.ds(pl.multiple_of(place * height, height), height)
        both = own_ref[:, :, rows, :] + moved_ref[:, :, rows, :].astype(f32)
        if k == 0:
            mine_ref[...] = both
        else:
            send_refs[k - 1][...] = both.astype(bf16)


def finish_kernel(count, *refs):
    out_ref = refs[-1]
    for s in range(out_ref.shape[0]):
        parts = refs[s * count : (s + 1) * count]
        for plane in (0, 1):
            for block in range(parts[0].shape[1]):
                total = parts[0][plane, block]
                for part in parts[1:]:
                    total = total + part[plane, block].astype(f32)
                out_ref[s, plane, :, block * COLS : (block + 1) * COLS] = total


def tables_of(tabs_ref):
    return tuple(tabs_ref[i] for i in range(4))


def wave_kernel(count, meta_ref, *refs):
    rows_hbm = refs[:count]
    (probe_hbm, kernel_hbm, tabs_hbm, wave_ref,
     shards, probe_ref, kernel_ref, tabs, rows_ref, sems) = refs[count:]
    extent = probe_ref.shape[0]
    once = start_all(copies_of(
        shard_copies(rows_hbm, shards)
        + [(probe_hbm, probe_ref), (kernel_hbm, kernel_ref), (tabs_hbm, tabs)], sems))

    def ready():
        wait_all(once)
        load_rows(meta_ref[4 * K + 2], shards, rows_ref)

    def body(items, group, slot):
        tables = tables_of(tabs)
        probe = halves((probe_ref[:, :extent], probe_ref[:, extent:]))
        fields = []
        for at in items:
            w = window(rows_ref, meta_ref[K + at], meta_ref[2 * K + at], extent)
            fields.append(tuple(product(p, q) for p, q in zip(probe, w)))
        spread = [by_kernel(x, kernel_ref, False) for x in forward(fields, tables)]
        for at, wave in zip(items, inverse(spread, tables)):
            wave_ref[at, 0] = wave[0]
            wave_ref[at, 1] = wave[1]

    group_loop(meta_ref, ready, body)


def far_kernel(count, meta_ref, *refs):
    rows_hbm = refs[:count]
    (wave_ref, tabs_hbm, far_hbm, kept_hbm,
     shards, tabs, rows_ref, far_buf, kept_buf, sems, out_sems) = refs[count:]
    extent = wave_ref.shape[-1]
    once = start_all(copies_of(shard_copies(rows_hbm, shards) + [(tabs_hbm, tabs)], sems))

    def ready():
        wait_all(once)
        load_rows(meta_ref[4 * K + 2], shards, rows_ref)

    def outgoing(group, slot):
        return copies_of(
            [(far_buf.at[slot], far_hbm.at[group]), (kept_buf.at[slot], kept_hbm.at[group])], out_sems.at[slot]
        )

    def body(items, group, slot):
        fields = []
        for i, at in enumerate(items):
            w = window(rows_ref, meta_ref[K + at], meta_ref[2 * K + at], extent)
            wave = wave_ref[at, 0], wave_ref[at, 1]
            for plane in (0, 1):
                kept_buf[slot, i, plane] = wave[plane].astype(bf16)
            fields.append(tuple(product(p, q) for p, q in zip(halves(wave), w)))
        for i, far in enumerate(forward(fields, tables_of(tabs))):
            for k in (0, 1):
                far_buf[slot, i, k] = far[k]

    group_loop(meta_ref, ready, body, None, outgoing)


def misfit_kernel(count, meta_ref, *refs):
    rows_hbm = refs[:count]
    (kept_hbm, far_hbm, images_hbm, kernel_hbm, tabs_hbm, back_ref, totals_ref, lower_ref,
     shards, kernel_ref, tabs, rows_ref, kept_buf, far_buf, image_buf, sems, in_sems) = refs[count:]
    extent = images_hbm.shape[1]
    h = extent // 2
    once = start_all(copies_of(
        shard_copies(rows_hbm, shards) + [(kernel_hbm, kernel_ref), (tabs_hbm, tabs)], sems))

    def ready():
        totals_ref[...] = jnp.zeros_like(totals_ref)
        wait_all(once)
        load_rows(meta_ref[4 * K + 2], shards, rows_ref)

    def incoming(group, slot):
        return copies_of(
            [(kept_hbm.at[group], kept_buf.at[slot]), (far_hbm.at[group], far_buf.at[slot])]
            + [(images_hbm.at[meta_ref[GROUP * group + i]], image_buf.at[slot, i]) for i in range(GROUP)],
            in_sems.at[slot],
        )

    def body(items, group, slot):
        tables = tables_of(tabs)
        far_grads = []
        for i, at in enumerate(items):
            parts = []
            for k in (0, 1):
                re, im = far_buf[slot, i, k, :h], far_buf[slot, i, k, h:]
                image = image_buf[slot, i, k * h : (k + 1) * h, :].astype(f32)
                misfit = re * re + im * im - image
                parts.append(jnp.concatenate([re * misfit, im * misfit], 0).astype(bf16))
            far_grads.append(parts)
        back = []
        for i, (at, grad) in enumerate(zip(items, inverse(far_grads, tables))):
            grad = halves(grad)
            wave = halves((kept_buf[slot, i, 0].astype(f32), kept_buf[slot, i, 1].astype(f32)))
            col = meta_ref[2 * K + at]
            add_window(
                totals_ref, meta_ref[3 * K + at], col,
                [product_conj(p, q) for p, q in zip(wave, grad)],
            )
            w = window(rows_ref, meta_ref[K + at], col, extent)
            back.append(tuple(product_conj(p, q) for p, q in zip(w, grad)))
        for at, field in zip(items, forward(back, tables)):
            for k, part in enumerate(by_kernel(field, kernel_ref, True)):
                back_ref[at, k] = part

    group_loop(meta_ref, ready, body, incoming)
    give_lower(totals_ref, lower_ref)


def exit_kernel(meta_ref, back_ref, probe_hbm, tabs_hbm, totals_ref, lower_ref, probe_ref, tabs, sems):
    extent = probe_ref.shape[0]
    once = start_all(copies_of([(probe_hbm, probe_ref), (tabs_hbm, tabs)], sems))

    def ready():
        totals_ref[...] = jnp.zeros_like(totals_ref)
        wait_all(once)

    def body(items, group, slot):
        probe = halves((probe_ref[:, :extent], probe_ref[:, extent:]))
        fields = [(back_ref[at, 0], back_ref[at, 1]) for at in items]
        for at, grad in zip(items, inverse(fields, tables_of(tabs))):
            add_window(
                totals_ref, meta_ref[3 * K + at], meta_ref[2 * K + at],
                [product_conj(p, q) for p, q in zip(probe, halves(grad))],
            )

    group_loop(meta_ref, ready, body)
    give_lower(totals_ref, lower_ref)


MIB = 1024 * 1024
VMEM = 60 * MIB
LIMIT = 46 * MIB


smem = pl.BlockSpec(memory_space=pltpu.SMEM)
vmem = pl.BlockSpec(memory_space=pltpu.VMEM)
hbm = pl.BlockSpec(memory_space=pltpu.HBM)
anywhere = pl.BlockSpec(memory_space=pl.ANY)


def call(kernel, name, ins, in_specs, outs, out_specs, scratch, estimate=None, limit=VMEM):
    return pl.pallas_call(
        kernel,
        in_specs=in_specs,
        out_specs=out_specs,
        out_shape=outs,
        scratch_shapes=scratch,
        compiler_params=pltpu.CompilerParams(vmem_limit_bytes=limit),
        cost_estimate=estimate,
        name=name,
    )(*ins)


def cost(transforms, extent):
    return pl.CostEstimate(
        flops=int(K * transforms * 8 * 2 * extent**3), bytes_accessed=0, transcendentals=0
    )


def sems(*shape):
    return pltpu.SemaphoreType.DMA(shape)


def like(x):
    return pltpu.VMEM(x.shape, x.dtype)


def route(images, here, owner_tile, row_offset, col_offset, permute, tiles):
    reads, extent = images.shape[:2]
    outs = [
        pltpu.HBM((CAP * tiles, extent, extent), bf16),
        jax.ShapeDtypeStruct((4 * K + 8,), jnp.int32),
    ]
    numbers = pltpu.SMEM(owner_tile.shape, jnp.int32)
    scratch = [
        numbers, numbers, numbers, pltpu.SMEM((K + 8,), jnp.int32),
        like(images), like(permute), like(images), like(images), sems(4), sems(reads), sems(reads),
    ]
    ins = [here, owner_tile, row_offset, col_offset, images, permute]
    return call(route_kernel, "route", ins, [smem] + [hbm] * 5, outs, [hbm, smem], scratch, cost(0.25, extent))


def shards_scratch(rows, slabs):
    return pltpu.VMEM((2, slabs) + rows[0].shape[-4:], bf16)


def rows_padded(rows, slabs):
    planes, blocks, height, _ = rows[0].shape[-4:]
    return pltpu.VMEM((planes, blocks, 2 * slabs * height, COLS), f32)


def groups(extent, dtype):
    return pltpu.HBM((K // GROUP, GROUP, 2, extent, extent), dtype)


def group_buffer(extent, dtype):
    return pltpu.VMEM((2, GROUP, 2, extent, extent), dtype)


def waves(meta, rows, probe, kernel, tabs, slabs):
    extent = probe.shape[0]
    scratch = [
        shards_scratch(rows, slabs), like(probe), like(kernel), like(tabs), rows_padded(rows, slabs),
        sems(2 * slabs + 3),
    ]
    return call(
        functools.partial(wave_kernel, len(rows)), "waves", [meta] + rows + [probe, kernel, tabs],
        [smem] + [anywhere] * len(rows) + [hbm] * 3, pltpu.VMEM((K, 2, extent, extent), f32), vmem, scratch,
        cost(2, extent), limit=32 * MIB,
    )


def fars(meta, rows, wave, tabs, slabs):
    extent = wave.shape[-1]
    scratch = [
        shards_scratch(rows, slabs), like(tabs), rows_padded(rows, slabs),
        group_buffer(extent, f32), group_buffer(extent, bf16), sems(2 * slabs + 1), sems(2, 2),
    ]
    return call(
        functools.partial(far_kernel, len(rows)), "fars", [meta] + rows + [wave, tabs],
        [smem] + [anywhere] * len(rows) + [vmem, hbm], [groups(extent, f32), groups(extent, bf16)], [hbm, hbm],
        scratch, cost(1, extent), limit=32 * MIB,
    )


def totals_out(extent, blocks):
    return [
        pltpu.VMEM((2, blocks, 3 * extent, COLS), f32),
        jax.ShapeDtypeStruct((2, blocks, extent, COLS), bf16),
    ]


def misfits(meta, rows, kept, far, images, kernel, tabs, slabs):
    extent = images.shape[1]
    scratch = [
        shards_scratch(rows, slabs), like(kernel), like(tabs), rows_padded(rows, slabs),
        group_buffer(extent, bf16), group_buffer(extent, f32), pltpu.VMEM((2, GROUP, extent, extent), bf16),
        sems(2 * slabs + 2), sems(2, 2 + GROUP),
    ]
    return call(
        functools.partial(misfit_kernel, len(rows)), "misfits", [meta] + rows + [kept, far, images, kernel, tabs],
        [smem] + [anywhere] * len(rows) + [hbm, hbm, anywhere, hbm, hbm],
        [pltpu.VMEM((K, 2, extent, extent), bf16)] + totals_out(extent, rows[0].shape[-3]), [vmem, vmem, vmem],
        scratch, cost(2, extent), limit=LIMIT,
    )


def exits(meta, back, probe, tabs, blocks):
    extent = probe.shape[0]
    return call(
        exit_kernel, "exits", [meta, back, probe, tabs], [smem, vmem, hbm, hbm], totals_out(extent, blocks),
        [vmem, vmem], [like(probe), like(tabs), sems(2)], cost(1, extent), limit=LIMIT,
    )


def combine(here, own, moved, count):
    shape = own.shape[:2] + (moved.shape[2] // count, COLS)
    outs = [jax.ShapeDtypeStruct(shape, f32 if k == 0 else bf16) for k in range(count)]
    return call(combine_kernel, "combine", [here, own, moved], [smem, vmem, vmem], outs, [vmem] * count, [], limit=VMEM // 4)


def finish(parts, count):
    blocks, height = parts[0].shape[1:3]
    out = jax.ShapeDtypeStruct((len(parts) // count, 2, height, blocks * COLS), f32)
    return call(
        functools.partial(finish_kernel, count), "finish", parts, [vmem] * len(parts), out, vmem, [], limit=VMEM // 4
    )


def passed_along(value, axis, steps):
    count = lax.axis_size(axis)
    pairs = [(source, (source + steps) % count) for source in range(count)]
    return lax.ppermute(value, axis, pairs)


def shards(intensities, object_field, probe_wave, owner_tile, row_offset, col_offset):
    tile_count = lax.axis_size("tile")
    slab_count = lax.axis_size("slab")
    extent = intensities.shape[1]
    depth, _, height, width = object_field.shape
    blocks = width // COLS
    tabs, kernel, permute = make_tables(extent)
    here = jnp.stack(
        [lax.axis_index("tile"), lax.axis_index("slab"), jnp.int32(slab_count)]
    ).astype(jnp.int32)
    own = jnp.transpose(
        object_field.reshape(depth, 2, height, blocks, COLS), (0, 1, 3, 2, 4)
    ).astype(bf16)
    tabs = jnp.stack(tabs)
    following = passed_along(own, "tile", -1)
    packed, meta = route(
        intensities, here, owner_tile, row_offset, col_offset,
        jnp.stack([permute, permute.T]), tile_count,
    )
    def gather(rows):
        return [rows] + [passed_along(rows, "slab", k) for k in range(1, slab_count)]

    mine0 = gather(own[0])
    packed, following, *mine0 = lax.optimization_barrier((packed, following, *mine0))
    images = lax.all_to_all(packed, "tile", split_axis=0, concat_axis=0, tiled=True)
    next0 = gather(following[0])
    both = jnp.stack([own[1], following[1]])
    *next0, both = lax.optimization_barrier((*next0, both))
    first = mine0 + next0
    second = gather(both)
    wave = waves(meta, first, probe_wave, kernel, tabs, slab_count)
    far, kept = fars(meta, second, wave, tabs, slab_count)
    back, total1, lower1 = misfits(meta, second, kept, far, images, kernel, tabs, slab_count)
    total0, lower0 = exits(meta, back, probe_wave, tabs, blocks)
    parts = []
    for total, lower in ((total0, lower0), (total1, lower1)):
        moved = passed_along(lower, "tile", 1)
        mine, *sends = combine(here, total, moved, slab_count)
        parts.append(mine)
        parts += [passed_along(x, "slab", k + 1) for k, x in enumerate(sends)]
    return finish(parts, slab_count)


def solution(mesh):
    placed = (
        P(("tile", "slab"), None, None),
        P(None, None, ("tile", "slab"), None),
        P(),
        P(),
        P(),
        P(),
    )
    return jax.shard_map(
        shards,
        mesh=mesh,
        in_specs=placed,
        out_specs=P(None, None, ("tile", "slab"), None),
        check_vma=False,
    )
```

time: 120 us -> 107 us (0.89)
  local copies, waits for them, and re-layouts: 20 us -> 0.07 us
  Pallas kernels: 37.5 us -> 44 us
  waiting for transfers between devices: 25.7 us -> 31.4 us
  starting transfers between devices: 34.8 us -> 29.1 us
    unnamed x36 -> x12, local copies, waits for them, and re-layouts: 20 us -> 0.03 us
    pallas_call x7 -> x8, Pallas kernels: 37.5 us -> 44 us  [call(): pl.pallas_call(kernel, in_specs=in_specs, out_specs=out_specs, out_shape=...]
    ppermute x18, starting transfers between devices: 31 us -> 24.6 us  [passed_along(): return lax.ppermute(value, axis, pairs)]
    ppermute x18, waiting for transfers between devices: 25.7 us -> 31.4 us  [passed_along(): return lax.ppermute(value, axis, pairs)]
  transfers between devices with their start and end apart: 19 -> 19, of which waited for: 5 -> 8; matrix products, arithmetic and copies ran while one was open for 0% -> 1% of each run, Pallas kernels for 11% -> 22%
where the time goes in v3:
time: 107 us; the launch traced here: 106 us
  Pallas kernels  44 us (41%)
  waiting for transfers between devices  31.4 us (29%)
  starting transfers between devices  29.1 us (27%)
  other arithmetic  1.71 us (2%)
    pallas_call x8, Pallas kernels, call(): pl.pallas_call(kernel, in_specs=in_specs, out_specs=out_specs, out_shape=...  44 us
    ppermute x18, waiting for transfers between devices, passed_along(): return lax.ppermute(value, axis, pairs)  31.4 us
    ppermute x18, starting transfers between devices, passed_along(): return lax.ppermute(value, axis, pairs)  24.6 us
    all_to_all x1, starting transfers between devices, shards(): lax.all_to_all(packed, 'tile', split_axis=0, concat_axis=0, tiled=True)  4.51 us
  transfers between devices with their start and end apart: 19, of which 8 were waited for; matrix products, arithmetic and copies ran while one was open for 1% of the time, Pallas kernels for 22%

profile of v3, /device:TPU:0, one launch (start us, length us, event | category | flops | bytes accessed | tf_op | source)
XLA Modules:
  0.0 106.4 jit_solution(4143775428603875179)
XLA Ops:
  0.0 1.0 bitcast_bitcast_fusion
  1.1 5.1 %collective-permute-start.3 = (bf16[2,3,64,128]{3,2,1,0:T(8,128)(2,1)S(1)}, bf16[2,3,64,128]{3,2,1,0:T(8,128)(2,1)S(1)}, u32[]{:S(2)}, u32[]{:S(2)}) collective-permute-start(bf16[2,3,64,128]{3,2,1,0:T(8,128)(2,1)S(1)} %get-tuple-element.37.refs_0_), channel_id=1, source_target_pairs={{0,3},{1,0},{2,1},{3,2},{4,7},{5,4},{6,5},{7,6},{8,11},{9,8},{10,9... | collective-permute-start | bytes 294920 | tf_op jit(solution)/shard_map/ppermute | solution.py:584
  6.2 0.0 collective-permute-start.2
  6.2 1.0 collective-permute-start.1
  7.2 1.0 collective-permute-start
  8.2 0.7 pad_add_fusion.here_ref
  8.9 5.3 %route.1 = (bf16[16,256,256]{2,1,0:T(8,128)(2,1)}, s32[72]{0:T(128)}) custom-call(s32[3]{0:T(128)} %pad_add_fusion.here_ref, s32[448]{0:T(512)} %owner_hbm.1, s32[448]{0:T(512)} %row_hbm.1, s32[448]{0:T(512)} %col_hbm.1, bf16[14,256,256]{2,1,0:T(8,128)(2,1)} %images_hbm.1, bf16[2,256,256]{2,1,0:T(8,128)(2,1)} %constant.33.permute_hbm), custom_call_target="tpu_custom_call" | custom-call | flops 1073741824 | tf_op jit(solution)/shard_map/route/pallas_call | solution.py:453
  14.2 0.0 collective-permute-done.3.refs_3_
  14.2 0.7 collective-permute-done.2.refs_2_
  14.9 0.0 collective-permute-done.1.refs_1_
  14.9 0.0 collective-permute-done
  14.9 0.0 copy-start.1
  14.9 0.0 copy-start.2
  14.9 0.0 copy-start.4
  14.9 0.0 copy-start.5
  15.0 4.5 %all-to-all-start = ((bf16[16,256,256]{2,1,0:T(8,128)(2,1)}), bf16[16,256,256]{2,1,0:T(8,128)(2,1)}, u32[]{:S(2)}, u32[]{:S(2)}) async-start(bf16[16,256,256]{2,1,0:T(8,128)(2,1)} %get-tuple-element.47), calls=%async_computation | async-start | bytes 4194304 | tf_op jit(solution)/shard_map/all_to_all | solution.py:611
  19.5 2.5 %collective-permute-start.6 = (bf16[2,3,64,128]{3,2,1,0:T(8,128)(2,1)S(1)}, bf16[2,3,64,128]{3,2,1,0:T(8,128)(2,1)S(1)}, u32[]{:S(2)}, u32[]{:S(2)}) collective-permute-start(bf16[2,3,64,128]{3,2,1,0:T(8,128)(2,1)S(1)} %get-tuple-element.41.refs_4_), channel_id=1, source_target_pairs={{0,3},{1,0},{2,1},{3,2},{4,7},{5,4},{6,5},{7,6},{8,11},{9,8},{10,9... | collective-permute-start | bytes 294920 | tf_op jit(solution)/shard_map/ppermute | solution.py:584
  22.0 0.9 collective-permute-start.5
  22.8 1.0 collective-permute-start.4
  23.9 1.3 %collective-permute-done.6.refs_7_ = bf16[2,3,64,128]{3,2,1,0:T(8,128)(2,1)S(1)} collective-permute-done((bf16[2,3,64,128]{3,2,1,0:T(8,128)(2,1)S(1)}, bf16[2,3,64,128]{3,2,1,0:T(8,128)(2,1)S(1)}, u32[]{:S(2)}, u32[]{:S(2)}) %collective-permute-start.6) | collective-permute-done | bytes 98336 | tf_op jit(solution)/shard_map/ppermute | solution.py:584
  25.1 7.1 %collective-permute-done.5.refs_6_ = bf16[2,3,64,128]{3,2,1,0:T(8,128)(2,1)S(1)} collective-permute-done((bf16[2,3,64,128]{3,2,1,0:T(8,128)(2,1)S(1)}, bf16[2,3,64,128]{3,2,1,0:T(8,128)(2,1)S(1)}, u32[]{:S(2)}, u32[]{:S(2)}) %collective-permute-start.5) | collective-permute-done | bytes 98336 | tf_op jit(solution)/shard_map/ppermute | solution.py:584
  32.2 0.0 collective-permute-done.4.refs_5_
  32.2 0.9 collective-permute-start.9
  33.1 1.1 %collective-permute-start.8 = (bf16[2,2,3,64,128]{4,3,2,1,0:T(8,128)(2,1)S(1)}, bf16[2,2,3,64,128]{4,3,2,1,0:T(8,128)(2,1)S(1)}, u32[]{:S(2)}, u32[]{:S(2)}) collective-permute-start(bf16[2,2,3,64,128]{4,3,2,1,0:T(8,128)(2,1)S(1)} %pad_maximum_fusion.refs_0_), channel_id=1, source_target_pairs={{0,2},{1,3},{2,0},{3,1},{4,6},{5,7},{6,4},{7,5},{8,10},{9,11},{10,... | collective-permute-start | bytes 589832 | tf_op jit(solution)/shard_map/ppermute | solution.py:584
  34.2 2.0 %collective-permute-start.7 = (bf16[2,2,3,64,128]{4,3,2,1,0:T(8,128)(2,1)S(1)}, bf16[2,2,3,64,128]{4,3,2,1,0:T(8,128)(2,1)S(1)}, u32[]{:S(2)}, u32[]{:S(2)}) collective-permute-start(bf16[2,2,3,64,128]{4,3,2,1,0:T(8,128)(2,1)S(1)} %pad_maximum_fusion.refs_0_), channel_id=1, source_target_pairs={{0,1},{1,2},{2,3},{3,0},{4,5},{5,6},{6,7},{7,4},{8,9},{9,10},{10,1... | collective-permute-start | bytes 589832 | tf_op jit(solution)/shard_map/ppermute | solution.py:584
  36.3 0.0 copy-done.1
  36.3 0.0 copy-done.2
  36.3 0.0 copy-done.4
  36.3 0.0 copy-done.5
  36.3 8.7 %waves.1.refs_4_ = f32[16,2,256,256]{3,2,1,0:T(8,128)S(1)} custom-call(s32[72]{0:T(128)S(1)} %copy-done.5, bf16[2,3,64,128]{3,2,1,0:T(8,128)(2,1)S(1)} %get-tuple-element.37.refs_0_, bf16[2,3,64,128]{3,2,1,0:T(8,128)(2,1)S(1)} %collective-permute-done.1.refs_1_, bf16[2,3,64,128]{3,2,1,0:T(8,128)(2,1)S(1)} %collective-permute-done.2.refs_2_, ...), custom_call_target="tpu_custom_call" | custom-call | flops 8589934592 | tf_op jit(solution)/shard_map/waves/pallas_call | solution.py:453
  45.0 0.0 collective-permute-done.9.refs_3_
  45.0 7.1 %collective-permute-done.8.refs_2_ = bf16[2,2,3,64,128]{4,3,2,1,0:T(8,128)(2,1)S(1)} collective-permute-done((bf16[2,2,3,64,128]{4,3,2,1,0:T(8,128)(2,1)S(1)}, bf16[2,2,3,64,128]{4,3,2,1,0:T(8,128)(2,1)S(1)}, u32[]{:S(2)}, u32[]{:S(2)}) %collective-permute-start.8) | collective-permute-done | bytes 196640 | tf_op jit(solution)/shard_map/ppermute | solution.py:584
  52.1 0.0 collective-permute-done.7.refs_1_
  52.1 8.3 %fars.1 = (f32[4,4,2,256,256]{4,3,2,1,0:T(8,128)}, bf16[4,4,2,256,256]{4,3,2,1,0:T(8,128)(2,1)}) custom-call(s32[72]{0:T(128)S(1)} %copy-done.5, bf16[2,2,3,64,128]{4,3,2,1,0:T(8,128)(2,1)S(1)} %pad_maximum_fusion.refs_0_, bf16[2,2,3,64,128]{4,3,2,1,0:T(8,128)(2,1)S(1)} %collective-permute-done.7.refs_1_, ...), custom_call_target="tpu_custom_call" | custom-call | flops 4294967296 | tf_op jit(solution)/shard_map/fars/pallas_call | solution.py:453
  60.4 0.0 all-to-all-done.refs_6_
  60.4 0.0 copy-start.3
  60.4 13.9 %misfits.1 = (bf16[16,2,256,256]{3,2,1,0:T(8,128)(2,1)S(1)}, f32[2,3,768,128]{3,2,1,0:T(8,128)S(1)}, bf16[2,3,256,128]{3,2,1,0:T(8,128)(2,1)S(1)}) custom-call(s32[72]{0:T(128)S(1)} %copy-done.5, bf16[2,2,3,64,128]{4,3,2,1,0:T(8,128)(2,1)S(1)} %pad_maximum_fusion.refs_0_, bf16[2,2,3,64,128]{4,3,2,1,0:T(8,128)(2,1)S(1)} %collective-permute-done.7.refs_1_, ...), custom_call_target="tpu_custom_call" | custom-call | flops 8589934592 | tf_op jit(solution)/shard_map/misfits/pallas_call | solution.py:453
  74.3 0.0 copy-done.3
  74.3 0.0 copy-start
  74.4 5.8 %exits.1 = (f32[2,3,768,128]{3,2,1,0:T(8,128)S(1)}, bf16[2,3,256,128]{3,2,1,0:T(8,128)(2,1)S(1)}) custom-call(s32[72]{0:T(128)S(1)} %copy-done.5, bf16[16,2,256,256]{3,2,1,0:T(8,128)(2,1)S(1)} %get-tuple-element.48.back_ref, f32[256,512]{1,0:T(8,128)S(1)} %copy-done.1, bf16[4,256,256]{2,1,0:T(8,128)(2,1)S(1)} %copy-done.3), custom_call_target="tpu_custom_call" | custom-call | flops 4294967296 | tf_op jit(solution)/shard_map/exits/pallas_call | solution.py:453
  80.1 0.1 collective-permute-start.10
  80.2 0.1 collective-permute-start.14
  80.3 8.0 %collective-permute-done.10.moved_ref = bf16[2,3,256,128]{3,2,1,0:T(8,128)(2,1)S(1)} collective-permute-done((bf16[2,3,256,128]{3,2,1,0:T(8,128)(2,1)S(1)}, bf16[2,3,256,128]{3,2,1,0:T(8,128)(2,1)S(1)}, u32[]{:S(2)}, u32[]{:S(2)}) %collective-permute-start.10) | collective-permute-done | bytes 393248 | tf_op jit(solution)/shard_map/ppermute | solution.py:584
  88.3 0.0 copy-done
  88.3 0.6 combine.2
  88.9 0.1 collective-permute-start.11
  89.0 1.4 %collective-permute-start.12 = (bf16[2,3,64,128]{3,2,1,0:T(8,128)(2,1)S(1)}, bf16[2,3,64,128]{3,2,1,0:T(8,128)(2,1)S(1)}, u32[]{:S(2)}, u32[]{:S(2)}) collective-permute-start(bf16[2,3,64,128]{3,2,1,0:T(8,128)(2,1)S(1)} %get-tuple-element.53), channel_id=1, source_target_pairs={{0,2},{1,3},{2,0},{3,1},{4,6},{5,7},{6,4},{7,5},{8,10},{9,11},{10,... | collective-permute-start | bytes 294920 | tf_op jit(solution)/shard_map/ppermute | solution.py:584
  90.4 2.8 %collective-permute-start.13 = (bf16[2,3,64,128]{3,2,1,0:T(8,128)(2,1)S(1)}, bf16[2,3,64,128]{3,2,1,0:T(8,128)(2,1)S(1)}, u32[]{:S(2)}, u32[]{:S(2)}) collective-permute-start(bf16[2,3,64,128]{3,2,1,0:T(8,128)(2,1)S(1)} %get-tuple-element.54), channel_id=1, source_target_pairs={{0,3},{1,0},{2,1},{3,2},{4,7},{5,4},{6,5},{7,6},{8,11},{9,8},{10,9... | collective-permute-start | bytes 294920 | tf_op jit(solution)/shard_map/ppermute | solution.py:584
  93.3 0.0 collective-permute-done.14.moved_ref
  93.3 0.6 combine.3
  93.9 0.2 collective-permute-start.15
  94.1 1.5 %collective-permute-start.16 = (bf16[2,3,64,128]{3,2,1,0:T(8,128)(2,1)S(1)}, bf16[2,3,64,128]{3,2,1,0:T(8,128)(2,1)S(1)}, u32[]{:S(2)}, u32[]{:S(2)}) collective-permute-start(bf16[2,3,64,128]{3,2,1,0:T(8,128)(2,1)S(1)} %get-tuple-element.59), channel_id=1, source_target_pairs={{0,2},{1,3},{2,0},{3,1},{4,6},{5,7},{6,4},{7,5},{8,10},{9,11},{10,... | collective-permute-start | bytes 294920 | tf_op jit(solution)/shard_map/ppermute | solution.py:584
  95.6 0.0 collective-permute-done.11.refs_1_
  95.6 2.8 %collective-permute-start.17 = (bf16[2,3,64,128]{3,2,1,0:T(8,128)(2,1)S(1)}, bf16[2,3,64,128]{3,2,1,0:T(8,128)(2,1)S(1)}, u32[]{:S(2)}, u32[]{:S(2)}) collective-permute-start(bf16[2,3,64,128]{3,2,1,0:T(8,128)(2,1)S(1)} %get-tuple-element.60), channel_id=1, source_target_pairs={{0,3},{1,0},{2,1},{3,2},{4,7},{5,4},{6,5},{7,6},{8,11},{9,8},{10,9... | collective-permute-start | bytes 294920 | tf_op jit(solution)/shard_map/ppermute | solution.py:584
  98.4 1.8 %collective-permute-done.12.refs_2_ = bf16[2,3,64,128]{3,2,1,0:T(8,128)(2,1)S(1)} collective-permute-done((bf16[2,3,64,128]{3,2,1,0:T(8,128)(2,1)S(1)}, bf16[2,3,64,128]{3,2,1,0:T(8,128)(2,1)S(1)}, u32[]{:S(2)}, u32[]{:S(2)}) %collective-permute-start.12) | collective-permute-done | bytes 98336 | tf_op jit(solution)/shard_map/ppermute | solution.py:584
  100.3 0.0 collective-permute-done.13.refs_3_
  100.3 1.2 %collective-permute-done.15.refs_5_ = bf16[2,3,64,128]{3,2,1,0:T(8,128)(2,1)S(1)} collective-permute-done((bf16[2,3,64,128]{3,2,1,0:T(8,128)(2,1)S(1)}, bf16[2,3,64,128]{3,2,1,0:T(8,128)(2,1)S(1)}, u32[]{:S(2)}, u32[]{:S(2)}) %collective-permute-start.15) | collective-permute-done | bytes 98336 | tf_op jit(solution)/shard_map/ppermute | solution.py:584
  101.5 4.1 %collective-permute-done.16.refs_6_ = bf16[2,3,64,128]{3,2,1,0:T(8,128)(2,1)S(1)} collective-permute-done((bf16[2,3,64,128]{3,2,1,0:T(8,128)(2,1)S(1)}, bf16[2,3,64,128]{3,2,1,0:T(8,128)(2,1)S(1)}, u32[]{:S(2)}, u32[]{:S(2)}) %collective-permute-start.16) | collective-permute-done | bytes 98336 | tf_op jit(solution)/shard_map/ppermute | solution.py:584
  105.6 0.0 collective-permute-done.17.refs_7_
  105.6 0.8 finish.1
  (3 shorter events, 0.1 us)
Async XLA Ops:
  1.1 13.1 %collective-permute-start.3 = (bf16[2,3,64,128]{3,2,1,0:T(8,128)(2,1)S(1)}, bf16[2,3,64,128]{3,2,1,0:T(8,128)(2,1)S(1)}, u32[]{:S(2)}, u32[]{:S(2)}) collective-permute-start(bf16[2,3,64,128]{3,2,1,0:T(8,128)(2,1)S(1)} %get-tuple-element.37.refs_0_), channel_id=1, source_target_pairs={{0,3},{1,0},{2,1},{3,2},{4,7},{5,4},{6,5},{7,6},{8,11},{9,8},{10,9... | collective-permute-start | bytes 294920 | tf_op jit(solution)/shard_map/ppermute | solution.py:584
  6.2 8.7 %collective-permute-start.2 = (bf16[2,3,64,128]{3,2,1,0:T(8,128)(2,1)S(1)}, bf16[2,3,64,128]{3,2,1,0:T(8,128)(2,1)S(1)}, u32[]{:S(2)}, u32[]{:S(2)}) collective-permute-start(bf16[2,3,64,128]{3,2,1,0:T(8,128)(2,1)S(1)} %get-tuple-element.37.refs_0_), channel_id=1, source_target_pairs={{0,2},{1,3},{2,0},{3,1},{4,6},{5,7},{6,4},{7,5},{8,10},{9,11},{10,... | collective-permute-start | bytes 294920 | tf_op jit(solution)/shard_map/ppermute | solution.py:584
  6.2 8.7 %collective-permute-start.1 = (bf16[2,3,64,128]{3,2,1,0:T(8,128)(2,1)S(1)}, bf16[2,3,64,128]{3,2,1,0:T(8,128)(2,1)S(1)}, u32[]{:S(2)}, u32[]{:S(2)}) collective-permute-start(bf16[2,3,64,128]{3,2,1,0:T(8,128)(2,1)S(1)} %get-tuple-element.37.refs_0_), channel_id=1, source_target_pairs={{0,1},{1,2},{2,3},{3,0},{4,5},{5,6},{6,7},{7,4},{8,9},{9,10},{10,1... | collective-permute-start | bytes 294920 | tf_op jit(solution)/shard_map/ppermute | solution.py:584
  7.2 7.7 %collective-permute-start = (bf16[2,2,3,64,128]{4,3,2,1,0:T(8,128)(2,1)S(1)}, bf16[2,2,3,64,128]{4,3,2,1,0:T(8,128)(2,1)S(1)}, u32[]{:S(2)}, u32[]{:S(2)}) collective-permute-start(bf16[2,2,3,64,128]{4,3,2,1,0:T(8,128)(2,1)S(1)} %bitcast_bitcast_fusion), channel_id=1, source_target_pairs={{0,28},{4,0},{8,4},{12,8},{16,12},{20,16},{24,20},{28,24},{1,29},{... | collective-permute-start | bytes 589832 | tf_op jit(solution)/shard_map/ppermute | solution.py:584
  14.9 21.3 %copy-start.1 = (f32[256,512]{1,0:T(8,128)S(1)}, f32[256,512]{1,0:T(8,128)}, u32[]{:S(2)}) copy-start(f32[256,512]{1,0:T(8,128)} %probe_hbm.1) | copy-start | bytes 1572868
  14.9 21.3 %copy-start.2 = (bf16[4,256,256]{2,1,0:T(8,128)(2,1)S(1)}, bf16[4,256,256]{2,1,0:T(8,128)(2,1)}, u32[]{:S(2)}) copy-start(bf16[4,256,256]{2,1,0:T(8,128)(2,1)} %constant.38.refs_10_.refs_5_.refs_8_.tabs_hbm) | copy-start | bytes 1572868
  14.9 21.3 %copy-start.4 = (f32[2,256,256]{2,1,0:T(8,128)S(1)}, f32[2,256,256]{2,1,0:T(8,128)}, u32[]{:S(2)}) copy-start(f32[2,256,256]{2,1,0:T(8,128)} %constant.27.clone.refs_9_.refs_7_) | copy-start | bytes 1572868
  14.9 21.3 %copy-start.5 = (s32[72]{0:T(128)S(1)}, s32[72]{0:T(128)}, u32[]{:S(2)}) copy-start(s32[72]{0:T(128)} %get-tuple-element.33.meta_ref) | copy-start | bytes 868
  15.0 45.4 %all-to-all-start = ((bf16[16,256,256]{2,1,0:T(8,128)(2,1)}), bf16[16,256,256]{2,1,0:T(8,128)(2,1)}, u32[]{:S(2)}, u32[]{:S(2)}) async-start(bf16[16,256,256]{2,1,0:T(8,128)(2,1)} %get-tuple-element.47), calls=%async_computation | async-start | bytes 4194304 | tf_op jit(solution)/shard_map/all_to_all | solution.py:611
  19.5 5.6 %collective-permute-start.6 = (bf16[2,3,64,128]{3,2,1,0:T(8,128)(2,1)S(1)}, bf16[2,3,64,128]{3,2,1,0:T(8,128)(2,1)S(1)}, u32[]{:S(2)}, u32[]{:S(2)}) collective-permute-start(bf16[2,3,64,128]{3,2,1,0:T(8,128)(2,1)S(1)} %get-tuple-element.41.refs_4_), channel_id=1, source_target_pairs={{0,3},{1,0},{2,1},{3,2},{4,7},{5,4},{6,5},{7,6},{8,11},{9,8},{10,9... | collective-permute-start | bytes 294920 | tf_op jit(solution)/shard_map/ppermute | solution.py:584
  22.0 10.2 %collective-permute-start.5 = (bf16[2,3,64,128]{3,2,1,0:T(8,128)(2,1)S(1)}, bf16[2,3,64,128]{3,2,1,0:T(8,128)(2,1)S(1)}, u32[]{:S(2)}, u32[]{:S(2)}) collective-permute-start(bf16[2,3,64,128]{3,2,1,0:T(8,128)(2,1)S(1)} %get-tuple-element.41.refs_4_), channel_id=1, source_target_pairs={{0,2},{1,3},{2,0},{3,1},{4,6},{5,7},{6,4},{7,5},{8,10},{9,11},{10,... | collective-permute-start | bytes 294920 | tf_op jit(solution)/shard_map/ppermute | solution.py:584
  22.8 9.4 %collective-permute-start.4 = (bf16[2,3,64,128]{3,2,1,0:T(8,128)(2,1)S(1)}, bf16[2,3,64,128]{3,2,1,0:T(8,128)(2,1)S(1)}, u32[]{:S(2)}, u32[]{:S(2)}) collective-permute-start(bf16[2,3,64,128]{3,2,1,0:T(8,128)(2,1)S(1)} %get-tuple-element.41.refs_4_), channel_id=1, source_target_pairs={{0,1},{1,2},{2,3},{3,0},{4,5},{5,6},{6,7},{7,4},{8,9},{9,10},{10,1... | collective-permute-start | bytes 294920 | tf_op jit(solution)/shard_map/ppermute | solution.py:584
  32.2 12.8 %collective-permute-start.9 = (bf16[2,2,3,64,128]{4,3,2,1,0:T(8,128)(2,1)S(1)}, bf16[2,2,3,64,128]{4,3,2,1,0:T(8,128)(2,1)S(1)}, u32[]{:S(2)}, u32[]{:S(2)}) collective-permute-start(bf16[2,2,3,64,128]{4,3,2,1,0:T(8,128)(2,1)S(1)} %pad_maximum_fusion.refs_0_), channel_id=1, source_target_pairs={{0,3},{1,0},{2,1},{3,2},{4,7},{5,4},{6,5},{7,6},{8,11},{9,8},{10,9... | collective-permute-start | bytes 589832 | tf_op jit(solution)/shard_map/ppermute | solution.py:584
  33.1 19.0 %collective-permute-start.8 = (bf16[2,2,3,64,128]{4,3,2,1,0:T(8,128)(2,1)S(1)}, bf16[2,2,3,64,128]{4,3,2,1,0:T(8,128)(2,1)S(1)}, u32[]{:S(2)}, u32[]{:S(2)}) collective-permute-start(bf16[2,2,3,64,128]{4,3,2,1,0:T(8,128)(2,1)S(1)} %pad_maximum_fusion.refs_0_), channel_id=1, source_target_pairs={{0,2},{1,3},{2,0},{3,1},{4,6},{5,7},{6,4},{7,5},{8,10},{9,11},{10,... | collective-permute-start | bytes 589832 | tf_op jit(solution)/shard_map/ppermute | solution.py:584
  34.2 17.8 %collective-permute-start.7 = (bf16[2,2,3,64,128]{4,3,2,1,0:T(8,128)(2,1)S(1)}, bf16[2,2,3,64,128]{4,3,2,1,0:T(8,128)(2,1)S(1)}, u32[]{:S(2)}, u32[]{:S(2)}) collective-permute-start(bf16[2,2,3,64,128]{4,3,2,1,0:T(8,128)(2,1)S(1)} %pad_maximum_fusion.refs_0_), channel_id=1, source_target_pairs={{0,1},{1,2},{2,3},{3,0},{4,5},{5,6},{6,7},{7,4},{8,9},{9,10},{10,1... | collective-permute-start | bytes 589832 | tf_op jit(solution)/shard_map/ppermute | solution.py:584
  60.4 13.9 %copy-start.3 = (bf16[4,256,256]{2,1,0:T(8,128)(2,1)S(1)}, bf16[4,256,256]{2,1,0:T(8,128)(2,1)}, u32[]{:S(2)}) copy-start(bf16[4,256,256]{2,1,0:T(8,128)(2,1)} %constant.38.refs_10_.refs_5_.refs_8_.tabs_hbm) | copy-start | bytes 1572868
  74.3 13.9 %copy-start = (s32[3]{0:T(128)S(1)}, s32[3]{0:T(128)}, u32[]{:S(2)}) copy-start(s32[3]{0:T(128)} %pad_add_fusion.here_ref) | copy-start | bytes 40
  80.1 8.2 %collective-permute-start.10 = (bf16[2,3,256,128]{3,2,1,0:T(8,128)(2,1)S(1)}, bf16[2,3,256,128]{3,2,1,0:T(8,128)(2,1)S(1)}, u32[]{:S(2)}, u32[]{:S(2)}) collective-permute-start(bf16[2,3,256,128]{3,2,1,0:T(8,128)(2,1)S(1)} %get-tuple-element.50), channel_id=1, source_target_pairs={{0,4},{4,8},{8,12},{12,16},{16,20},{20,24},{24,28},{28,0},{1,5},{5... | collective-permute-start | bytes 1179656 | tf_op jit(solution)/shard_map/ppermute | solution.py:584
  80.2 13.1 %collective-permute-start.14 = (bf16[2,3,256,128]{3,2,1,0:T(8,128)(2,1)S(1)}, bf16[2,3,256,128]{3,2,1,0:T(8,128)(2,1)S(1)}, u32[]{:S(2)}, u32[]{:S(2)}) collective-permute-start(bf16[2,3,256,128]{3,2,1,0:T(8,128)(2,1)S(1)} %get-tuple-element.56), channel_id=1, source_target_pairs={{0,4},{4,8},{8,12},{12,16},{16,20},{20,24},{24,28},{28,0},{1,5},{5... | collective-permute-start | bytes 1179656 | tf_op jit(solution)/shard_map/ppermute | solution.py:584
  88.9 6.7 %collective-permute-start.11 = (bf16[2,3,64,128]{3,2,1,0:T(8,128)(2,1)S(1)}, bf16[2,3,64,128]{3,2,1,0:T(8,128)(2,1)S(1)}, u32[]{:S(2)}, u32[]{:S(2)}) collective-permute-start(bf16[2,3,64,128]{3,2,1,0:T(8,128)(2,1)S(1)} %get-tuple-element.52), channel_id=1, source_target_pairs={{0,1},{1,2},{2,3},{3,0},{4,5},{5,6},{6,7},{7,4},{8,9},{9,10},{10,1... | collective-permute-start | bytes 294920 | tf_op jit(solution)/shard_map/ppermute | solution.py:584
  89.0 11.3 %collective-permute-start.12 = (bf16[2,3,64,128]{3,2,1,0:T(8,128)(2,1)S(1)}, bf16[2,3,64,128]{3,2,1,0:T(8,128)(2,1)S(1)}, u32[]{:S(2)}, u32[]{:S(2)}) collective-permute-start(bf16[2,3,64,128]{3,2,1,0:T(8,128)(2,1)S(1)} %get-tuple-element.53), channel_id=1, source_target_pairs={{0,2},{1,3},{2,0},{3,1},{4,6},{5,7},{6,4},{7,5},{8,10},{9,11},{10,... | collective-permute-start | bytes 294920 | tf_op jit(solution)/shard_map/ppermute | solution.py:584
  90.4 9.9 %collective-permute-start.13 = (bf16[2,3,64,128]{3,2,1,0:T(8,128)(2,1)S(1)}, bf16[2,3,64,128]{3,2,1,0:T(8,128)(2,1)S(1)}, u32[]{:S(2)}, u32[]{:S(2)}) collective-permute-start(bf16[2,3,64,128]{3,2,1,0:T(8,128)(2,1)S(1)} %get-tuple-element.54), channel_id=1, source_target_pairs={{0,3},{1,0},{2,1},{3,2},{4,7},{5,4},{6,5},{7,6},{8,11},{9,8},{10,9... | collective-permute-start | bytes 294920 | tf_op jit(solution)/shard_map/ppermute | solution.py:584
  93.9 7.6 %collective-permute-start.15 = (bf16[2,3,64,128]{3,2,1,0:T(8,128)(2,1)S(1)}, bf16[2,3,64,128]{3,2,1,0:T(8,128)(2,1)S(1)}, u32[]{:S(2)}, u32[]{:S(2)}) collective-permute-start(bf16[2,3,64,128]{3,2,1,0:T(8,128)(2,1)S(1)} %get-tuple-element.58), channel_id=1, source_target_pairs={{0,1},{1,2},{2,3},{3,0},{4,5},{5,6},{6,7},{7,4},{8,9},{9,10},{10,1... | collective-permute-start | bytes 294920 | tf_op jit(solution)/shard_map/ppermute | solution.py:584
  94.1 11.6 %collective-permute-start.16 = (bf16[2,3,64,128]{3,2,1,0:T(8,128)(2,1)S(1)}, bf16[2,3,64,128]{3,2,1,0:T(8,128)(2,1)S(1)}, u32[]{:S(2)}, u32[]{:S(2)}) collective-permute-start(bf16[2,3,64,128]{3,2,1,0:T(8,128)(2,1)S(1)} %get-tuple-element.59), channel_id=1, source_target_pairs={{0,2},{1,3},{2,0},{3,1},{4,6},{5,7},{6,4},{7,5},{8,10},{9,11},{10,... | collective-permute-start | bytes 294920 | tf_op jit(solution)/shard_map/ppermute | solution.py:584
  95.6 10.0 %collective-permute-start.17 = (bf16[2,3,64,128]{3,2,1,0:T(8,128)(2,1)S(1)}, bf16[2,3,64,128]{3,2,1,0:T(8,128)(2,1)S(1)}, u32[]{:S(2)}, u32[]{:S(2)}) collective-permute-start(bf16[2,3,64,128]{3,2,1,0:T(8,128)(2,1)S(1)} %get-tuple-element.60), channel_id=1, source_target_pairs={{0,3},{1,0},{2,1},{3,2},{4,7},{5,4},{6,5},{7,6},{8,11},{9,8},{10,9... | collective-permute-start | bytes 294920 | tf_op jit(solution)/shard_map/ppermute | solution.py:584

commit v4 on v3

--- a/solution.py
+++ b/solution.py
@@ -61,13 +61,19 @@
     )
 
 
+def folded(field):
+    l, r = field
+    return (
+        jnp.concatenate([l[0] + r[0], l[1] + r[1]], 1).astype(bf16),
+        jnp.concatenate([l[0] - r[0], l[1] - r[1]], 1).astype(bf16),
+    )
+
+
 def forward(items, tabs):
     a_even, t_even, a_odd, t_odd = tabs
     h = a_even.shape[0] // 2
-    sums = [jnp.concatenate([l[0] + r[0], l[1] + r[1]], 1).astype(bf16) for l, r in items]
-    diffs = [jnp.concatenate([l[0] - r[0], l[1] - r[1]], 1).astype(bf16) for l, r in items]
-    even = row_dot(sums, a_even)
-    odd = row_dot(diffs, a_odd)
+    even = row_dot([x[0] for x in items], a_even)
+    odd = row_dot([x[1] for x in items], a_odd)
     plus = [quads(a[:h] + a[h:], b[:h] + b[h:], h).astype(bf16) for a, b in zip(even, odd)]
     minus = [quads(a[:h] - a[h:], b[:h] - b[h:], h).astype(bf16) for a, b in zip(even, odd)]
     return list(zip([dot(t_even, x) for x in plus], [dot(t_odd, x) for x in minus]))
@@ -309,8 +315,8 @@
 
 def wave_kernel(count, meta_ref, *refs):
     rows_hbm = refs[:count]
-    (probe_hbm, kernel_hbm, tabs_hbm, wave_ref,
-     shards, probe_ref, kernel_ref, tabs, rows_ref, sems) = refs[count:]
+    (probe_hbm, kernel_hbm, tabs_hbm, wave_hbm,
+     shards, probe_ref, kernel_ref, tabs, rows_ref, wave_buf, sems, out_sems) = refs[count:]
     extent = probe_ref.shape[0]
     once = start_all(copies_of(
         shard_copies(rows_hbm, shards)
@@ -319,6 +325,9 @@
     def ready():
         wait_all(once)
         load_rows(meta_ref[4 * K + 2], shards, rows_ref)
+
+    def outgoing(group, slot):
+        return copies_of([(wave_buf.at[slot], wave_hbm.at[group])], out_sems.at[slot])
 
     def body(items, group, slot):
         tables = tables_of(tabs)
@@ -326,54 +335,22 @@
         fields = []
         for at in items:
             w = window(rows_ref, meta_ref[K + at], meta_ref[2 * K + at], extent)
-            fields.append(tuple(product(p, q) for p, q in zip(probe, w)))
+            fields.append(folded(tuple(product(p, q) for p, q in zip(probe, w))))
         spread = [by_kernel(x, kernel_ref, False) for x in forward(fields, tables)]
-        for at, wave in zip(items, inverse(spread, tables)):
-            wave_ref[at, 0] = wave[0]
-            wave_ref[at, 1] = wave[1]
-
-    group_loop(meta_ref, ready, body)
-
-
-def far_kernel(count, meta_ref, *refs):
-    rows_hbm = refs[:count]
-    (wave_ref, tabs_hbm, far_hbm, kept_hbm,
-     shards, tabs, rows_ref, far_buf, kept_buf, sems, out_sems) = refs[count:]
-    extent = wave_ref.shape[-1]
-    once = start_all(copies_of(shard_copies(rows_hbm, shards) + [(tabs_hbm, tabs)], sems))
-
-    def ready():
-        wait_all(once)
-        load_rows(meta_ref[4 * K + 2], shards, rows_ref)
-
-    def outgoing(group, slot):
-        return copies_of(
-            [(far_buf.at[slot], far_hbm.at[group]), (kept_buf.at[slot], kept_hbm.at[group])], out_sems.at[slot]
-        )
-
-    def body(items, group, slot):
-        fields = []
-        for i, at in enumerate(items):
-            w = window(rows_ref, meta_ref[K + at], meta_ref[2 * K + at], extent)
-            wave = wave_ref[at, 0], wave_ref[at, 1]
-            for plane in (0, 1):
-                kept_buf[slot, i, plane] = wave[plane].astype(bf16)
-            fields.append(tuple(product(p, q) for p, q in zip(halves(wave), w)))
-        for i, far in enumerate(forward(fields, tables_of(tabs))):
-            for k in (0, 1):
-                far_buf[slot, i, k] = far[k]
+        for i, wave in enumerate(inverse(spread, tables)):
+            wave_buf[slot, i, 0] = wave[0]
+            wave_buf[slot, i, 1] = wave[1]
 
     group_loop(meta_ref, ready, body, None, outgoing)
 
 
 def misfit_kernel(count, meta_ref, *refs):
     rows_hbm = refs[:count]
-    (kept_hbm, far_hbm, images_hbm, kernel_hbm, tabs_hbm, back_ref, totals_ref, lower_ref,
-     shards, kernel_ref, tabs, rows_ref, kept_buf, far_buf, image_buf, sems, in_sems) = refs[count:]
+    (wave_hbm, images_hbm, tabs_hbm, back_ref, totals_ref, lower_ref,
+     shards, tabs, rows_ref, wave_buf, image_buf, sems, in_sems) = refs[count:]
     extent = images_hbm.shape[1]
     h = extent // 2
-    once = start_all(copies_of(
-        shard_copies(rows_hbm, shards) + [(kernel_hbm, kernel_ref), (tabs_hbm, tabs)], sems))
+    once = start_all(copies_of(shard_copies(rows_hbm, shards) + [(tabs_hbm, tabs)], sems))
 
     def ready():
         totals_ref[...] = jnp.zeros_like(totals_ref)
@@ -382,39 +359,59 @@
 
     def incoming(group, slot):
         return copies_of(
-            [(kept_hbm.at[group], kept_buf.at[slot]), (far_hbm.at[group], far_buf.at[slot])]
+            [(wave_hbm.at[group], wave_buf.at[slot])]
             + [(images_hbm.at[meta_ref[GROUP * group + i]], image_buf.at[slot, i]) for i in range(GROUP)],
             in_sems.at[slot],
         )
 
     def body(items, group, slot):
         tables = tables_of(tabs)
+
+        def wave_of(i):
+            return halves((wave_buf[slot, i, 0], wave_buf[slot, i, 1]))
+
+        fields = []
+        for i, at in enumerate(items):
+            w = window(rows_ref, meta_ref[K + at], meta_ref[2 * K + at], extent)
+            fields.append(folded(tuple(product(p, q) for p, q in zip(wave_of(i), w))))
         far_grads = []
-        for i, at in enumerate(items):
+        for i, far in enumerate(forward(fields, tables)):
             parts = []
-            for k in (0, 1):
-                re, im = far_buf[slot, i, k, :h], far_buf[slot, i, k, h:]
+            for k, part in enumerate(far):
+                re, im = part[:h], part[h:]
                 image = image_buf[slot, i, k * h : (k + 1) * h, :].astype(f32)
                 misfit = re * re + im * im - image
                 parts.append(jnp.concatenate([re * misfit, im * misfit], 0).astype(bf16))
             far_grads.append(parts)
-        back = []
         for i, (at, grad) in enumerate(zip(items, inverse(far_grads, tables))):
             grad = halves(grad)
-            wave = halves((kept_buf[slot, i, 0].astype(f32), kept_buf[slot, i, 1].astype(f32)))
             col = meta_ref[2 * K + at]
             add_window(
                 totals_ref, meta_ref[3 * K + at], col,
-                [product_conj(p, q) for p, q in zip(wave, grad)],
+                [product_conj(p, q) for p, q in zip(wave_of(i), grad)],
             )
             w = window(rows_ref, meta_ref[K + at], col, extent)
-            back.append(tuple(product_conj(p, q) for p, q in zip(w, grad)))
-        for at, field in zip(items, forward(back, tables)):
+            back = folded(tuple(product_conj(p, q) for p, q in zip(w, grad)))
+            for k in (0, 1):
+                back_ref[at, k] = back[k]
+
+    group_loop(meta_ref, ready, body, incoming)
+    give_lower(totals_ref, lower_ref)
+
+
+def back_kernel(meta_ref, fields_ref, kernel_hbm, tabs_hbm, back_ref, kernel_ref, tabs, sems):
+    once = start_all(copies_of([(kernel_hbm, kernel_ref), (tabs_hbm, tabs)], sems))
+
+    def ready():
+        wait_all(once)
+
+    def body(items, group, slot):
+        fields = [(fields_ref[at, 0], fields_ref[at, 1]) for at in items]
+        for at, field in zip(items, forward(fields, tables_of(tabs))):
             for k, part in enumerate(by_kernel(field, kernel_ref, True)):
                 back_ref[at, k] = part
 
-    group_loop(meta_ref, ready, body, incoming)
-    give_lower(totals_ref, lower_ref)
+    group_loop(meta_ref, ready, body)
 
 
 def exit_kernel(meta_ref, back_ref, probe_hbm, tabs_hbm, totals_ref, lower_ref, probe_ref, tabs, sems):
@@ -512,25 +509,12 @@
     extent = probe.shape[0]
     scratch = [
         shards_scratch(rows, slabs), like(probe), like(kernel), like(tabs), rows_padded(rows, slabs),
-        sems(2 * slabs + 3),
+        group_buffer(extent, f32), sems(2 * slabs + 3), sems(2, 1),
     ]
     return call(
         functools.partial(wave_kernel, len(rows)), "waves", [meta] + rows + [probe, kernel, tabs],
-        [smem] + [anywhere] * len(rows) + [hbm] * 3, pltpu.VMEM((K, 2, extent, extent), f32), vmem, scratch,
-        cost(2, extent), limit=32 * MIB,
-    )
-
-
-def fars(meta, rows, wave, tabs, slabs):
-    extent = wave.shape[-1]
-    scratch = [
-        shards_scratch(rows, slabs), like(tabs), rows_padded(rows, slabs),
-        group_buffer(extent, f32), group_buffer(extent, bf16), sems(2 * slabs + 1), sems(2, 2),
-    ]
-    return call(
-        functools.partial(far_kernel, len(rows)), "fars", [meta] + rows + [wave, tabs],
-        [smem] + [anywhere] * len(rows) + [vmem, hbm], [groups(extent, f32), groups(extent, bf16)], [hbm, hbm],
-        scratch, cost(1, extent), limit=32 * MIB,
+        [smem] + [anywhere] * len(rows) + [hbm] * 3, groups(extent, f32), hbm, scratch,
+        cost(2, extent),
     )
 
 
@@ -541,18 +525,27 @@
     ]
 
 
-def misfits(meta, rows, kept, far, images, kernel, tabs, slabs):
+def misfits(meta, rows, wave, images, tabs, slabs):
     extent = images.shape[1]
     scratch = [
-        shards_scratch(rows, slabs), like(kernel), like(tabs), rows_padded(rows, slabs),
-        group_buffer(extent, bf16), group_buffer(extent, f32), pltpu.VMEM((2, GROUP, extent, extent), bf16),
-        sems(2 * slabs + 2), sems(2, 2 + GROUP),
+        shards_scratch(rows, slabs), like(tabs), rows_padded(rows, slabs),
+        group_buffer(extent, f32), pltpu.VMEM((2, GROUP, extent, extent), bf16),
+        sems(2 * slabs + 1), sems(2, 1 + GROUP),
     ]
     return call(
-        functools.partial(misfit_kernel, len(rows)), "misfits", [meta] + rows + [kept, far, images, kernel, tabs],
-        [smem] + [anywhere] * len(rows) + [hbm, hbm, anywhere, hbm, hbm],
+        functools.partial(misfit_kernel, len(rows)), "misfits", [meta] + rows + [wave, images, tabs],
+        [smem] + [anywhere] * len(rows) + [hbm, anywhere, hbm],
         [pltpu.VMEM((K, 2, extent, extent), bf16)] + totals_out(extent, rows[0].shape[-3]), [vmem, vmem, vmem],
         scratch, cost(2, extent), limit=LIMIT,
+    )
+
+
+def backs(meta, fields, kernel, tabs):
+    extent = kernel.shape[1]
+    return call(
+        back_kernel, "backs", [meta, fields, kernel, tabs], [smem, vmem, hbm, hbm],
+        pltpu.VMEM((K, 2, extent, extent), bf16), vmem, [like(kernel), like(tabs), sems(2)],
+        cost(1, extent), limit=30 * MIB,
     )
 
 
@@ -560,7 +553,7 @@
     extent = probe.shape[0]
     return call(
         exit_kernel, "exits", [meta, back, probe, tabs], [smem, vmem, hbm, hbm], totals_out(extent, blocks),
-        [vmem, vmem], [like(probe), like(tabs), sems(2)], cost(1, extent), limit=LIMIT,
+        [vmem, vmem], [like(probe), like(tabs), sems(2)], cost(0.1, extent), limit=30 * MIB,
     )
 
 
@@ -610,21 +603,20 @@
     packed, following, *mine0 = lax.optimization_barrier((packed, following, *mine0))
     images = lax.all_to_all(packed, "tile", split_axis=0, concat_axis=0, tiled=True)
     next0 = gather(following[0])
-    both = jnp.stack([own[1], following[1]])
-    *next0, both = lax.optimization_barrier((*next0, both))
+    second = gather(jnp.stack([own[1], following[1]]))
     first = mine0 + next0
-    second = gather(both)
     wave = waves(meta, first, probe_wave, kernel, tabs, slab_count)
-    far, kept = fars(meta, second, wave, tabs, slab_count)
-    back, total1, lower1 = misfits(meta, second, kept, far, images, kernel, tabs, slab_count)
+    fields, total1, lower1 = misfits(meta, second, wave, images, tabs, slab_count)
+    moved1 = passed_along(lower1, "tile", 1)
+    back = backs(meta, fields, kernel, tabs)
+    mine1, *sends1 = combine(here, total1, moved1, slab_count)
     total0, lower0 = exits(meta, back, probe_wave, tabs, blocks)
-    parts = []
-    for total, lower in ((total0, lower0), (total1, lower1)):
-        moved = passed_along(lower, "tile", 1)
-        mine, *sends = combine(here, total, moved, slab_count)
-        parts.append(mine)
-        parts += [passed_along(x, "slab", k + 1) for k, x in enumerate(sends)]
-    return finish(parts, slab_count)
+    lower0, mine1, *sends1 = lax.optimization_barrier((lower0, mine1, *sends1))
+    moved0 = passed_along(lower0, "tile", 1)
+    parts1 = [mine1] + [passed_along(x, "slab", k + 1) for k, x in enumerate(sends1)]
+    mine0, *sends0 = combine(here, total0, moved0, slab_count)
+    parts0 = [mine0] + [passed_along(x, "slab", k + 1) for k, x in enumerate(sends0)]
+    return finish(parts0 + parts1, slab_count)
 
 
 def solution(mesh):

time: 107 us -> 97.6 us (0.912)
  waiting for transfers between devices: 31.4 us -> 15.7 us
  starting transfers between devices: 29.1 us -> 36.6 us
  Pallas kernels: 44 us -> 42 us
    ppermute x18, waiting for transfers between devices: 31.4 us -> 15.7 us  [passed_along(): return lax.ppermute(value, axis, pairs)]
    ppermute x18, starting transfers between devices: 24.6 us -> 32.2 us  [passed_along(): return lax.ppermute(value, axis, pairs)]
    pallas_call x8, Pallas kernels: 44 us -> 42 us  [call(): pl.pallas_call(kernel, in_specs=in_specs, out_specs=out_specs, out_shape=...]
  transfers between devices with their start and end apart: 19 -> 19, of which waited for: 8 -> 4; matrix products, arithmetic and copies ran while one was open for 1% -> 1% of each run, Pallas kernels for 22% -> 27%
where the time goes in v4:
time: 97.6 us; the launch traced here: 97 us
  Pallas kernels  42 us (43%)
  starting transfers between devices  36.6 us (38%)
  waiting for transfers between devices  15.7 us (16%)
  other arithmetic  1.69 us (2%)
    pallas_call x8, Pallas kernels, call(): pl.pallas_call(kernel, in_specs=in_specs, out_specs=out_specs, out_shape=...  42 us
    ppermute x18, starting transfers between devices, passed_along(): return lax.ppermute(value, axis, pairs)  32.2 us
    ppermute x18, waiting for transfers between devices, passed_along(): return lax.ppermute(value, axis, pairs)  15.7 us
    all_to_all x1, starting transfers between devices, shards(): lax.all_to_all(packed, 'tile', split_axis=0, concat_axis=0, tiled=True)  4.37 us
  transfers between devices with their start and end apart: 19, of which 4 were waited for; matrix products, arithmetic and copies ran while one was open for 1% of the time, Pallas kernels for 27%

profile of v4, /device:TPU:0, one launch (start us, length us, event | category | flops | bytes accessed | tf_op | source)
XLA Modules:
  0.0 97.0 jit_solution(6828586030438811747)
XLA Ops:
  0.0 1.0 %bitcast_bitcast_fusion = bf16[2,2,3,64,128]{4,3,2,1,0:T(8,128)(2,1)S(1)} fusion(f32[2,2,64,384]{3,2,1,0:T(8,128)} %param.13), kind=kLoop, calls=%fused_computation | loop fusion | flops 98304 | bytes 589824 | tf_op jit(solution)/shard_map/convert_element_type | solution.py:592
  1.1 0.0 copy-start.5
  1.1 5.1 %collective-permute-start.3 = (bf16[2,3,64,128]{3,2,1,0:T(8,128)(2,1)S(1)}, bf16[2,3,64,128]{3,2,1,0:T(8,128)(2,1)S(1)}, u32[]{:S(2)}, u32[]{:S(2)}) collective-permute-start(bf16[2,3,64,128]{3,2,1,0:T(8,128)(2,1)S(1)} %get-tuple-element.34.refs_0_), channel_id=1, source_target_pairs={{0,3},{1,0},{2,1},{3,2},{4,7},{5,4},{6,5},{7,6},{8,11},{9,8},{10,9... | collective-permute-start | bytes 294920 | tf_op jit(solution)/shard_map/ppermute | solution.py:577
  6.2 0.0 collective-permute-start.2
  6.2 1.0 %collective-permute-start.1 = (bf16[2,3,64,128]{3,2,1,0:T(8,128)(2,1)S(1)}, bf16[2,3,64,128]{3,2,1,0:T(8,128)(2,1)S(1)}, u32[]{:S(2)}, u32[]{:S(2)}) collective-permute-start(bf16[2,3,64,128]{3,2,1,0:T(8,128)(2,1)S(1)} %get-tuple-element.34.refs_0_), channel_id=1, source_target_pairs={{0,1},{1,2},{2,3},{3,0},{4,5},{5,6},{6,7},{7,4},{8,9},{9,10},{10,1... | collective-permute-start | bytes 294920 | tf_op jit(solution)/shard_map/ppermute | solution.py:577
  7.2 1.0 %collective-permute-start = (bf16[2,2,3,64,128]{4,3,2,1,0:T(8,128)(2,1)S(1)}, bf16[2,2,3,64,128]{4,3,2,1,0:T(8,128)(2,1)S(1)}, u32[]{:S(2)}, u32[]{:S(2)}) collective-permute-start(bf16[2,2,3,64,128]{4,3,2,1,0:T(8,128)(2,1)S(1)} %bitcast_bitcast_fusion), channel_id=1, source_target_pairs={{0,28},{4,0},{8,4},{12,8},{16,12},{20,16},{24,20},{28,24},{1,29},{... | collective-permute-start | bytes 589832 | tf_op jit(solution)/shard_map/ppermute | solution.py:577
  8.2 0.6 pad_add_fusion.here_ref
  8.9 5.3 %route.1 = (bf16[16,256,256]{2,1,0:T(8,128)(2,1)}, s32[72]{0:T(128)}) custom-call(s32[3]{0:T(128)} %pad_add_fusion.here_ref, s32[448]{0:T(512)} %owner_hbm.1, s32[448]{0:T(512)} %row_hbm.1, s32[448]{0:T(512)} %col_hbm.1, bf16[14,256,256]{2,1,0:T(8,128)(2,1)} %images_hbm.1, bf16[2,256,256]{2,1,0:T(8,128)(2,1)} %constant.33.permute_hbm), custom_call_target="tpu_custom_call" | custom-call | flops 1073741824 | tf_op jit(solution)/shard_map/route/pallas_call | solution.py:450
  14.2 0.0 collective-permute-done.3.refs_3_
  14.2 0.0 copy-start.7
  14.2 0.7 collective-permute-done.2.refs_2_
  14.9 0.0 collective-permute-done.1.refs_1_
  14.9 0.0 collective-permute-done
  14.9 0.0 copy-done.5
  14.9 4.4 %all-to-all-start = ((bf16[16,256,256]{2,1,0:T(8,128)(2,1)}), bf16[16,256,256]{2,1,0:T(8,128)(2,1)}, u32[]{:S(2)}, u32[]{:S(2)}) async-start(bf16[16,256,256]{2,1,0:T(8,128)(2,1)} %get-tuple-element.38), calls=%async_computation | async-start | bytes 4194304 | tf_op jit(solution)/shard_map/all_to_all | solution.py:604
  19.3 0.0 copy-start.6
  19.3 2.5 %collective-permute-start.9 = (bf16[2,3,64,128]{3,2,1,0:T(8,128)(2,1)S(1)}, bf16[2,3,64,128]{3,2,1,0:T(8,128)(2,1)S(1)}, u32[]{:S(2)}, u32[]{:S(2)}) collective-permute-start(bf16[2,3,64,128]{3,2,1,0:T(8,128)(2,1)S(1)} %get-tuple-element.57.refs_4_), channel_id=1, source_target_pairs={{0,3},{1,0},{2,1},{3,2},{4,7},{5,4},{6,5},{7,6},{8,11},{9,8},{10,9... | collective-permute-start | bytes 294920 | tf_op jit(solution)/shard_map/ppermute | solution.py:577
  21.8 0.8 collective-permute-start.8
  22.6 1.1 %collective-permute-start.7 = (bf16[2,3,64,128]{3,2,1,0:T(8,128)(2,1)S(1)}, bf16[2,3,64,128]{3,2,1,0:T(8,128)(2,1)S(1)}, u32[]{:S(2)}, u32[]{:S(2)}) collective-permute-start(bf16[2,3,64,128]{3,2,1,0:T(8,128)(2,1)S(1)} %get-tuple-element.57.refs_4_), channel_id=1, source_target_pairs={{0,1},{1,2},{2,3},{3,0},{4,5},{5,6},{6,7},{7,4},{8,9},{9,10},{10,1... | collective-permute-start | bytes 294920 | tf_op jit(solution)/shard_map/ppermute | solution.py:577
  23.7 0.0 copy-done.7
  23.7 0.0 copy-done.8
  23.8 0.0 copy-done.9
  23.8 2.8 %collective-permute-start.6 = (bf16[2,2,3,64,128]{4,3,2,1,0:T(8,128)(2,1)S(1)}, bf16[2,2,3,64,128]{4,3,2,1,0:T(8,128)(2,1)S(1)}, u32[]{:S(2)}, u32[]{:S(2)}) collective-permute-start(bf16[2,2,3,64,128]{4,3,2,1,0:T(8,128)(2,1)S(1)} %pad_maximum_fusion.refs_0_), channel_id=1, source_target_pairs={{0,3},{1,0},{2,1},{3,2},{4,7},{5,4},{6,5},{7,6},{8,11},{9,8},{10,9... | collective-permute-start | bytes 589832 | tf_op jit(solution)/shard_map/ppermute | solution.py:577
  26.6 0.3 collective-permute-start.5
  26.9 0.0 collective-permute-done.9.refs_7_
  26.9 0.3 collective-permute-start.4
  27.2 5.1 %collective-permute-done.8.refs_6_ = bf16[2,3,64,128]{3,2,1,0:T(8,128)(2,1)S(1)} collective-permute-done((bf16[2,3,64,128]{3,2,1,0:T(8,128)(2,1)S(1)}, bf16[2,3,64,128]{3,2,1,0:T(8,128)(2,1)S(1)}, u32[]{:S(2)}, u32[]{:S(2)}) %collective-permute-start.8) | collective-permute-done | bytes 98336 | tf_op jit(solution)/shard_map/ppermute | solution.py:577
  32.3 0.0 collective-permute-done.7.refs_5_
  32.3 0.0 copy-done.6
  32.3 0.0 copy-done.10
  32.3 0.6 copy-done.11
  33.0 0.0 copy-done.12
  33.0 10.9 %waves.1.refs_4_ = f32[4,4,2,256,256]{4,3,2,1,0:T(8,128)} custom-call(s32[72]{0:T(128)} %get-tuple-element.31.meta_ref, bf16[2,3,64,128]{3,2,1,0:T(8,128)(2,1)} %copy-done.5, bf16[2,3,64,128]{3,2,1,0:T(8,128)(2,1)} %copy-done.9, bf16[2,3,64,128]{3,2,1,0:T(8,128)(2,1)} %copy-done.8, bf16[2,3,64,128]{3,2,1,0:T(8,128)(2,1)} %copy-done.7, ...), custom_call_target="tpu_custom_call" | custom-call | flops 8589934592 | tf_op jit(solution)/shard_map/waves/pallas_call | solution.py:450
  43.9 0.0 copy-start.4
  43.9 0.0 collective-permute-done.6.refs_3_
  43.9 5.0 %collective-permute-done.5.refs_2_ = bf16[2,2,3,64,128]{4,3,2,1,0:T(8,128)(2,1)S(1)} collective-permute-done((bf16[2,2,3,64,128]{4,3,2,1,0:T(8,128)(2,1)S(1)}, bf16[2,2,3,64,128]{4,3,2,1,0:T(8,128)(2,1)S(1)}, u32[]{:S(2)}, u32[]{:S(2)}) %collective-permute-start.5) | collective-permute-done | bytes 196640 | tf_op jit(solution)/shard_map/ppermute | solution.py:577
  48.9 0.0 collective-permute-done.4.refs_1_
  48.9 0.0 all-to-all-done.refs_5_
  48.9 0.0 copy-done.1
  48.9 0.0 copy-done.3
  48.9 14.3 %misfits.1 = (bf16[16,2,256,256]{3,2,1,0:T(8,128)(2,1)S(1)}, f32[2,3,768,128]{3,2,1,0:T(8,128)S(1)}, bf16[2,3,256,128]{3,2,1,0:T(8,128)(2,1)S(1)}) custom-call(s32[72]{0:T(128)S(1)} %copy-done.3, bf16[2,2,3,64,128]{4,3,2,1,0:T(8,128)(2,1)S(1)} %pad_maximum_fusion.refs_0_, bf16[2,2,3,64,128]{4,3,2,1,0:T(8,128)(2,1)S(1)} %collective-permute-done.4.refs_1_, ...), custom_call_target="tpu_custom_call" | custom-call | flops 8589934592 | tf_op jit(solution)/shard_map/misfits/pallas_call | solution.py:450
  63.2 0.3 collective-permute-start.10
  63.5 0.0 copy-done.4
  63.5 3.9 %backs.1.back_ref = bf16[16,2,256,256]{3,2,1,0:T(8,128)(2,1)S(1)} custom-call(s32[72]{0:T(128)S(1)} %copy-done.3, bf16[16,2,256,256]{3,2,1,0:T(8,128)(2,1)S(1)} %get-tuple-element.39.fields_ref, f32[2,256,256]{2,1,0:T(8,128)S(1)} %copy-done.4, bf16[4,256,256]{2,1,0:T(8,128)(2,1)S(1)} %copy-done.1), custom_call_target="tpu_custom_call" | custom-call | flops 4294967296 | tf_op jit(solution)/shard_map/backs/pallas_call | solution.py:450
  67.3 0.0 copy-done
  67.4 5.7 %exits.1 = (f32[2,3,768,128]{3,2,1,0:T(8,128)S(1)}, bf16[2,3,256,128]{3,2,1,0:T(8,128)(2,1)S(1)}) custom-call(s32[72]{0:T(128)S(1)} %copy-done.3, bf16[16,2,256,256]{3,2,1,0:T(8,128)(2,1)S(1)} %backs.1.back_ref, f32[256,512]{1,0:T(8,128)S(1)} %copy-done, bf16[4,256,256]{2,1,0:T(8,128)(2,1)S(1)} %copy-done.1), custom_call_target="tpu_custom_call" | custom-call | flops 429496736 | tf_op jit(solution)/shard_map/exits/pallas_call | solution.py:450
  73.1 0.0 collective-permute-done.10.moved_ref
  73.1 0.6 combine.2
  73.7 2.1 %collective-permute-start.11 = (bf16[2,3,256,128]{3,2,1,0:T(8,128)(2,1)S(1)}, bf16[2,3,256,128]{3,2,1,0:T(8,128)(2,1)S(1)}, u32[]{:S(2)}, u32[]{:S(2)}) collective-permute-start(bf16[2,3,256,128]{3,2,1,0:T(8,128)(2,1)S(1)} %get-tuple-element.48), channel_id=1, source_target_pairs={{0,4},{4,8},{8,12},{12,16},{16,20},{20,24},{24,28},{28,0},{1,5},{5... | collective-permute-start | bytes 1179656 | tf_op jit(solution)/shard_map/ppermute | solution.py:577
  75.8 3.6 %collective-permute-start.15 = (bf16[2,3,64,128]{3,2,1,0:T(8,128)(2,1)S(1)}, bf16[2,3,64,128]{3,2,1,0:T(8,128)(2,1)S(1)}, u32[]{:S(2)}, u32[]{:S(2)}) collective-permute-start(bf16[2,3,64,128]{3,2,1,0:T(8,128)(2,1)S(1)} %get-tuple-element.54), channel_id=1, source_target_pairs={{0,1},{1,2},{2,3},{3,0},{4,5},{5,6},{6,7},{7,4},{8,9},{9,10},{10,1... | collective-permute-start | bytes 294920 | tf_op jit(solution)/shard_map/ppermute | solution.py:577
  79.3 0.6 collective-permute-start.16
  79.9 2.7 %collective-permute-start.17 = (bf16[2,3,64,128]{3,2,1,0:T(8,128)(2,1)S(1)}, bf16[2,3,64,128]{3,2,1,0:T(8,128)(2,1)S(1)}, u32[]{:S(2)}, u32[]{:S(2)}) collective-permute-start(bf16[2,3,64,128]{3,2,1,0:T(8,128)(2,1)S(1)} %get-tuple-element.56), channel_id=1, source_target_pairs={{0,3},{1,0},{2,1},{3,2},{4,7},{5,4},{6,5},{7,6},{8,11},{9,8},{10,9... | collective-permute-start | bytes 294920 | tf_op jit(solution)/shard_map/ppermute | solution.py:577
  82.6 0.0 collective-permute-done.11.moved_ref
  82.6 0.6 combine.3
  83.2 3.0 %collective-permute-start.12 = (bf16[2,3,64,128]{3,2,1,0:T(8,128)(2,1)S(1)}, bf16[2,3,64,128]{3,2,1,0:T(8,128)(2,1)S(1)}, u32[]{:S(2)}, u32[]{:S(2)}) collective-permute-start(bf16[2,3,64,128]{3,2,1,0:T(8,128)(2,1)S(1)} %get-tuple-element.50), channel_id=1, source_target_pairs={{0,1},{1,2},{2,3},{3,0},{4,5},{5,6},{6,7},{7,4},{8,9},{9,10},{10,1... | collective-permute-start | bytes 294920 | tf_op jit(solution)/shard_map/ppermute | solution.py:577
  86.2 2.3 %collective-permute-start.13 = (bf16[2,3,64,128]{3,2,1,0:T(8,128)(2,1)S(1)}, bf16[2,3,64,128]{3,2,1,0:T(8,128)(2,1)S(1)}, u32[]{:S(2)}, u32[]{:S(2)}) collective-permute-start(bf16[2,3,64,128]{3,2,1,0:T(8,128)(2,1)S(1)} %get-tuple-element.51), channel_id=1, source_target_pairs={{0,2},{1,3},{2,0},{3,1},{4,6},{5,7},{6,4},{7,5},{8,10},{9,11},{10,... | collective-permute-start | bytes 294920 | tf_op jit(solution)/shard_map/ppermute | solution.py:577
  88.5 0.0 collective-permute-done.15.refs_5_
  88.5 2.8 %collective-permute-start.14 = (bf16[2,3,64,128]{3,2,1,0:T(8,128)(2,1)S(1)}, bf16[2,3,64,128]{3,2,1,0:T(8,128)(2,1)S(1)}, u32[]{:S(2)}, u32[]{:S(2)}) collective-permute-start(bf16[2,3,64,128]{3,2,1,0:T(8,128)(2,1)S(1)} %get-tuple-element.52), channel_id=1, source_target_pairs={{0,3},{1,0},{2,1},{3,2},{4,7},{5,4},{6,5},{7,6},{8,11},{9,8},{10,9... | collective-permute-start | bytes 294920 | tf_op jit(solution)/shard_map/ppermute | solution.py:577
  91.3 0.0 collective-permute-done.16.refs_6_
  91.3 0.0 collective-permute-done.17.refs_7_
  91.3 0.0 collective-permute-done.12.refs_1_
  91.3 4.8 %collective-permute-done.13.refs_2_ = bf16[2,3,64,128]{3,2,1,0:T(8,128)(2,1)S(1)} collective-permute-done((bf16[2,3,64,128]{3,2,1,0:T(8,128)(2,1)S(1)}, bf16[2,3,64,128]{3,2,1,0:T(8,128)(2,1)S(1)}, u32[]{:S(2)}, u32[]{:S(2)}) %collective-permute-start.13) | collective-permute-done | bytes 98336 | tf_op jit(solution)/shard_map/ppermute | solution.py:577
  96.1 0.0 collective-permute-done.14.refs_3_
  96.1 0.8 finish.1
  (13 shorter events, 0.1 us)
Async XLA Ops:
  1.1 13.9 %copy-start.5 = (bf16[2,3,64,128]{3,2,1,0:T(8,128)(2,1)}, bf16[2,3,64,128]{3,2,1,0:T(8,128)(2,1)S(1)}, u32[]{:S(2)}) copy-start(bf16[2,3,64,128]{3,2,1,0:T(8,128)(2,1)S(1)} %get-tuple-element.34.refs_0_) | copy-start | bytes 294916
  1.1 13.1 %collective-permute-start.3 = (bf16[2,3,64,128]{3,2,1,0:T(8,128)(2,1)S(1)}, bf16[2,3,64,128]{3,2,1,0:T(8,128)(2,1)S(1)}, u32[]{:S(2)}, u32[]{:S(2)}) collective-permute-start(bf16[2,3,64,128]{3,2,1,0:T(8,128)(2,1)S(1)} %get-tuple-element.34.refs_0_), channel_id=1, source_target_pairs={{0,3},{1,0},{2,1},{3,2},{4,7},{5,4},{6,5},{7,6},{8,11},{9,8},{10,9... | collective-permute-start | bytes 294920 | tf_op jit(solution)/shard_map/ppermute | solution.py:577
  6.2 8.7 %collective-permute-start.2 = (bf16[2,3,64,128]{3,2,1,0:T(8,128)(2,1)S(1)}, bf16[2,3,64,128]{3,2,1,0:T(8,128)(2,1)S(1)}, u32[]{:S(2)}, u32[]{:S(2)}) collective-permute-start(bf16[2,3,64,128]{3,2,1,0:T(8,128)(2,1)S(1)} %get-tuple-element.34.refs_0_), channel_id=1, source_target_pairs={{0,2},{1,3},{2,0},{3,1},{4,6},{5,7},{6,4},{7,5},{8,10},{9,11},{10,... | collective-permute-start | bytes 294920 | tf_op jit(solution)/shard_map/ppermute | solution.py:577
  6.2 8.7 %collective-permute-start.1 = (bf16[2,3,64,128]{3,2,1,0:T(8,128)(2,1)S(1)}, bf16[2,3,64,128]{3,2,1,0:T(8,128)(2,1)S(1)}, u32[]{:S(2)}, u32[]{:S(2)}) collective-permute-start(bf16[2,3,64,128]{3,2,1,0:T(8,128)(2,1)S(1)} %get-tuple-element.34.refs_0_), channel_id=1, source_target_pairs={{0,1},{1,2},{2,3},{3,0},{4,5},{5,6},{6,7},{7,4},{8,9},{9,10},{10,1... | collective-permute-start | bytes 294920 | tf_op jit(solution)/shard_map/ppermute | solution.py:577
  7.2 7.7 %collective-permute-start = (bf16[2,2,3,64,128]{4,3,2,1,0:T(8,128)(2,1)S(1)}, bf16[2,2,3,64,128]{4,3,2,1,0:T(8,128)(2,1)S(1)}, u32[]{:S(2)}, u32[]{:S(2)}) collective-permute-start(bf16[2,2,3,64,128]{4,3,2,1,0:T(8,128)(2,1)S(1)} %bitcast_bitcast_fusion), channel_id=1, source_target_pairs={{0,28},{4,0},{8,4},{12,8},{16,12},{20,16},{24,20},{28,24},{1,29},{... | collective-permute-start | bytes 589832 | tf_op jit(solution)/shard_map/ppermute | solution.py:577
  14.2 9.6 %copy-start.7 = (bf16[2,3,64,128]{3,2,1,0:T(8,128)(2,1)}, bf16[2,3,64,128]{3,2,1,0:T(8,128)(2,1)S(1)}, u32[]{:S(2)}) copy-start(bf16[2,3,64,128]{3,2,1,0:T(8,128)(2,1)S(1)} %collective-permute-done.3.refs_3_) | copy-start | bytes 294916
  14.9 8.8 %copy-start.8 = (bf16[2,3,64,128]{3,2,1,0:T(8,128)(2,1)}, bf16[2,3,64,128]{3,2,1,0:T(8,128)(2,1)S(1)}, u32[]{:S(2)}) copy-start(bf16[2,3,64,128]{3,2,1,0:T(8,128)(2,1)S(1)} %collective-permute-done.2.refs_2_) | copy-start | bytes 294916
  14.9 8.8 %copy-start.9 = (bf16[2,3,64,128]{3,2,1,0:T(8,128)(2,1)}, bf16[2,3,64,128]{3,2,1,0:T(8,128)(2,1)S(1)}, u32[]{:S(2)}) copy-start(bf16[2,3,64,128]{3,2,1,0:T(8,128)(2,1)S(1)} %collective-permute-done.1.refs_1_) | copy-start | bytes 294916
  14.9 34.0 %all-to-all-start = ((bf16[16,256,256]{2,1,0:T(8,128)(2,1)}), bf16[16,256,256]{2,1,0:T(8,128)(2,1)}, u32[]{:S(2)}, u32[]{:S(2)}) async-start(bf16[16,256,256]{2,1,0:T(8,128)(2,1)} %get-tuple-element.38), calls=%async_computation | async-start | bytes 4194304 | tf_op jit(solution)/shard_map/all_to_all | solution.py:604
  19.3 13.0 %copy-start.6 = (bf16[2,3,64,128]{3,2,1,0:T(8,128)(2,1)}, bf16[2,3,64,128]{3,2,1,0:T(8,128)(2,1)S(1)}, u32[]{:S(2)}) copy-start(bf16[2,3,64,128]{3,2,1,0:T(8,128)(2,1)S(1)} %get-tuple-element.57.refs_4_) | copy-start | bytes 294916
  19.3 7.6 %collective-permute-start.9 = (bf16[2,3,64,128]{3,2,1,0:T(8,128)(2,1)S(1)}, bf16[2,3,64,128]{3,2,1,0:T(8,128)(2,1)S(1)}, u32[]{:S(2)}, u32[]{:S(2)}) collective-permute-start(bf16[2,3,64,128]{3,2,1,0:T(8,128)(2,1)S(1)} %get-tuple-element.57.refs_4_), channel_id=1, source_target_pairs={{0,3},{1,0},{2,1},{3,2},{4,7},{5,4},{6,5},{7,6},{8,11},{9,8},{10,9... | collective-permute-start | bytes 294920 | tf_op jit(solution)/shard_map/ppermute | solution.py:577
  21.8 10.5 %collective-permute-start.8 = (bf16[2,3,64,128]{3,2,1,0:T(8,128)(2,1)S(1)}, bf16[2,3,64,128]{3,2,1,0:T(8,128)(2,1)S(1)}, u32[]{:S(2)}, u32[]{:S(2)}) collective-permute-start(bf16[2,3,64,128]{3,2,1,0:T(8,128)(2,1)S(1)} %get-tuple-element.57.refs_4_), channel_id=1, source_target_pairs={{0,2},{1,3},{2,0},{3,1},{4,6},{5,7},{6,4},{7,5},{8,10},{9,11},{10,... | collective-permute-start | bytes 294920 | tf_op jit(solution)/shard_map/ppermute | solution.py:577
  22.6 9.7 %collective-permute-start.7 = (bf16[2,3,64,128]{3,2,1,0:T(8,128)(2,1)S(1)}, bf16[2,3,64,128]{3,2,1,0:T(8,128)(2,1)S(1)}, u32[]{:S(2)}, u32[]{:S(2)}) collective-permute-start(bf16[2,3,64,128]{3,2,1,0:T(8,128)(2,1)S(1)} %get-tuple-element.57.refs_4_), channel_id=1, source_target_pairs={{0,1},{1,2},{2,3},{3,0},{4,5},{5,6},{6,7},{7,4},{8,9},{9,10},{10,1... | collective-permute-start | bytes 294920 | tf_op jit(solution)/shard_map/ppermute | solution.py:577
  23.8 20.1 %collective-permute-start.6 = (bf16[2,2,3,64,128]{4,3,2,1,0:T(8,128)(2,1)S(1)}, bf16[2,2,3,64,128]{4,3,2,1,0:T(8,128)(2,1)S(1)}, u32[]{:S(2)}, u32[]{:S(2)}) collective-permute-start(bf16[2,2,3,64,128]{4,3,2,1,0:T(8,128)(2,1)S(1)} %pad_maximum_fusion.refs_0_), channel_id=1, source_target_pairs={{0,3},{1,0},{2,1},{3,2},{4,7},{5,4},{6,5},{7,6},{8,11},{9,8},{10,9... | collective-permute-start | bytes 589832 | tf_op jit(solution)/shard_map/ppermute | solution.py:577
  26.6 22.3 %collective-permute-start.5 = (bf16[2,2,3,64,128]{4,3,2,1,0:T(8,128)(2,1)S(1)}, bf16[2,2,3,64,128]{4,3,2,1,0:T(8,128)(2,1)S(1)}, u32[]{:S(2)}, u32[]{:S(2)}) collective-permute-start(bf16[2,2,3,64,128]{4,3,2,1,0:T(8,128)(2,1)S(1)} %pad_maximum_fusion.refs_0_), channel_id=1, source_target_pairs={{0,2},{1,3},{2,0},{3,1},{4,6},{5,7},{6,4},{7,5},{8,10},{9,11},{10,... | collective-permute-start | bytes 589832 | tf_op jit(solution)/shard_map/ppermute | solution.py:577
  26.9 5.4 %copy-start.10 = (bf16[2,3,64,128]{3,2,1,0:T(8,128)(2,1)}, bf16[2,3,64,128]{3,2,1,0:T(8,128)(2,1)S(1)}, u32[]{:S(2)}) copy-start(bf16[2,3,64,128]{3,2,1,0:T(8,128)(2,1)S(1)} %collective-permute-done.9.refs_7_) | copy-start | bytes 294916
  26.9 22.0 %collective-permute-start.4 = (bf16[2,2,3,64,128]{4,3,2,1,0:T(8,128)(2,1)S(1)}, bf16[2,2,3,64,128]{4,3,2,1,0:T(8,128)(2,1)S(1)}, u32[]{:S(2)}, u32[]{:S(2)}) collective-permute-start(bf16[2,2,3,64,128]{4,3,2,1,0:T(8,128)(2,1)S(1)} %pad_maximum_fusion.refs_0_), channel_id=1, source_target_pairs={{0,1},{1,2},{2,3},{3,0},{4,5},{5,6},{6,7},{7,4},{8,9},{9,10},{10,1... | collective-permute-start | bytes 589832 | tf_op jit(solution)/shard_map/ppermute | solution.py:577
  32.3 0.6 copy-start.11
  32.3 0.7 copy-start.12
  33.0 15.9 %copy-start.1 = (bf16[4,256,256]{2,1,0:T(8,128)(2,1)S(1)}, bf16[4,256,256]{2,1,0:T(8,128)(2,1)}, u32[]{:S(2)}) copy-start(bf16[4,256,256]{2,1,0:T(8,128)(2,1)} %constant.38.refs_10_.refs_6_.tabs_hbm) | copy-start | bytes 1572868
  33.0 15.9 %copy-start.3 = (s32[72]{0:T(128)S(1)}, s32[72]{0:T(128)}, u32[]{:S(2)}) copy-start(s32[72]{0:T(128)} %get-tuple-element.31.meta_ref) | copy-start | bytes 868
  43.9 19.6 %copy-start.4 = (f32[2,256,256]{2,1,0:T(8,128)S(1)}, f32[2,256,256]{2,1,0:T(8,128)}, u32[]{:S(2)}) copy-start(f32[2,256,256]{2,1,0:T(8,128)} %constant.27.clone.refs_9_.kernel_hbm) | copy-start | bytes 1572868
  63.2 9.9 %collective-permute-start.10 = (bf16[2,3,256,128]{3,2,1,0:T(8,128)(2,1)S(1)}, bf16[2,3,256,128]{3,2,1,0:T(8,128)(2,1)S(1)}, u32[]{:S(2)}, u32[]{:S(2)}) collective-permute-start(bf16[2,3,256,128]{3,2,1,0:T(8,128)(2,1)S(1)} %get-tuple-element.43), channel_id=1, source_target_pairs={{0,4},{4,8},{8,12},{12,16},{16,20},{20,24},{24,28},{28,0},{1,5},{5... | collective-permute-start | bytes 1179656 | tf_op jit(solution)/shard_map/ppermute | solution.py:577
  63.5 3.9 %copy-start = (f32[256,512]{1,0:T(8,128)S(1)}, f32[256,512]{1,0:T(8,128)}, u32[]{:S(2)}) copy-start(f32[256,512]{1,0:T(8,128)} %probe_hbm.1) | copy-start | bytes 1572868
  67.3 5.7 %copy-start.2 = (s32[3]{0:T(128)S(1)}, s32[3]{0:T(128)}, u32[]{:S(2)}) copy-start(s32[3]{0:T(128)} %pad_add_fusion.here_ref) | copy-start | bytes 40
  73.7 8.9 %collective-permute-start.11 = (bf16[2,3,256,128]{3,2,1,0:T(8,128)(2,1)S(1)}, bf16[2,3,256,128]{3,2,1,0:T(8,128)(2,1)S(1)}, u32[]{:S(2)}, u32[]{:S(2)}) collective-permute-start(bf16[2,3,256,128]{3,2,1,0:T(8,128)(2,1)S(1)} %get-tuple-element.48), channel_id=1, source_target_pairs={{0,4},{4,8},{8,12},{12,16},{16,20},{20,24},{24,28},{28,0},{1,5},{5... | collective-permute-start | bytes 1179656 | tf_op jit(solution)/shard_map/ppermute | solution.py:577
  75.8 12.7 %collective-permute-start.15 = (bf16[2,3,64,128]{3,2,1,0:T(8,128)(2,1)S(1)}, bf16[2,3,64,128]{3,2,1,0:T(8,128)(2,1)S(1)}, u32[]{:S(2)}, u32[]{:S(2)}) collective-permute-start(bf16[2,3,64,128]{3,2,1,0:T(8,128)(2,1)S(1)} %get-tuple-element.54), channel_id=1, source_target_pairs={{0,1},{1,2},{2,3},{3,0},{4,5},{5,6},{6,7},{7,4},{8,9},{9,10},{10,1... | collective-permute-start | bytes 294920 | tf_op jit(solution)/shard_map/ppermute | solution.py:577
  79.3 12.0 %collective-permute-start.16 = (bf16[2,3,64,128]{3,2,1,0:T(8,128)(2,1)S(1)}, bf16[2,3,64,128]{3,2,1,0:T(8,128)(2,1)S(1)}, u32[]{:S(2)}, u32[]{:S(2)}) collective-permute-start(bf16[2,3,64,128]{3,2,1,0:T(8,128)(2,1)S(1)} %get-tuple-element.55), channel_id=1, source_target_pairs={{0,2},{1,3},{2,0},{3,1},{4,6},{5,7},{6,4},{7,5},{8,10},{9,11},{10,... | collective-permute-start | bytes 294920 | tf_op jit(solution)/shard_map/ppermute | solution.py:577
  79.9 11.4 %collective-permute-start.17 = (bf16[2,3,64,128]{3,2,1,0:T(8,128)(2,1)S(1)}, bf16[2,3,64,128]{3,2,1,0:T(8,128)(2,1)S(1)}, u32[]{:S(2)}, u32[]{:S(2)}) collective-permute-start(bf16[2,3,64,128]{3,2,1,0:T(8,128)(2,1)S(1)} %get-tuple-element.56), channel_id=1, source_target_pairs={{0,3},{1,0},{2,1},{3,2},{4,7},{5,4},{6,5},{7,6},{8,11},{9,8},{10,9... | collective-permute-start | bytes 294920 | tf_op jit(solution)/shard_map/ppermute | solution.py:577
  83.2 8.1 %collective-permute-start.12 = (bf16[2,3,64,128]{3,2,1,0:T(8,128)(2,1)S(1)}, bf16[2,3,64,128]{3,2,1,0:T(8,128)(2,1)S(1)}, u32[]{:S(2)}, u32[]{:S(2)}) collective-permute-start(bf16[2,3,64,128]{3,2,1,0:T(8,128)(2,1)S(1)} %get-tuple-element.50), channel_id=1, source_target_pairs={{0,1},{1,2},{2,3},{3,0},{4,5},{5,6},{6,7},{7,4},{8,9},{9,10},{10,1... | collective-permute-start | bytes 294920 | tf_op jit(solution)/shard_map/ppermute | solution.py:577
  86.2 10.0 %collective-permute-start.13 = (bf16[2,3,64,128]{3,2,1,0:T(8,128)(2,1)S(1)}, bf16[2,3,64,128]{3,2,1,0:T(8,128)(2,1)S(1)}, u32[]{:S(2)}, u32[]{:S(2)}) collective-permute-start(bf16[2,3,64,128]{3,2,1,0:T(8,128)(2,1)S(1)} %get-tuple-element.51), channel_id=1, source_target_pairs={{0,2},{1,3},{2,0},{3,1},{4,6},{5,7},{6,4},{7,5},{8,10},{9,11},{10,... | collective-permute-start | bytes 294920 | tf_op jit(solution)/shard_map/ppermute | solution.py:577
  88.5 7.7 %collective-permute-start.14 = (bf16[2,3,64,128]{3,2,1,0:T(8,128)(2,1)S(1)}, bf16[2,3,64,128]{3,2,1,0:T(8,128)(2,1)S(1)}, u32[]{:S(2)}, u32[]{:S(2)}) collective-permute-start(bf16[2,3,64,128]{3,2,1,0:T(8,128)(2,1)S(1)} %get-tuple-element.52), channel_id=1, source_target_pairs={{0,3},{1,0},{2,1},{3,2},{4,7},{5,4},{6,5},{7,6},{8,11},{9,8},{10,9... | collective-permute-start | bytes 294920 | tf_op jit(solution)/shard_map/ppermute | solution.py:577

commit v5 on v4

--- a/solution.py
+++ b/solution.py
@@ -13,6 +13,8 @@
 K = 16
 CAP = 2
 GROUP = 4
+WIDE = 8
+CHUNK = 64
 COLS = 128
 chirp_strength = 40.0
 bf16 = jnp.bfloat16
@@ -165,12 +167,12 @@
             rows_ref[:, :, pl.ds(start, height), :] = shards[side, k].astype(f32)
 
 
-def group_count(meta_ref):
-    return lax.div(meta_ref[4 * K] + GROUP - 1, GROUP)
-
-
-def group_loop(meta_ref, ready, body, incoming=None, outgoing=None):
-    last = group_count(meta_ref)
+def group_count(meta_ref, size):
+    return lax.div(meta_ref[4 * K] + size - 1, size)
+
+
+def group_loop(meta_ref, ready, body, incoming=None, outgoing=None, size=GROUP):
+    last = group_count(meta_ref, size)
 
     def each(make, group, do):
         if make is not None:
@@ -194,7 +196,7 @@
         def _():
             each(outgoing, group - 2, lambda c: c.wait())
 
-        body([GROUP * group + j for j in range(GROUP)], group, lax.rem(group, 2))
+        body([size * group + j for j in range(size)], group, lax.rem(group, 2))
         each(outgoing, group, lambda c: c.start())
         return carry
 
@@ -206,11 +208,15 @@
             each(outgoing, last - back, lambda c: c.wait())
 
 
-def add_window(totals_ref, top, col, term):
-    extent = term[0][0].shape[0]
+def rows_of(field, start, count):
+    return tuple(tuple(part[start : start + count] for part in side) for side in field)
+
+
+def add_window(totals_ref, top, col, term, start=0):
+    count = term[0][0].shape[0]
     for j in (0, 1):
         for plane in (0, 1):
-            place = (plane, col + j, pl.ds(top, extent), slice(None))
+            place = (plane, col + j, pl.ds(top + start, count), slice(None))
             totals_ref[place] += term[j][plane]
 
 
@@ -385,53 +391,46 @@
             far_grads.append(parts)
         for i, (at, grad) in enumerate(zip(items, inverse(far_grads, tables))):
             grad = halves(grad)
-            col = meta_ref[2 * K + at]
-            add_window(
-                totals_ref, meta_ref[3 * K + at], col,
-                [product_conj(p, q) for p, q in zip(wave_of(i), grad)],
-            )
-            w = window(rows_ref, meta_ref[K + at], col, extent)
-            back = folded(tuple(product_conj(p, q) for p, q in zip(w, grad)))
-            for k in (0, 1):
-                back_ref[at, k] = back[k]
+            top, col = meta_ref[K + at], meta_ref[2 * K + at]
+            target = meta_ref[3 * K + at]
+            for start in range(0, extent, CHUNK):
+                rows = slice(start, start + CHUNK)
+                part = rows_of(grad, start, CHUNK)
+                wave = halves((wave_buf[slot, i, 0, rows], wave_buf[slot, i, 1, rows]))
+                term = [product_conj(p, q) for p, q in zip(wave, part)]
+                add_window(totals_ref, target, col, term, start)
+                w = window(rows_ref, top + start, col, CHUNK)
+                back = folded(tuple(product_conj(p, q) for p, q in zip(w, part)))
+                for k in (0, 1):
+                    back_ref[at, k, rows] = back[k]
 
     group_loop(meta_ref, ready, body, incoming)
     give_lower(totals_ref, lower_ref)
 
 
-def back_kernel(meta_ref, fields_ref, kernel_hbm, tabs_hbm, back_ref, kernel_ref, tabs, sems):
-    once = start_all(copies_of([(kernel_hbm, kernel_ref), (tabs_hbm, tabs)], sems))
-
-    def ready():
-        wait_all(once)
-
-    def body(items, group, slot):
-        fields = [(fields_ref[at, 0], fields_ref[at, 1]) for at in items]
-        for at, field in zip(items, forward(fields, tables_of(tabs))):
-            for k, part in enumerate(by_kernel(field, kernel_ref, True)):
-                back_ref[at, k] = part
-
-    group_loop(meta_ref, ready, body)
-
-
-def exit_kernel(meta_ref, back_ref, probe_hbm, tabs_hbm, totals_ref, lower_ref, probe_ref, tabs, sems):
+def exit_kernel(
+    meta_ref, fields_ref, probe_hbm, kernel_hbm, tabs_hbm, totals_ref, lower_ref, probe_ref, kernel_ref, tabs, sems
+):
     extent = probe_ref.shape[0]
-    once = start_all(copies_of([(probe_hbm, probe_ref), (tabs_hbm, tabs)], sems))
+    once = start_all(copies_of([(probe_hbm, probe_ref), (kernel_hbm, kernel_ref), (tabs_hbm, tabs)], sems))
 
     def ready():
         totals_ref[...] = jnp.zeros_like(totals_ref)
         wait_all(once)
 
     def body(items, group, slot):
-        probe = halves((probe_ref[:, :extent], probe_ref[:, extent:]))
-        fields = [(back_ref[at, 0], back_ref[at, 1]) for at in items]
-        for at, grad in zip(items, inverse(fields, tables_of(tabs))):
-            add_window(
-                totals_ref, meta_ref[3 * K + at], meta_ref[2 * K + at],
-                [product_conj(p, q) for p, q in zip(probe, halves(grad))],
-            )
-
-    group_loop(meta_ref, ready, body)
+        tables = tables_of(tabs)
+        fields = [(fields_ref[at, 0], fields_ref[at, 1]) for at in items]
+        back = [by_kernel(x, kernel_ref, True) for x in forward(fields, tables)]
+        grads = [halves(x) for x in inverse(back, tables)]
+        for start in range(0, extent, CHUNK):
+            rows = slice(start, start + CHUNK)
+            probe = halves((probe_ref[rows, :extent], probe_ref[rows, extent:]))
+            for at, grad in zip(items, grads):
+                term = [product_conj(p, q) for p, q in zip(probe, rows_of(grad, start, CHUNK))]
+                add_window(totals_ref, meta_ref[3 * K + at], meta_ref[2 * K + at], term, start)
+
+    group_loop(meta_ref, ready, body, size=WIDE)
     give_lower(totals_ref, lower_ref)
 
 
@@ -540,20 +539,12 @@
     )
 
 
-def backs(meta, fields, kernel, tabs):
-    extent = kernel.shape[1]
-    return call(
-        back_kernel, "backs", [meta, fields, kernel, tabs], [smem, vmem, hbm, hbm],
-        pltpu.VMEM((K, 2, extent, extent), bf16), vmem, [like(kernel), like(tabs), sems(2)],
-        cost(1, extent), limit=30 * MIB,
-    )
-
-
-def exits(meta, back, probe, tabs, blocks):
+def exits(meta, fields, probe, kernel, tabs, blocks):
     extent = probe.shape[0]
     return call(
-        exit_kernel, "exits", [meta, back, probe, tabs], [smem, vmem, hbm, hbm], totals_out(extent, blocks),
-        [vmem, vmem], [like(probe), like(tabs), sems(2)], cost(0.1, extent), limit=30 * MIB,
+        exit_kernel, "exits", [meta, fields, probe, kernel, tabs], [smem, vmem, hbm, hbm, hbm],
+        totals_out(extent, blocks), [vmem, vmem], [like(probe), like(kernel), like(tabs), sems(3)],
+        cost(0.1, extent), limit=30 * MIB,
     )
 
 
@@ -608,9 +599,8 @@
     wave = waves(meta, first, probe_wave, kernel, tabs, slab_count)
     fields, total1, lower1 = misfits(meta, second, wave, images, tabs, slab_count)
     moved1 = passed_along(lower1, "tile", 1)
-    back = backs(meta, fields, kernel, tabs)
     mine1, *sends1 = combine(here, total1, moved1, slab_count)
-    total0, lower0 = exits(meta, back, probe_wave, tabs, blocks)
+    total0, lower0 = exits(meta, fields, probe_wave, kernel, tabs, blocks)
     lower0, mine1, *sends1 = lax.optimization_barrier((lower0, mine1, *sends1))
     moved0 = passed_along(lower0, "tile", 1)
     parts1 = [mine1] + [passed_along(x, "slab", k + 1) for k, x in enumerate(sends1)]

time: 97.6 us -> 96.1 us (0.985)
  Pallas kernels: 42 us -> 40.9 us
    pallas_call x8 -> x7, Pallas kernels: 42 us -> 40.9 us  [call(): pl.pallas_call(kernel, in_specs=in_specs, out_specs=out_specs, out_shape=...]
  transfers between devices with their start and end apart: 19 -> 19, of which waited for: 4 -> 5; matrix products, arithmetic and copies ran while one was open for 1% -> 1% of each run, Pallas kernels for 27% -> 26%
where the time goes in v5:
time: 96.1 us; the launch traced here: 95.2 us
  Pallas kernels  40.9 us (43%)
  starting transfers between devices  35.7 us (37%)
  waiting for transfers between devices  15.9 us (17%)
  other arithmetic  1.69 us (2%)
    pallas_call x7, Pallas kernels, call(): pl.pallas_call(kernel, in_specs=in_specs, out_specs=out_specs, out_shape=...  40.9 us
    ppermute x18, starting transfers between devices, passed_along(): return lax.ppermute(value, axis, pairs)  31.3 us
    ppermute x18, waiting for transfers between devices, passed_along(): return lax.ppermute(value, axis, pairs)  15.9 us
    all_to_all x1, starting transfers between devices, shards(): lax.all_to_all(packed, 'tile', split_axis=0, concat_axis=0, tiled=True)  4.37 us
  transfers between devices with their start and end apart: 19, of which 5 were waited for; matrix products, arithmetic and copies ran while one was open for 1% of the time, Pallas kernels for 26%

profile of v5, /device:TPU:0, one launch (start us, length us, event | category | flops | bytes accessed | tf_op | source)
XLA Modules:
  0.0 95.2 jit_solution(10293767153841474992)
XLA Ops:
  0.0 1.0 %bitcast_bitcast_fusion = bf16[2,2,3,64,128]{4,3,2,1,0:T(8,128)(2,1)S(1)} fusion(f32[2,2,64,384]{3,2,1,0:T(8,128)} %param.13), kind=kLoop, calls=%fused_computation | loop fusion | flops 98304 | bytes 589824 | tf_op jit(solution)/shard_map/convert_element_type | solution.py:583
  1.1 0.0 copy-start.5
  1.1 5.1 %collective-permute-start.3 = (bf16[2,3,64,128]{3,2,1,0:T(8,128)(2,1)S(1)}, bf16[2,3,64,128]{3,2,1,0:T(8,128)(2,1)S(1)}, u32[]{:S(2)}, u32[]{:S(2)}) collective-permute-start(bf16[2,3,64,128]{3,2,1,0:T(8,128)(2,1)S(1)} %get-tuple-element.34.refs_0_), channel_id=1, source_target_pairs={{0,3},{1,0},{2,1},{3,2},{4,7},{5,4},{6,5},{7,6},{8,11},{9,8},{10,9... | collective-permute-start | bytes 294920 | tf_op jit(solution)/shard_map/ppermute | solution.py:568
  6.2 0.0 collective-permute-start.2
  6.2 1.0 %collective-permute-start.1 = (bf16[2,3,64,128]{3,2,1,0:T(8,128)(2,1)S(1)}, bf16[2,3,64,128]{3,2,1,0:T(8,128)(2,1)S(1)}, u32[]{:S(2)}, u32[]{:S(2)}) collective-permute-start(bf16[2,3,64,128]{3,2,1,0:T(8,128)(2,1)S(1)} %get-tuple-element.34.refs_0_), channel_id=1, source_target_pairs={{0,1},{1,2},{2,3},{3,0},{4,5},{5,6},{6,7},{7,4},{8,9},{9,10},{10,1... | collective-permute-start | bytes 294920 | tf_op jit(solution)/shard_map/ppermute | solution.py:568
  7.2 1.0 %collective-permute-start = (bf16[2,2,3,64,128]{4,3,2,1,0:T(8,128)(2,1)S(1)}, bf16[2,2,3,64,128]{4,3,2,1,0:T(8,128)(2,1)S(1)}, u32[]{:S(2)}, u32[]{:S(2)}) collective-permute-start(bf16[2,2,3,64,128]{4,3,2,1,0:T(8,128)(2,1)S(1)} %bitcast_bitcast_fusion), channel_id=1, source_target_pairs={{0,28},{4,0},{8,4},{12,8},{16,12},{20,16},{24,20},{28,24},{1,29},{... | collective-permute-start | bytes 589832 | tf_op jit(solution)/shard_map/ppermute | solution.py:568
  8.2 0.6 pad_add_fusion.here_ref
  8.9 5.3 %route.1 = (bf16[16,256,256]{2,1,0:T(8,128)(2,1)}, s32[72]{0:T(128)}) custom-call(s32[3]{0:T(128)} %pad_add_fusion.here_ref, s32[448]{0:T(512)} %owner_hbm.1, s32[448]{0:T(512)} %row_hbm.1, s32[448]{0:T(512)} %col_hbm.1, bf16[14,256,256]{2,1,0:T(8,128)(2,1)} %images_hbm.1, bf16[2,256,256]{2,1,0:T(8,128)(2,1)} %constant.33.permute_hbm), custom_call_target="tpu_custom_call" | custom-call | flops 1073741824 | tf_op jit(solution)/shard_map/route/pallas_call | solution.py:449
  14.1 0.0 collective-permute-done.3.refs_3_
  14.2 0.0 copy-start.7
  14.2 0.8 collective-permute-done.2.refs_2_
  14.9 0.0 collective-permute-done.1.refs_1_
  14.9 0.0 collective-permute-done
  14.9 0.0 copy-done.5
  14.9 4.4 %all-to-all-start = ((bf16[16,256,256]{2,1,0:T(8,128)(2,1)}), bf16[16,256,256]{2,1,0:T(8,128)(2,1)}, u32[]{:S(2)}, u32[]{:S(2)}) async-start(bf16[16,256,256]{2,1,0:T(8,128)(2,1)} %get-tuple-element.38), calls=%async_computation | async-start | bytes 4194304 | tf_op jit(solution)/shard_map/all_to_all | solution.py:595
  19.3 0.0 copy-start.6
  19.3 2.5 %collective-permute-start.9 = (bf16[2,3,64,128]{3,2,1,0:T(8,128)(2,1)S(1)}, bf16[2,3,64,128]{3,2,1,0:T(8,128)(2,1)S(1)}, u32[]{:S(2)}, u32[]{:S(2)}) collective-permute-start(bf16[2,3,64,128]{3,2,1,0:T(8,128)(2,1)S(1)} %get-tuple-element.57.refs_4_), channel_id=1, source_target_pairs={{0,3},{1,0},{2,1},{3,2},{4,7},{5,4},{6,5},{7,6},{8,11},{9,8},{10,9... | collective-permute-start | bytes 294920 | tf_op jit(solution)/shard_map/ppermute | solution.py:568
  21.8 0.9 collective-permute-start.8
  22.7 1.0 %collective-permute-start.7 = (bf16[2,3,64,128]{3,2,1,0:T(8,128)(2,1)S(1)}, bf16[2,3,64,128]{3,2,1,0:T(8,128)(2,1)S(1)}, u32[]{:S(2)}, u32[]{:S(2)}) collective-permute-start(bf16[2,3,64,128]{3,2,1,0:T(8,128)(2,1)S(1)} %get-tuple-element.57.refs_4_), channel_id=1, source_target_pairs={{0,1},{1,2},{2,3},{3,0},{4,5},{5,6},{6,7},{7,4},{8,9},{9,10},{10,1... | collective-permute-start | bytes 294920 | tf_op jit(solution)/shard_map/ppermute | solution.py:568
  23.7 0.0 copy-done.7
  23.7 0.0 copy-done.8
  23.8 0.0 copy-done.9
  23.8 2.8 %collective-permute-start.6 = (bf16[2,2,3,64,128]{4,3,2,1,0:T(8,128)(2,1)S(1)}, bf16[2,2,3,64,128]{4,3,2,1,0:T(8,128)(2,1)S(1)}, u32[]{:S(2)}, u32[]{:S(2)}) collective-permute-start(bf16[2,2,3,64,128]{4,3,2,1,0:T(8,128)(2,1)S(1)} %pad_maximum_fusion.refs_0_), channel_id=1, source_target_pairs={{0,3},{1,0},{2,1},{3,2},{4,7},{5,4},{6,5},{7,6},{8,11},{9,8},{10,9... | collective-permute-start | bytes 589832 | tf_op jit(solution)/shard_map/ppermute | solution.py:568
  26.6 0.3 collective-permute-start.5
  26.9 0.0 collective-permute-done.9.refs_7_
  26.9 0.4 collective-permute-start.4
  27.3 5.1 %collective-permute-done.8.refs_6_ = bf16[2,3,64,128]{3,2,1,0:T(8,128)(2,1)S(1)} collective-permute-done((bf16[2,3,64,128]{3,2,1,0:T(8,128)(2,1)S(1)}, bf16[2,3,64,128]{3,2,1,0:T(8,128)(2,1)S(1)}, u32[]{:S(2)}, u32[]{:S(2)}) %collective-permute-start.8) | collective-permute-done | bytes 98336 | tf_op jit(solution)/shard_map/ppermute | solution.py:568
  32.4 0.0 collective-permute-done.7.refs_5_
  32.4 0.0 copy-done.6
  32.4 0.0 copy-done.10
  32.4 0.6 copy-done.11
  33.0 0.0 copy-done.12
  33.1 10.9 %waves.1.refs_4_ = f32[4,4,2,256,256]{4,3,2,1,0:T(8,128)} custom-call(s32[72]{0:T(128)} %get-tuple-element.31.meta_ref, bf16[2,3,64,128]{3,2,1,0:T(8,128)(2,1)} %copy-done.5, bf16[2,3,64,128]{3,2,1,0:T(8,128)(2,1)} %copy-done.9, bf16[2,3,64,128]{3,2,1,0:T(8,128)(2,1)} %copy-done.8, bf16[2,3,64,128]{3,2,1,0:T(8,128)(2,1)} %copy-done.7, ...), custom_call_target="tpu_custom_call" | custom-call | flops 8589934592 | tf_op jit(solution)/shard_map/waves/pallas_call | solution.py:449
  44.0 0.0 copy-start
  44.0 0.0 copy-start.2
  44.0 0.0 collective-permute-done.6.refs_3_
  44.0 4.9 %collective-permute-done.5.refs_2_ = bf16[2,2,3,64,128]{4,3,2,1,0:T(8,128)(2,1)S(1)} collective-permute-done((bf16[2,2,3,64,128]{4,3,2,1,0:T(8,128)(2,1)S(1)}, bf16[2,2,3,64,128]{4,3,2,1,0:T(8,128)(2,1)S(1)}, u32[]{:S(2)}, u32[]{:S(2)}) %collective-permute-start.5) | collective-permute-done | bytes 196640 | tf_op jit(solution)/shard_map/ppermute | solution.py:568
  48.9 0.0 collective-permute-done.4.refs_1_
  48.9 0.0 all-to-all-done.refs_5_
  48.9 0.0 copy-done.1
  48.9 0.0 copy-done.4
  48.9 14.6 %misfits.1 = (bf16[16,2,256,256]{3,2,1,0:T(8,128)(2,1)S(1)}, f32[2,3,768,128]{3,2,1,0:T(8,128)S(1)}, bf16[2,3,256,128]{3,2,1,0:T(8,128)(2,1)S(1)}) custom-call(s32[72]{0:T(128)S(1)} %copy-done.4, bf16[2,2,3,64,128]{4,3,2,1,0:T(8,128)(2,1)S(1)} %pad_maximum_fusion.refs_0_, bf16[2,2,3,64,128]{4,3,2,1,0:T(8,128)(2,1)S(1)} %collective-permute-done.4.refs_1_, ...), custom_call_target="tpu_custom_call" | custom-call | flops 8589934592 | tf_op jit(solution)/shard_map/misfits/pallas_call | solution.py:449
  63.5 0.1 collective-permute-start.10
  63.6 0.0 copy-done
  63.6 0.0 copy-done.2
  63.6 8.1 %exits.1 = (f32[2,3,768,128]{3,2,1,0:T(8,128)S(1)}, bf16[2,3,256,128]{3,2,1,0:T(8,128)(2,1)S(1)}) custom-call(s32[72]{0:T(128)S(1)} %copy-done.4, bf16[16,2,256,256]{3,2,1,0:T(8,128)(2,1)S(1)} %get-tuple-element.39.fields_ref, f32[256,512]{1,0:T(8,128)S(1)} %copy-done, f32[2,256,256]{2,1,0:T(8,128)S(1)} %copy-done.2, bf16[4,256,256]{2,1,0:T(8,128)(2,1)S(1)} %copy-done.1), custom_call_target="tpu_custom_call" | custom-call | flops 429496736 | tf_op jit(solution)/shard_map/exits/pallas_call | solution.py:449
  71.7 0.0 collective-permute-done.10.moved_ref
  71.8 0.6 combine.2
  72.4 1.7 %collective-permute-start.11 = (bf16[2,3,256,128]{3,2,1,0:T(8,128)(2,1)S(1)}, bf16[2,3,256,128]{3,2,1,0:T(8,128)(2,1)S(1)}, u32[]{:S(2)}, u32[]{:S(2)}) collective-permute-start(bf16[2,3,256,128]{3,2,1,0:T(8,128)(2,1)S(1)} %get-tuple-element.48), channel_id=1, source_target_pairs={{0,4},{4,8},{8,12},{12,16},{16,20},{20,24},{24,28},{28,0},{1,5},{5... | collective-permute-start | bytes 1179656 | tf_op jit(solution)/shard_map/ppermute | solution.py:568
  74.0 3.4 %collective-permute-start.15 = (bf16[2,3,64,128]{3,2,1,0:T(8,128)(2,1)S(1)}, bf16[2,3,64,128]{3,2,1,0:T(8,128)(2,1)S(1)}, u32[]{:S(2)}, u32[]{:S(2)}) collective-permute-start(bf16[2,3,64,128]{3,2,1,0:T(8,128)(2,1)S(1)} %get-tuple-element.54), channel_id=1, source_target_pairs={{0,1},{1,2},{2,3},{3,0},{4,5},{5,6},{6,7},{7,4},{8,9},{9,10},{10,1... | collective-permute-start | bytes 294920 | tf_op jit(solution)/shard_map/ppermute | solution.py:568
  77.4 2.0 %collective-permute-start.16 = (bf16[2,3,64,128]{3,2,1,0:T(8,128)(2,1)S(1)}, bf16[2,3,64,128]{3,2,1,0:T(8,128)(2,1)S(1)}, u32[]{:S(2)}, u32[]{:S(2)}) collective-permute-start(bf16[2,3,64,128]{3,2,1,0:T(8,128)(2,1)S(1)} %get-tuple-element.55), channel_id=1, source_target_pairs={{0,2},{1,3},{2,0},{3,1},{4,6},{5,7},{6,4},{7,5},{8,10},{9,11},{10,... | collective-permute-start | bytes 294920 | tf_op jit(solution)/shard_map/ppermute | solution.py:568
  79.4 2.9 %collective-permute-start.17 = (bf16[2,3,64,128]{3,2,1,0:T(8,128)(2,1)S(1)}, bf16[2,3,64,128]{3,2,1,0:T(8,128)(2,1)S(1)}, u32[]{:S(2)}, u32[]{:S(2)}) collective-permute-start(bf16[2,3,64,128]{3,2,1,0:T(8,128)(2,1)S(1)} %get-tuple-element.56), channel_id=1, source_target_pairs={{0,3},{1,0},{2,1},{3,2},{4,7},{5,4},{6,5},{7,6},{8,11},{9,8},{10,9... | collective-permute-start | bytes 294920 | tf_op jit(solution)/shard_map/ppermute | solution.py:568
  82.3 0.0 collective-permute-done.11.moved_ref
  82.3 0.6 combine.3
  83.0 1.5 %collective-permute-start.12 = (bf16[2,3,64,128]{3,2,1,0:T(8,128)(2,1)S(1)}, bf16[2,3,64,128]{3,2,1,0:T(8,128)(2,1)S(1)}, u32[]{:S(2)}, u32[]{:S(2)}) collective-permute-start(bf16[2,3,64,128]{3,2,1,0:T(8,128)(2,1)S(1)} %get-tuple-element.50), channel_id=1, source_target_pairs={{0,1},{1,2},{2,3},{3,0},{4,5},{5,6},{6,7},{7,4},{8,9},{9,10},{10,1... | collective-permute-start | bytes 294920 | tf_op jit(solution)/shard_map/ppermute | solution.py:568
  84.4 2.0 %collective-permute-start.13 = (bf16[2,3,64,128]{3,2,1,0:T(8,128)(2,1)S(1)}, bf16[2,3,64,128]{3,2,1,0:T(8,128)(2,1)S(1)}, u32[]{:S(2)}, u32[]{:S(2)}) collective-permute-start(bf16[2,3,64,128]{3,2,1,0:T(8,128)(2,1)S(1)} %get-tuple-element.51), channel_id=1, source_target_pairs={{0,2},{1,3},{2,0},{3,1},{4,6},{5,7},{6,4},{7,5},{8,10},{9,11},{10,... | collective-permute-start | bytes 294920 | tf_op jit(solution)/shard_map/ppermute | solution.py:568
  86.4 0.0 collective-permute-done.15.refs_5_
  86.4 2.8 %collective-permute-start.14 = (bf16[2,3,64,128]{3,2,1,0:T(8,128)(2,1)S(1)}, bf16[2,3,64,128]{3,2,1,0:T(8,128)(2,1)S(1)}, u32[]{:S(2)}, u32[]{:S(2)}) collective-permute-start(bf16[2,3,64,128]{3,2,1,0:T(8,128)(2,1)S(1)} %get-tuple-element.52), channel_id=1, source_target_pairs={{0,3},{1,0},{2,1},{3,2},{4,7},{5,4},{6,5},{7,6},{8,11},{9,8},{10,9... | collective-permute-start | bytes 294920 | tf_op jit(solution)/shard_map/ppermute | solution.py:568
  89.3 0.0 collective-permute-done.16.refs_6_
  89.3 0.0 collective-permute-done.17.refs_7_
  89.3 1.2 %collective-permute-done.12.refs_1_ = bf16[2,3,64,128]{3,2,1,0:T(8,128)(2,1)S(1)} collective-permute-done((bf16[2,3,64,128]{3,2,1,0:T(8,128)(2,1)S(1)}, bf16[2,3,64,128]{3,2,1,0:T(8,128)(2,1)S(1)}, u32[]{:S(2)}, u32[]{:S(2)}) %collective-permute-start.12) | collective-permute-done | bytes 98336 | tf_op jit(solution)/shard_map/ppermute | solution.py:568
  90.5 3.9 %collective-permute-done.13.refs_2_ = bf16[2,3,64,128]{3,2,1,0:T(8,128)(2,1)S(1)} collective-permute-done((bf16[2,3,64,128]{3,2,1,0:T(8,128)(2,1)S(1)}, bf16[2,3,64,128]{3,2,1,0:T(8,128)(2,1)S(1)}, u32[]{:S(2)}, u32[]{:S(2)}) %collective-permute-start.13) | collective-permute-done | bytes 98336 | tf_op jit(solution)/shard_map/ppermute | solution.py:568
  94.4 0.0 collective-permute-done.14.refs_3_
  94.4 0.8 finish.1
  (12 shorter events, 0.1 us)
Async XLA Ops:
  1.1 13.9 %copy-start.5 = (bf16[2,3,64,128]{3,2,1,0:T(8,128)(2,1)}, bf16[2,3,64,128]{3,2,1,0:T(8,128)(2,1)S(1)}, u32[]{:S(2)}) copy-start(bf16[2,3,64,128]{3,2,1,0:T(8,128)(2,1)S(1)} %get-tuple-element.34.refs_0_) | copy-start | bytes 294916
  1.1 13.1 %collective-permute-start.3 = (bf16[2,3,64,128]{3,2,1,0:T(8,128)(2,1)S(1)}, bf16[2,3,64,128]{3,2,1,0:T(8,128)(2,1)S(1)}, u32[]{:S(2)}, u32[]{:S(2)}) collective-permute-start(bf16[2,3,64,128]{3,2,1,0:T(8,128)(2,1)S(1)} %get-tuple-element.34.refs_0_), channel_id=1, source_target_pairs={{0,3},{1,0},{2,1},{3,2},{4,7},{5,4},{6,5},{7,6},{8,11},{9,8},{10,9... | collective-permute-start | bytes 294920 | tf_op jit(solution)/shard_map/ppermute | solution.py:568
  6.2 8.7 %collective-permute-start.2 = (bf16[2,3,64,128]{3,2,1,0:T(8,128)(2,1)S(1)}, bf16[2,3,64,128]{3,2,1,0:T(8,128)(2,1)S(1)}, u32[]{:S(2)}, u32[]{:S(2)}) collective-permute-start(bf16[2,3,64,128]{3,2,1,0:T(8,128)(2,1)S(1)} %get-tuple-element.34.refs_0_), channel_id=1, source_target_pairs={{0,2},{1,3},{2,0},{3,1},{4,6},{5,7},{6,4},{7,5},{8,10},{9,11},{10,... | collective-permute-start | bytes 294920 | tf_op jit(solution)/shard_map/ppermute | solution.py:568
  6.2 8.7 %collective-permute-start.1 = (bf16[2,3,64,128]{3,2,1,0:T(8,128)(2,1)S(1)}, bf16[2,3,64,128]{3,2,1,0:T(8,128)(2,1)S(1)}, u32[]{:S(2)}, u32[]{:S(2)}) collective-permute-start(bf16[2,3,64,128]{3,2,1,0:T(8,128)(2,1)S(1)} %get-tuple-element.34.refs_0_), channel_id=1, source_target_pairs={{0,1},{1,2},{2,3},{3,0},{4,5},{5,6},{6,7},{7,4},{8,9},{9,10},{10,1... | collective-permute-start | bytes 294920 | tf_op jit(solution)/shard_map/ppermute | solution.py:568
  7.2 7.7 %collective-permute-start = (bf16[2,2,3,64,128]{4,3,2,1,0:T(8,128)(2,1)S(1)}, bf16[2,2,3,64,128]{4,3,2,1,0:T(8,128)(2,1)S(1)}, u32[]{:S(2)}, u32[]{:S(2)}) collective-permute-start(bf16[2,2,3,64,128]{4,3,2,1,0:T(8,128)(2,1)S(1)} %bitcast_bitcast_fusion), channel_id=1, source_target_pairs={{0,28},{4,0},{8,4},{12,8},{16,12},{20,16},{24,20},{28,24},{1,29},{... | collective-permute-start | bytes 589832 | tf_op jit(solution)/shard_map/ppermute | solution.py:568
  14.2 9.6 %copy-start.7 = (bf16[2,3,64,128]{3,2,1,0:T(8,128)(2,1)}, bf16[2,3,64,128]{3,2,1,0:T(8,128)(2,1)S(1)}, u32[]{:S(2)}) copy-start(bf16[2,3,64,128]{3,2,1,0:T(8,128)(2,1)S(1)} %collective-permute-done.3.refs_3_) | copy-start | bytes 294916
  14.9 8.8 %copy-start.8 = (bf16[2,3,64,128]{3,2,1,0:T(8,128)(2,1)}, bf16[2,3,64,128]{3,2,1,0:T(8,128)(2,1)S(1)}, u32[]{:S(2)}) copy-start(bf16[2,3,64,128]{3,2,1,0:T(8,128)(2,1)S(1)} %collective-permute-done.2.refs_2_) | copy-start | bytes 294916
  14.9 8.8 %copy-start.9 = (bf16[2,3,64,128]{3,2,1,0:T(8,128)(2,1)}, bf16[2,3,64,128]{3,2,1,0:T(8,128)(2,1)S(1)}, u32[]{:S(2)}) copy-start(bf16[2,3,64,128]{3,2,1,0:T(8,128)(2,1)S(1)} %collective-permute-done.1.refs_1_) | copy-start | bytes 294916
  14.9 34.0 %all-to-all-start = ((bf16[16,256,256]{2,1,0:T(8,128)(2,1)}), bf16[16,256,256]{2,1,0:T(8,128)(2,1)}, u32[]{:S(2)}, u32[]{:S(2)}) async-start(bf16[16,256,256]{2,1,0:T(8,128)(2,1)} %get-tuple-element.38), calls=%async_computation | async-start | bytes 4194304 | tf_op jit(solution)/shard_map/all_to_all | solution.py:595
  19.3 13.0 %copy-start.6 = (bf16[2,3,64,128]{3,2,1,0:T(8,128)(2,1)}, bf16[2,3,64,128]{3,2,1,0:T(8,128)(2,1)S(1)}, u32[]{:S(2)}) copy-start(bf16[2,3,64,128]{3,2,1,0:T(8,128)(2,1)S(1)} %get-tuple-element.57.refs_4_) | copy-start | bytes 294916
  19.3 7.5 %collective-permute-start.9 = (bf16[2,3,64,128]{3,2,1,0:T(8,128)(2,1)S(1)}, bf16[2,3,64,128]{3,2,1,0:T(8,128)(2,1)S(1)}, u32[]{:S(2)}, u32[]{:S(2)}) collective-permute-start(bf16[2,3,64,128]{3,2,1,0:T(8,128)(2,1)S(1)} %get-tuple-element.57.refs_4_), channel_id=1, source_target_pairs={{0,3},{1,0},{2,1},{3,2},{4,7},{5,4},{6,5},{7,6},{8,11},{9,8},{10,9... | collective-permute-start | bytes 294920 | tf_op jit(solution)/shard_map/ppermute | solution.py:568
  21.8 10.6 %collective-permute-start.8 = (bf16[2,3,64,128]{3,2,1,0:T(8,128)(2,1)S(1)}, bf16[2,3,64,128]{3,2,1,0:T(8,128)(2,1)S(1)}, u32[]{:S(2)}, u32[]{:S(2)}) collective-permute-start(bf16[2,3,64,128]{3,2,1,0:T(8,128)(2,1)S(1)} %get-tuple-element.57.refs_4_), channel_id=1, source_target_pairs={{0,2},{1,3},{2,0},{3,1},{4,6},{5,7},{6,4},{7,5},{8,10},{9,11},{10,... | collective-permute-start | bytes 294920 | tf_op jit(solution)/shard_map/ppermute | solution.py:568
  22.7 9.7 %collective-permute-start.7 = (bf16[2,3,64,128]{3,2,1,0:T(8,128)(2,1)S(1)}, bf16[2,3,64,128]{3,2,1,0:T(8,128)(2,1)S(1)}, u32[]{:S(2)}, u32[]{:S(2)}) collective-permute-start(bf16[2,3,64,128]{3,2,1,0:T(8,128)(2,1)S(1)} %get-tuple-element.57.refs_4_), channel_id=1, source_target_pairs={{0,1},{1,2},{2,3},{3,0},{4,5},{5,6},{6,7},{7,4},{8,9},{9,10},{10,1... | collective-permute-start | bytes 294920 | tf_op jit(solution)/shard_map/ppermute | solution.py:568
  23.8 20.3 %collective-permute-start.6 = (bf16[2,2,3,64,128]{4,3,2,1,0:T(8,128)(2,1)S(1)}, bf16[2,2,3,64,128]{4,3,2,1,0:T(8,128)(2,1)S(1)}, u32[]{:S(2)}, u32[]{:S(2)}) collective-permute-start(bf16[2,2,3,64,128]{4,3,2,1,0:T(8,128)(2,1)S(1)} %pad_maximum_fusion.refs_0_), channel_id=1, source_target_pairs={{0,3},{1,0},{2,1},{3,2},{4,7},{5,4},{6,5},{7,6},{8,11},{9,8},{10,9... | collective-permute-start | bytes 589832 | tf_op jit(solution)/shard_map/ppermute | solution.py:568
  26.6 22.3 %collective-permute-start.5 = (bf16[2,2,3,64,128]{4,3,2,1,0:T(8,128)(2,1)S(1)}, bf16[2,2,3,64,128]{4,3,2,1,0:T(8,128)(2,1)S(1)}, u32[]{:S(2)}, u32[]{:S(2)}) collective-permute-start(bf16[2,2,3,64,128]{4,3,2,1,0:T(8,128)(2,1)S(1)} %pad_maximum_fusion.refs_0_), channel_id=1, source_target_pairs={{0,2},{1,3},{2,0},{3,1},{4,6},{5,7},{6,4},{7,5},{8,10},{9,11},{10,... | collective-permute-start | bytes 589832 | tf_op jit(solution)/shard_map/ppermute | solution.py:568
  26.9 5.5 %copy-start.10 = (bf16[2,3,64,128]{3,2,1,0:T(8,128)(2,1)}, bf16[2,3,64,128]{3,2,1,0:T(8,128)(2,1)S(1)}, u32[]{:S(2)}) copy-start(bf16[2,3,64,128]{3,2,1,0:T(8,128)(2,1)S(1)} %collective-permute-done.9.refs_7_) | copy-start | bytes 294916
  26.9 22.1 %collective-permute-start.4 = (bf16[2,2,3,64,128]{4,3,2,1,0:T(8,128)(2,1)S(1)}, bf16[2,2,3,64,128]{4,3,2,1,0:T(8,128)(2,1)S(1)}, u32[]{:S(2)}, u32[]{:S(2)}) collective-permute-start(bf16[2,2,3,64,128]{4,3,2,1,0:T(8,128)(2,1)S(1)} %pad_maximum_fusion.refs_0_), channel_id=1, source_target_pairs={{0,1},{1,2},{2,3},{3,0},{4,5},{5,6},{6,7},{7,4},{8,9},{9,10},{10,1... | collective-permute-start | bytes 589832 | tf_op jit(solution)/shard_map/ppermute | solution.py:568
  32.4 0.6 copy-start.11
  32.4 0.7 copy-start.12
  33.0 15.9 %copy-start.1 = (bf16[4,256,256]{2,1,0:T(8,128)(2,1)S(1)}, bf16[4,256,256]{2,1,0:T(8,128)(2,1)}, u32[]{:S(2)}) copy-start(bf16[4,256,256]{2,1,0:T(8,128)(2,1)} %constant.38.refs_10_.refs_6_.tabs_hbm) | copy-start | bytes 1572868
  33.0 15.9 %copy-start.4 = (s32[72]{0:T(128)S(1)}, s32[72]{0:T(128)}, u32[]{:S(2)}) copy-start(s32[72]{0:T(128)} %get-tuple-element.31.meta_ref) | copy-start | bytes 868
  44.0 19.6 %copy-start = (f32[256,512]{1,0:T(8,128)S(1)}, f32[256,512]{1,0:T(8,128)}, u32[]{:S(2)}) copy-start(f32[256,512]{1,0:T(8,128)} %probe_hbm.1) | copy-start | bytes 1572868
  44.0 19.6 %copy-start.2 = (f32[2,256,256]{2,1,0:T(8,128)S(1)}, f32[2,256,256]{2,1,0:T(8,128)}, u32[]{:S(2)}) copy-start(f32[2,256,256]{2,1,0:T(8,128)} %constant.27.clone.refs_9_.kernel_hbm) | copy-start | bytes 1572868
  63.5 8.2 %collective-permute-start.10 = (bf16[2,3,256,128]{3,2,1,0:T(8,128)(2,1)S(1)}, bf16[2,3,256,128]{3,2,1,0:T(8,128)(2,1)S(1)}, u32[]{:S(2)}, u32[]{:S(2)}) collective-permute-start(bf16[2,3,256,128]{3,2,1,0:T(8,128)(2,1)S(1)} %get-tuple-element.43), channel_id=1, source_target_pairs={{0,4},{4,8},{8,12},{12,16},{16,20},{20,24},{24,28},{28,0},{1,5},{5... | collective-permute-start | bytes 1179656 | tf_op jit(solution)/shard_map/ppermute | solution.py:568
  63.6 8.1 %copy-start.3 = (s32[3]{0:T(128)S(1)}, s32[3]{0:T(128)}, u32[]{:S(2)}) copy-start(s32[3]{0:T(128)} %pad_add_fusion.here_ref) | copy-start | bytes 40
  72.4 10.0 %collective-permute-start.11 = (bf16[2,3,256,128]{3,2,1,0:T(8,128)(2,1)S(1)}, bf16[2,3,256,128]{3,2,1,0:T(8,128)(2,1)S(1)}, u32[]{:S(2)}, u32[]{:S(2)}) collective-permute-start(bf16[2,3,256,128]{3,2,1,0:T(8,128)(2,1)S(1)} %get-tuple-element.48), channel_id=1, source_target_pairs={{0,4},{4,8},{8,12},{12,16},{16,20},{20,24},{24,28},{28,0},{1,5},{5... | collective-permute-start | bytes 1179656 | tf_op jit(solution)/shard_map/ppermute | solution.py:568
  74.0 12.4 %collective-permute-start.15 = (bf16[2,3,64,128]{3,2,1,0:T(8,128)(2,1)S(1)}, bf16[2,3,64,128]{3,2,1,0:T(8,128)(2,1)S(1)}, u32[]{:S(2)}, u32[]{:S(2)}) collective-permute-start(bf16[2,3,64,128]{3,2,1,0:T(8,128)(2,1)S(1)} %get-tuple-element.54), channel_id=1, source_target_pairs={{0,1},{1,2},{2,3},{3,0},{4,5},{5,6},{6,7},{7,4},{8,9},{9,10},{10,1... | collective-permute-start | bytes 294920 | tf_op jit(solution)/shard_map/ppermute | solution.py:568
  77.4 11.9 %collective-permute-start.16 = (bf16[2,3,64,128]{3,2,1,0:T(8,128)(2,1)S(1)}, bf16[2,3,64,128]{3,2,1,0:T(8,128)(2,1)S(1)}, u32[]{:S(2)}, u32[]{:S(2)}) collective-permute-start(bf16[2,3,64,128]{3,2,1,0:T(8,128)(2,1)S(1)} %get-tuple-element.55), channel_id=1, source_target_pairs={{0,2},{1,3},{2,0},{3,1},{4,6},{5,7},{6,4},{7,5},{8,10},{9,11},{10,... | collective-permute-start | bytes 294920 | tf_op jit(solution)/shard_map/ppermute | solution.py:568
  79.4 9.9 %collective-permute-start.17 = (bf16[2,3,64,128]{3,2,1,0:T(8,128)(2,1)S(1)}, bf16[2,3,64,128]{3,2,1,0:T(8,128)(2,1)S(1)}, u32[]{:S(2)}, u32[]{:S(2)}) collective-permute-start(bf16[2,3,64,128]{3,2,1,0:T(8,128)(2,1)S(1)} %get-tuple-element.56), channel_id=1, source_target_pairs={{0,3},{1,0},{2,1},{3,2},{4,7},{5,4},{6,5},{7,6},{8,11},{9,8},{10,9... | collective-permute-start | bytes 294920 | tf_op jit(solution)/shard_map/ppermute | solution.py:568
  83.0 7.5 %collective-permute-start.12 = (bf16[2,3,64,128]{3,2,1,0:T(8,128)(2,1)S(1)}, bf16[2,3,64,128]{3,2,1,0:T(8,128)(2,1)S(1)}, u32[]{:S(2)}, u32[]{:S(2)}) collective-permute-start(bf16[2,3,64,128]{3,2,1,0:T(8,128)(2,1)S(1)} %get-tuple-element.50), channel_id=1, source_target_pairs={{0,1},{1,2},{2,3},{3,0},{4,5},{5,6},{6,7},{7,4},{8,9},{9,10},{10,1... | collective-permute-start | bytes 294920 | tf_op jit(solution)/shard_map/ppermute | solution.py:568
  84.4 9.9 %collective-permute-start.13 = (bf16[2,3,64,128]{3,2,1,0:T(8,128)(2,1)S(1)}, bf16[2,3,64,128]{3,2,1,0:T(8,128)(2,1)S(1)}, u32[]{:S(2)}, u32[]{:S(2)}) collective-permute-start(bf16[2,3,64,128]{3,2,1,0:T(8,128)(2,1)S(1)} %get-tuple-element.51), channel_id=1, source_target_pairs={{0,2},{1,3},{2,0},{3,1},{4,6},{5,7},{6,4},{7,5},{8,10},{9,11},{10,... | collective-permute-start | bytes 294920 | tf_op jit(solution)/shard_map/ppermute | solution.py:568
  86.4 7.9 %collective-permute-start.14 = (bf16[2,3,64,128]{3,2,1,0:T(8,128)(2,1)S(1)}, bf16[2,3,64,128]{3,2,1,0:T(8,128)(2,1)S(1)}, u32[]{:S(2)}, u32[]{:S(2)}) collective-permute-start(bf16[2,3,64,128]{3,2,1,0:T(8,128)(2,1)S(1)} %get-tuple-element.52), channel_id=1, source_target_pairs={{0,3},{1,0},{2,1},{3,2},{4,7},{5,4},{6,5},{7,6},{8,11},{9,8},{10,9... | collective-permute-start | bytes 294920 | tf_op jit(solution)/shard_map/ppermute | solution.py:568

commit v6 on v5

--- a/solution.py
+++ b/solution.py
@@ -112,6 +112,10 @@
 
 def product_conj(a, b):
     return a[0] * b[0] + a[1] * b[1], a[0] * b[1] - a[1] * b[0]
+
+
+def cut(x):
+    return x[0].astype(bf16), x[1].astype(bf16)
 
 
 def halves(x, h=COLS):
@@ -337,15 +341,15 @@
 
     def body(items, group, slot):
         tables = tables_of(tabs)
-        probe = halves((probe_ref[:, :extent], probe_ref[:, extent:]))
+        probe = [cut(side) for side in halves((probe_ref[:, :extent], probe_ref[:, extent:]))]
         fields = []
         for at in items:
             w = window(rows_ref, meta_ref[K + at], meta_ref[2 * K + at], extent)
-            fields.append(folded(tuple(product(p, q) for p, q in zip(probe, w))))
+            fields.append(folded(tuple(product(p, cut(q)) for p, q in zip(probe, w))))
         spread = [by_kernel(x, kernel_ref, False) for x in forward(fields, tables)]
         for i, wave in enumerate(inverse(spread, tables)):
-            wave_buf[slot, i, 0] = wave[0]
-            wave_buf[slot, i, 1] = wave[1]
+            wave_buf[slot, i, 0] = wave[0].astype(bf16)
+            wave_buf[slot, i, 1] = wave[1].astype(bf16)
 
     group_loop(meta_ref, ready, body, None, outgoing)
 
@@ -379,7 +383,7 @@
         fields = []
         for i, at in enumerate(items):
             w = window(rows_ref, meta_ref[K + at], meta_ref[2 * K + at], extent)
-            fields.append(folded(tuple(product(p, q) for p, q in zip(wave_of(i), w))))
+            fields.append(folded(tuple(product(cut(p), cut(q)) for p, q in zip(wave_of(i), w))))
         far_grads = []
         for i, far in enumerate(forward(fields, tables)):
             parts = []
@@ -396,11 +400,11 @@
             for start in range(0, extent, CHUNK):
                 rows = slice(start, start + CHUNK)
                 part = rows_of(grad, start, CHUNK)
-                wave = halves((wave_buf[slot, i, 0, rows], wave_buf[slot, i, 1, rows]))
+                wave = halves((wave_buf[slot, i, 0, rows].astype(f32), wave_buf[slot, i, 1, rows].astype(f32)))
                 term = [product_conj(p, q) for p, q in zip(wave, part)]
                 add_window(totals_ref, target, col, term, start)
                 w = window(rows_ref, top + start, col, CHUNK)
-                back = folded(tuple(product_conj(p, q) for p, q in zip(w, part)))
+                back = folded(tuple(product_conj(cut(p), cut(q)) for p, q in zip(w, part)))
                 for k in (0, 1):
                     back_ref[at, k, rows] = back[k]
 
@@ -508,11 +512,11 @@
     extent = probe.shape[0]
     scratch = [
         shards_scratch(rows, slabs), like(probe), like(kernel), like(tabs), rows_padded(rows, slabs),
-        group_buffer(extent, f32), sems(2 * slabs + 3), sems(2, 1),
+        group_buffer(extent, bf16), sems(2 * slabs + 3), sems(2, 1),
     ]
     return call(
         functools.partial(wave_kernel, len(rows)), "waves", [meta] + rows + [probe, kernel, tabs],
-        [smem] + [anywhere] * len(rows) + [hbm] * 3, groups(extent, f32), hbm, scratch,
+        [smem] + [anywhere] * len(rows) + [hbm] * 3, groups(extent, bf16), hbm, scratch,
         cost(2, extent),
     )
 
@@ -528,7 +532,7 @@
     extent = images.shape[1]
     scratch = [
         shards_scratch(rows, slabs), like(tabs), rows_padded(rows, slabs),
-        group_buffer(extent, f32), pltpu.VMEM((2, GROUP, extent, extent), bf16),
+        group_buffer(extent, bf16), pltpu.VMEM((2, GROUP, extent, extent), bf16),
         sems(2 * slabs + 1), sems(2, 1 + GROUP),
     ]
     return call(

time: 96.1 us -> 93.6 us (0.974)
  Pallas kernels: 40.9 us -> 38.3 us
  waiting for transfers between devices: 15.9 us -> 17 us
    pallas_call x7, Pallas kernels: 40.9 us -> 38.3 us  [call(): pl.pallas_call(kernel, in_specs=in_specs, out_specs=out_specs, out_shape=...]
    ppermute x18, waiting for transfers between devices: 15.9 us -> 17 us  [passed_along(): return lax.ppermute(value, axis, pairs)]
  transfers between devices with their start and end apart: 19 -> 19, of which waited for: 5 -> 6; matrix products, arithmetic and copies ran while one was open for 1% -> 1% of each run, Pallas kernels for 26% -> 26%
where the time goes in v6:
time: 93.6 us; the launch traced here: 92.7 us
  Pallas kernels  38.3 us (41%)
  starting transfers between devices  34.8 us (37%)
  waiting for transfers between devices  17 us (18%)
  other arithmetic  1.6 us (2%)
    pallas_call x7, Pallas kernels, call(): pl.pallas_call(kernel, in_specs=in_specs, out_specs=out_specs, out_shape=...  38.3 us
    ppermute x18, starting transfers between devices, passed_along(): return lax.ppermute(value, axis, pairs)  30.4 us
    ppermute x18, waiting for transfers between devices, passed_along(): return lax.ppermute(value, axis, pairs)  17 us
    all_to_all x1, starting transfers between devices, shards(): lax.all_to_all(packed, 'tile', split_axis=0, concat_axis=0, tiled=True)  4.36 us
  transfers between devices with their start and end apart: 19, of which 6 were waited for; matrix products, arithmetic and copies ran while one was open for 1% of the time, Pallas kernels for 26%

profile of v6, /device:TPU:0, one launch (start us, length us, event | category | flops | bytes accessed | tf_op | source)
XLA Modules:
  0.0 92.7 jit_solution(11936446800670836457)
XLA Ops:
  0.0 1.0 %bitcast_bitcast_fusion = bf16[2,2,3,64,128]{4,3,2,1,0:T(8,128)(2,1)S(1)} fusion(f32[2,2,64,384]{3,2,1,0:T(8,128)} %param.13), kind=kLoop, calls=%fused_computation | loop fusion | flops 98304 | bytes 589824 | tf_op jit(solution)/shard_map/convert_element_type | solution.py:587
  1.1 0.0 copy-start.5
  1.1 5.1 %collective-permute-start.3 = (bf16[2,3,64,128]{3,2,1,0:T(8,128)(2,1)S(1)}, bf16[2,3,64,128]{3,2,1,0:T(8,128)(2,1)S(1)}, u32[]{:S(2)}, u32[]{:S(2)}) collective-permute-start(bf16[2,3,64,128]{3,2,1,0:T(8,128)(2,1)S(1)} %get-tuple-element.34.refs_0_), channel_id=1, source_target_pairs={{0,3},{1,0},{2,1},{3,2},{4,7},{5,4},{6,5},{7,6},{8,11},{9,8},{10,9... | collective-permute-start | bytes 294920 | tf_op jit(solution)/shard_map/ppermute | solution.py:572
  6.2 0.0 collective-permute-start.2
  6.2 1.0 %collective-permute-start.1 = (bf16[2,3,64,128]{3,2,1,0:T(8,128)(2,1)S(1)}, bf16[2,3,64,128]{3,2,1,0:T(8,128)(2,1)S(1)}, u32[]{:S(2)}, u32[]{:S(2)}) collective-permute-start(bf16[2,3,64,128]{3,2,1,0:T(8,128)(2,1)S(1)} %get-tuple-element.34.refs_0_), channel_id=1, source_target_pairs={{0,1},{1,2},{2,3},{3,0},{4,5},{5,6},{6,7},{7,4},{8,9},{9,10},{10,1... | collective-permute-start | bytes 294920 | tf_op jit(solution)/shard_map/ppermute | solution.py:572
  7.2 1.0 %collective-permute-start = (bf16[2,2,3,64,128]{4,3,2,1,0:T(8,128)(2,1)S(1)}, bf16[2,2,3,64,128]{4,3,2,1,0:T(8,128)(2,1)S(1)}, u32[]{:S(2)}, u32[]{:S(2)}) collective-permute-start(bf16[2,2,3,64,128]{4,3,2,1,0:T(8,128)(2,1)S(1)} %bitcast_bitcast_fusion), channel_id=1, source_target_pairs={{0,28},{4,0},{8,4},{12,8},{16,12},{20,16},{24,20},{28,24},{1,29},{... | collective-permute-start | bytes 589832 | tf_op jit(solution)/shard_map/ppermute | solution.py:572
  8.2 0.6 pad_add_fusion.here_ref
  8.8 5.3 %route.1 = (bf16[16,256,256]{2,1,0:T(8,128)(2,1)}, s32[72]{0:T(128)}) custom-call(s32[3]{0:T(128)} %pad_add_fusion.here_ref, s32[448]{0:T(512)} %owner_hbm.1, s32[448]{0:T(512)} %row_hbm.1, s32[448]{0:T(512)} %col_hbm.1, bf16[14,256,256]{2,1,0:T(8,128)(2,1)} %images_hbm.1, bf16[2,256,256]{2,1,0:T(8,128)(2,1)} %constant.33.permute_hbm), custom_call_target="tpu_custom_call" | custom-call | flops 1073741824 | tf_op jit(solution)/shard_map/route/pallas_call | solution.py:453
  14.1 0.0 collective-permute-done.3.refs_3_
  14.1 0.0 copy-start.7
  14.1 0.8 collective-permute-done.2.refs_2_
  14.9 0.0 collective-permute-done.1.refs_1_
  14.9 0.0 collective-permute-done
  14.9 0.0 copy-done.5
  14.9 4.4 %all-to-all-start = ((bf16[16,256,256]{2,1,0:T(8,128)(2,1)}), bf16[16,256,256]{2,1,0:T(8,128)(2,1)}, u32[]{:S(2)}, u32[]{:S(2)}) async-start(bf16[16,256,256]{2,1,0:T(8,128)(2,1)} %get-tuple-element.38), calls=%async_computation | async-start | bytes 4194304 | tf_op jit(solution)/shard_map/all_to_all | solution.py:599
  19.3 0.0 copy-start.6
  19.3 2.4 %collective-permute-start.9 = (bf16[2,3,64,128]{3,2,1,0:T(8,128)(2,1)S(1)}, bf16[2,3,64,128]{3,2,1,0:T(8,128)(2,1)S(1)}, u32[]{:S(2)}, u32[]{:S(2)}) collective-permute-start(bf16[2,3,64,128]{3,2,1,0:T(8,128)(2,1)S(1)} %get-tuple-element.57.refs_4_), channel_id=1, source_target_pairs={{0,3},{1,0},{2,1},{3,2},{4,7},{5,4},{6,5},{7,6},{8,11},{9,8},{10,9... | collective-permute-start | bytes 294920 | tf_op jit(solution)/shard_map/ppermute | solution.py:572
  21.7 0.9 collective-permute-start.8
  22.6 1.1 %collective-permute-start.7 = (bf16[2,3,64,128]{3,2,1,0:T(8,128)(2,1)S(1)}, bf16[2,3,64,128]{3,2,1,0:T(8,128)(2,1)S(1)}, u32[]{:S(2)}, u32[]{:S(2)}) collective-permute-start(bf16[2,3,64,128]{3,2,1,0:T(8,128)(2,1)S(1)} %get-tuple-element.57.refs_4_), channel_id=1, source_target_pairs={{0,1},{1,2},{2,3},{3,0},{4,5},{5,6},{6,7},{7,4},{8,9},{9,10},{10,1... | collective-permute-start | bytes 294920 | tf_op jit(solution)/shard_map/ppermute | solution.py:572
  23.7 0.0 copy-done.7
  23.7 0.0 copy-done.8
  23.7 0.0 copy-done.9
  23.8 2.8 %collective-permute-start.6 = (bf16[2,2,3,64,128]{4,3,2,1,0:T(8,128)(2,1)S(1)}, bf16[2,2,3,64,128]{4,3,2,1,0:T(8,128)(2,1)S(1)}, u32[]{:S(2)}, u32[]{:S(2)}) collective-permute-start(bf16[2,2,3,64,128]{4,3,2,1,0:T(8,128)(2,1)S(1)} %pad_maximum_fusion.refs_0_), channel_id=1, source_target_pairs={{0,3},{1,0},{2,1},{3,2},{4,7},{5,4},{6,5},{7,6},{8,11},{9,8},{10,9... | collective-permute-start | bytes 589832 | tf_op jit(solution)/shard_map/ppermute | solution.py:572
  26.5 0.3 collective-permute-start.5
  26.8 0.0 collective-permute-done.9.refs_7_
  26.8 0.4 collective-permute-start.4
  27.2 5.1 %collective-permute-done.8.refs_6_ = bf16[2,3,64,128]{3,2,1,0:T(8,128)(2,1)S(1)} collective-permute-done((bf16[2,3,64,128]{3,2,1,0:T(8,128)(2,1)S(1)}, bf16[2,3,64,128]{3,2,1,0:T(8,128)(2,1)S(1)}, u32[]{:S(2)}, u32[]{:S(2)}) %collective-permute-start.8) | collective-permute-done | bytes 98336 | tf_op jit(solution)/shard_map/ppermute | solution.py:572
  32.3 0.0 collective-permute-done.7.refs_5_
  32.3 0.0 copy-done.6
  32.3 0.0 copy-done.10
  32.3 0.6 copy-done.11
  32.9 0.0 copy-done.12
  33.0 9.8 %waves.1.refs_4_ = bf16[4,4,2,256,256]{4,3,2,1,0:T(8,128)(2,1)} custom-call(s32[72]{0:T(128)} %get-tuple-element.31.meta_ref, bf16[2,3,64,128]{3,2,1,0:T(8,128)(2,1)} %copy-done.5, bf16[2,3,64,128]{3,2,1,0:T(8,128)(2,1)} %copy-done.9, bf16[2,3,64,128]{3,2,1,0:T(8,128)(2,1)} %copy-done.8, bf16[2,3,64,128]{3,2,1,0:T(8,128)(2,1)} %copy-done.7, ...), custom_call_target="tpu_custom_call" | custom-call | flops 8589934592 | tf_op jit(solution)/shard_map/waves/pallas_call | solution.py:453
  42.8 0.0 copy-start
  42.8 0.0 copy-start.2
  42.8 0.0 collective-permute-done.6.refs_3_
  42.8 6.0 %collective-permute-done.5.refs_2_ = bf16[2,2,3,64,128]{4,3,2,1,0:T(8,128)(2,1)S(1)} collective-permute-done((bf16[2,2,3,64,128]{4,3,2,1,0:T(8,128)(2,1)S(1)}, bf16[2,2,3,64,128]{4,3,2,1,0:T(8,128)(2,1)S(1)}, u32[]{:S(2)}, u32[]{:S(2)}) %collective-permute-start.5) | collective-permute-done | bytes 196640 | tf_op jit(solution)/shard_map/ppermute | solution.py:572
  48.8 0.0 collective-permute-done.4.refs_1_
  48.8 0.0 all-to-all-done.refs_5_
  48.8 0.0 copy-done.1
  48.9 13.2 %misfits.1 = (bf16[16,2,256,256]{3,2,1,0:T(8,128)(2,1)S(1)}, f32[2,3,768,128]{3,2,1,0:T(8,128)S(1)}, bf16[2,3,256,128]{3,2,1,0:T(8,128)(2,1)S(1)}) custom-call(s32[72]{0:T(128)S(1)} %copy-done.4, bf16[2,2,3,64,128]{4,3,2,1,0:T(8,128)(2,1)S(1)} %pad_maximum_fusion.refs_0_, bf16[2,2,3,64,128]{4,3,2,1,0:T(8,128)(2,1)S(1)} %collective-permute-done.4.refs_1_, ...), custom_call_target="tpu_custom_call" | custom-call | flops 8589934592 | tf_op jit(solution)/shard_map/misfits/pallas_call | solution.py:453
  62.0 0.1 collective-permute-start.10
  62.1 0.0 copy-done
  62.1 0.0 copy-done.2
  62.1 0.0 copy-start.3
  62.1 8.0 %exits.1 = (f32[2,3,768,128]{3,2,1,0:T(8,128)S(1)}, bf16[2,3,256,128]{3,2,1,0:T(8,128)(2,1)S(1)}) custom-call(s32[72]{0:T(128)S(1)} %copy-done.4, bf16[16,2,256,256]{3,2,1,0:T(8,128)(2,1)S(1)} %get-tuple-element.39.fields_ref, f32[256,512]{1,0:T(8,128)S(1)} %copy-done, f32[2,256,256]{2,1,0:T(8,128)S(1)} %copy-done.2, bf16[4,256,256]{2,1,0:T(8,128)(2,1)S(1)} %copy-done.1), custom_call_target="tpu_custom_call" | custom-call | flops 429496736 | tf_op jit(solution)/shard_map/exits/pallas_call | solution.py:453
  70.1 0.1 collective-permute-done.10.moved_ref
  70.2 0.6 combine.2
  70.8 1.8 %collective-permute-start.11 = (bf16[2,3,256,128]{3,2,1,0:T(8,128)(2,1)S(1)}, bf16[2,3,256,128]{3,2,1,0:T(8,128)(2,1)S(1)}, u32[]{:S(2)}, u32[]{:S(2)}) collective-permute-start(bf16[2,3,256,128]{3,2,1,0:T(8,128)(2,1)S(1)} %get-tuple-element.48), channel_id=1, source_target_pairs={{0,4},{4,8},{8,12},{12,16},{16,20},{20,24},{24,28},{28,0},{1,5},{5... | collective-permute-start | bytes 1179656 | tf_op jit(solution)/shard_map/ppermute | solution.py:572
  72.6 0.8 collective-permute-start.15
  73.4 3.7 %collective-permute-start.16 = (bf16[2,3,64,128]{3,2,1,0:T(8,128)(2,1)S(1)}, bf16[2,3,64,128]{3,2,1,0:T(8,128)(2,1)S(1)}, u32[]{:S(2)}, u32[]{:S(2)}) collective-permute-start(bf16[2,3,64,128]{3,2,1,0:T(8,128)(2,1)S(1)} %get-tuple-element.55), channel_id=1, source_target_pairs={{0,2},{1,3},{2,0},{3,1},{4,6},{5,7},{6,4},{7,5},{8,10},{9,11},{10,... | collective-permute-start | bytes 294920 | tf_op jit(solution)/shard_map/ppermute | solution.py:572
  77.1 2.9 %collective-permute-start.17 = (bf16[2,3,64,128]{3,2,1,0:T(8,128)(2,1)S(1)}, bf16[2,3,64,128]{3,2,1,0:T(8,128)(2,1)S(1)}, u32[]{:S(2)}, u32[]{:S(2)}) collective-permute-start(bf16[2,3,64,128]{3,2,1,0:T(8,128)(2,1)S(1)} %get-tuple-element.56), channel_id=1, source_target_pairs={{0,3},{1,0},{2,1},{3,2},{4,7},{5,4},{6,5},{7,6},{8,11},{9,8},{10,9... | collective-permute-start | bytes 294920 | tf_op jit(solution)/shard_map/ppermute | solution.py:572
  80.0 0.0 collective-permute-done.11.moved_ref
  80.0 0.6 combine.3
  80.7 1.5 %collective-permute-start.12 = (bf16[2,3,64,128]{3,2,1,0:T(8,128)(2,1)S(1)}, bf16[2,3,64,128]{3,2,1,0:T(8,128)(2,1)S(1)}, u32[]{:S(2)}, u32[]{:S(2)}) collective-permute-start(bf16[2,3,64,128]{3,2,1,0:T(8,128)(2,1)S(1)} %get-tuple-element.50), channel_id=1, source_target_pairs={{0,1},{1,2},{2,3},{3,0},{4,5},{5,6},{6,7},{7,4},{8,9},{9,10},{10,1... | collective-permute-start | bytes 294920 | tf_op jit(solution)/shard_map/ppermute | solution.py:572
  82.1 1.9 %collective-permute-start.13 = (bf16[2,3,64,128]{3,2,1,0:T(8,128)(2,1)S(1)}, bf16[2,3,64,128]{3,2,1,0:T(8,128)(2,1)S(1)}, u32[]{:S(2)}, u32[]{:S(2)}) collective-permute-start(bf16[2,3,64,128]{3,2,1,0:T(8,128)(2,1)S(1)} %get-tuple-element.51), channel_id=1, source_target_pairs={{0,2},{1,3},{2,0},{3,1},{4,6},{5,7},{6,4},{7,5},{8,10},{9,11},{10,... | collective-permute-start | bytes 294920 | tf_op jit(solution)/shard_map/ppermute | solution.py:572
  84.1 0.0 collective-permute-done.15.refs_5_
  84.1 2.8 %collective-permute-start.14 = (bf16[2,3,64,128]{3,2,1,0:T(8,128)(2,1)S(1)}, bf16[2,3,64,128]{3,2,1,0:T(8,128)(2,1)S(1)}, u32[]{:S(2)}, u32[]{:S(2)}) collective-permute-start(bf16[2,3,64,128]{3,2,1,0:T(8,128)(2,1)S(1)} %get-tuple-element.52), channel_id=1, source_target_pairs={{0,3},{1,0},{2,1},{3,2},{4,7},{5,4},{6,5},{7,6},{8,11},{9,8},{10,9... | collective-permute-start | bytes 294920 | tf_op jit(solution)/shard_map/ppermute | solution.py:572
  86.9 0.0 collective-permute-done.16.refs_6_
  86.9 0.0 collective-permute-done.17.refs_7_
  86.9 1.3 %collective-permute-done.12.refs_1_ = bf16[2,3,64,128]{3,2,1,0:T(8,128)(2,1)S(1)} collective-permute-done((bf16[2,3,64,128]{3,2,1,0:T(8,128)(2,1)S(1)}, bf16[2,3,64,128]{3,2,1,0:T(8,128)(2,1)S(1)}, u32[]{:S(2)}, u32[]{:S(2)}) %collective-permute-start.12) | collective-permute-done | bytes 98336 | tf_op jit(solution)/shard_map/ppermute | solution.py:572
  88.2 3.7 %collective-permute-done.13.refs_2_ = bf16[2,3,64,128]{3,2,1,0:T(8,128)(2,1)S(1)} collective-permute-done((bf16[2,3,64,128]{3,2,1,0:T(8,128)(2,1)S(1)}, bf16[2,3,64,128]{3,2,1,0:T(8,128)(2,1)S(1)}, u32[]{:S(2)}, u32[]{:S(2)}) %collective-permute-start.13) | collective-permute-done | bytes 98336 | tf_op jit(solution)/shard_map/ppermute | solution.py:572
  91.9 0.0 collective-permute-done.14.refs_3_
  91.9 0.8 finish.1
  (12 shorter events, 0.1 us)
Async XLA Ops:
  1.1 13.9 %copy-start.5 = (bf16[2,3,64,128]{3,2,1,0:T(8,128)(2,1)}, bf16[2,3,64,128]{3,2,1,0:T(8,128)(2,1)S(1)}, u32[]{:S(2)}) copy-start(bf16[2,3,64,128]{3,2,1,0:T(8,128)(2,1)S(1)} %get-tuple-element.34.refs_0_) | copy-start | bytes 294916
  1.1 13.0 %collective-permute-start.3 = (bf16[2,3,64,128]{3,2,1,0:T(8,128)(2,1)S(1)}, bf16[2,3,64,128]{3,2,1,0:T(8,128)(2,1)S(1)}, u32[]{:S(2)}, u32[]{:S(2)}) collective-permute-start(bf16[2,3,64,128]{3,2,1,0:T(8,128)(2,1)S(1)} %get-tuple-element.34.refs_0_), channel_id=1, source_target_pairs={{0,3},{1,0},{2,1},{3,2},{4,7},{5,4},{6,5},{7,6},{8,11},{9,8},{10,9... | collective-permute-start | bytes 294920 | tf_op jit(solution)/shard_map/ppermute | solution.py:572
  6.2 8.7 %collective-permute-start.2 = (bf16[2,3,64,128]{3,2,1,0:T(8,128)(2,1)S(1)}, bf16[2,3,64,128]{3,2,1,0:T(8,128)(2,1)S(1)}, u32[]{:S(2)}, u32[]{:S(2)}) collective-permute-start(bf16[2,3,64,128]{3,2,1,0:T(8,128)(2,1)S(1)} %get-tuple-element.34.refs_0_), channel_id=1, source_target_pairs={{0,2},{1,3},{2,0},{3,1},{4,6},{5,7},{6,4},{7,5},{8,10},{9,11},{10,... | collective-permute-start | bytes 294920 | tf_op jit(solution)/shard_map/ppermute | solution.py:572
  6.2 8.7 %collective-permute-start.1 = (bf16[2,3,64,128]{3,2,1,0:T(8,128)(2,1)S(1)}, bf16[2,3,64,128]{3,2,1,0:T(8,128)(2,1)S(1)}, u32[]{:S(2)}, u32[]{:S(2)}) collective-permute-start(bf16[2,3,64,128]{3,2,1,0:T(8,128)(2,1)S(1)} %get-tuple-element.34.refs_0_), channel_id=1, source_target_pairs={{0,1},{1,2},{2,3},{3,0},{4,5},{5,6},{6,7},{7,4},{8,9},{9,10},{10,1... | collective-permute-start | bytes 294920 | tf_op jit(solution)/shard_map/ppermute | solution.py:572
  7.2 7.7 %collective-permute-start = (bf16[2,2,3,64,128]{4,3,2,1,0:T(8,128)(2,1)S(1)}, bf16[2,2,3,64,128]{4,3,2,1,0:T(8,128)(2,1)S(1)}, u32[]{:S(2)}, u32[]{:S(2)}) collective-permute-start(bf16[2,2,3,64,128]{4,3,2,1,0:T(8,128)(2,1)S(1)} %bitcast_bitcast_fusion), channel_id=1, source_target_pairs={{0,28},{4,0},{8,4},{12,8},{16,12},{20,16},{24,20},{28,24},{1,29},{... | collective-permute-start | bytes 589832 | tf_op jit(solution)/shard_map/ppermute | solution.py:572
  14.1 9.7 %copy-start.7 = (bf16[2,3,64,128]{3,2,1,0:T(8,128)(2,1)}, bf16[2,3,64,128]{3,2,1,0:T(8,128)(2,1)S(1)}, u32[]{:S(2)}) copy-start(bf16[2,3,64,128]{3,2,1,0:T(8,128)(2,1)S(1)} %collective-permute-done.3.refs_3_) | copy-start | bytes 294916
  14.9 8.8 %copy-start.8 = (bf16[2,3,64,128]{3,2,1,0:T(8,128)(2,1)}, bf16[2,3,64,128]{3,2,1,0:T(8,128)(2,1)S(1)}, u32[]{:S(2)}) copy-start(bf16[2,3,64,128]{3,2,1,0:T(8,128)(2,1)S(1)} %collective-permute-done.2.refs_2_) | copy-start | bytes 294916
  14.9 8.8 %copy-start.9 = (bf16[2,3,64,128]{3,2,1,0:T(8,128)(2,1)}, bf16[2,3,64,128]{3,2,1,0:T(8,128)(2,1)S(1)}, u32[]{:S(2)}) copy-start(bf16[2,3,64,128]{3,2,1,0:T(8,128)(2,1)S(1)} %collective-permute-done.1.refs_1_) | copy-start | bytes 294916
  14.9 33.9 %all-to-all-start = ((bf16[16,256,256]{2,1,0:T(8,128)(2,1)}), bf16[16,256,256]{2,1,0:T(8,128)(2,1)}, u32[]{:S(2)}, u32[]{:S(2)}) async-start(bf16[16,256,256]{2,1,0:T(8,128)(2,1)} %get-tuple-element.38), calls=%async_computation | async-start | bytes 4194304 | tf_op jit(solution)/shard_map/all_to_all | solution.py:599
  19.3 12.9 %copy-start.6 = (bf16[2,3,64,128]{3,2,1,0:T(8,128)(2,1)}, bf16[2,3,64,128]{3,2,1,0:T(8,128)(2,1)S(1)}, u32[]{:S(2)}) copy-start(bf16[2,3,64,128]{3,2,1,0:T(8,128)(2,1)S(1)} %get-tuple-element.57.refs_4_) | copy-start | bytes 294916
  19.3 7.4 %collective-permute-start.9 = (bf16[2,3,64,128]{3,2,1,0:T(8,128)(2,1)S(1)}, bf16[2,3,64,128]{3,2,1,0:T(8,128)(2,1)S(1)}, u32[]{:S(2)}, u32[]{:S(2)}) collective-permute-start(bf16[2,3,64,128]{3,2,1,0:T(8,128)(2,1)S(1)} %get-tuple-element.57.refs_4_), channel_id=1, source_target_pairs={{0,3},{1,0},{2,1},{3,2},{4,7},{5,4},{6,5},{7,6},{8,11},{9,8},{10,9... | collective-permute-start | bytes 294920 | tf_op jit(solution)/shard_map/ppermute | solution.py:572
  21.7 10.5 %collective-permute-start.8 = (bf16[2,3,64,128]{3,2,1,0:T(8,128)(2,1)S(1)}, bf16[2,3,64,128]{3,2,1,0:T(8,128)(2,1)S(1)}, u32[]{:S(2)}, u32[]{:S(2)}) collective-permute-start(bf16[2,3,64,128]{3,2,1,0:T(8,128)(2,1)S(1)} %get-tuple-element.57.refs_4_), channel_id=1, source_target_pairs={{0,2},{1,3},{2,0},{3,1},{4,6},{5,7},{6,4},{7,5},{8,10},{9,11},{10,... | collective-permute-start | bytes 294920 | tf_op jit(solution)/shard_map/ppermute | solution.py:572
  22.6 9.7 %collective-permute-start.7 = (bf16[2,3,64,128]{3,2,1,0:T(8,128)(2,1)S(1)}, bf16[2,3,64,128]{3,2,1,0:T(8,128)(2,1)S(1)}, u32[]{:S(2)}, u32[]{:S(2)}) collective-permute-start(bf16[2,3,64,128]{3,2,1,0:T(8,128)(2,1)S(1)} %get-tuple-element.57.refs_4_), channel_id=1, source_target_pairs={{0,1},{1,2},{2,3},{3,0},{4,5},{5,6},{6,7},{7,4},{8,9},{9,10},{10,1... | collective-permute-start | bytes 294920 | tf_op jit(solution)/shard_map/ppermute | solution.py:572
  23.8 19.1 %collective-permute-start.6 = (bf16[2,2,3,64,128]{4,3,2,1,0:T(8,128)(2,1)S(1)}, bf16[2,2,3,64,128]{4,3,2,1,0:T(8,128)(2,1)S(1)}, u32[]{:S(2)}, u32[]{:S(2)}) collective-permute-start(bf16[2,2,3,64,128]{4,3,2,1,0:T(8,128)(2,1)S(1)} %pad_maximum_fusion.refs_0_), channel_id=1, source_target_pairs={{0,3},{1,0},{2,1},{3,2},{4,7},{5,4},{6,5},{7,6},{8,11},{9,8},{10,9... | collective-permute-start | bytes 589832 | tf_op jit(solution)/shard_map/ppermute | solution.py:572
  26.5 22.3 %collective-permute-start.5 = (bf16[2,2,3,64,128]{4,3,2,1,0:T(8,128)(2,1)S(1)}, bf16[2,2,3,64,128]{4,3,2,1,0:T(8,128)(2,1)S(1)}, u32[]{:S(2)}, u32[]{:S(2)}) collective-permute-start(bf16[2,2,3,64,128]{4,3,2,1,0:T(8,128)(2,1)S(1)} %pad_maximum_fusion.refs_0_), channel_id=1, source_target_pairs={{0,2},{1,3},{2,0},{3,1},{4,6},{5,7},{6,4},{7,5},{8,10},{9,11},{10,... | collective-permute-start | bytes 589832 | tf_op jit(solution)/shard_map/ppermute | solution.py:572
  26.8 5.5 %copy-start.10 = (bf16[2,3,64,128]{3,2,1,0:T(8,128)(2,1)}, bf16[2,3,64,128]{3,2,1,0:T(8,128)(2,1)S(1)}, u32[]{:S(2)}) copy-start(bf16[2,3,64,128]{3,2,1,0:T(8,128)(2,1)S(1)} %collective-permute-done.9.refs_7_) | copy-start | bytes 294916
  26.8 22.0 %collective-permute-start.4 = (bf16[2,2,3,64,128]{4,3,2,1,0:T(8,128)(2,1)S(1)}, bf16[2,2,3,64,128]{4,3,2,1,0:T(8,128)(2,1)S(1)}, u32[]{:S(2)}, u32[]{:S(2)}) collective-permute-start(bf16[2,2,3,64,128]{4,3,2,1,0:T(8,128)(2,1)S(1)} %pad_maximum_fusion.refs_0_), channel_id=1, source_target_pairs={{0,1},{1,2},{2,3},{3,0},{4,5},{5,6},{6,7},{7,4},{8,9},{9,10},{10,1... | collective-permute-start | bytes 589832 | tf_op jit(solution)/shard_map/ppermute | solution.py:572
  32.3 0.6 copy-start.11
  32.3 0.7 copy-start.12
  33.0 15.9 %copy-start.1 = (bf16[4,256,256]{2,1,0:T(8,128)(2,1)S(1)}, bf16[4,256,256]{2,1,0:T(8,128)(2,1)}, u32[]{:S(2)}) copy-start(bf16[4,256,256]{2,1,0:T(8,128)(2,1)} %constant.38.refs_10_.refs_6_.tabs_hbm) | copy-start | bytes 1572868
  33.0 15.9 %copy-start.4 = (s32[72]{0:T(128)S(1)}, s32[72]{0:T(128)}, u32[]{:S(2)}) copy-start(s32[72]{0:T(128)} %get-tuple-element.31.meta_ref) | copy-start | bytes 868
  42.8 19.3 %copy-start = (f32[256,512]{1,0:T(8,128)S(1)}, f32[256,512]{1,0:T(8,128)}, u32[]{:S(2)}) copy-start(f32[256,512]{1,0:T(8,128)} %probe_hbm.1) | copy-start | bytes 1572868
  42.8 19.3 %copy-start.2 = (f32[2,256,256]{2,1,0:T(8,128)S(1)}, f32[2,256,256]{2,1,0:T(8,128)}, u32[]{:S(2)}) copy-start(f32[2,256,256]{2,1,0:T(8,128)} %constant.27.clone.refs_9_.kernel_hbm) | copy-start | bytes 1572868
  62.0 8.2 %collective-permute-start.10 = (bf16[2,3,256,128]{3,2,1,0:T(8,128)(2,1)S(1)}, bf16[2,3,256,128]{3,2,1,0:T(8,128)(2,1)S(1)}, u32[]{:S(2)}, u32[]{:S(2)}) collective-permute-start(bf16[2,3,256,128]{3,2,1,0:T(8,128)(2,1)S(1)} %get-tuple-element.43), channel_id=1, source_target_pairs={{0,4},{4,8},{8,12},{12,16},{16,20},{20,24},{24,28},{28,0},{1,5},{5... | collective-permute-start | bytes 1179656 | tf_op jit(solution)/shard_map/ppermute | solution.py:572
  62.1 8.1 %copy-start.3 = (s32[3]{0:T(128)S(1)}, s32[3]{0:T(128)}, u32[]{:S(2)}) copy-start(s32[3]{0:T(128)} %pad_add_fusion.here_ref) | copy-start | bytes 40
  70.8 9.2 %collective-permute-start.11 = (bf16[2,3,256,128]{3,2,1,0:T(8,128)(2,1)S(1)}, bf16[2,3,256,128]{3,2,1,0:T(8,128)(2,1)S(1)}, u32[]{:S(2)}, u32[]{:S(2)}) collective-permute-start(bf16[2,3,256,128]{3,2,1,0:T(8,128)(2,1)S(1)} %get-tuple-element.48), channel_id=1, source_target_pairs={{0,4},{4,8},{8,12},{12,16},{16,20},{20,24},{24,28},{28,0},{1,5},{5... | collective-permute-start | bytes 1179656 | tf_op jit(solution)/shard_map/ppermute | solution.py:572
  72.6 11.4 %collective-permute-start.15 = (bf16[2,3,64,128]{3,2,1,0:T(8,128)(2,1)S(1)}, bf16[2,3,64,128]{3,2,1,0:T(8,128)(2,1)S(1)}, u32[]{:S(2)}, u32[]{:S(2)}) collective-permute-start(bf16[2,3,64,128]{3,2,1,0:T(8,128)(2,1)S(1)} %get-tuple-element.54), channel_id=1, source_target_pairs={{0,1},{1,2},{2,3},{3,0},{4,5},{5,6},{6,7},{7,4},{8,9},{9,10},{10,1... | collective-permute-start | bytes 294920 | tf_op jit(solution)/shard_map/ppermute | solution.py:572
  73.4 13.5 %collective-permute-start.16 = (bf16[2,3,64,128]{3,2,1,0:T(8,128)(2,1)S(1)}, bf16[2,3,64,128]{3,2,1,0:T(8,128)(2,1)S(1)}, u32[]{:S(2)}, u32[]{:S(2)}) collective-permute-start(bf16[2,3,64,128]{3,2,1,0:T(8,128)(2,1)S(1)} %get-tuple-element.55), channel_id=1, source_target_pairs={{0,2},{1,3},{2,0},{3,1},{4,6},{5,7},{6,4},{7,5},{8,10},{9,11},{10,... | collective-permute-start | bytes 294920 | tf_op jit(solution)/shard_map/ppermute | solution.py:572
  77.1 9.8 %collective-permute-start.17 = (bf16[2,3,64,128]{3,2,1,0:T(8,128)(2,1)S(1)}, bf16[2,3,64,128]{3,2,1,0:T(8,128)(2,1)S(1)}, u32[]{:S(2)}, u32[]{:S(2)}) collective-permute-start(bf16[2,3,64,128]{3,2,1,0:T(8,128)(2,1)S(1)} %get-tuple-element.56), channel_id=1, source_target_pairs={{0,3},{1,0},{2,1},{3,2},{4,7},{5,4},{6,5},{7,6},{8,11},{9,8},{10,9... | collective-permute-start | bytes 294920 | tf_op jit(solution)/shard_map/ppermute | solution.py:572
  80.7 7.5 %collective-permute-start.12 = (bf16[2,3,64,128]{3,2,1,0:T(8,128)(2,1)S(1)}, bf16[2,3,64,128]{3,2,1,0:T(8,128)(2,1)S(1)}, u32[]{:S(2)}, u32[]{:S(2)}) collective-permute-start(bf16[2,3,64,128]{3,2,1,0:T(8,128)(2,1)S(1)} %get-tuple-element.50), channel_id=1, source_target_pairs={{0,1},{1,2},{2,3},{3,0},{4,5},{5,6},{6,7},{7,4},{8,9},{9,10},{10,1... | collective-permute-start | bytes 294920 | tf_op jit(solution)/shard_map/ppermute | solution.py:572
  82.1 9.7 %collective-permute-start.13 = (bf16[2,3,64,128]{3,2,1,0:T(8,128)(2,1)S(1)}, bf16[2,3,64,128]{3,2,1,0:T(8,128)(2,1)S(1)}, u32[]{:S(2)}, u32[]{:S(2)}) collective-permute-start(bf16[2,3,64,128]{3,2,1,0:T(8,128)(2,1)S(1)} %get-tuple-element.51), channel_id=1, source_target_pairs={{0,2},{1,3},{2,0},{3,1},{4,6},{5,7},{6,4},{7,5},{8,10},{9,11},{10,... | collective-permute-start | bytes 294920 | tf_op jit(solution)/shard_map/ppermute | solution.py:572
  84.1 7.8 %collective-permute-start.14 = (bf16[2,3,64,128]{3,2,1,0:T(8,128)(2,1)S(1)}, bf16[2,3,64,128]{3,2,1,0:T(8,128)(2,1)S(1)}, u32[]{:S(2)}, u32[]{:S(2)}) collective-permute-start(bf16[2,3,64,128]{3,2,1,0:T(8,128)(2,1)S(1)} %get-tuple-element.52), channel_id=1, source_target_pairs={{0,3},{1,0},{2,1},{3,2},{4,7},{5,4},{6,5},{7,6},{8,11},{9,8},{10,9... | collective-permute-start | bytes 294920 | tf_op jit(solution)/shard_map/ppermute | solution.py:572

commit v7 on v6

--- a/solution.py
+++ b/solution.py
@@ -71,17 +71,19 @@
     )
 
 
-def forward(items, tabs):
+def forward(items, tabs, narrow=False):
     a_even, t_even, a_odd, t_odd = tabs
     h = a_even.shape[0] // 2
     even = row_dot([x[0] for x in items], a_even)
     odd = row_dot([x[1] for x in items], a_odd)
+    if narrow:
+        even, odd = [x.astype(bf16) for x in even], [x.astype(bf16) for x in odd]
     plus = [quads(a[:h] + a[h:], b[:h] + b[h:], h).astype(bf16) for a, b in zip(even, odd)]
     minus = [quads(a[:h] - a[h:], b[:h] - b[h:], h).astype(bf16) for a, b in zip(even, odd)]
     return list(zip([dot(t_even, x) for x in plus], [dot(t_odd, x) for x in minus]))
 
 
-def inverse(items, tabs):
+def inverse(items, tabs, narrow=False):
     a_even, t_even, a_odd, t_odd = tabs
     h = a_even.shape[0] // 2
 
@@ -93,6 +95,8 @@
 
     even = row_dot([side(x, 0) for x in items], t_even)
     odd = row_dot([side(x, 1) for x in items], t_odd)
+    if narrow:
+        even, odd = [x.astype(bf16) for x in even], [x.astype(bf16) for x in odd]
     plus = [a + b for a, b in zip(even, odd)]
     minus = [a - b for a, b in zip(even, odd)]
     low = [dot(a_even, quads(a[:h], b[:h], h).astype(bf16)) for a, b in zip(plus, minus)]
@@ -346,8 +350,8 @@
         for at in items:
             w = window(rows_ref, meta_ref[K + at], meta_ref[2 * K + at], extent)
             fields.append(folded(tuple(product(p, cut(q)) for p, q in zip(probe, w))))
-        spread = [by_kernel(x, kernel_ref, False) for x in forward(fields, tables)]
-        for i, wave in enumerate(inverse(spread, tables)):
+        spread = [by_kernel(x, kernel_ref, False) for x in forward(fields, tables, True)]
+        for i, wave in enumerate(inverse(spread, tables, True)):
             wave_buf[slot, i, 0] = wave[0].astype(bf16)
             wave_buf[slot, i, 1] = wave[1].astype(bf16)
 
@@ -385,7 +389,7 @@
             w = window(rows_ref, meta_ref[K + at], meta_ref[2 * K + at], extent)
             fields.append(folded(tuple(product(cut(p), cut(q)) for p, q in zip(wave_of(i), w))))
         far_grads = []
-        for i, far in enumerate(forward(fields, tables)):
+        for i, far in enumerate(forward(fields, tables, True)):
             parts = []
             for k, part in enumerate(far):
                 re, im = part[:h], part[h:]
@@ -393,7 +397,7 @@
                 misfit = re * re + im * im - image
                 parts.append(jnp.concatenate([re * misfit, im * misfit], 0).astype(bf16))
             far_grads.append(parts)
-        for i, (at, grad) in enumerate(zip(items, inverse(far_grads, tables))):
+        for i, (at, grad) in enumerate(zip(items, inverse(far_grads, tables, True))):
             grad = halves(grad)
             top, col = meta_ref[K + at], meta_ref[2 * K + at]
             target = meta_ref[3 * K + at]

time: 93.6 us -> 93.1 us (level)
  transfers between devices with their start and end apart: 19 -> 19, of which waited for: 6 -> 5; matrix products, arithmetic and copies ran while one was open for 1% -> 1% of each run, Pallas kernels for 26% -> 25%
where the time goes in v7:
time: 93.1 us; the launch traced here: 92.4 us
  Pallas kernels  38 us (41%)
  starting transfers between devices  34.7 us (37%)
  waiting for transfers between devices  17.1 us (18%)
  other arithmetic  1.6 us (2%)
    pallas_call x7, Pallas kernels, call(): pl.pallas_call(kernel, in_specs=in_specs, out_specs=out_specs, out_shape=...  38 us
    ppermute x18, starting transfers between devices, passed_along(): return lax.ppermute(value, axis, pairs)  30.3 us
    ppermute x18, waiting for transfers between devices, passed_along(): return lax.ppermute(value, axis, pairs)  17.1 us
    all_to_all x1, starting transfers between devices, shards(): lax.all_to_all(packed, 'tile', split_axis=0, concat_axis=0, tiled=True)  4.36 us
  transfers between devices with their start and end apart: 19, of which 5 were waited for; matrix products, arithmetic and copies ran while one was open for 1% of the time, Pallas kernels for 25%

profile of v7, /device:TPU:0, one launch (start us, length us, event | category | flops | bytes accessed | tf_op | source)
XLA Modules:
  0.0 92.4 jit_solution(12182369314002577969)
XLA Ops:
  0.0 1.0 %bitcast_bitcast_fusion = bf16[2,2,3,64,128]{4,3,2,1,0:T(8,128)(2,1)S(1)} fusion(f32[2,2,64,384]{3,2,1,0:T(8,128)} %param.13), kind=kLoop, calls=%fused_computation | loop fusion | flops 98304 | bytes 589824 | tf_op jit(solution)/shard_map/convert_element_type | solution.py:591
  1.1 0.0 copy-start.5
  1.1 5.1 %collective-permute-start.3 = (bf16[2,3,64,128]{3,2,1,0:T(8,128)(2,1)S(1)}, bf16[2,3,64,128]{3,2,1,0:T(8,128)(2,1)S(1)}, u32[]{:S(2)}, u32[]{:S(2)}) collective-permute-start(bf16[2,3,64,128]{3,2,1,0:T(8,128)(2,1)S(1)} %get-tuple-element.34.refs_0_), channel_id=1, source_target_pairs={{0,3},{1,0},{2,1},{3,2},{4,7},{5,4},{6,5},{7,6},{8,11},{9,8},{10,9... | collective-permute-start | bytes 294920 | tf_op jit(solution)/shard_map/ppermute | solution.py:576
  6.2 0.0 collective-permute-start.2
  6.2 1.0 %collective-permute-start.1 = (bf16[2,3,64,128]{3,2,1,0:T(8,128)(2,1)S(1)}, bf16[2,3,64,128]{3,2,1,0:T(8,128)(2,1)S(1)}, u32[]{:S(2)}, u32[]{:S(2)}) collective-permute-start(bf16[2,3,64,128]{3,2,1,0:T(8,128)(2,1)S(1)} %get-tuple-element.34.refs_0_), channel_id=1, source_target_pairs={{0,1},{1,2},{2,3},{3,0},{4,5},{5,6},{6,7},{7,4},{8,9},{9,10},{10,1... | collective-permute-start | bytes 294920 | tf_op jit(solution)/shard_map/ppermute | solution.py:576
  7.2 1.0 %collective-permute-start = (bf16[2,2,3,64,128]{4,3,2,1,0:T(8,128)(2,1)S(1)}, bf16[2,2,3,64,128]{4,3,2,1,0:T(8,128)(2,1)S(1)}, u32[]{:S(2)}, u32[]{:S(2)}) collective-permute-start(bf16[2,2,3,64,128]{4,3,2,1,0:T(8,128)(2,1)S(1)} %bitcast_bitcast_fusion), channel_id=1, source_target_pairs={{0,28},{4,0},{8,4},{12,8},{16,12},{20,16},{24,20},{28,24},{1,29},{... | collective-permute-start | bytes 589832 | tf_op jit(solution)/shard_map/ppermute | solution.py:576
  8.2 0.6 pad_add_fusion.here_ref
  8.8 5.2 %route.1 = (bf16[16,256,256]{2,1,0:T(8,128)(2,1)}, s32[72]{0:T(128)}) custom-call(s32[3]{0:T(128)} %pad_add_fusion.here_ref, s32[448]{0:T(512)} %owner_hbm.1, s32[448]{0:T(512)} %row_hbm.1, s32[448]{0:T(512)} %col_hbm.1, bf16[14,256,256]{2,1,0:T(8,128)(2,1)} %images_hbm.1, bf16[2,256,256]{2,1,0:T(8,128)(2,1)} %constant.33.permute_hbm), custom_call_target="tpu_custom_call" | custom-call | flops 1073741824 | tf_op jit(solution)/shard_map/route/pallas_call | solution.py:457
  14.0 0.0 collective-permute-done.3.refs_3_
  14.0 0.0 copy-start.7
  14.1 0.9 collective-permute-done.2.refs_2_
  14.9 0.0 collective-permute-done.1.refs_1_
  14.9 0.0 collective-permute-done
  14.9 0.0 copy-done.5
  14.9 4.4 %all-to-all-start = ((bf16[16,256,256]{2,1,0:T(8,128)(2,1)}), bf16[16,256,256]{2,1,0:T(8,128)(2,1)}, u32[]{:S(2)}, u32[]{:S(2)}) async-start(bf16[16,256,256]{2,1,0:T(8,128)(2,1)} %get-tuple-element.38), calls=%async_computation | async-start | bytes 4194304 | tf_op jit(solution)/shard_map/all_to_all | solution.py:603
  19.3 0.0 copy-start.6
  19.3 2.4 %collective-permute-start.9 = (bf16[2,3,64,128]{3,2,1,0:T(8,128)(2,1)S(1)}, bf16[2,3,64,128]{3,2,1,0:T(8,128)(2,1)S(1)}, u32[]{:S(2)}, u32[]{:S(2)}) collective-permute-start(bf16[2,3,64,128]{3,2,1,0:T(8,128)(2,1)S(1)} %get-tuple-element.57.refs_4_), channel_id=1, source_target_pairs={{0,3},{1,0},{2,1},{3,2},{4,7},{5,4},{6,5},{7,6},{8,11},{9,8},{10,9... | collective-permute-start | bytes 294920 | tf_op jit(solution)/shard_map/ppermute | solution.py:576
  21.7 0.8 collective-permute-start.8
  22.6 1.2 %collective-permute-start.7 = (bf16[2,3,64,128]{3,2,1,0:T(8,128)(2,1)S(1)}, bf16[2,3,64,128]{3,2,1,0:T(8,128)(2,1)S(1)}, u32[]{:S(2)}, u32[]{:S(2)}) collective-permute-start(bf16[2,3,64,128]{3,2,1,0:T(8,128)(2,1)S(1)} %get-tuple-element.57.refs_4_), channel_id=1, source_target_pairs={{0,1},{1,2},{2,3},{3,0},{4,5},{5,6},{6,7},{7,4},{8,9},{9,10},{10,1... | collective-permute-start | bytes 294920 | tf_op jit(solution)/shard_map/ppermute | solution.py:576
  23.7 0.0 copy-done.7
  23.7 0.0 copy-done.8
  23.7 0.0 copy-done.9
  23.8 2.7 %collective-permute-start.6 = (bf16[2,2,3,64,128]{4,3,2,1,0:T(8,128)(2,1)S(1)}, bf16[2,2,3,64,128]{4,3,2,1,0:T(8,128)(2,1)S(1)}, u32[]{:S(2)}, u32[]{:S(2)}) collective-permute-start(bf16[2,2,3,64,128]{4,3,2,1,0:T(8,128)(2,1)S(1)} %pad_maximum_fusion.refs_0_), channel_id=1, source_target_pairs={{0,3},{1,0},{2,1},{3,2},{4,7},{5,4},{6,5},{7,6},{8,11},{9,8},{10,9... | collective-permute-start | bytes 589832 | tf_op jit(solution)/shard_map/ppermute | solution.py:576
  26.5 0.3 collective-permute-start.5
  26.8 0.0 collective-permute-done.9.refs_7_
  26.8 0.4 collective-permute-start.4
  27.1 5.1 %collective-permute-done.8.refs_6_ = bf16[2,3,64,128]{3,2,1,0:T(8,128)(2,1)S(1)} collective-permute-done((bf16[2,3,64,128]{3,2,1,0:T(8,128)(2,1)S(1)}, bf16[2,3,64,128]{3,2,1,0:T(8,128)(2,1)S(1)}, u32[]{:S(2)}, u32[]{:S(2)}) %collective-permute-start.8) | collective-permute-done | bytes 98336 | tf_op jit(solution)/shard_map/ppermute | solution.py:576
  32.3 0.0 collective-permute-done.7.refs_5_
  32.3 0.0 copy-done.6
  32.3 0.0 copy-done.10
  32.3 0.6 copy-done.11
  32.9 0.0 copy-done.12
  33.0 9.7 %waves.1.refs_4_ = bf16[4,4,2,256,256]{4,3,2,1,0:T(8,128)(2,1)} custom-call(s32[72]{0:T(128)} %get-tuple-element.31.meta_ref, bf16[2,3,64,128]{3,2,1,0:T(8,128)(2,1)} %copy-done.5, bf16[2,3,64,128]{3,2,1,0:T(8,128)(2,1)} %copy-done.9, bf16[2,3,64,128]{3,2,1,0:T(8,128)(2,1)} %copy-done.8, bf16[2,3,64,128]{3,2,1,0:T(8,128)(2,1)} %copy-done.7, ...), custom_call_target="tpu_custom_call" | custom-call | flops 8589934592 | tf_op jit(solution)/shard_map/waves/pallas_call | solution.py:457
  42.6 0.0 copy-start
  42.7 0.0 copy-start.2
  42.7 0.0 collective-permute-done.6.refs_3_
  42.7 6.1 %collective-permute-done.5.refs_2_ = bf16[2,2,3,64,128]{4,3,2,1,0:T(8,128)(2,1)S(1)} collective-permute-done((bf16[2,2,3,64,128]{4,3,2,1,0:T(8,128)(2,1)S(1)}, bf16[2,2,3,64,128]{4,3,2,1,0:T(8,128)(2,1)S(1)}, u32[]{:S(2)}, u32[]{:S(2)}) %collective-permute-start.5) | collective-permute-done | bytes 196640 | tf_op jit(solution)/shard_map/ppermute | solution.py:576
  48.8 0.0 collective-permute-done.4.refs_1_
  48.8 0.0 all-to-all-done.refs_5_
  48.8 0.0 copy-done.1
  48.8 0.0 copy-done.4
  48.8 13.0 %misfits.1 = (bf16[16,2,256,256]{3,2,1,0:T(8,128)(2,1)S(1)}, f32[2,3,768,128]{3,2,1,0:T(8,128)S(1)}, bf16[2,3,256,128]{3,2,1,0:T(8,128)(2,1)S(1)}) custom-call(s32[72]{0:T(128)S(1)} %copy-done.4, bf16[2,2,3,64,128]{4,3,2,1,0:T(8,128)(2,1)S(1)} %pad_maximum_fusion.refs_0_, bf16[2,2,3,64,128]{4,3,2,1,0:T(8,128)(2,1)S(1)} %collective-permute-done.4.refs_1_, ...), custom_call_target="tpu_custom_call" | custom-call | flops 8589934592 | tf_op jit(solution)/shard_map/misfits/pallas_call | solution.py:457
  61.8 0.1 collective-permute-start.10
  61.9 0.0 copy-done
  61.9 8.0 %exits.1 = (f32[2,3,768,128]{3,2,1,0:T(8,128)S(1)}, bf16[2,3,256,128]{3,2,1,0:T(8,128)(2,1)S(1)}) custom-call(s32[72]{0:T(128)S(1)} %copy-done.4, bf16[16,2,256,256]{3,2,1,0:T(8,128)(2,1)S(1)} %get-tuple-element.39.fields_ref, f32[256,512]{1,0:T(8,128)S(1)} %copy-done, f32[2,256,256]{2,1,0:T(8,128)S(1)} %copy-done.2, bf16[4,256,256]{2,1,0:T(8,128)(2,1)S(1)} %copy-done.1), custom_call_target="tpu_custom_call" | custom-call | flops 429496736 | tf_op jit(solution)/shard_map/exits/pallas_call | solution.py:457
  69.9 0.0 collective-permute-done.10.moved_ref
  70.0 0.0 copy-done.3
  70.0 0.6 combine.2
  70.6 1.7 %collective-permute-start.11 = (bf16[2,3,256,128]{3,2,1,0:T(8,128)(2,1)S(1)}, bf16[2,3,256,128]{3,2,1,0:T(8,128)(2,1)S(1)}, u32[]{:S(2)}, u32[]{:S(2)}) collective-permute-start(bf16[2,3,256,128]{3,2,1,0:T(8,128)(2,1)S(1)} %get-tuple-element.48), channel_id=1, source_target_pairs={{0,4},{4,8},{8,12},{12,16},{16,20},{20,24},{24,28},{28,0},{1,5},{5... | collective-permute-start | bytes 1179656 | tf_op jit(solution)/shard_map/ppermute | solution.py:576
  72.3 0.8 collective-permute-start.15
  73.1 3.5 %collective-permute-start.16 = (bf16[2,3,64,128]{3,2,1,0:T(8,128)(2,1)S(1)}, bf16[2,3,64,128]{3,2,1,0:T(8,128)(2,1)S(1)}, u32[]{:S(2)}, u32[]{:S(2)}) collective-permute-start(bf16[2,3,64,128]{3,2,1,0:T(8,128)(2,1)S(1)} %get-tuple-element.55), channel_id=1, source_target_pairs={{0,2},{1,3},{2,0},{3,1},{4,6},{5,7},{6,4},{7,5},{8,10},{9,11},{10,... | collective-permute-start | bytes 294920 | tf_op jit(solution)/shard_map/ppermute | solution.py:576
  76.7 2.9 %collective-permute-start.17 = (bf16[2,3,64,128]{3,2,1,0:T(8,128)(2,1)S(1)}, bf16[2,3,64,128]{3,2,1,0:T(8,128)(2,1)S(1)}, u32[]{:S(2)}, u32[]{:S(2)}) collective-permute-start(bf16[2,3,64,128]{3,2,1,0:T(8,128)(2,1)S(1)} %get-tuple-element.56), channel_id=1, source_target_pairs={{0,3},{1,0},{2,1},{3,2},{4,7},{5,4},{6,5},{7,6},{8,11},{9,8},{10,9... | collective-permute-start | bytes 294920 | tf_op jit(solution)/shard_map/ppermute | solution.py:576
  79.6 0.0 collective-permute-done.11.moved_ref
  79.6 0.6 combine.3
  80.2 1.6 %collective-permute-start.12 = (bf16[2,3,64,128]{3,2,1,0:T(8,128)(2,1)S(1)}, bf16[2,3,64,128]{3,2,1,0:T(8,128)(2,1)S(1)}, u32[]{:S(2)}, u32[]{:S(2)}) collective-permute-start(bf16[2,3,64,128]{3,2,1,0:T(8,128)(2,1)S(1)} %get-tuple-element.50), channel_id=1, source_target_pairs={{0,1},{1,2},{2,3},{3,0},{4,5},{5,6},{6,7},{7,4},{8,9},{9,10},{10,1... | collective-permute-start | bytes 294920 | tf_op jit(solution)/shard_map/ppermute | solution.py:576
  81.8 1.9 %collective-permute-start.13 = (bf16[2,3,64,128]{3,2,1,0:T(8,128)(2,1)S(1)}, bf16[2,3,64,128]{3,2,1,0:T(8,128)(2,1)S(1)}, u32[]{:S(2)}, u32[]{:S(2)}) collective-permute-start(bf16[2,3,64,128]{3,2,1,0:T(8,128)(2,1)S(1)} %get-tuple-element.51), channel_id=1, source_target_pairs={{0,2},{1,3},{2,0},{3,1},{4,6},{5,7},{6,4},{7,5},{8,10},{9,11},{10,... | collective-permute-start | bytes 294920 | tf_op jit(solution)/shard_map/ppermute | solution.py:576
  83.8 0.0 collective-permute-done.15.refs_5_
  83.8 2.8 %collective-permute-start.14 = (bf16[2,3,64,128]{3,2,1,0:T(8,128)(2,1)S(1)}, bf16[2,3,64,128]{3,2,1,0:T(8,128)(2,1)S(1)}, u32[]{:S(2)}, u32[]{:S(2)}) collective-permute-start(bf16[2,3,64,128]{3,2,1,0:T(8,128)(2,1)S(1)} %get-tuple-element.52), channel_id=1, source_target_pairs={{0,3},{1,0},{2,1},{3,2},{4,7},{5,4},{6,5},{7,6},{8,11},{9,8},{10,9... | collective-permute-start | bytes 294920 | tf_op jit(solution)/shard_map/ppermute | solution.py:576
  86.6 0.0 collective-permute-done.16.refs_6_
  86.6 0.0 collective-permute-done.17.refs_7_
  86.6 1.1 %collective-permute-done.12.refs_1_ = bf16[2,3,64,128]{3,2,1,0:T(8,128)(2,1)S(1)} collective-permute-done((bf16[2,3,64,128]{3,2,1,0:T(8,128)(2,1)S(1)}, bf16[2,3,64,128]{3,2,1,0:T(8,128)(2,1)S(1)}, u32[]{:S(2)}, u32[]{:S(2)}) %collective-permute-start.12) | collective-permute-done | bytes 98336 | tf_op jit(solution)/shard_map/ppermute | solution.py:576
  87.7 3.8 %collective-permute-done.13.refs_2_ = bf16[2,3,64,128]{3,2,1,0:T(8,128)(2,1)S(1)} collective-permute-done((bf16[2,3,64,128]{3,2,1,0:T(8,128)(2,1)S(1)}, bf16[2,3,64,128]{3,2,1,0:T(8,128)(2,1)S(1)}, u32[]{:S(2)}, u32[]{:S(2)}) %collective-permute-start.13) | collective-permute-done | bytes 98336 | tf_op jit(solution)/shard_map/ppermute | solution.py:576
  91.5 0.0 collective-permute-done.14.refs_3_
  91.5 0.8 finish.1
  (12 shorter events, 0.1 us)
Async XLA Ops:
  1.1 13.9 %copy-start.5 = (bf16[2,3,64,128]{3,2,1,0:T(8,128)(2,1)}, bf16[2,3,64,128]{3,2,1,0:T(8,128)(2,1)S(1)}, u32[]{:S(2)}) copy-start(bf16[2,3,64,128]{3,2,1,0:T(8,128)(2,1)S(1)} %get-tuple-element.34.refs_0_) | copy-start | bytes 294916
  1.1 13.0 %collective-permute-start.3 = (bf16[2,3,64,128]{3,2,1,0:T(8,128)(2,1)S(1)}, bf16[2,3,64,128]{3,2,1,0:T(8,128)(2,1)S(1)}, u32[]{:S(2)}, u32[]{:S(2)}) collective-permute-start(bf16[2,3,64,128]{3,2,1,0:T(8,128)(2,1)S(1)} %get-tuple-element.34.refs_0_), channel_id=1, source_target_pairs={{0,3},{1,0},{2,1},{3,2},{4,7},{5,4},{6,5},{7,6},{8,11},{9,8},{10,9... | collective-permute-start | bytes 294920 | tf_op jit(solution)/shard_map/ppermute | solution.py:576
  6.2 8.7 %collective-permute-start.2 = (bf16[2,3,64,128]{3,2,1,0:T(8,128)(2,1)S(1)}, bf16[2,3,64,128]{3,2,1,0:T(8,128)(2,1)S(1)}, u32[]{:S(2)}, u32[]{:S(2)}) collective-permute-start(bf16[2,3,64,128]{3,2,1,0:T(8,128)(2,1)S(1)} %get-tuple-element.34.refs_0_), channel_id=1, source_target_pairs={{0,2},{1,3},{2,0},{3,1},{4,6},{5,7},{6,4},{7,5},{8,10},{9,11},{10,... | collective-permute-start | bytes 294920 | tf_op jit(solution)/shard_map/ppermute | solution.py:576
  6.2 8.7 %collective-permute-start.1 = (bf16[2,3,64,128]{3,2,1,0:T(8,128)(2,1)S(1)}, bf16[2,3,64,128]{3,2,1,0:T(8,128)(2,1)S(1)}, u32[]{:S(2)}, u32[]{:S(2)}) collective-permute-start(bf16[2,3,64,128]{3,2,1,0:T(8,128)(2,1)S(1)} %get-tuple-element.34.refs_0_), channel_id=1, source_target_pairs={{0,1},{1,2},{2,3},{3,0},{4,5},{5,6},{6,7},{7,4},{8,9},{9,10},{10,1... | collective-permute-start | bytes 294920 | tf_op jit(solution)/shard_map/ppermute | solution.py:576
  7.2 7.7 %collective-permute-start = (bf16[2,2,3,64,128]{4,3,2,1,0:T(8,128)(2,1)S(1)}, bf16[2,2,3,64,128]{4,3,2,1,0:T(8,128)(2,1)S(1)}, u32[]{:S(2)}, u32[]{:S(2)}) collective-permute-start(bf16[2,2,3,64,128]{4,3,2,1,0:T(8,128)(2,1)S(1)} %bitcast_bitcast_fusion), channel_id=1, source_target_pairs={{0,28},{4,0},{8,4},{12,8},{16,12},{20,16},{24,20},{28,24},{1,29},{... | collective-permute-start | bytes 589832 | tf_op jit(solution)/shard_map/ppermute | solution.py:576
  14.0 9.7 %copy-start.7 = (bf16[2,3,64,128]{3,2,1,0:T(8,128)(2,1)}, bf16[2,3,64,128]{3,2,1,0:T(8,128)(2,1)S(1)}, u32[]{:S(2)}) copy-start(bf16[2,3,64,128]{3,2,1,0:T(8,128)(2,1)S(1)} %collective-permute-done.3.refs_3_) | copy-start | bytes 294916
  14.9 8.8 %copy-start.8 = (bf16[2,3,64,128]{3,2,1,0:T(8,128)(2,1)}, bf16[2,3,64,128]{3,2,1,0:T(8,128)(2,1)S(1)}, u32[]{:S(2)}) copy-start(bf16[2,3,64,128]{3,2,1,0:T(8,128)(2,1)S(1)} %collective-permute-done.2.refs_2_) | copy-start | bytes 294916
  14.9 8.8 %copy-start.9 = (bf16[2,3,64,128]{3,2,1,0:T(8,128)(2,1)}, bf16[2,3,64,128]{3,2,1,0:T(8,128)(2,1)S(1)}, u32[]{:S(2)}) copy-start(bf16[2,3,64,128]{3,2,1,0:T(8,128)(2,1)S(1)} %collective-permute-done.1.refs_1_) | copy-start | bytes 294916
  14.9 33.9 %all-to-all-start = ((bf16[16,256,256]{2,1,0:T(8,128)(2,1)}), bf16[16,256,256]{2,1,0:T(8,128)(2,1)}, u32[]{:S(2)}, u32[]{:S(2)}) async-start(bf16[16,256,256]{2,1,0:T(8,128)(2,1)} %get-tuple-element.38), calls=%async_computation | async-start | bytes 4194304 | tf_op jit(solution)/shard_map/all_to_all | solution.py:603
  19.3 12.9 %copy-start.6 = (bf16[2,3,64,128]{3,2,1,0:T(8,128)(2,1)}, bf16[2,3,64,128]{3,2,1,0:T(8,128)(2,1)S(1)}, u32[]{:S(2)}) copy-start(bf16[2,3,64,128]{3,2,1,0:T(8,128)(2,1)S(1)} %get-tuple-element.57.refs_4_) | copy-start | bytes 294916
  19.3 7.4 %collective-permute-start.9 = (bf16[2,3,64,128]{3,2,1,0:T(8,128)(2,1)S(1)}, bf16[2,3,64,128]{3,2,1,0:T(8,128)(2,1)S(1)}, u32[]{:S(2)}, u32[]{:S(2)}) collective-permute-start(bf16[2,3,64,128]{3,2,1,0:T(8,128)(2,1)S(1)} %get-tuple-element.57.refs_4_), channel_id=1, source_target_pairs={{0,3},{1,0},{2,1},{3,2},{4,7},{5,4},{6,5},{7,6},{8,11},{9,8},{10,9... | collective-permute-start | bytes 294920 | tf_op jit(solution)/shard_map/ppermute | solution.py:576
  21.7 10.5 %collective-permute-start.8 = (bf16[2,3,64,128]{3,2,1,0:T(8,128)(2,1)S(1)}, bf16[2,3,64,128]{3,2,1,0:T(8,128)(2,1)S(1)}, u32[]{:S(2)}, u32[]{:S(2)}) collective-permute-start(bf16[2,3,64,128]{3,2,1,0:T(8,128)(2,1)S(1)} %get-tuple-element.57.refs_4_), channel_id=1, source_target_pairs={{0,2},{1,3},{2,0},{3,1},{4,6},{5,7},{6,4},{7,5},{8,10},{9,11},{10,... | collective-permute-start | bytes 294920 | tf_op jit(solution)/shard_map/ppermute | solution.py:576
  22.6 9.7 %collective-permute-start.7 = (bf16[2,3,64,128]{3,2,1,0:T(8,128)(2,1)S(1)}, bf16[2,3,64,128]{3,2,1,0:T(8,128)(2,1)S(1)}, u32[]{:S(2)}, u32[]{:S(2)}) collective-permute-start(bf16[2,3,64,128]{3,2,1,0:T(8,128)(2,1)S(1)} %get-tuple-element.57.refs_4_), channel_id=1, source_target_pairs={{0,1},{1,2},{2,3},{3,0},{4,5},{5,6},{6,7},{7,4},{8,9},{9,10},{10,1... | collective-permute-start | bytes 294920 | tf_op jit(solution)/shard_map/ppermute | solution.py:576
  23.8 18.9 %collective-permute-start.6 = (bf16[2,2,3,64,128]{4,3,2,1,0:T(8,128)(2,1)S(1)}, bf16[2,2,3,64,128]{4,3,2,1,0:T(8,128)(2,1)S(1)}, u32[]{:S(2)}, u32[]{:S(2)}) collective-permute-start(bf16[2,2,3,64,128]{4,3,2,1,0:T(8,128)(2,1)S(1)} %pad_maximum_fusion.refs_0_), channel_id=1, source_target_pairs={{0,3},{1,0},{2,1},{3,2},{4,7},{5,4},{6,5},{7,6},{8,11},{9,8},{10,9... | collective-permute-start | bytes 589832 | tf_op jit(solution)/shard_map/ppermute | solution.py:576
  26.5 22.3 %collective-permute-start.5 = (bf16[2,2,3,64,128]{4,3,2,1,0:T(8,128)(2,1)S(1)}, bf16[2,2,3,64,128]{4,3,2,1,0:T(8,128)(2,1)S(1)}, u32[]{:S(2)}, u32[]{:S(2)}) collective-permute-start(bf16[2,2,3,64,128]{4,3,2,1,0:T(8,128)(2,1)S(1)} %pad_maximum_fusion.refs_0_), channel_id=1, source_target_pairs={{0,2},{1,3},{2,0},{3,1},{4,6},{5,7},{6,4},{7,5},{8,10},{9,11},{10,... | collective-permute-start | bytes 589832 | tf_op jit(solution)/shard_map/ppermute | solution.py:576
  26.8 5.5 %copy-start.10 = (bf16[2,3,64,128]{3,2,1,0:T(8,128)(2,1)}, bf16[2,3,64,128]{3,2,1,0:T(8,128)(2,1)S(1)}, u32[]{:S(2)}) copy-start(bf16[2,3,64,128]{3,2,1,0:T(8,128)(2,1)S(1)} %collective-permute-done.9.refs_7_) | copy-start | bytes 294916
  26.8 22.0 %collective-permute-start.4 = (bf16[2,2,3,64,128]{4,3,2,1,0:T(8,128)(2,1)S(1)}, bf16[2,2,3,64,128]{4,3,2,1,0:T(8,128)(2,1)S(1)}, u32[]{:S(2)}, u32[]{:S(2)}) collective-permute-start(bf16[2,2,3,64,128]{4,3,2,1,0:T(8,128)(2,1)S(1)} %pad_maximum_fusion.refs_0_), channel_id=1, source_target_pairs={{0,1},{1,2},{2,3},{3,0},{4,5},{5,6},{6,7},{7,4},{8,9},{9,10},{10,1... | collective-permute-start | bytes 589832 | tf_op jit(solution)/shard_map/ppermute | solution.py:576
  32.3 0.6 copy-start.11
  32.3 0.7 copy-start.12
  32.9 15.9 %copy-start.1 = (bf16[4,256,256]{2,1,0:T(8,128)(2,1)S(1)}, bf16[4,256,256]{2,1,0:T(8,128)(2,1)}, u32[]{:S(2)}) copy-start(bf16[4,256,256]{2,1,0:T(8,128)(2,1)} %constant.38.refs_10_.refs_6_.tabs_hbm) | copy-start | bytes 1572868
  32.9 15.9 %copy-start.4 = (s32[72]{0:T(128)S(1)}, s32[72]{0:T(128)}, u32[]{:S(2)}) copy-start(s32[72]{0:T(128)} %get-tuple-element.31.meta_ref) | copy-start | bytes 868
  42.6 19.3 %copy-start = (f32[256,512]{1,0:T(8,128)S(1)}, f32[256,512]{1,0:T(8,128)}, u32[]{:S(2)}) copy-start(f32[256,512]{1,0:T(8,128)} %probe_hbm.1) | copy-start | bytes 1572868
  42.7 19.3 %copy-start.2 = (f32[2,256,256]{2,1,0:T(8,128)S(1)}, f32[2,256,256]{2,1,0:T(8,128)}, u32[]{:S(2)}) copy-start(f32[2,256,256]{2,1,0:T(8,128)} %constant.27.clone.refs_9_.kernel_hbm) | copy-start | bytes 1572868
  61.8 8.2 %collective-permute-start.10 = (bf16[2,3,256,128]{3,2,1,0:T(8,128)(2,1)S(1)}, bf16[2,3,256,128]{3,2,1,0:T(8,128)(2,1)S(1)}, u32[]{:S(2)}, u32[]{:S(2)}) collective-permute-start(bf16[2,3,256,128]{3,2,1,0:T(8,128)(2,1)S(1)} %get-tuple-element.43), channel_id=1, source_target_pairs={{0,4},{4,8},{8,12},{12,16},{16,20},{20,24},{24,28},{28,0},{1,5},{5... | collective-permute-start | bytes 1179656 | tf_op jit(solution)/shard_map/ppermute | solution.py:576
  61.9 8.1 %copy-start.3 = (s32[3]{0:T(128)S(1)}, s32[3]{0:T(128)}, u32[]{:S(2)}) copy-start(s32[3]{0:T(128)} %pad_add_fusion.here_ref) | copy-start | bytes 40
  70.6 9.0 %collective-permute-start.11 = (bf16[2,3,256,128]{3,2,1,0:T(8,128)(2,1)S(1)}, bf16[2,3,256,128]{3,2,1,0:T(8,128)(2,1)S(1)}, u32[]{:S(2)}, u32[]{:S(2)}) collective-permute-start(bf16[2,3,256,128]{3,2,1,0:T(8,128)(2,1)S(1)} %get-tuple-element.48), channel_id=1, source_target_pairs={{0,4},{4,8},{8,12},{12,16},{16,20},{20,24},{24,28},{28,0},{1,5},{5... | collective-permute-start | bytes 1179656 | tf_op jit(solution)/shard_map/ppermute | solution.py:576
  72.3 11.4 %collective-permute-start.15 = (bf16[2,3,64,128]{3,2,1,0:T(8,128)(2,1)S(1)}, bf16[2,3,64,128]{3,2,1,0:T(8,128)(2,1)S(1)}, u32[]{:S(2)}, u32[]{:S(2)}) collective-permute-start(bf16[2,3,64,128]{3,2,1,0:T(8,128)(2,1)S(1)} %get-tuple-element.54), channel_id=1, source_target_pairs={{0,1},{1,2},{2,3},{3,0},{4,5},{5,6},{6,7},{7,4},{8,9},{9,10},{10,1... | collective-permute-start | bytes 294920 | tf_op jit(solution)/shard_map/ppermute | solution.py:576
  73.1 13.5 %collective-permute-start.16 = (bf16[2,3,64,128]{3,2,1,0:T(8,128)(2,1)S(1)}, bf16[2,3,64,128]{3,2,1,0:T(8,128)(2,1)S(1)}, u32[]{:S(2)}, u32[]{:S(2)}) collective-permute-start(bf16[2,3,64,128]{3,2,1,0:T(8,128)(2,1)S(1)} %get-tuple-element.55), channel_id=1, source_target_pairs={{0,2},{1,3},{2,0},{3,1},{4,6},{5,7},{6,4},{7,5},{8,10},{9,11},{10,... | collective-permute-start | bytes 294920 | tf_op jit(solution)/shard_map/ppermute | solution.py:576
  76.7 10.0 %collective-permute-start.17 = (bf16[2,3,64,128]{3,2,1,0:T(8,128)(2,1)S(1)}, bf16[2,3,64,128]{3,2,1,0:T(8,128)(2,1)S(1)}, u32[]{:S(2)}, u32[]{:S(2)}) collective-permute-start(bf16[2,3,64,128]{3,2,1,0:T(8,128)(2,1)S(1)} %get-tuple-element.56), channel_id=1, source_target_pairs={{0,3},{1,0},{2,1},{3,2},{4,7},{5,4},{6,5},{7,6},{8,11},{9,8},{10,9... | collective-permute-start | bytes 294920 | tf_op jit(solution)/shard_map/ppermute | solution.py:576
  80.2 7.5 %collective-permute-start.12 = (bf16[2,3,64,128]{3,2,1,0:T(8,128)(2,1)S(1)}, bf16[2,3,64,128]{3,2,1,0:T(8,128)(2,1)S(1)}, u32[]{:S(2)}, u32[]{:S(2)}) collective-permute-start(bf16[2,3,64,128]{3,2,1,0:T(8,128)(2,1)S(1)} %get-tuple-element.50), channel_id=1, source_target_pairs={{0,1},{1,2},{2,3},{3,0},{4,5},{5,6},{6,7},{7,4},{8,9},{9,10},{10,1... | collective-permute-start | bytes 294920 | tf_op jit(solution)/shard_map/ppermute | solution.py:576
  81.8 9.7 %collective-permute-start.13 = (bf16[2,3,64,128]{3,2,1,0:T(8,128)(2,1)S(1)}, bf16[2,3,64,128]{3,2,1,0:T(8,128)(2,1)S(1)}, u32[]{:S(2)}, u32[]{:S(2)}) collective-permute-start(bf16[2,3,64,128]{3,2,1,0:T(8,128)(2,1)S(1)} %get-tuple-element.51), channel_id=1, source_target_pairs={{0,2},{1,3},{2,0},{3,1},{4,6},{5,7},{6,4},{7,5},{8,10},{9,11},{10,... | collective-permute-start | bytes 294920 | tf_op jit(solution)/shard_map/ppermute | solution.py:576
  83.8 7.8 %collective-permute-start.14 = (bf16[2,3,64,128]{3,2,1,0:T(8,128)(2,1)S(1)}, bf16[2,3,64,128]{3,2,1,0:T(8,128)(2,1)S(1)}, u32[]{:S(2)}, u32[]{:S(2)}) collective-permute-start(bf16[2,3,64,128]{3,2,1,0:T(8,128)(2,1)S(1)} %get-tuple-element.52), channel_id=1, source_target_pairs={{0,3},{1,0},{2,1},{3,2},{4,7},{5,4},{6,5},{7,6},{8,11},{9,8},{10,9... | collective-permute-start | bytes 294920 | tf_op jit(solution)/shard_map/ppermute | solution.py:576

commit v8 on v7

--- a/solution.py
+++ b/solution.py
@@ -225,7 +225,7 @@
     for j in (0, 1):
         for plane in (0, 1):
             place = (plane, col + j, pl.ds(top + start, count), slice(None))
-            totals_ref[place] += term[j][plane]
+            totals_ref[place] += term[j][plane].astype(f32)
 
 
 def route_kernel(
@@ -404,11 +404,12 @@
             for start in range(0, extent, CHUNK):
                 rows = slice(start, start + CHUNK)
                 part = rows_of(grad, start, CHUNK)
-                wave = halves((wave_buf[slot, i, 0, rows].astype(f32), wave_buf[slot, i, 1, rows].astype(f32)))
-                term = [product_conj(p, q) for p, q in zip(wave, part)]
+                wave = halves((wave_buf[slot, i, 0, rows], wave_buf[slot, i, 1, rows]))
+                short = [cut(side) for side in part]
+                term = [product_conj(p, q) for p, q in zip(wave, short)]
                 add_window(totals_ref, target, col, term, start)
                 w = window(rows_ref, top + start, col, CHUNK)
-                back = folded(tuple(product_conj(cut(p), cut(q)) for p, q in zip(w, part)))
+                back = folded(tuple(product_conj(cut(p), q) for p, q in zip(w, short)))
                 for k in (0, 1):
                     back_ref[at, k, rows] = back[k]
 

time: 93.1 us -> 93.2 us (level)
  no operation moved by 1% of the time
where the time goes in v8:
time: 93.2 us; the launch traced here: 92.7 us
  Pallas kernels  38.1 us (41%)
  starting transfers between devices  34.6 us (37%)
  waiting for transfers between devices  17.4 us (19%)
  other arithmetic  1.6 us (2%)
    pallas_call x7, Pallas kernels, call(): pl.pallas_call(kernel, in_specs=in_specs, out_specs=out_specs, out_shape=...  38.1 us
    ppermute x18, starting transfers between devices, passed_along(): return lax.ppermute(value, axis, pairs)  30.2 us
    ppermute x18, waiting for transfers between devices, passed_along(): return lax.ppermute(value, axis, pairs)  17.4 us
    all_to_all x1, starting transfers between devices, shards(): lax.all_to_all(packed, 'tile', split_axis=0, concat_axis=0, tiled=True)  4.36 us
  transfers between devices with their start and end apart: 19, of which 5 were waited for; matrix products, arithmetic and copies ran while one was open for 1% of the time, Pallas kernels for 25%

profile of v8, /device:TPU:0, one launch (start us, length us, event | category | flops | bytes accessed | tf_op | source)
XLA Modules:
  0.0 92.7 jit_solution(16312542760408358089)
XLA Ops:
  0.0 1.0 %bitcast_bitcast_fusion = bf16[2,2,3,64,128]{4,3,2,1,0:T(8,128)(2,1)S(1)} fusion(f32[2,2,64,384]{3,2,1,0:T(8,128)} %param.13), kind=kLoop, calls=%fused_computation | loop fusion | flops 98304 | bytes 589824 | tf_op jit(solution)/shard_map/convert_element_type | solution.py:592
  1.1 0.0 copy-start.5
  1.1 5.1 %collective-permute-start.3 = (bf16[2,3,64,128]{3,2,1,0:T(8,128)(2,1)S(1)}, bf16[2,3,64,128]{3,2,1,0:T(8,128)(2,1)S(1)}, u32[]{:S(2)}, u32[]{:S(2)}) collective-permute-start(bf16[2,3,64,128]{3,2,1,0:T(8,128)(2,1)S(1)} %get-tuple-element.34.refs_0_), channel_id=1, source_target_pairs={{0,3},{1,0},{2,1},{3,2},{4,7},{5,4},{6,5},{7,6},{8,11},{9,8},{10,9... | collective-permute-start | bytes 294920 | tf_op jit(solution)/shard_map/ppermute | solution.py:577
  6.2 0.0 collective-permute-start.2
  6.2 1.0 %collective-permute-start.1 = (bf16[2,3,64,128]{3,2,1,0:T(8,128)(2,1)S(1)}, bf16[2,3,64,128]{3,2,1,0:T(8,128)(2,1)S(1)}, u32[]{:S(2)}, u32[]{:S(2)}) collective-permute-start(bf16[2,3,64,128]{3,2,1,0:T(8,128)(2,1)S(1)} %get-tuple-element.34.refs_0_), channel_id=1, source_target_pairs={{0,1},{1,2},{2,3},{3,0},{4,5},{5,6},{6,7},{7,4},{8,9},{9,10},{10,1... | collective-permute-start | bytes 294920 | tf_op jit(solution)/shard_map/ppermute | solution.py:577
  7.2 1.0 %collective-permute-start = (bf16[2,2,3,64,128]{4,3,2,1,0:T(8,128)(2,1)S(1)}, bf16[2,2,3,64,128]{4,3,2,1,0:T(8,128)(2,1)S(1)}, u32[]{:S(2)}, u32[]{:S(2)}) collective-permute-start(bf16[2,2,3,64,128]{4,3,2,1,0:T(8,128)(2,1)S(1)} %bitcast_bitcast_fusion), channel_id=1, source_target_pairs={{0,28},{4,0},{8,4},{12,8},{16,12},{20,16},{24,20},{28,24},{1,29},{... | collective-permute-start | bytes 589832 | tf_op jit(solution)/shard_map/ppermute | solution.py:577
  8.2 0.6 pad_add_fusion.here_ref
  8.8 5.3 %route.1 = (bf16[16,256,256]{2,1,0:T(8,128)(2,1)}, s32[72]{0:T(128)}) custom-call(s32[3]{0:T(128)} %pad_add_fusion.here_ref, s32[448]{0:T(512)} %owner_hbm.1, s32[448]{0:T(512)} %row_hbm.1, s32[448]{0:T(512)} %col_hbm.1, bf16[14,256,256]{2,1,0:T(8,128)(2,1)} %images_hbm.1, bf16[2,256,256]{2,1,0:T(8,128)(2,1)} %constant.33.permute_hbm), custom_call_target="tpu_custom_call" | custom-call | flops 1073741824 | tf_op jit(solution)/shard_map/route/pallas_call | solution.py:458
  14.1 0.0 collective-permute-done.3.refs_3_
  14.1 0.0 copy-start.7
  14.1 0.8 collective-permute-done.2.refs_2_
  14.9 0.0 collective-permute-done.1.refs_1_
  14.9 0.0 collective-permute-done
  14.9 0.0 copy-done.5
  14.9 4.4 %all-to-all-start = ((bf16[16,256,256]{2,1,0:T(8,128)(2,1)}), bf16[16,256,256]{2,1,0:T(8,128)(2,1)}, u32[]{:S(2)}, u32[]{:S(2)}) async-start(bf16[16,256,256]{2,1,0:T(8,128)(2,1)} %get-tuple-element.38), calls=%async_computation | async-start | bytes 4194304 | tf_op jit(solution)/shard_map/all_to_all | solution.py:604
  19.3 0.0 copy-start.6
  19.3 2.3 %collective-permute-start.9 = (bf16[2,3,64,128]{3,2,1,0:T(8,128)(2,1)S(1)}, bf16[2,3,64,128]{3,2,1,0:T(8,128)(2,1)S(1)}, u32[]{:S(2)}, u32[]{:S(2)}) collective-permute-start(bf16[2,3,64,128]{3,2,1,0:T(8,128)(2,1)S(1)} %get-tuple-element.57.refs_4_), channel_id=1, source_target_pairs={{0,3},{1,0},{2,1},{3,2},{4,7},{5,4},{6,5},{7,6},{8,11},{9,8},{10,9... | collective-permute-start | bytes 294920 | tf_op jit(solution)/shard_map/ppermute | solution.py:577
  21.7 0.9 collective-permute-start.8
  22.6 1.1 %collective-permute-start.7 = (bf16[2,3,64,128]{3,2,1,0:T(8,128)(2,1)S(1)}, bf16[2,3,64,128]{3,2,1,0:T(8,128)(2,1)S(1)}, u32[]{:S(2)}, u32[]{:S(2)}) collective-permute-start(bf16[2,3,64,128]{3,2,1,0:T(8,128)(2,1)S(1)} %get-tuple-element.57.refs_4_), channel_id=1, source_target_pairs={{0,1},{1,2},{2,3},{3,0},{4,5},{5,6},{6,7},{7,4},{8,9},{9,10},{10,1... | collective-permute-start | bytes 294920 | tf_op jit(solution)/shard_map/ppermute | solution.py:577
  23.7 0.0 copy-done.7
  23.7 0.0 copy-done.8
  23.7 0.0 copy-done.9
  23.8 2.7 %collective-permute-start.6 = (bf16[2,2,3,64,128]{4,3,2,1,0:T(8,128)(2,1)S(1)}, bf16[2,2,3,64,128]{4,3,2,1,0:T(8,128)(2,1)S(1)}, u32[]{:S(2)}, u32[]{:S(2)}) collective-permute-start(bf16[2,2,3,64,128]{4,3,2,1,0:T(8,128)(2,1)S(1)} %pad_maximum_fusion.refs_0_), channel_id=1, source_target_pairs={{0,3},{1,0},{2,1},{3,2},{4,7},{5,4},{6,5},{7,6},{8,11},{9,8},{10,9... | collective-permute-start | bytes 589832 | tf_op jit(solution)/shard_map/ppermute | solution.py:577
  26.5 0.3 collective-permute-start.5
  26.8 0.0 collective-permute-done.9.refs_7_
  26.8 0.4 collective-permute-start.4
  27.1 5.1 %collective-permute-done.8.refs_6_ = bf16[2,3,64,128]{3,2,1,0:T(8,128)(2,1)S(1)} collective-permute-done((bf16[2,3,64,128]{3,2,1,0:T(8,128)(2,1)S(1)}, bf16[2,3,64,128]{3,2,1,0:T(8,128)(2,1)S(1)}, u32[]{:S(2)}, u32[]{:S(2)}) %collective-permute-start.8) | collective-permute-done | bytes 98336 | tf_op jit(solution)/shard_map/ppermute | solution.py:577
  32.3 0.0 collective-permute-done.7.refs_5_
  32.3 0.0 copy-done.6
  32.3 0.0 copy-done.10
  32.3 0.6 copy-done.11
  32.9 0.0 copy-done.12
  33.0 9.7 %waves.1.refs_4_ = bf16[4,4,2,256,256]{4,3,2,1,0:T(8,128)(2,1)} custom-call(s32[72]{0:T(128)} %get-tuple-element.31.meta_ref, bf16[2,3,64,128]{3,2,1,0:T(8,128)(2,1)} %copy-done.5, bf16[2,3,64,128]{3,2,1,0:T(8,128)(2,1)} %copy-done.9, bf16[2,3,64,128]{3,2,1,0:T(8,128)(2,1)} %copy-done.8, bf16[2,3,64,128]{3,2,1,0:T(8,128)(2,1)} %copy-done.7, ...), custom_call_target="tpu_custom_call" | custom-call | flops 8589934592 | tf_op jit(solution)/shard_map/waves/pallas_call | solution.py:458
  42.7 0.0 copy-start
  42.7 0.0 copy-start.2
  42.7 0.0 collective-permute-done.6.refs_3_
  42.7 6.1 %collective-permute-done.5.refs_2_ = bf16[2,2,3,64,128]{4,3,2,1,0:T(8,128)(2,1)S(1)} collective-permute-done((bf16[2,2,3,64,128]{4,3,2,1,0:T(8,128)(2,1)S(1)}, bf16[2,2,3,64,128]{4,3,2,1,0:T(8,128)(2,1)S(1)}, u32[]{:S(2)}, u32[]{:S(2)}) %collective-permute-start.5) | collective-permute-done | bytes 196640 | tf_op jit(solution)/shard_map/ppermute | solution.py:577
  48.8 0.0 collective-permute-done.4.refs_1_
  48.8 0.0 all-to-all-done.refs_5_
  48.8 0.0 copy-done.1
  48.8 0.0 copy-done.4
  48.8 13.1 %misfits.1 = (bf16[16,2,256,256]{3,2,1,0:T(8,128)(2,1)S(1)}, f32[2,3,768,128]{3,2,1,0:T(8,128)S(1)}, bf16[2,3,256,128]{3,2,1,0:T(8,128)(2,1)S(1)}) custom-call(s32[72]{0:T(128)S(1)} %copy-done.4, bf16[2,2,3,64,128]{4,3,2,1,0:T(8,128)(2,1)S(1)} %pad_maximum_fusion.refs_0_, bf16[2,2,3,64,128]{4,3,2,1,0:T(8,128)(2,1)S(1)} %collective-permute-done.4.refs_1_, ...), custom_call_target="tpu_custom_call" | custom-call | flops 8589934592 | tf_op jit(solution)/shard_map/misfits/pallas_call | solution.py:458
  61.9 0.1 collective-permute-start.10
  62.0 0.0 copy-done
  62.0 8.0 %exits.1 = (f32[2,3,768,128]{3,2,1,0:T(8,128)S(1)}, bf16[2,3,256,128]{3,2,1,0:T(8,128)(2,1)S(1)}) custom-call(s32[72]{0:T(128)S(1)} %copy-done.4, bf16[16,2,256,256]{3,2,1,0:T(8,128)(2,1)S(1)} %get-tuple-element.39.fields_ref, f32[256,512]{1,0:T(8,128)S(1)} %copy-done, f32[2,256,256]{2,1,0:T(8,128)S(1)} %copy-done.2, bf16[4,256,256]{2,1,0:T(8,128)(2,1)S(1)} %copy-done.1), custom_call_target="tpu_custom_call" | custom-call | flops 429496736 | tf_op jit(solution)/shard_map/exits/pallas_call | solution.py:458
  70.0 0.0 collective-permute-done.10.moved_ref
  70.1 0.0 copy-done.3
  70.1 0.6 combine.2
  70.7 1.8 %collective-permute-start.11 = (bf16[2,3,256,128]{3,2,1,0:T(8,128)(2,1)S(1)}, bf16[2,3,256,128]{3,2,1,0:T(8,128)(2,1)S(1)}, u32[]{:S(2)}, u32[]{:S(2)}) collective-permute-start(bf16[2,3,256,128]{3,2,1,0:T(8,128)(2,1)S(1)} %get-tuple-element.48), channel_id=1, source_target_pairs={{0,4},{4,8},{8,12},{12,16},{16,20},{20,24},{24,28},{28,0},{1,5},{5... | collective-permute-start | bytes 1179656 | tf_op jit(solution)/shard_map/ppermute | solution.py:577
  72.5 2.1 %collective-permute-start.15 = (bf16[2,3,64,128]{3,2,1,0:T(8,128)(2,1)S(1)}, bf16[2,3,64,128]{3,2,1,0:T(8,128)(2,1)S(1)}, u32[]{:S(2)}, u32[]{:S(2)}) collective-permute-start(bf16[2,3,64,128]{3,2,1,0:T(8,128)(2,1)S(1)} %get-tuple-element.54), channel_id=1, source_target_pairs={{0,1},{1,2},{2,3},{3,0},{4,5},{5,6},{6,7},{7,4},{8,9},{9,10},{10,1... | collective-permute-start | bytes 294920 | tf_op jit(solution)/shard_map/ppermute | solution.py:577
  74.6 2.0 %collective-permute-start.16 = (bf16[2,3,64,128]{3,2,1,0:T(8,128)(2,1)S(1)}, bf16[2,3,64,128]{3,2,1,0:T(8,128)(2,1)S(1)}, u32[]{:S(2)}, u32[]{:S(2)}) collective-permute-start(bf16[2,3,64,128]{3,2,1,0:T(8,128)(2,1)S(1)} %get-tuple-element.55), channel_id=1, source_target_pairs={{0,2},{1,3},{2,0},{3,1},{4,6},{5,7},{6,4},{7,5},{8,10},{9,11},{10,... | collective-permute-start | bytes 294920 | tf_op jit(solution)/shard_map/ppermute | solution.py:577
  76.6 2.9 %collective-permute-start.17 = (bf16[2,3,64,128]{3,2,1,0:T(8,128)(2,1)S(1)}, bf16[2,3,64,128]{3,2,1,0:T(8,128)(2,1)S(1)}, u32[]{:S(2)}, u32[]{:S(2)}) collective-permute-start(bf16[2,3,64,128]{3,2,1,0:T(8,128)(2,1)S(1)} %get-tuple-element.56), channel_id=1, source_target_pairs={{0,3},{1,0},{2,1},{3,2},{4,7},{5,4},{6,5},{7,6},{8,11},{9,8},{10,9... | collective-permute-start | bytes 294920 | tf_op jit(solution)/shard_map/ppermute | solution.py:577
  79.5 0.0 collective-permute-done.11.moved_ref
  79.5 0.6 combine.3
  80.1 1.4 %collective-permute-start.12 = (bf16[2,3,64,128]{3,2,1,0:T(8,128)(2,1)S(1)}, bf16[2,3,64,128]{3,2,1,0:T(8,128)(2,1)S(1)}, u32[]{:S(2)}, u32[]{:S(2)}) collective-permute-start(bf16[2,3,64,128]{3,2,1,0:T(8,128)(2,1)S(1)} %get-tuple-element.50), channel_id=1, source_target_pairs={{0,1},{1,2},{2,3},{3,0},{4,5},{5,6},{6,7},{7,4},{8,9},{9,10},{10,1... | collective-permute-start | bytes 294920 | tf_op jit(solution)/shard_map/ppermute | solution.py:577
  81.5 2.2 %collective-permute-start.13 = (bf16[2,3,64,128]{3,2,1,0:T(8,128)(2,1)S(1)}, bf16[2,3,64,128]{3,2,1,0:T(8,128)(2,1)S(1)}, u32[]{:S(2)}, u32[]{:S(2)}) collective-permute-start(bf16[2,3,64,128]{3,2,1,0:T(8,128)(2,1)S(1)} %get-tuple-element.51), channel_id=1, source_target_pairs={{0,2},{1,3},{2,0},{3,1},{4,6},{5,7},{6,4},{7,5},{8,10},{9,11},{10,... | collective-permute-start | bytes 294920 | tf_op jit(solution)/shard_map/ppermute | solution.py:577
  83.8 0.0 collective-permute-done.15.refs_5_
  83.8 2.8 %collective-permute-start.14 = (bf16[2,3,64,128]{3,2,1,0:T(8,128)(2,1)S(1)}, bf16[2,3,64,128]{3,2,1,0:T(8,128)(2,1)S(1)}, u32[]{:S(2)}, u32[]{:S(2)}) collective-permute-start(bf16[2,3,64,128]{3,2,1,0:T(8,128)(2,1)S(1)} %get-tuple-element.52), channel_id=1, source_target_pairs={{0,3},{1,0},{2,1},{3,2},{4,7},{5,4},{6,5},{7,6},{8,11},{9,8},{10,9... | collective-permute-start | bytes 294920 | tf_op jit(solution)/shard_map/ppermute | solution.py:577
  86.6 0.0 collective-permute-done.16.refs_6_
  86.6 0.0 collective-permute-done.17.refs_7_
  86.6 1.0 %collective-permute-done.12.refs_1_ = bf16[2,3,64,128]{3,2,1,0:T(8,128)(2,1)S(1)} collective-permute-done((bf16[2,3,64,128]{3,2,1,0:T(8,128)(2,1)S(1)}, bf16[2,3,64,128]{3,2,1,0:T(8,128)(2,1)S(1)}, u32[]{:S(2)}, u32[]{:S(2)}) %collective-permute-start.12) | collective-permute-done | bytes 98336 | tf_op jit(solution)/shard_map/ppermute | solution.py:577
  87.7 4.2 %collective-permute-done.13.refs_2_ = bf16[2,3,64,128]{3,2,1,0:T(8,128)(2,1)S(1)} collective-permute-done((bf16[2,3,64,128]{3,2,1,0:T(8,128)(2,1)S(1)}, bf16[2,3,64,128]{3,2,1,0:T(8,128)(2,1)S(1)}, u32[]{:S(2)}, u32[]{:S(2)}) %collective-permute-start.13) | collective-permute-done | bytes 98336 | tf_op jit(solution)/shard_map/ppermute | solution.py:577
  91.8 0.0 collective-permute-done.14.refs_3_
  91.8 0.8 finish.1
  (12 shorter events, 0.1 us)
Async XLA Ops:
  1.1 13.9 %copy-start.5 = (bf16[2,3,64,128]{3,2,1,0:T(8,128)(2,1)}, bf16[2,3,64,128]{3,2,1,0:T(8,128)(2,1)S(1)}, u32[]{:S(2)}) copy-start(bf16[2,3,64,128]{3,2,1,0:T(8,128)(2,1)S(1)} %get-tuple-element.34.refs_0_) | copy-start | bytes 294916
  1.1 13.0 %collective-permute-start.3 = (bf16[2,3,64,128]{3,2,1,0:T(8,128)(2,1)S(1)}, bf16[2,3,64,128]{3,2,1,0:T(8,128)(2,1)S(1)}, u32[]{:S(2)}, u32[]{:S(2)}) collective-permute-start(bf16[2,3,64,128]{3,2,1,0:T(8,128)(2,1)S(1)} %get-tuple-element.34.refs_0_), channel_id=1, source_target_pairs={{0,3},{1,0},{2,1},{3,2},{4,7},{5,4},{6,5},{7,6},{8,11},{9,8},{10,9... | collective-permute-start | bytes 294920 | tf_op jit(solution)/shard_map/ppermute | solution.py:577
  6.2 8.7 %collective-permute-start.2 = (bf16[2,3,64,128]{3,2,1,0:T(8,128)(2,1)S(1)}, bf16[2,3,64,128]{3,2,1,0:T(8,128)(2,1)S(1)}, u32[]{:S(2)}, u32[]{:S(2)}) collective-permute-start(bf16[2,3,64,128]{3,2,1,0:T(8,128)(2,1)S(1)} %get-tuple-element.34.refs_0_), channel_id=1, source_target_pairs={{0,2},{1,3},{2,0},{3,1},{4,6},{5,7},{6,4},{7,5},{8,10},{9,11},{10,... | collective-permute-start | bytes 294920 | tf_op jit(solution)/shard_map/ppermute | solution.py:577
  6.2 8.7 %collective-permute-start.1 = (bf16[2,3,64,128]{3,2,1,0:T(8,128)(2,1)S(1)}, bf16[2,3,64,128]{3,2,1,0:T(8,128)(2,1)S(1)}, u32[]{:S(2)}, u32[]{:S(2)}) collective-permute-start(bf16[2,3,64,128]{3,2,1,0:T(8,128)(2,1)S(1)} %get-tuple-element.34.refs_0_), channel_id=1, source_target_pairs={{0,1},{1,2},{2,3},{3,0},{4,5},{5,6},{6,7},{7,4},{8,9},{9,10},{10,1... | collective-permute-start | bytes 294920 | tf_op jit(solution)/shard_map/ppermute | solution.py:577
  7.2 7.7 %collective-permute-start = (bf16[2,2,3,64,128]{4,3,2,1,0:T(8,128)(2,1)S(1)}, bf16[2,2,3,64,128]{4,3,2,1,0:T(8,128)(2,1)S(1)}, u32[]{:S(2)}, u32[]{:S(2)}) collective-permute-start(bf16[2,2,3,64,128]{4,3,2,1,0:T(8,128)(2,1)S(1)} %bitcast_bitcast_fusion), channel_id=1, source_target_pairs={{0,28},{4,0},{8,4},{12,8},{16,12},{20,16},{24,20},{28,24},{1,29},{... | collective-permute-start | bytes 589832 | tf_op jit(solution)/shard_map/ppermute | solution.py:577
  14.1 9.7 %copy-start.7 = (bf16[2,3,64,128]{3,2,1,0:T(8,128)(2,1)}, bf16[2,3,64,128]{3,2,1,0:T(8,128)(2,1)S(1)}, u32[]{:S(2)}) copy-start(bf16[2,3,64,128]{3,2,1,0:T(8,128)(2,1)S(1)} %collective-permute-done.3.refs_3_) | copy-start | bytes 294916
  14.9 8.8 %copy-start.8 = (bf16[2,3,64,128]{3,2,1,0:T(8,128)(2,1)}, bf16[2,3,64,128]{3,2,1,0:T(8,128)(2,1)S(1)}, u32[]{:S(2)}) copy-start(bf16[2,3,64,128]{3,2,1,0:T(8,128)(2,1)S(1)} %collective-permute-done.2.refs_2_) | copy-start | bytes 294916
  14.9 8.8 %copy-start.9 = (bf16[2,3,64,128]{3,2,1,0:T(8,128)(2,1)}, bf16[2,3,64,128]{3,2,1,0:T(8,128)(2,1)S(1)}, u32[]{:S(2)}) copy-start(bf16[2,3,64,128]{3,2,1,0:T(8,128)(2,1)S(1)} %collective-permute-done.1.refs_1_) | copy-start | bytes 294916
  14.9 33.9 %all-to-all-start = ((bf16[16,256,256]{2,1,0:T(8,128)(2,1)}), bf16[16,256,256]{2,1,0:T(8,128)(2,1)}, u32[]{:S(2)}, u32[]{:S(2)}) async-start(bf16[16,256,256]{2,1,0:T(8,128)(2,1)} %get-tuple-element.38), calls=%async_computation | async-start | bytes 4194304 | tf_op jit(solution)/shard_map/all_to_all | solution.py:604
  19.3 13.0 %copy-start.6 = (bf16[2,3,64,128]{3,2,1,0:T(8,128)(2,1)}, bf16[2,3,64,128]{3,2,1,0:T(8,128)(2,1)S(1)}, u32[]{:S(2)}) copy-start(bf16[2,3,64,128]{3,2,1,0:T(8,128)(2,1)S(1)} %get-tuple-element.57.refs_4_) | copy-start | bytes 294916
  19.3 7.4 %collective-permute-start.9 = (bf16[2,3,64,128]{3,2,1,0:T(8,128)(2,1)S(1)}, bf16[2,3,64,128]{3,2,1,0:T(8,128)(2,1)S(1)}, u32[]{:S(2)}, u32[]{:S(2)}) collective-permute-start(bf16[2,3,64,128]{3,2,1,0:T(8,128)(2,1)S(1)} %get-tuple-element.57.refs_4_), channel_id=1, source_target_pairs={{0,3},{1,0},{2,1},{3,2},{4,7},{5,4},{6,5},{7,6},{8,11},{9,8},{10,9... | collective-permute-start | bytes 294920 | tf_op jit(solution)/shard_map/ppermute | solution.py:577
  21.7 10.6 %collective-permute-start.8 = (bf16[2,3,64,128]{3,2,1,0:T(8,128)(2,1)S(1)}, bf16[2,3,64,128]{3,2,1,0:T(8,128)(2,1)S(1)}, u32[]{:S(2)}, u32[]{:S(2)}) collective-permute-start(bf16[2,3,64,128]{3,2,1,0:T(8,128)(2,1)S(1)} %get-tuple-element.57.refs_4_), channel_id=1, source_target_pairs={{0,2},{1,3},{2,0},{3,1},{4,6},{5,7},{6,4},{7,5},{8,10},{9,11},{10,... | collective-permute-start | bytes 294920 | tf_op jit(solution)/shard_map/ppermute | solution.py:577
  22.6 9.7 %collective-permute-start.7 = (bf16[2,3,64,128]{3,2,1,0:T(8,128)(2,1)S(1)}, bf16[2,3,64,128]{3,2,1,0:T(8,128)(2,1)S(1)}, u32[]{:S(2)}, u32[]{:S(2)}) collective-permute-start(bf16[2,3,64,128]{3,2,1,0:T(8,128)(2,1)S(1)} %get-tuple-element.57.refs_4_), channel_id=1, source_target_pairs={{0,1},{1,2},{2,3},{3,0},{4,5},{5,6},{6,7},{7,4},{8,9},{9,10},{10,1... | collective-permute-start | bytes 294920 | tf_op jit(solution)/shard_map/ppermute | solution.py:577
  23.8 18.9 %collective-permute-start.6 = (bf16[2,2,3,64,128]{4,3,2,1,0:T(8,128)(2,1)S(1)}, bf16[2,2,3,64,128]{4,3,2,1,0:T(8,128)(2,1)S(1)}, u32[]{:S(2)}, u32[]{:S(2)}) collective-permute-start(bf16[2,2,3,64,128]{4,3,2,1,0:T(8,128)(2,1)S(1)} %pad_maximum_fusion.refs_0_), channel_id=1, source_target_pairs={{0,3},{1,0},{2,1},{3,2},{4,7},{5,4},{6,5},{7,6},{8,11},{9,8},{10,9... | collective-permute-start | bytes 589832 | tf_op jit(solution)/shard_map/ppermute | solution.py:577
  26.5 22.3 %collective-permute-start.5 = (bf16[2,2,3,64,128]{4,3,2,1,0:T(8,128)(2,1)S(1)}, bf16[2,2,3,64,128]{4,3,2,1,0:T(8,128)(2,1)S(1)}, u32[]{:S(2)}, u32[]{:S(2)}) collective-permute-start(bf16[2,2,3,64,128]{4,3,2,1,0:T(8,128)(2,1)S(1)} %pad_maximum_fusion.refs_0_), channel_id=1, source_target_pairs={{0,2},{1,3},{2,0},{3,1},{4,6},{5,7},{6,4},{7,5},{8,10},{9,11},{10,... | collective-permute-start | bytes 589832 | tf_op jit(solution)/shard_map/ppermute | solution.py:577
  26.8 5.5 %copy-start.10 = (bf16[2,3,64,128]{3,2,1,0:T(8,128)(2,1)}, bf16[2,3,64,128]{3,2,1,0:T(8,128)(2,1)S(1)}, u32[]{:S(2)}) copy-start(bf16[2,3,64,128]{3,2,1,0:T(8,128)(2,1)S(1)} %collective-permute-done.9.refs_7_) | copy-start | bytes 294916
  26.8 22.1 %collective-permute-start.4 = (bf16[2,2,3,64,128]{4,3,2,1,0:T(8,128)(2,1)S(1)}, bf16[2,2,3,64,128]{4,3,2,1,0:T(8,128)(2,1)S(1)}, u32[]{:S(2)}, u32[]{:S(2)}) collective-permute-start(bf16[2,2,3,64,128]{4,3,2,1,0:T(8,128)(2,1)S(1)} %pad_maximum_fusion.refs_0_), channel_id=1, source_target_pairs={{0,1},{1,2},{2,3},{3,0},{4,5},{5,6},{6,7},{7,4},{8,9},{9,10},{10,1... | collective-permute-start | bytes 589832 | tf_op jit(solution)/shard_map/ppermute | solution.py:577
  32.3 0.6 copy-start.11
  32.3 0.7 copy-start.12
  33.0 15.9 %copy-start.1 = (bf16[4,256,256]{2,1,0:T(8,128)(2,1)S(1)}, bf16[4,256,256]{2,1,0:T(8,128)(2,1)}, u32[]{:S(2)}) copy-start(bf16[4,256,256]{2,1,0:T(8,128)(2,1)} %constant.38.refs_10_.refs_6_.tabs_hbm) | copy-start | bytes 1572868
  33.0 15.9 %copy-start.4 = (s32[72]{0:T(128)S(1)}, s32[72]{0:T(128)}, u32[]{:S(2)}) copy-start(s32[72]{0:T(128)} %get-tuple-element.31.meta_ref) | copy-start | bytes 868
  42.7 19.3 %copy-start = (f32[256,512]{1,0:T(8,128)S(1)}, f32[256,512]{1,0:T(8,128)}, u32[]{:S(2)}) copy-start(f32[256,512]{1,0:T(8,128)} %probe_hbm.1) | copy-start | bytes 1572868
  42.7 19.3 %copy-start.2 = (f32[2,256,256]{2,1,0:T(8,128)S(1)}, f32[2,256,256]{2,1,0:T(8,128)}, u32[]{:S(2)}) copy-start(f32[2,256,256]{2,1,0:T(8,128)} %constant.27.clone.refs_9_.kernel_hbm) | copy-start | bytes 1572868
  61.9 8.2 %collective-permute-start.10 = (bf16[2,3,256,128]{3,2,1,0:T(8,128)(2,1)S(1)}, bf16[2,3,256,128]{3,2,1,0:T(8,128)(2,1)S(1)}, u32[]{:S(2)}, u32[]{:S(2)}) collective-permute-start(bf16[2,3,256,128]{3,2,1,0:T(8,128)(2,1)S(1)} %get-tuple-element.43), channel_id=1, source_target_pairs={{0,4},{4,8},{8,12},{12,16},{16,20},{20,24},{24,28},{28,0},{1,5},{5... | collective-permute-start | bytes 1179656 | tf_op jit(solution)/shard_map/ppermute | solution.py:577
  62.0 8.1 %copy-start.3 = (s32[3]{0:T(128)S(1)}, s32[3]{0:T(128)}, u32[]{:S(2)}) copy-start(s32[3]{0:T(128)} %pad_add_fusion.here_ref) | copy-start | bytes 40
  70.7 8.8 %collective-permute-start.11 = (bf16[2,3,256,128]{3,2,1,0:T(8,128)(2,1)S(1)}, bf16[2,3,256,128]{3,2,1,0:T(8,128)(2,1)S(1)}, u32[]{:S(2)}, u32[]{:S(2)}) collective-permute-start(bf16[2,3,256,128]{3,2,1,0:T(8,128)(2,1)S(1)} %get-tuple-element.48), channel_id=1, source_target_pairs={{0,4},{4,8},{8,12},{12,16},{16,20},{20,24},{24,28},{28,0},{1,5},{5... | collective-permute-start | bytes 1179656 | tf_op jit(solution)/shard_map/ppermute | solution.py:577
  72.5 11.3 %collective-permute-start.15 = (bf16[2,3,64,128]{3,2,1,0:T(8,128)(2,1)S(1)}, bf16[2,3,64,128]{3,2,1,0:T(8,128)(2,1)S(1)}, u32[]{:S(2)}, u32[]{:S(2)}) collective-permute-start(bf16[2,3,64,128]{3,2,1,0:T(8,128)(2,1)S(1)} %get-tuple-element.54), channel_id=1, source_target_pairs={{0,1},{1,2},{2,3},{3,0},{4,5},{5,6},{6,7},{7,4},{8,9},{9,10},{10,1... | collective-permute-start | bytes 294920 | tf_op jit(solution)/shard_map/ppermute | solution.py:577
  74.6 12.0 %collective-permute-start.16 = (bf16[2,3,64,128]{3,2,1,0:T(8,128)(2,1)S(1)}, bf16[2,3,64,128]{3,2,1,0:T(8,128)(2,1)S(1)}, u32[]{:S(2)}, u32[]{:S(2)}) collective-permute-start(bf16[2,3,64,128]{3,2,1,0:T(8,128)(2,1)S(1)} %get-tuple-element.55), channel_id=1, source_target_pairs={{0,2},{1,3},{2,0},{3,1},{4,6},{5,7},{6,4},{7,5},{8,10},{9,11},{10,... | collective-permute-start | bytes 294920 | tf_op jit(solution)/shard_map/ppermute | solution.py:577
  76.6 10.0 %collective-permute-start.17 = (bf16[2,3,64,128]{3,2,1,0:T(8,128)(2,1)S(1)}, bf16[2,3,64,128]{3,2,1,0:T(8,128)(2,1)S(1)}, u32[]{:S(2)}, u32[]{:S(2)}) collective-permute-start(bf16[2,3,64,128]{3,2,1,0:T(8,128)(2,1)S(1)} %get-tuple-element.56), channel_id=1, source_target_pairs={{0,3},{1,0},{2,1},{3,2},{4,7},{5,4},{6,5},{7,6},{8,11},{9,8},{10,9... | collective-permute-start | bytes 294920 | tf_op jit(solution)/shard_map/ppermute | solution.py:577
  80.1 7.5 %collective-permute-start.12 = (bf16[2,3,64,128]{3,2,1,0:T(8,128)(2,1)S(1)}, bf16[2,3,64,128]{3,2,1,0:T(8,128)(2,1)S(1)}, u32[]{:S(2)}, u32[]{:S(2)}) collective-permute-start(bf16[2,3,64,128]{3,2,1,0:T(8,128)(2,1)S(1)} %get-tuple-element.50), channel_id=1, source_target_pairs={{0,1},{1,2},{2,3},{3,0},{4,5},{5,6},{6,7},{7,4},{8,9},{9,10},{10,1... | collective-permute-start | bytes 294920 | tf_op jit(solution)/shard_map/ppermute | solution.py:577
  81.5 10.3 %collective-permute-start.13 = (bf16[2,3,64,128]{3,2,1,0:T(8,128)(2,1)S(1)}, bf16[2,3,64,128]{3,2,1,0:T(8,128)(2,1)S(1)}, u32[]{:S(2)}, u32[]{:S(2)}) collective-permute-start(bf16[2,3,64,128]{3,2,1,0:T(8,128)(2,1)S(1)} %get-tuple-element.51), channel_id=1, source_target_pairs={{0,2},{1,3},{2,0},{3,1},{4,6},{5,7},{6,4},{7,5},{8,10},{9,11},{10,... | collective-permute-start | bytes 294920 | tf_op jit(solution)/shard_map/ppermute | solution.py:577
  83.8 8.0 %collective-permute-start.14 = (bf16[2,3,64,128]{3,2,1,0:T(8,128)(2,1)S(1)}, bf16[2,3,64,128]{3,2,1,0:T(8,128)(2,1)S(1)}, u32[]{:S(2)}, u32[]{:S(2)}) collective-permute-start(bf16[2,3,64,128]{3,2,1,0:T(8,128)(2,1)S(1)} %get-tuple-element.52), channel_id=1, source_target_pairs={{0,3},{1,0},{2,1},{3,2},{4,7},{5,4},{6,5},{7,6},{8,11},{9,8},{10,9... | collective-permute-start | bytes 294920 | tf_op jit(solution)/shard_map/ppermute | solution.py:577
